TPU v7x, 32 devices: a whole 2x2x4 slice. The times are simulated.
32 devices in a mesh: dp: 16 (over z, x, core), tensor: 2 (over y).
Axes of the slice: x: 2, y: 2, z: 4, core: 2. Of those that a mesh axis runs over, the one named last changes fastest.
Arguments:
- tokens: bfloat16 [12288, 2048], P(('dp', 'tensor')), may hold values from -6 to 6
- segments: int32 [16, 768], P('dp'), may hold values from 0 to 6, as said below
- q_weight: bfloat16 [2048, 2048], P('dp', 'tensor'), may hold values from -0.125 to 0.125
- k_weight: bfloat16 [2048, 256], P('dp', 'tensor'), may hold values from -0.125 to 0.125
- v_weight: bfloat16 [2048, 256], P('dp', 'tensor'), may hold values from -0.125 to 0.125
- o_weight: bfloat16 [2048, 2048], P('dp', 'tensor'), may hold values from -0.375 to 0.375
- attention_gain: float32 [2048], replicated, may hold values from 0.5 to 1.5
- gate_weight: bfloat16 [2048, 5632], P('dp', 'tensor'), may hold values from -0.125 to 0.125
- up_weight: bfloat16 [2048, 5632], P('dp', 'tensor'), may hold values from -0.125 to 0.125
- down_weight: bfloat16 [2048, 5632], P('dp', 'tensor'), may hold values from -0.109375 to 0.109375
- feed_gain: float32 [2048], replicated, may hold values from 0.5 to 1.5
- out_grad: bfloat16 [12288, 2048], P(('dp', 'tensor')), may hold values from -6 to 6
Outputs:
- block_out: bfloat16 [12288, 2048], P(('dp', 'tensor'))
- input_grad: bfloat16 [12288, 2048], P(('dp', 'tensor'))
- q_weight_grad: float32 [2048, 2048], P('dp', 'tensor')
- k_weight_grad: float32 [2048, 256], P('dp', 'tensor')
- v_weight_grad: float32 [2048, 256], P('dp', 'tensor')
- o_weight_grad: float32 [2048, 2048], P('dp', 'tensor')
- attention_gain_grad: float32 [2048], replicated
- gate_weight_grad: float32 [2048, 5632], P('dp', 'tensor')
- up_weight_grad: float32 [2048, 5632], P('dp', 'tensor')
- down_weight_grad: float32 [2048, 5632], P('dp', 'tensor')
- feed_gain_grad: float32 [2048], replicated
Inputs may be any that keep to these rules, and one draw needn't show every extreme that they name: `segments`: along each row the numbers never fall, begin at 0 and end at 6; the document holding places 768 / 2 - 1 and 384 of a row runs over more than 2 * (96) tokens.
All inputs are finite; a program needn't handle non-finite values.
Results may differ from a plain program's by a relative error of at most 0.015.
Values may be sent and summed in bfloat16 or wider, within the bound.
No kernel may reach another device: no remote copies, remote signals or barrier semaphores. Data moves between devices by JAX's collectives and lax.ppermute only.
A program may use at most 160 MiB of HBM per device.

v0:
```python
import jax
import jax.numpy as jnp
from jax import lax
from jax.sharding import PartitionSpec as P

HEAD_DIM = 64


epsilon = 1e-05
rope_base = 10000.0


def dot_plain(left_side, right_side):
    return jnp.dot(left_side, right_side, preferred_element_type=jnp.float32)


def dot_trans(left_side, right_side):
    return lax.dot_general(
        left_side, right_side, (((1,), (1,)), ((), ())), preferred_element_type=jnp.float32
    )


def dot_inner(left_side, right_side):
    return lax.dot_general(
        left_side, right_side, (((0,), (0,)), ((), ())), preferred_element_type=jnp.float32
    )


def rotary_tables(segment_row):
    length = segment_row.shape[0]
    before = jnp.sum((segment_row[None, :] < segment_row[:, None]).astype(jnp.int32), axis=1)
    places = (jnp.arange(length, dtype=jnp.int32) - before).astype(jnp.float32)
    half_dim = HEAD_DIM // 2
    frequency = rope_base ** (-2.0 * jnp.arange(half_dim).astype(jnp.float32) / HEAD_DIM)
    angles = places[:, None] * frequency[None, :]
    return (jnp.cos(angles)[:, None, :], jnp.sin(angles)[:, None, :])


def rotate(vectors, cosine_table, sine_table):
    half_dim = vectors.shape[-1] // 2
    first_half = vectors[..., :half_dim]
    second = vectors[..., half_dim:]
    return jnp.concatenate(
        [
            first_half * cosine_table - second * sine_table,
            second * cosine_table + first_half * sine_table,
        ],
        axis=-1,
    )


def inverse_rms(activity):
    return lax.rsqrt(jnp.mean(activity * activity, axis=-1, keepdims=True) + epsilon)


def norm_back(activity, inverse, gain_vec, incoming):
    scaled = incoming * gain_vec
    return inverse * scaled - activity * (inverse * inverse * inverse) * jnp.mean(
        scaled * activity, axis=-1, keepdims=True
    )


def attend_forward(query_group, key_one, value_one, allowed, score_scale):
    raw_scores = jnp.einsum("qgd,sd->gqs", query_group, key_one, preferred_element_type=jnp.float32)
    scores = jnp.where(allowed[None], raw_scores * score_scale, -1e30)
    row_max = jnp.max(scores, axis=-1, keepdims=True)
    powers = jnp.exp(scores - row_max)
    totals = jnp.sum(powers, axis=-1, keepdims=True)
    attend_prob = (powers / totals).astype(jnp.bfloat16)
    head_out = jnp.einsum("gqs,sd->qgd", attend_prob, value_one, preferred_element_type=jnp.float32)
    return (head_out, row_max + jnp.log(totals))


def attend_backward(query_group, key_one, value_one, log_total, grad_group, allowed, score_scale):
    raw_scores = jnp.einsum("qgd,sd->gqs", query_group, key_one, preferred_element_type=jnp.float32)
    scores = jnp.where(allowed[None], raw_scores * score_scale, -1e30)
    attend_prob = jnp.exp(scores - log_total)
    low_prob = attend_prob.astype(jnp.bfloat16)
    value_grad = jnp.einsum("gqs,qgd->sd", low_prob, grad_group, preferred_element_type=jnp.float32)
    prob_grad = jnp.einsum("qgd,sd->gqs", grad_group, value_one, preferred_element_type=jnp.float32)
    centre = jnp.sum(attend_prob * prob_grad, axis=-1, keepdims=True)
    score_grad = (attend_prob * (prob_grad - centre) * score_scale).astype(jnp.bfloat16)
    query_grad = jnp.einsum("gqs,sd->qgd", score_grad, key_one, preferred_element_type=jnp.float32)
    key_grad = jnp.einsum(
        "gqs,qgd->sd", score_grad, query_group, preferred_element_type=jnp.float32
    )
    return (query_grad, key_grad, value_grad)


def shards(
    tokens,
    segments,
    q_weight,
    k_weight,
    v_weight,
    o_weight,
    attention_gain,
    gate_weight,
    up_weight,
    down_weight,
    feed_gain,
    out_grad,
):
    query_width = q_weight.shape[1]
    key_width = k_weight.shape[1]
    hidden_width = gate_weight.shape[1]
    local_heads = query_width // HEAD_DIM
    local_kv = key_width // HEAD_DIM
    group_size = local_heads // local_kv
    score_scale = HEAD_DIM ** (-0.5)
    segment_row = segments[0]
    length = segment_row.shape[0]
    cosine_table, sine_table = rotary_tables(segment_row)
    places = jnp.arange(length)
    allowed = (segment_row[:, None] == segment_row[None, :]) & (places[:, None] >= places[None, :])
    inputs = tokens.astype(jnp.float32)
    inverse_first = inverse_rms(inputs)
    normed_first = (inputs * inverse_first * attention_gain).astype(jnp.bfloat16)
    query_full, key_full, value_full, output_full = (
        lax.all_gather(q_weight, "dp", axis=0, tiled=True),
        lax.all_gather(k_weight, "dp", axis=0, tiled=True),
        lax.all_gather(v_weight, "dp", axis=0, tiled=True),
        lax.all_gather(o_weight, "dp", axis=0, tiled=True),
    )
    normed_seq = lax.all_gather(normed_first, "tensor", axis=0, tiled=True)
    query_lin = dot_plain(normed_seq, query_full).reshape(length, local_heads, HEAD_DIM)
    key_lin = dot_plain(normed_seq, key_full).reshape(length, local_kv, HEAD_DIM)
    value_low = (
        dot_plain(normed_seq, value_full).astype(jnp.bfloat16).reshape(length, local_kv, HEAD_DIM)
    )
    query_rot = rotate(query_lin, cosine_table, sine_table).astype(jnp.bfloat16)
    key_rot = rotate(key_lin, cosine_table, sine_table).astype(jnp.bfloat16)
    query_stack = query_rot.reshape(length, local_kv, group_size, HEAD_DIM).transpose(1, 0, 2, 3)
    key_stack = key_rot.transpose(1, 0, 2)
    value_stack = value_low.transpose(1, 0, 2)

    def forward_head(stacked):
        return attend_forward(stacked[0], stacked[1], stacked[2], allowed, score_scale)

    head_outs, log_totals = lax.map(forward_head, (query_stack, key_stack, value_stack))
    mixed = head_outs.transpose(1, 0, 2, 3).reshape(length, query_width).astype(jnp.bfloat16)
    middle = inputs + lax.psum_scatter(
        dot_trans(mixed, output_full), "tensor", scatter_dimension=0, tiled=True
    )
    inverse_second = inverse_rms(middle)
    normed_second = (middle * inverse_second * feed_gain).astype(jnp.bfloat16)
    gate_full, up_full, down_full = (
        lax.all_gather(gate_weight, "dp", axis=0, tiled=True),
        lax.all_gather(up_weight, "dp", axis=0, tiled=True),
        lax.all_gather(down_weight, "dp", axis=0, tiled=True),
    )
    normed_feed = lax.all_gather(normed_second, "tensor", axis=0, tiled=True)
    gate_value = dot_plain(normed_feed, gate_full)
    up_value = dot_plain(normed_feed, up_full)
    sigmoid_gate = jax.nn.sigmoid(gate_value)
    silu_gate = gate_value * sigmoid_gate
    hidden = (silu_gate * up_value).astype(jnp.bfloat16)
    block_out = (
        middle
        + lax.psum_scatter(
            dot_trans(hidden, down_full).astype(jnp.bfloat16),
            "tensor",
            scatter_dimension=0,
            tiled=True,
        ).astype(jnp.float32)
    ).astype(jnp.bfloat16)
    back_weights = (
        lax.all_gather(q_weight, "dp", axis=0, tiled=True),
        lax.all_gather(k_weight, "dp", axis=0, tiled=True),
        lax.all_gather(v_weight, "dp", axis=0, tiled=True),
        lax.all_gather(o_weight, "dp", axis=0, tiled=True),
        lax.all_gather(gate_weight, "dp", axis=0, tiled=True),
        lax.all_gather(up_weight, "dp", axis=0, tiled=True),
        lax.all_gather(down_weight, "dp", axis=0, tiled=True),
    )
    query_back, key_back, value_back, output_back, gate_back, up_back, down_back = back_weights
    grad_seq = lax.all_gather(out_grad, "tensor", axis=0, tiled=True)
    hidden_grad = dot_plain(grad_seq, down_back)
    gate_grad = (
        hidden_grad * up_value * sigmoid_gate * (1.0 + gate_value * (1.0 - sigmoid_gate))
    ).astype(jnp.bfloat16)
    up_grad = (hidden_grad * silu_gate).astype(jnp.bfloat16)
    feed_normed_grad = lax.psum_scatter(
        dot_trans(gate_grad, gate_back) + dot_trans(up_grad, up_back),
        "tensor",
        scatter_dimension=0,
        tiled=True,
    )
    middle_grad = out_grad.astype(jnp.float32) + norm_back(
        middle, inverse_second, feed_gain, feed_normed_grad
    )
    feed_gain_part = jnp.sum(feed_normed_grad * middle * inverse_second, axis=0)
    attn_out_grad = middle_grad.astype(jnp.bfloat16)
    attn_grad_seq = lax.all_gather(attn_out_grad, "tensor", axis=0, tiled=True)
    mixed_grad = dot_plain(attn_grad_seq, output_back).astype(jnp.bfloat16)
    mixed_stack = mixed_grad.reshape(length, local_kv, group_size, HEAD_DIM).transpose(1, 0, 2, 3)

    def backward_head(stacked):
        return attend_backward(
            stacked[0], stacked[1], stacked[2], stacked[3], stacked[4], allowed, score_scale
        )

    query_grads, key_grads, value_grads = lax.map(
        backward_head, (query_stack, key_stack, value_stack, log_totals, mixed_stack)
    )
    query_heads = query_grads.transpose(1, 0, 2, 3).reshape(length, local_heads, HEAD_DIM)
    query_lin_grad = (
        rotate(query_heads, cosine_table, -sine_table)
        .reshape(length, query_width)
        .astype(jnp.bfloat16)
    )
    key_lin_grad = (
        rotate(key_grads.transpose(1, 0, 2), cosine_table, -sine_table)
        .reshape(length, key_width)
        .astype(jnp.bfloat16)
    )
    value_lin_grad = value_grads.transpose(1, 0, 2).reshape(length, key_width).astype(jnp.bfloat16)
    normed_grad = lax.psum_scatter(
        (
            dot_trans(query_lin_grad, query_back)
            + dot_trans(key_lin_grad, key_back)
            + dot_trans(value_lin_grad, value_back)
        ).astype(jnp.bfloat16),
        "tensor",
        scatter_dimension=0,
        tiled=True,
    ).astype(jnp.float32)
    input_grad = (
        middle_grad + norm_back(inputs, inverse_first, attention_gain, normed_grad)
    ).astype(jnp.bfloat16)
    attention_gain_part = jnp.sum(normed_grad * inputs * inverse_first, axis=0)
    attn_cols = 2 * query_width + 2 * key_width
    summed_grads = lax.psum_scatter(
        jnp.concatenate(
            [
                jnp.concatenate(
                    [
                        dot_inner(normed_seq, query_lin_grad),
                        dot_inner(normed_seq, key_lin_grad),
                        dot_inner(normed_seq, value_lin_grad),
                        dot_inner(attn_grad_seq, mixed),
                    ],
                    axis=1,
                ),
                jnp.concatenate(
                    [
                        dot_inner(normed_feed, gate_grad),
                        dot_inner(normed_feed, up_grad),
                        dot_inner(grad_seq, hidden),
                    ],
                    axis=1,
                ),
            ],
            axis=1,
        ),
        "dp",
        scatter_dimension=0,
        tiled=True,
    )
    attn_grads = summed_grads[:, :attn_cols]
    feed_grads = summed_grads[:, attn_cols:]
    gain_sums = lax.psum((attention_gain_part, feed_gain_part), ("dp", "tensor"))
    query_weight_grad = attn_grads[:, :query_width]
    key_weight_grad = attn_grads[:, query_width : query_width + key_width]
    value_weight_grad = attn_grads[:, query_width + key_width : query_width + 2 * key_width]
    output_weight_grad = attn_grads[:, query_width + 2 * key_width :]
    gate_weight_grad = feed_grads[:, :hidden_width]
    up_weight_grad = feed_grads[:, hidden_width : 2 * hidden_width]
    down_weight_grad = feed_grads[:, 2 * hidden_width :]
    return (
        block_out,
        input_grad,
        query_weight_grad,
        key_weight_grad,
        value_weight_grad,
        output_weight_grad,
        gain_sums[0],
        gate_weight_grad,
        up_weight_grad,
        down_weight_grad,
        gain_sums[1],
    )


def solution(mesh):
    return jax.shard_map(
        shards,
        mesh=mesh,
        in_specs=(
            P(("dp", "tensor"), None),
            P("dp", None),
            P("dp", "tensor"),
            P("dp", "tensor"),
            P("dp", "tensor"),
            P("dp", "tensor"),
            P(),
            P("dp", "tensor"),
            P("dp", "tensor"),
            P("dp", "tensor"),
            P(),
            P(("dp", "tensor"), None),
        ),
        out_specs=(
            P(("dp", "tensor"), None),
            P(("dp", "tensor"), None),
            P("dp", "tensor"),
            P("dp", "tensor"),
            P("dp", "tensor"),
            P("dp", "tensor"),
            P(),
            P("dp", "tensor"),
            P("dp", "tensor"),
            P("dp", "tensor"),
            P(),
        ),
        check_vma=False,
    )
```

profile of v0, /device:TPU:0, one launch (start us, length us, event | category | flops | bytes accessed | tf_op | source)
XLA Modules:
  0.0 1914.3 jit_solution(192053527146027332)
XLA Ops:
  16.5 26.0 %all_gather.42 = bf16[2048,128]{1,0:T(8,128)(2,1)} all-gather(bf16[128,128]{1,0:T(8,128)(2,1)S(1)} %copy-done.23), channel_id=1, replica_groups=mesh['dp'=16,'tensor'=2] {'dp'}, dimensions={0}, use_global_device_ids=true | all-gather | bytes 557056 | tf_op jit(solution)/shard_map/all_gather | solution.py:121
  42.5 20.3 %all_gather.41 = bf16[2048,128]{1,0:T(8,128)(2,1)} all-gather(bf16[128,128]{1,0:T(8,128)(2,1)S(1)} %copy-done.24), channel_id=1, replica_groups=mesh['dp'=16,'tensor'=2] {'dp'}, dimensions={0}, use_global_device_ids=true | all-gather | bytes 557056 | tf_op jit(solution)/shard_map/all_gather | solution.py:122
  69.1 44.8 %all-gather.12.cloned.1.call-done = bf16[2048,1024]{1,0:T(8,128)(2,1)} async-done(((bf16[128,1024]{1,0:T(8,128)(2,1)}), bf16[2048,1024]{1,0:T(8,128)(2,1)}) %all-gather.12.cloned.1.call-update) | async-done | bytes 4194320 | tf_op jit(solution)/shard_map/all_gather | solution.py:120
  120.4 61.1 %while.30 = (s32[]{:T(128)}, bf16[2,768,8,64]{1,3,2,0:T(8,128)(2,1)}, f32[2,8,768,1]{2,1,3,0:T(8,128)}, bf16[2,768,64]{1,2,0:T(8,128)(2,1)S(1)}, bf16[2,768,64]{...) while((s32[]{:T(128)}, ...), condition=%wide.region_5.6_spmd.clone.clone, body=%wide.region_2.5_spmd.clone.sunk.clone | while | flops 1266345984 | bytes 62133392 | solution.py:140
  139.3 10.9 bitcast_dynamic-update-slice_fusion.10
  159.6 10.5 fusion.178
  170.1 10.4 bitcast_dynamic-update-slice_fusion.10
  191.0 75.1 %reduce-scatter.6.cloned.1.call-done = f32[384,2048]{1,0:T(8,128)} async-done(((f32[768,2048]{1,0:T(8,128)}), f32[384,2048]{1,0:T(8,128)}) %reduce-scatter.6.cloned.1.call-update) | async-done | bytes 3145744 | tf_op jit(solution)/shard_map/reduce_scatter | solution.py:142
  274.3 88.5 %all-gather.20.cloned.1.call-done = bf16[2048,2816]{1,0:T(8,128)(2,1)} async-done(((bf16[128,2816]{1,0:T(8,128)(2,1)}), bf16[2048,2816]{1,0:T(8,128)(2,1)}) %all-gather.20.cloned.1.call-update) | async-done | bytes 11534352 | tf_op jit(solution)/shard_map/all_gather | solution.py:149
  362.8 45.2 %all-gather.16.cloned.1.call-done = bf16[768,2048]{1,0:T(8,128)(2,1)} async-done(((bf16[384,2048]{1,0:T(8,128)(2,1)}), bf16[768,2048]{1,0:T(8,128)(2,1)}) %all-gather.16.cloned.1.call-update) | async-done | bytes 3145744 | tf_op jit(solution)/shard_map/all_gather | solution.py:152
  408.0 15.8 fusion.95
  423.8 81.1 %all-gather.18.cloned.1.call-done = bf16[2048,2816]{1,0:T(8,128)(2,1)} async-done(((bf16[128,2816]{1,0:T(8,128)(2,1)}), bf16[2048,2816]{1,0:T(8,128)(2,1)}) %all-gather.18.cloned.1.call-update) | async-done | bytes 11534352 | tf_op jit(solution)/shard_map/all_gather | solution.py:148
  504.9 15.8 fusion.94
  520.7 29.0 %all-gather.24.cloned.1.call-done = bf16[768,2048]{1,0:T(8,128)(2,1)} async-done(((bf16[384,2048]{1,0:T(8,128)(2,1)}), bf16[768,2048]{1,0:T(8,128)(2,1)}) %all-gather.24.cloned.1.call-update) | async-done | bytes 3145744 | tf_op jit(solution)/shard_map/all_gather | solution.py:177
  549.7 96.9 %all-gather.22.cloned.1.call-done = bf16[2048,2816]{1,0:T(8,128)(2,1)} async-done(((bf16[128,2816]{1,0:T(8,128)(2,1)}), bf16[2048,2816]{1,0:T(8,128)(2,1)}) %all-gather.22.cloned.1.call-update) | async-done | bytes 11534352 | tf_op jit(solution)/shard_map/all_gather | solution.py:150
  646.6 22.6 %multiply_convert_fusion = (bf16[768,2816]{1,0:T(8,128)(2,1)}, bf16[768,2816]{1,0:T(8,128)(2,1)}, bf16[768,2816]{1,0:T(8,128)(2,1)}) fusion(f32[768,2816]{1,0:T(8,128)} %fusion.94, f32[768,2816]{1,0:T(8,128)} %fusion.95, bf16[768,2048]{1,0:T(8,128)(2,1)} %all-gather.24.cloned.1.call-done, bf16[2048,2816]{1,0:T(8,128)(2,1)} %all-gather.22.cloned.1.call-done), kind=kOutput, calls=%fused_computation.78 | convolution fusion | flops 8890810368 | bytes 44957696 | tf_op jit(solution)/shard_map/dot_general | solution.py:14
  669.2 13.6 fusion.96
  682.8 13.6 convolution_add_fusion
  696.5 14.4 convolution_convert_fusion
  711.0 60.8 %reduce-scatter.10.cloned.1.call-done = f32[384,2048]{1,0:T(8,128)} async-done(((f32[768,2048]{1,0:T(8,128)}), f32[384,2048]{1,0:T(8,128)}) %reduce-scatter.10.cloned.1.call-update) | async-done | bytes 3145744 | tf_op jit(solution)/shard_map/reduce_scatter | solution.py:183
  776.0 41.4 %reduce-scatter.8.cloned.1.call-done = bf16[384,2048]{1,0:T(8,128)(2,1)} async-done(((bf16[768,2048]{1,0:T(8,128)(2,1)}), bf16[384,2048]{1,0:T(8,128)(2,1)}) %reduce-scatter.8.cloned.1.call-update) | async-done | bytes 1572880 | tf_op jit(solution)/shard_map/reduce_scatter | solution.py:160
  825.1 45.0 %all-gather.26.cloned.1.call-done = bf16[768,2048]{1,0:T(8,128)(2,1)} async-done(((bf16[384,2048]{1,0:T(8,128)(2,1)}), bf16[768,2048]{1,0:T(8,128)(2,1)}) %all-gather.26.cloned.1.call-update) | async-done | bytes 3145744 | tf_op jit(solution)/shard_map/all_gather | solution.py:194
  880.4 147.4 %while.31 = (s32[]{:T(128)}, f32[2,768,8,64]{1,3,2,0:T(8,128)}, f32[2,768,64]{1,2,0:T(8,128)S(1)}, bf16[2,768,64]{1,2,0:T(8,128)(2,1)S(1)}, bf16[2,768,64]{1,2,0...) while((s32[]{:T(128)}, f32[2,768,8,64]{1,3,2,0:T(8,128)}, ...), condition=%wide.region_13.14_spmd.clone.clone, body=%wide.region_11.13_spmd.clone.sunk.clone | while | flops 3144365568 | bytes 292241536 | solution.py:203
  899.4 26.9 %fusion.190 = f32[2,768,64]{1,2,0:T(8,128)S(1)} fusion(f32[2,768,64]{1,2,0:T(8,128)S(1)} %get-tuple-element.401, s32[]{:T(128)S(6)} %copy.90, f32[768,768,8]{1,0,2:T(8,128)} %fusion.187, f32[768,768,8]{1,0,2:T(8,128)} %copy-done, f32[8,768]{1,0:T(8,128)S(1)} %dynamic-slice_bitcast_fusion.3, pred[768,768]{0,1:T(8,128)(4,1)S(1)} %fusion.189, ...), kind=kOutput, calls=%fused_computation.42.clone.1.clone | convolution fusion | flops 655891200 | bytes 77710336 | tf_op jit(solution)/shard_map/while/body/eval_jaxpr/gqs,qgd->sd/dot_general | solution.py:84
  926.3 28.0 %bitcast_dynamic-update-slice_fusion.12 = f32[2,768,8,64]{1,3,2,0:T(8,128)} fusion(f32[2,768,8,64]{1,3,2,0:T(8,128)} %get-tuple-element.400, s32[]{:T(128)S(6)} %copy.90, f32[768,768,8]{1,0,2:T(8,128)} %fusion.187, f32[768,768,8]{1,0,2:T(8,128)} %copy-done, f32[8,768]{1,0:T(8,128)S(1)} %dynamic-slice_bitcast_fusion.3, ...), kind=kOutput, calls=%fused_computation.40.clone.1.clone | convolution fusion | flops 655891200 | bytes 78398464 | tf_op jit(solution)/shard_map/while/body/eval_jaxpr/gqs,sd->qgd/dot_general | solution.py:83
  972.8 26.9 %fusion.190 = f32[2,768,64]{1,2,0:T(8,128)S(1)} fusion(f32[2,768,64]{1,2,0:T(8,128)S(1)} %get-tuple-element.401, s32[]{:T(128)S(6)} %copy.90, f32[768,768,8]{1,0,2:T(8,128)} %fusion.187, f32[768,768,8]{1,0,2:T(8,128)} %copy-done, f32[8,768]{1,0:T(8,128)S(1)} %dynamic-slice_bitcast_fusion.3, pred[768,768]{0,1:T(8,128)(4,1)S(1)} %fusion.189, ...), kind=kOutput, calls=%fused_computation.42.clone.1.clone | convolution fusion | flops 655891200 | bytes 77710336 | tf_op jit(solution)/shard_map/while/body/eval_jaxpr/gqs,qgd->sd/dot_general | solution.py:84
  999.7 28.0 %bitcast_dynamic-update-slice_fusion.12 = f32[2,768,8,64]{1,3,2,0:T(8,128)} fusion(f32[2,768,8,64]{1,3,2,0:T(8,128)} %get-tuple-element.400, s32[]{:T(128)S(6)} %copy.90, f32[768,768,8]{1,0,2:T(8,128)} %fusion.187, f32[768,768,8]{1,0,2:T(8,128)} %copy-done, f32[8,768]{1,0:T(8,128)S(1)} %dynamic-slice_bitcast_fusion.3, ...), kind=kOutput, calls=%fused_computation.40.clone.1.clone | convolution fusion | flops 655891200 | bytes 78398464 | tf_op jit(solution)/shard_map/while/body/eval_jaxpr/gqs,sd->qgd/dot_general | solution.py:83
  1057.2 12.7 convolution_dynamic-update-slice_fusion.1
  1069.9 12.6 convolution_dynamic-update-slice_fusion
  1082.6 13.2 bitcast_dynamic-update-slice_fusion.3
  1099.6 39.5 %all-reduce = (f32[2048]{0:T(1024)}, f32[2048]{0:T(1024)}) all-reduce(f32[2048]{0:T(1024)S(1)} %get-tuple-element.150, f32[2048]{0:T(1024)S(1)} %copy-done.22), channel_id=1, replica_groups=mesh['dp'=16,'tensor'=2] {'dp','tensor'}, use_global_device_ids=true, to_apply=%region_18.19 | all-reduce | flops 4096 | bytes 32768 | tf_op jit(solution)/shard_map/psum | solution.py:262
  1143.8 755.5 %reduce-scatter.14.cloned.1.call-done = f32[128,10752]{1,0:T(8,128)} async-done(((f32[2048,10752]{1,0:T(8,128)}), f32[128,10752]{1,0:T(8,128)}) %reduce-scatter.14.cloned.1.call-update) | async-done | bytes 5505040 | tf_op jit(solution)/shard_map/reduce_scatter | solution.py:233
  (183 shorter events, 173.6 us)
Async XLA Ops:
  7.2 56.6 %all-gather.10.cloned.1.call-start = ((), (), s32[]{:S(2)}) async-start(), calls=%async_computation.5 | async-start | bytes 4718592 | tf_op jit(solution)/shard_map/all_gather | solution.py:125
  7.2 8.9 copy-start.28
  7.2 9.3 copy-start.23
  7.2 35.2 %copy-start.24 = (bf16[128,128]{1,0:T(8,128)(2,1)S(1)}, bf16[128,128]{1,0:T(8,128)(2,1)}, u32[]{:S(2)}) copy-start(bf16[128,128]{1,0:T(8,128)(2,1)} %param.20) | copy-start | bytes 98308
  13.2 100.7 %all-gather.12.cloned.1.call-start = ((), (), s32[]{:S(2)}) async-start(), calls=%async_computation.6 | async-start | bytes 4456448 | tf_op jit(solution)/shard_map/all_gather | solution.py:120
  14.0 167.5 %all-gather.14.cloned.1.call-start = ((), (), s32[]{:S(2)}) async-start(), calls=%async_computation.7 | async-start | bytes 4456448 | tf_op jit(solution)/shard_map/all_gather | solution.py:123
  14.7 251.3 %reduce-scatter.6.cloned.1.call-start = ((), (), s32[]{:S(2)}) async-start(), calls=%async_computation.8 | async-start | bytes 9437184 | tf_op jit(solution)/shard_map/reduce_scatter | solution.py:142
  63.8 55.7 %copy-start.9 = (f32[768,32]{0,1:T(8,128)}, f32[768,32]{0,1:T(8,128)S(1)}, u32[]{:S(2)}) copy-start(f32[768,32]{0,1:T(8,128)S(1)} %get-tuple-element.215) | copy-start | bytes 294916
  139.3 10.9 copy-start.17
  170.1 10.4 copy-start.17
  190.3 80.2 %copy-start.20 = (f32[2048]{0:T(1024)S(1)}, f32[2048]{0:T(1024)}, u32[]{:S(2)}) copy-start(f32[2048]{0:T(1024)} %param.26) | copy-start | bytes 24580
  190.3 172.5 %all-gather.20.cloned.1.call-start = ((), (), s32[]{:S(2)}) async-start(), calls=%async_computation.11 | async-start | bytes 12255232 | tf_op jit(solution)/shard_map/all_gather | solution.py:149
  190.9 217.1 %all-gather.16.cloned.1.call-start = ((), (), s32[]{:S(2)}) async-start(), calls=%async_computation.9 | async-start | bytes 4718592 | tf_op jit(solution)/shard_map/all_gather | solution.py:152
  272.1 232.8 %all-gather.18.cloned.1.call-start = ((), (), s32[]{:S(2)}) async-start(), calls=%async_computation.10 | async-start | bytes 12255232 | tf_op jit(solution)/shard_map/all_gather | solution.py:148
  272.8 276.9 %all-gather.24.cloned.1.call-start = ((), (), s32[]{:S(2)}) async-start(), calls=%async_computation.14 | async-start | bytes 4718592 | tf_op jit(solution)/shard_map/all_gather | solution.py:177
  273.6 373.0 %all-gather.22.cloned.1.call-start = ((), (), s32[]{:S(2)}) async-start(), calls=%async_computation.12 | async-start | bytes 12255232 | tf_op jit(solution)/shard_map/all_gather | solution.py:150
  274.3 497.5 %reduce-scatter.10.cloned.1.call-start = ((), (), s32[]{:S(2)}) async-start(), calls=%async_computation.15 | async-start | bytes 9437184 | tf_op jit(solution)/shard_map/reduce_scatter | solution.py:183
  669.2 13.6 copy-start.33
  696.5 121.0 %reduce-scatter.8.cloned.1.call-start = ((), (), s32[]{:S(2)}) async-start(), calls=%async_computation.13 | async-start | bytes 4718592 | tf_op jit(solution)/shard_map/reduce_scatter | solution.py:160
  711.0 159.2 %all-gather.26.cloned.1.call-start = ((), (), s32[]{:S(2)}) async-start(), calls=%async_computation.16 | async-start | bytes 4718592 | tf_op jit(solution)/shard_map/all_gather | solution.py:194
  825.0 270.8 %reduce-scatter.12.cloned.1.call-start = ((), (), s32[]{:S(2)}) async-start(), calls=%async_computation.17 | async-start | bytes 4718592 | tf_op jit(solution)/shard_map/reduce_scatter | solution.py:218
  825.1 55.3 %copy-start.19 = (f32[2,8,768,1]{2,1,3,0:T(8,128)S(1)}, f32[2,8,768,1]{2,1,3,0:T(8,128)}, u32[]{:S(2)}) copy-start(f32[2,8,768,1]{2,1,3,0:T(8,128)} %get-tuple-element.395) | copy-start | bytes 147460
  880.4 147.5 %copy-start.10 = (f32[768,32]{0,1:T(8,128)S(1)}, f32[768,32]{0,1:T(8,128)}, u32[]{:S(2)}) copy-start(f32[768,32]{0,1:T(8,128)} %copy-done.9) | copy-start | bytes 294916
  880.4 147.5 %copy-start.14 = (f32[768,32]{0,1:T(8,128)S(1)}, f32[768,32]{0,1:T(8,128)}, u32[]{:S(2)}) copy-start(f32[768,32]{0,1:T(8,128)} %get-tuple-element.213) | copy-start | bytes 294916
  1039.1 860.2 %reduce-scatter.14.cloned.1.call-start = ((), (), s32[]{:S(2)}) async-start(), calls=%async_computation.18 | async-start | bytes 93585408 | tf_op jit(solution)/shard_map/reduce_scatter | solution.py:233
  1051.4 18.5 slice-start
  1057.2 12.7 slice-start.1
  1057.2 25.4 %slice-start.4 = ((s8[4325376]{0:T(1024)(128)(4,1)}), s8[131072]{0:T(1024)(128)(4,1)S(1)}, s32[]{:S(2)}) async-start(s8[4325376]{0:T(1024)(128)(4,1)} %bitcast.312), calls=%async_computation.23 | async-start | bytes 262144
  1069.9 12.7 copy-start.31
  1069.9 12.7 slice-start.5
  1095.7 43.4 %copy-start.27 = (f32[384]{0:T(512)S(1)}, f32[384]{0:T(512)}, u32[]{:S(2)}) copy-start(f32[384]{0:T(512)} %get-tuple-element.216) | copy-start | bytes 4612
  1097.1 42.0 %copy-start.5 = (bf16[384,2048]{1,0:T(8,128)(2,1)S(1)}, bf16[384,2048]{1,0:T(8,128)(2,1)}, u32[]{:S(2)}) copy-start(bf16[384,2048]{1,0:T(8,128)(2,1)} %reduce-scatter.12.cloned.1.call-done) | copy-start | bytes 4718596
  (25 other events, 80.5 us)
Sparse Core Ops, SparseCore 0:
  13.4 47.6 all-gather.9
  63.2 50.7 all-gather.11
  116.1 49.2 all-gather.13
  190.4 75.5 reduce-scatter.5
  268.5 94.3 all-gather.19
  364.9 43.1 all-gather.15
  410.5 94.3 all-gather.17
  506.5 43.0 all-gather.23
  552.2 94.3 all-gather.21
  696.6 75.2 reduce-scatter.9
  774.1 43.3 reduce-scatter.7
  825.2 44.9 all-gather.25
  1039.2 43.3 reduce-scatter.11
  1095.9 803.3 reduce-scatter.13
where the time goes:
time: 1920 us; the launch traced here: 1910 us
  waiting for transfers between devices  1370 us (71%)
  matrix products  370 us (19%)
  blocking collectives  85.7 us (4%)
  other arithmetic  56.9 us (3%)
    reduce_scatter x1, waiting for transfers between devices, shards(): lax.psum_scatter(jnp.concatenate([jnp.concatenate([dot_inner(normed_seq,...  756 us
    all_gather x1, waiting for transfers between devices, shards(): lax.all_gather(down_weight, 'dp', axis=0, tiled=True)  96.9 us
    all_gather x1, waiting for transfers between devices, shards(): lax.all_gather(up_weight, 'dp', axis=0, tiled=True)  88.5 us
    all_gather x1, waiting for transfers between devices, shards(): lax.all_gather(gate_weight, 'dp', axis=0, tiled=True)  81.1 us
    reduce_scatter x1, waiting for transfers between devices, shards(): lax.psum_scatter(dot_trans(mixed, output_full), 'tensor', scatter_dimensi...  75.1 us
    dot_general x7, matrix products, dot_plain(): return jnp.dot(left_side, right_side, preferred_element_type=jnp.float32)  72.6 us
    reduce_scatter x1, waiting for transfers between devices, shards(): lax.psum_scatter(dot_trans(gate_grad, gate_back) + dot_trans(up_grad, up_...  60.8 us
    dot_general x7, matrix products, dot_trans(): lax.dot_general(left_side, right_side, (((1,), (1,)), ((), ())), preferre...  57.6 us
  transfers between devices with their start and end apart: 14, of which 11 were waited for; matrix products, arithmetic and copies ran while one was open for 10% of the time, Pallas kernels for 0%

commit v1 on v0

v1 whole, which is shorter than its diff:
```python
import functools

import jax
import jax.numpy as jnp
from jax import lax
from jax.experimental import pallas as pl
from jax.experimental.pallas import tpu as pltpu
from jax.sharding import Mesh, PartitionSpec as P

HEAD_DIM = 64
SWAP = ((0, 1), (1, 0))
QUERIES = 256
VMEM = 40 * 2**20
epsilon = 1e-05
rope_base = 10000.0
bf16 = jnp.bfloat16
f32 = jnp.float32


def dot_plain(left, right):
    return jnp.dot(left, right, preferred_element_type=f32)


def dot_trans(left, right):
    return lax.dot_general(left, right, (((1,), (1,)), ((), ())), preferred_element_type=f32)


def dot_inner(left, right):
    return lax.dot_general(left, right, (((0,), (0,)), ((), ())), preferred_element_type=f32)


def rotary_tables(segment_row):
    length = segment_row.shape[0]
    before = jnp.sum((segment_row[None, :] < segment_row[:, None]).astype(jnp.int32), axis=1)
    places = (jnp.arange(length, dtype=jnp.int32) - before).astype(f32)
    half_dim = HEAD_DIM // 2
    frequency = rope_base ** (-2.0 * jnp.arange(half_dim).astype(f32) / HEAD_DIM)
    angles = places[:, None] * frequency[None, :]
    cosine, sine = jnp.cos(angles), jnp.sin(angles)
    return (jnp.concatenate([cosine] * 4, axis=1), jnp.concatenate([-sine, sine] * 2, axis=1))


def first_blocks(segment_row):
    starts, ends = segment_row[::QUERIES], segment_row[QUERIES - 1 :: QUERIES]
    return jnp.sum((ends[None, :] < starts[:, None]).astype(jnp.int32), axis=1)


def inverse_rms(activity):
    return lax.rsqrt(jnp.mean(activity * activity, axis=-1, keepdims=True) + epsilon)


def norm_back(activity, inverse, gain_vec, incoming):
    scaled = incoming * gain_vec
    return inverse * scaled - activity * (inverse * inverse * inverse) * jnp.mean(
        scaled * activity, axis=-1, keepdims=True
    )


def lanes_of(shape):
    return lax.broadcasted_iota(jnp.int32, shape, len(shape) - 1)


def turn(block, cosine, sine):
    low_half = lanes_of(block.shape) % HEAD_DIM < HEAD_DIM // 2
    other = jnp.where(low_half, pltpu.roll(block, 96, 1), pltpu.roll(block, 32, 1))
    return block * cosine + other * sine


def rope_kernel(rotated, qkv_ref, cos_ref, sin_ref, out_ref):
    block = qkv_ref[...]

    @pl.when(pl.program_id(0) < rotated)
    def _():
        out_ref[...] = turn(block, cos_ref[...], sin_ref[...]).astype(bf16)

    @pl.when(pl.program_id(0) >= rotated)
    def _():
        out_ref[...] = block.astype(bf16)


def rope(qkv, cosine, sine, rotated):
    length, width = qkv.shape
    block = pl.BlockSpec((length, 128), lambda j: (0, j))
    table = pl.BlockSpec((length, 128), lambda j: (0, 0))
    return pl.pallas_call(
        functools.partial(rope_kernel, rotated),
        grid=(width // 128,),
        in_specs=[block, table, table],
        out_specs=block,
        out_shape=jax.ShapeDtypeStruct((length, width), bf16),
        compiler_params=pltpu.CompilerParams(vmem_limit_bytes=VMEM),
        cost_estimate=pl.CostEstimate(
            flops=4 * length * width, bytes_accessed=6 * length * width, transcendentals=0
        ),
    )(qkv, cosine, sine)


def widen(pair_ref, wide_ref, group):
    pair = pair_ref[...]
    keep = (lanes_of(pair.shape) < HEAD_DIM) == (group == 0)
    half = jnp.where(keep, pair, pltpu.roll(pair.astype(f32), HEAD_DIM, 1).astype(bf16))
    wide_ref[:, :128] = half
    wide_ref[:, 128:] = half


def seen_bias(col_ref, row_ref, start, keys, step):
    queries = col_ref.shape[0]
    same = col_ref[...] == row_ref[:, pl.ds(start, keys)]
    q_at = lax.broadcasted_iota(jnp.int32, (queries, keys), 0) + step * queries
    k_at = lax.broadcasted_iota(jnp.int32, (queries, keys), 1) + start
    return jnp.where(same & (q_at >= k_at), 0.0, -1e30).astype(f32)


def forward_kernel(scale, low_ref, q_ref, k_ref, v_ref, col_ref, row_ref, o_ref, lse_ref, kw_ref, vw_ref):
    group, step = pl.program_id(0), pl.program_id(1)
    queries = q_ref.shape[0]

    @pl.when(step == 0)
    def _():
        widen(k_ref, kw_ref, group)
        widen(v_ref, vw_ref, group)

    def run(blocks):
        keys = blocks * queries
        start = pl.multiple_of(low_ref[step] * queries, queries)
        bias = seen_bias(col_ref, row_ref, start, keys, step)
        key = kw_ref[pl.ds(start, keys), :]
        value = vw_ref[pl.ds(start, keys), :]
        head_of = lanes_of((queries, 256)) // HEAD_DIM
        lse = jnp.zeros((queries, 128), f32)
        for quad in range(q_ref.shape[1] // 256):
            wide = q_ref[:, quad * 256 : quad * 256 + 256]
            out = jnp.zeros((queries, 256), f32)
            for j in range(4):
                one = jnp.where(head_of == j, wide, jnp.zeros_like(wide))
                scores = dot_trans(one, key) * scale + bias
                top = jnp.max(scores, axis=1, keepdims=True)
                powers = jnp.exp(scores - top)
                sums = jnp.sum(powers, axis=1, keepdims=True)
                prob = (powers * (1.0 / sums)).astype(bf16)
                out = jnp.where(head_of == j, dot_plain(prob, value), out)
                lse = jnp.where(lanes_of(lse.shape) == quad * 4 + j, top + jnp.log(sums), lse)
            o_ref[:, quad * 256 : quad * 256 + 256] = out.astype(bf16)
        lse_ref[...] = lse

    for blocks in range(1, row_ref.shape[1] // queries + 1):
        pl.when(step + 1 - low_ref[step] == blocks)(functools.partial(run, blocks))


def backward_kernel(
    scale, low_ref, q_ref, k_ref, v_ref, g_ref, lse_ref, col_ref, row_ref, cos_ref, sin_ref, kcos_ref, ksin_ref,
    dq_ref, dk_ref, dv_ref, kw_ref, vw_ref, dkw_ref, dvw_ref,
):
    group, step = pl.program_id(0), pl.program_id(1)
    queries = q_ref.shape[0]

    @pl.when(step == 0)
    def _():
        widen(k_ref, kw_ref, group)
        widen(v_ref, vw_ref, group)
        dkw_ref[...] = jnp.zeros_like(dkw_ref)
        dvw_ref[...] = jnp.zeros_like(dvw_ref)

    def run(blocks):
        keys = blocks * queries
        start = pl.multiple_of(low_ref[step] * queries, queries)
        bias = seen_bias(col_ref, row_ref, start, keys, step)
        key = kw_ref[pl.ds(start, keys), :]
        value = vw_ref[pl.ds(start, keys), :]
        head_of = lanes_of((queries, 256)) // HEAD_DIM
        cosine, sine = cos_ref[...], sin_ref[...]
        for quad in range(q_ref.shape[1] // 256):
            wide = q_ref[:, quad * 256 : quad * 256 + 256]
            grads = g_ref[:, quad * 256 : quad * 256 + 256]
            out = jnp.zeros((queries, 256), f32)
            for j in range(4):
                at = quad * 4 + j
                one = jnp.where(head_of == j, wide, jnp.zeros_like(wide))
                grad = jnp.where(head_of == j, grads, jnp.zeros_like(grads))
                prob = jnp.exp(dot_trans(one, key) * scale + bias - lse_ref[:, at : at + 1])
                prob_grad = dot_trans(grad, value)
                centre = jnp.sum(prob * prob_grad, axis=1, keepdims=True)
                score_grad = (prob * (prob_grad - centre) * scale).astype(bf16)
                dvw_ref[pl.ds(start, keys), :] += dot_inner(prob.astype(bf16), grad)
                dkw_ref[pl.ds(start, keys), :] += dot_inner(score_grad, one)
                out = jnp.where(head_of == j, dot_plain(score_grad, key), out)
            for half in range(2):
                piece = turn(out[:, half * 128 : half * 128 + 128], cosine, -sine)
                dq_ref[:, quad * 256 + half * 128 : quad * 256 + half * 128 + 128] = piece.astype(bf16)

    for blocks in range(1, row_ref.shape[1] // queries + 1):
        pl.when(step + 1 - low_ref[step] == blocks)(functools.partial(run, blocks))

    @pl.when(step == pl.num_programs(1) - 1)
    def _():
        mine = (lanes_of(dk_ref.shape) < HEAD_DIM) == (group == 0)

        def fold(ref):
            pair = ref[:, :128] + ref[:, 128:]
            return pair + pltpu.roll(pair, HEAD_DIM, 1)

        dk = turn(fold(dkw_ref), kcos_ref[...], -ksin_ref[...]).astype(bf16)
        dk_ref[...] = jnp.where(mine, dk, dk_ref[...])
        dv_ref[...] = jnp.where(mine, fold(dvw_ref).astype(bf16), dv_ref[...])


def attention_specs(length, queries, wide):
    at = lambda g, i, low: (i, g)
    pair = lambda first: pl.BlockSpec((length, 128), lambda g, i, low: (0, first))
    col = pl.BlockSpec((queries, 1), lambda g, i, low: (i, 0))
    row = pl.BlockSpec((1, length), lambda g, i, low: (0, 0))
    return pl.BlockSpec((queries, wide), at), pair, col, row


def attend(rotated, query_width, first_seen, segment_row, scale):
    length = rotated.shape[0]
    queries = length // first_seen.shape[0]
    groups = 2
    wide = query_width // groups
    heads, pair, col, row = attention_specs(length, queries, wide)
    first = query_width // 128
    return pl.pallas_call(
        functools.partial(forward_kernel, scale),
        grid_spec=pltpu.PrefetchScalarGridSpec(
            num_scalar_prefetch=1,
            grid=(groups, length // queries),
            in_specs=[heads, pair(first), pair(first + 1), col, row],
            out_specs=[heads, pl.BlockSpec((queries, 128), lambda g, i, low: (i, g))],
            scratch_shapes=[pltpu.VMEM((length, 256), bf16), pltpu.VMEM((length, 256), bf16)],
        ),
        out_shape=[
            jax.ShapeDtypeStruct((length, query_width), bf16),
            jax.ShapeDtypeStruct((length, groups * 128), f32),
        ],
        compiler_params=pltpu.CompilerParams(vmem_limit_bytes=VMEM),
        cost_estimate=pl.CostEstimate(
            flops=10 * length * length * query_width, bytes_accessed=4 * length * query_width,
            transcendentals=0,
        ),
    )(first_seen, rotated, rotated, rotated, segment_row.reshape(length, 1), segment_row.reshape(1, length))


def attend_back(rotated, grads, lse, query_width, first_seen, segment_row, cosine, sine, scale):
    length = rotated.shape[0]
    queries = length // first_seen.shape[0]
    groups = 2
    wide = query_width // groups
    heads, pair, col, row = attention_specs(length, queries, wide)
    first = query_width // 128
    table = pl.BlockSpec((queries, 128), lambda g, i, low: (i, 0))
    return pl.pallas_call(
        functools.partial(backward_kernel, scale),
        grid_spec=pltpu.PrefetchScalarGridSpec(
            num_scalar_prefetch=1,
            grid=(groups, length // queries),
            in_specs=[
                heads, pair(first), pair(first + 1), heads,
                pl.BlockSpec((queries, 128), lambda g, i, low: (i, g)),
                col, row, table, table, pair(0), pair(0),
            ],
            out_specs=[heads, pair(0), pair(0)],
            scratch_shapes=[
                pltpu.VMEM((length, 256), bf16), pltpu.VMEM((length, 256), bf16),
                pltpu.VMEM((length, 256), f32), pltpu.VMEM((length, 256), f32),
            ],
        ),
        out_shape=[
            jax.ShapeDtypeStruct((length, query_width), bf16),
            jax.ShapeDtypeStruct((length, 128), bf16),
            jax.ShapeDtypeStruct((length, 128), bf16),
        ],
        compiler_params=pltpu.CompilerParams(vmem_limit_bytes=VMEM),
        cost_estimate=pl.CostEstimate(
            flops=30 * length * length * query_width, bytes_accessed=8 * length * query_width,
            transcendentals=0,
        ),
    )(
        first_seen, rotated, rotated, rotated, grads, lse,
        segment_row.reshape(length, 1), segment_row.reshape(1, length), cosine, sine, cosine, sine,
    )


def make_shards(outer):
    def relative(array):
        rows, width = array.shape
        blocks = array.reshape(rows, outer, 2, 2, width // (4 * outer))
        blocks = jnp.where(lax.axis_index("x") == 0, blocks, blocks[:, :, ::-1])
        blocks = jnp.where(lax.axis_index("core") == 0, blocks, blocks[:, :, :, ::-1])
        return blocks.transpose(0, 3, 2, 1, 4).reshape(rows, width)

    def natural(array):
        rows, width = array.shape
        blocks = array.reshape(rows, 2, 2, outer, width // (4 * outer)).transpose(0, 3, 2, 1, 4)
        blocks = jnp.where(lax.axis_index("x") == 0, blocks, blocks[:, :, ::-1])
        blocks = jnp.where(lax.axis_index("core") == 0, blocks, blocks[:, :, :, ::-1])
        return blocks.reshape(rows, width)

    def gather(weight):
        along = lax.all_gather(weight, "z", axis=0, tiled=True)
        across = lax.ppermute(along, "x", SWAP)
        return jnp.concatenate(
            [along, across, lax.ppermute(along, "core", SWAP), lax.ppermute(across, "core", SWAP)],
            axis=0,
        )

    def scatter(left, right):
        half = left.shape[1] // 2
        quarter = half // 2
        for_core = dot_inner(left[:, half:], right).astype(bf16)
        from_core = lax.ppermute(for_core, "core", SWAP)
        for_x = (dot_inner(left[:, quarter:half], right) + from_core[quarter:].astype(f32)).astype(bf16)
        from_x = lax.ppermute(for_x, "x", SWAP)
        kept = (
            dot_inner(left[:, :quarter], right)
            + from_core[:quarter].astype(f32)
            + from_x.astype(f32)
        ).astype(bf16)
        return lax.psum_scatter(kept, "z", scatter_dimension=0, tiled=True).astype(f32)

    def total(vector):
        for axis in ("core", "x", "tensor"):
            vector = vector + lax.ppermute(vector, axis, SWAP)
        step = 1
        while step < outer:
            vector = vector + lax.ppermute(vector, "z", [(i, i ^ step) for i in range(outer)])
            step *= 2
        return vector

    def both_halves(own):
        other = lax.ppermute(own, "tensor", SWAP)
        return jnp.where(
            lax.axis_index("tensor") == 0,
            jnp.concatenate([own, other], axis=0),
            jnp.concatenate([other, own], axis=0),
        )

    def reduce_halves(product, *operands):
        rows = operands[0].shape[0] // 2
        place = lax.axis_index("tensor")

        def cut(at):
            return [lax.dynamic_slice_in_dim(o, at * rows, rows, axis=0) for o in operands]

        sent = lax.ppermute(product(*cut(1 - place)).astype(bf16), "tensor", SWAP)
        return product(*cut(place)) + sent.astype(f32)

    def shards(
        tokens,
        segments,
        q_weight,
        k_weight,
        v_weight,
        o_weight,
        attention_gain,
        gate_weight,
        up_weight,
        down_weight,
        feed_gain,
        out_grad,
    ):
        query_width = q_weight.shape[1]
        key_width = k_weight.shape[1]
        score_scale = HEAD_DIM ** (-0.5)
        qkv_full = gather(jnp.concatenate([q_weight, k_weight, v_weight], axis=1))
        output_full = gather(o_weight)
        gate_full = gather(gate_weight)
        up_full = gather(up_weight)
        down_full = gather(down_weight)

        attention_gain = relative(attention_gain[None])
        feed_gain = relative(feed_gain[None])
        tokens = relative(tokens)
        out_grad = relative(out_grad)

        segment_row = segments[0]
        cosine, sine = rotary_tables(segment_row)
        first_seen = first_blocks(segment_row)
        inputs = tokens.astype(f32)
        inverse_first = inverse_rms(inputs)
        normed_first = (inputs * inverse_first * attention_gain).astype(bf16)
        normed_seq = both_halves(normed_first)
        grad_seq = both_halves(out_grad)
        qkv = dot_plain(normed_seq, qkv_full)
        rotated = rope(qkv, cosine, sine, (query_width + key_width) // 128)
        mixed, log_totals = attend(rotated, query_width, first_seen, segment_row, score_scale)
        middle = inputs + reduce_halves(lambda m: dot_trans(m, output_full), mixed)
        inverse_second = inverse_rms(middle)
        normed_second = (middle * inverse_second * feed_gain).astype(bf16)
        normed_feed = both_halves(normed_second)
        gate_value = dot_plain(normed_feed, gate_full).astype(bf16)
        up_value = dot_plain(normed_feed, up_full).astype(bf16)
        hidden = (jax.nn.silu(gate_value.astype(f32)) * up_value.astype(f32)).astype(bf16)
        down_weight_grad = scatter(grad_seq, hidden)
        hidden_grad = dot_plain(grad_seq, down_full)
        gate_value, up_value = gate_value.astype(f32), up_value.astype(f32)
        sigmoid_gate = jax.nn.sigmoid(gate_value)
        gate_grad = (
            hidden_grad * up_value * sigmoid_gate * (1.0 + gate_value * (1.0 - sigmoid_gate))
        ).astype(bf16)
        up_grad = (hidden_grad * gate_value * sigmoid_gate).astype(bf16)
        block_out = (middle + reduce_halves(lambda h: dot_trans(h, down_full), hidden)).astype(bf16)
        feed_normed_grad = reduce_halves(
            lambda g, u: dot_trans(g, gate_full) + dot_trans(u, up_full), gate_grad, up_grad
        )
        gate_weight_grad = scatter(normed_feed, gate_grad)
        up_weight_grad = scatter(normed_feed, up_grad)
        middle_grad = out_grad.astype(f32) + norm_back(
            middle, inverse_second, feed_gain, feed_normed_grad
        )
        feed_gain_part = jnp.sum(feed_normed_grad * middle * inverse_second, axis=0)
        attn_out_grad = middle_grad.astype(bf16)
        attn_grad_seq = both_halves(attn_out_grad)
        output_weight_grad = scatter(attn_grad_seq, mixed)
        mixed_grad = dot_plain(attn_grad_seq, output_full).astype(bf16)
        qkv_grad = jnp.concatenate(
            attend_back(
                rotated,
                mixed_grad,
                log_totals,
                query_width,
                first_seen,
                segment_row,
                cosine,
                sine,
                score_scale,
            ),
            axis=1,
        )
        qkv_weight_grad = scatter(normed_seq, qkv_grad)
        normed_grad = reduce_halves(lambda g: dot_trans(g, qkv_full), qkv_grad)
        input_grad = (
            middle_grad + norm_back(inputs, inverse_first, attention_gain, normed_grad)
        ).astype(bf16)
        attention_gain_part = jnp.sum(normed_grad * inputs * inverse_first, axis=0)
        feed_gain_grad = total(natural(feed_gain_part[None]))[0]
        attention_gain_grad = total(natural(attention_gain_part[None]))[0]
        return (
            natural(block_out),
            natural(input_grad),
            qkv_weight_grad[:, :query_width],
            qkv_weight_grad[:, query_width : query_width + key_width],
            qkv_weight_grad[:, query_width + key_width :],
            output_weight_grad,
            attention_gain_grad,
            gate_weight_grad,
            up_weight_grad,
            down_weight_grad,
            feed_gain_grad,
        )

    return shards


def solution(mesh):
    outer = mesh.shape["dp"] // 4
    fine = Mesh(
        mesh.devices.reshape(outer, 2, 2, mesh.shape["tensor"]), ("z", "x", "core", "tensor")
    )
    dp = ("z", "x", "core")
    every = P(dp + ("tensor",), None)
    weight = P(dp, "tensor")
    return jax.shard_map(
        make_shards(outer),
        mesh=fine,
        in_specs=(
            every,
            P(dp, None),
            weight,
            weight,
            weight,
            weight,
            P(),
            weight,
            weight,
            weight,
            P(),
            every,
        ),
        out_specs=(every, every, weight, weight, weight, weight, P(), weight, weight, weight, P()),
        check_vma=False,
    )
```

time: 1920 us -> 948 us (0.49)
  waiting for transfers between devices: 1370 us -> 437 us
  matrix products: 370 us -> 225 us
  blocking collectives: 85.7 us -> 0 us
  local copies, waits for them, and re-layouts: 17.9 us -> 86.3 us
  Pallas kernels: 0 us -> 54.9 us
  starting transfers between devices: 0.56 us -> 38.6 us
  other arithmetic: 56.9 us -> 84.9 us
    reduce_scatter x5, waiting for transfers between devices: 933 us -> 0.01 us  [scatter(): lax.psum_scatter(kept, 'z', scatter_dimension=0, tiled=True).astype(f32)]
    ppermute x0 -> x43, waiting for transfers between devices: none -> 309 us  [the longest x5 197 us: scatter(): from_x = lax.ppermute(for_x, 'x', SWAP)]
    all_gather x9 -> x5, waiting for transfers between devices: 430 us -> 126 us  [gather(): along = lax.all_gather(weight, 'z', axis=0, tiled=True)]
    dot_general x35 -> x30, matrix products: 370 us -> 225 us  [the longest x10 92.7 us: dot_trans(): lax.dot_general(left, right, (((1,), (1,)), ((), ())), preferred_element_...]
    pallas_call x0 -> x3, Pallas kernels: none -> 54.9 us  [the longest x1 35 us: attend_back(): pl.pallas_call(functools.partial(backward_kernel, scale), grid_spec=pltpu...]
    all_gather x2 -> x0, blocking collectives: 46.2 us -> none  [the longest x1 26 us: shards(): lax.all_gather(k_weight, 'dp', axis=0, tiled=True)]
    psum x1 -> x0, blocking collectives: 39.5 us -> none  [shards(): lax.psum((attention_gain_part, feed_gain_part), ('dp', 'tensor'))]
    unnamed x74 -> x95, local copies, waits for them, and re-layouts: 5.88 us -> 44.5 us
  transfers between devices with their start and end apart: 14 -> 53, of which waited for: 11 -> 20; matrix products, arithmetic and copies ran while one was open for 10% -> 35% of each run, Pallas kernels for 0% -> 6%
where the time goes in v1:
time: 948 us; the launch traced here: 942 us
  waiting for transfers between devices  437 us (46%)
  matrix products  225 us (24%)
  local copies, waits for them, and re-layouts  86.3 us (9%)
  other arithmetic  84.9 us (9%)
  Pallas kernels  54.9 us (6%)
  starting transfers between devices  38.6 us (4%)
  between operations  15.5 us (2%)
    ppermute x5, waiting for transfers between devices, scatter(): from_x = lax.ppermute(for_x, 'x', SWAP)  197 us
    all_gather x5, waiting for transfers between devices, gather(): along = lax.all_gather(weight, 'z', axis=0, tiled=True)  126 us
    dot_general x10, matrix products, dot_trans(): lax.dot_general(left, right, (((1,), (1,)), ((), ())), preferred_element_...  92.7 us
    dot_general x15, matrix products, dot_inner(): lax.dot_general(left, right, (((0,), (0,)), ((), ())), preferred_element_...  71.3 us
    dot_general x5, matrix products, dot_plain(): return jnp.dot(left, right, preferred_element_type=f32)  60.8 us
    ppermute x5, waiting for transfers between devices, gather(): across = lax.ppermute(along, 'x', SWAP)  44.8 us
    unnamed x95, local copies, waits for them, and re-layouts  44.5 us
    pallas_call x1, Pallas kernels, attend_back(): pl.pallas_call(functools.partial(backward_kernel, scale), grid_spec=pltpu...  35 us
  transfers between devices with their start and end apart: 53, of which 20 were waited for; matrix products, arithmetic and copies ran while one was open for 35% of the time, Pallas kernels for 6%

profile of v1, /device:TPU:0, one launch (start us, length us, event | category | flops | bytes accessed | tf_op | source)
XLA Modules:
  0.0 942.2 jit_solution(16103885425518348697)
XLA Ops:
  37.8 7.8 all-gather.6.cloned.1.call-done
  48.5 25.6 %all-gather.8.cloned.1.call-done = bf16[512,1024]{1,0:T(8,128)(2,1)} async-done(((bf16[128,1024]{1,0:T(8,128)(2,1)}), bf16[512,1024]{1,0:T(8,128)(2,1)}) %all-gather.8.cloned.1.call-update) | async-done | bytes 1048592 | tf_op jit(solution)/shard_map/all_gather | solution.py:299
  110.1 24.4 %all-gather.14.cloned.1.call-done = bf16[512,2816]{1,0:T(8,128)(2,1)} async-done(((bf16[128,2816]{1,0:T(8,128)(2,1)}), bf16[512,2816]{1,0:T(8,128)(2,1)}) %all-gather.14.cloned.1.call-update) | async-done | bytes 2883600 | tf_op jit(solution)/shard_map/all_gather | solution.py:299
  135.9 57.9 %all-gather.12.cloned.1.call-done = bf16[512,2816]{1,0:T(8,128)(2,1)} async-done(((bf16[128,2816]{1,0:T(8,128)(2,1)}), bf16[512,2816]{1,0:T(8,128)(2,1)}) %all-gather.12.cloned.1.call-update) | async-done | bytes 2883600 | tf_op jit(solution)/shard_map/all_gather | solution.py:299
  196.4 7.7 fusion.60.qkv_ref
  207.8 16.2 %shard_map.204 = (bf16[768,1024]{1,0:T(8,128)(2,1)S(1)}, f32[768,256]{1,0:T(8,128)S(1)}) custom-call(s32[3]{0:T(128)S(1)} %convert_reduce_fusion.1.low_ref, bf16[768,1280]{1,0:T(8,128)(2,1)S(1)} %shard_map.203.q_ref.k_ref.v_ref, bf16[768,1280]{1,0:T(8,128)(2,1)S(1)} %shard_map.203.q_ref.k_ref.v_ref, bf16[768,1280]{1,0:T(8,128)(2,1)S(1)} %shard_map.203.q_ref.k_ref.v_ref, ...), custom_call_target="tpu_custom_call" | custom-call | flops 6039797760 | bytes 3145728 | tf_op jit(solution)/shard_map/pallas_call | solution.py:222
  242.8 10.3 %all-gather.10.cloned.1.call-done = bf16[512,2816]{1,0:T(8,128)(2,1)} async-done(((bf16[128,2816]{1,0:T(8,128)(2,1)}), bf16[512,2816]{1,0:T(8,128)(2,1)}) %all-gather.10.cloned.1.call-update) | async-done | bytes 2883600 | tf_op jit(solution)/shard_map/all_gather | solution.py:299
  256.6 8.7 collective-permute-done.7
  284.2 38.2 %collective-permute-done.9 = bf16[512,2816]{1,0:T(8,128)(2,1)S(1)} collective-permute-done((bf16[512,2816]{1,0:T(8,128)(2,1)}, bf16[512,2816]{1,0:T(8,128)(2,1)S(1)}, u32[]{:S(2)}, u32[]{:S(2)}) %collective-permute-start.9) | collective-permute-done | bytes 2883616 | tf_op jit(solution)/shard_map/ppermute | solution.py:300
  334.4 14.3 %convolution_convert_fusion.3 = bf16[768,2816]{1,0:T(8,128)(2,1)} fusion(bf16[768,2048]{1,0:T(8,128)(2,1)S(1)} %maximum_select_fusion.1, bf16[2048,2816]{1,0:T(8,128)(2,1)} %constant_dynamic-update-slice_fusion.12), kind=kOutput, calls=%fused_computation.25 | convolution fusion | flops 8860532736 | bytes 19005440 | tf_op jit(solution)/shard_map/dot_general | solution.py:21
  350.4 14.1 %convolution_convert_fusion.4 = bf16[768,2816]{1,0:T(8,128)(2,1)} fusion(bf16[768,2048]{1,0:T(8,128)(2,1)S(1)} %maximum_select_fusion.1, bf16[2048,2816]{1,0:T(8,128)(2,1)} %constant_dynamic-update-slice_fusion.8), kind=kOutput, calls=%fused_computation.26 | convolution fusion | flops 8860532736 | bytes 19005440 | tf_op jit(solution)/shard_map/dot_general | solution.py:21
  367.5 19.2 %fusion.3 = (bf16[768,2816]{1,0:T(8,128)(2,1)}, bf16[768,2816]{1,0:T(8,128)(2,1)}, bf16[768,2816]{1,0:T(8,128)(2,1)}) fusion(bf16[768,2816]{1,0:T(8,128)(2,1)} %convolution_convert_fusion.3, bf16[768,2816]{1,0:T(8,128)(2,1)} %convolution_convert_fusion.4, bf16[768,2048]{1,0:T(8,128)(2,1)S(1)} %copy-done.13, ...), kind=kOutput, calls=%fused_computation.9 | convolution fusion | flops 8897298432 | bytes 36306944 | tf_op jit(solution)/shard_map/dot_general | solution.py:21
  386.7 11.3 %fusion.14 = f32[384,2048]{1,0:T(8,128)} fusion(bf16[2048,2816]{1,0:T(8,128)(2,1)} %constant_dynamic-update-slice_fusion.12, bf16[768,2816]{1,0:T(8,128)(2,1)} %get-tuple-element.29, s32[]{:T(128)S(6)} %select_n.121), kind=kOutput, calls=%fused_computation.66 | convolution fusion | flops 4429185024 | bytes 16842756 | tf_op jit(solution)/shard_map/dot_general | solution.py:25
  397.9 11.6 %add_convert_fusion.7 = bf16[384,2048]{1,0:T(8,128)(2,1)} fusion(f32[384,2048]{1,0:T(8,128)} %fusion.14, bf16[2048,2816]{1,0:T(8,128)(2,1)} %constant_dynamic-update-slice_fusion.8, bf16[768,2816]{1,0:T(8,128)(2,1)} %get-tuple-element.28, s32[]{:T(128)S(6)} %select_n.121), kind=kOutput, calls=%fused_computation.46 | convolution fusion | flops 4430757888 | bytes 18415620 | tf_op jit(solution)/shard_map/dot_general | solution.py:25
  411.0 11.3 %fusion.19 = f32[384,2048]{1,0:T(8,128)} fusion(bf16[2048,2816]{1,0:T(8,128)(2,1)} %constant_dynamic-update-slice_fusion.8, bf16[768,2816]{1,0:T(8,128)(2,1)} %get-tuple-element.28, s32[]{:T(128)S(6)} %select_n.120), kind=kOutput, calls=%fused_computation.71 | convolution fusion | flops 4429185024 | bytes 16842756 | tf_op jit(solution)/shard_map/dot_general | solution.py:25
  422.3 10.0 %fusion.17 = f32[384,2048]{1,0:T(8,128)} fusion(bf16[2048,2816]{1,0:T(8,128)(2,1)} %constant_dynamic-update-slice_fusion.12, bf16[768,2816]{1,0:T(8,128)(2,1)S(1)} %copy-done.8, s32[]{:T(128)S(6)} %select_n.120), kind=kOutput, calls=%fused_computation.69 | convolution fusion | flops 4429185024 | bytes 16842756 | tf_op jit(solution)/shard_map/dot_general | solution.py:25
  432.3 13.9 %collective-permute-done.20 = bf16[384,2048]{1,0:T(8,128)(2,1)} collective-permute-done((bf16[384,2048]{1,0:T(8,128)(2,1)}, bf16[384,2048]{1,0:T(8,128)(2,1)}, u32[]{:S(2)}, u32[]{:S(2)}) %collective-permute-start.20) | collective-permute-done | bytes 1572896 | tf_op jit(solution)/shard_map/ppermute | solution.py:344
  456.8 8.7 convolution_convert_fusion.2
  465.6 25.3 %collective-permute-done.21 = bf16[384,2048]{1,0:T(8,128)(2,1)S(1)} collective-permute-done((bf16[384,2048]{1,0:T(8,128)(2,1)S(1)}, bf16[384,2048]{1,0:T(8,128)(2,1)S(1)}, u32[]{:S(2)}, u32[]{:S(2)}) %collective-permute-start.21) | collective-permute-done | bytes 1572896 | tf_op jit(solution)/shard_map/ppermute | solution.py:330
  500.0 35.0 %shard_map.205 = (bf16[768,1024]{1,0:T(8,128)(2,1)S(1)}, bf16[768,128]{1,0:T(8,128)(2,1)S(1)}, bf16[768,128]{1,0:T(8,128)(2,1)S(1)}) custom-call(s32[3]{0:T(128)S(1)} %convert_reduce_fusion.1.low_ref, bf16[768,1280]{1,0:T(8,128)(2,1)S(1)} %copy-done.1, bf16[768,1280]{1,0:T(8,128)(2,1)S(1)} %copy-done.1, bf16[768,1280]{1,0:T(8,128)(2,1)S(1)} %copy-done.1, ...), custom_call_target="tpu_custom_call" | custom-call | flops 18119393280 | bytes 6291456 | tf_op jit(solution)/shard_map/pallas_call | solution.py:251
  552.0 16.0 %collective-permute-done.26 = bf16[512,1024]{1,0:T(8,128)(2,1)S(1)} collective-permute-done((bf16[512,1024]{1,0:T(8,128)(2,1)S(1)}, bf16[512,1024]{1,0:T(8,128)(2,1)S(1)}, u32[]{:S(2)}, u32[]{:S(2)}) %collective-permute-start.26) | collective-permute-done | bytes 1048608 | tf_op jit(solution)/shard_map/ppermute | solution.py:312
  574.7 7.2 add_convert_fusion.5
  582.6 22.4 %collective-permute-done.24 = bf16[512,1280]{1,0:T(8,128)(2,1)S(1)} collective-permute-done((bf16[512,1280]{1,0:T(8,128)(2,1)S(1)}, bf16[512,1280]{1,0:T(8,128)(2,1)S(1)}, u32[]{:S(2)}, u32[]{:S(2)}) %collective-permute-start.24) | collective-permute-done | bytes 1310752 | tf_op jit(solution)/shard_map/ppermute | solution.py:312
  613.7 51.3 %collective-permute-done.33 = bf16[512,2816]{1,0:T(8,128)(2,1)} collective-permute-done((bf16[512,2816]{1,0:T(8,128)(2,1)}, bf16[512,2816]{1,0:T(8,128)(2,1)}, u32[]{:S(2)}, u32[]{:S(2)}) %collective-permute-start.33) | collective-permute-done | bytes 2883616 | tf_op jit(solution)/shard_map/ppermute | solution.py:312
  670.6 10.0 %convolution_convert_fusion = bf16[1024,2816]{1,0:T(8,128)(2,1)} fusion(bf16[768,2816]{1,0:T(8,128)(2,1)} %get-tuple-element.30, bf16[768,2048]{1,0:T(8,128)(2,1)} %maximum_select_fusion.2), kind=kOutput, calls=%fused_computation.22 | convolution fusion | flops 4432068608 | bytes 11665408 | tf_op jit(solution)/shard_map/dot_general | solution.py:29
  688.9 61.0 %collective-permute-done.35 = bf16[512,2816]{1,0:T(8,128)(2,1)S(1)} collective-permute-done((bf16[512,2816]{1,0:T(8,128)(2,1)S(1)}, bf16[512,2816]{1,0:T(8,128)(2,1)S(1)}, u32[]{:S(2)}, u32[]{:S(2)}) %collective-permute-start.35) | collective-permute-done | bytes 2883616 | tf_op jit(solution)/shard_map/ppermute | solution.py:312
  754.8 7.3 add_convert_fusion.1
  763.5 10.8 %convolution_convert_fusion.7 = bf16[384,2048]{1,0:T(8,128)(2,1)} fusion(bf16[2048,2816]{1,0:T(8,128)(2,1)} %constant_dynamic-update-slice_fusion.16, bf16[768,2816]{1,0:T(8,128)(2,1)} %get-tuple-element.30, s32[]{:T(128)S(6)} %select_n.121), kind=kOutput, calls=%fused_computation.55 | convolution fusion | flops 4429971456 | bytes 15269892 | tf_op jit(solution)/shard_map/dot_general | solution.py:25
  780.7 45.9 %collective-permute-done.37 = bf16[512,2816]{1,0:T(8,128)(2,1)} collective-permute-done((bf16[512,2816]{1,0:T(8,128)(2,1)}, bf16[512,2816]{1,0:T(8,128)(2,1)}, u32[]{:S(2)}, u32[]{:S(2)}) %collective-permute-start.37) | collective-permute-done | bytes 2883616 | tf_op jit(solution)/shard_map/ppermute | solution.py:312
  847.4 13.6 %add_convert_fusion.8 = bf16[384,2048]{1,0:T(8,128)(2,1)} fusion(f32[384,2048]{1,0:T(8,128)S(1)} %copy-done.7, bf16[384,2048]{1,0:T(8,128)(2,1)} %collective-permute-done.18, bf16[2048,2816]{1,0:T(8,128)(2,1)} %constant_dynamic-update-slice_fusion.16, bf16[768,2816]{1,0:T(8,128)(2,1)S(1)} %bitcast.66, s32[]{:T(128)S(6)} %select_n.120), kind=kOutput, calls=%fused_computation.47 | convolution fusion | flops 4432330752 | bytes 19988484 | tf_op jit(solution)/shard_map/dot_general | solution.py:25
  871.0 11.5 %collective-permute-done.22 = bf16[384,2048]{1,0:T(8,128)(2,1)} collective-permute-done((bf16[384,2048]{1,0:T(8,128)(2,1)}, bf16[384,2048]{1,0:T(8,128)(2,1)}, u32[]{:S(2)}, u32[]{:S(2)}) %collective-permute-start.22) | collective-permute-done | bytes 1572896 | tf_op jit(solution)/shard_map/ppermute | solution.py:344
  882.5 7.2 multiply_reduce_fusion.1
  (302 shorter events, 291.3 us)
Async XLA Ops:
  7.2 38.4 %all-gather.6.cloned.1.call-start = ((), (), s32[]{:S(2)}) async-start(), calls=%async_computation.5 | async-start | bytes 1638400 | tf_op jit(solution)/shard_map/all_gather | solution.py:299
  9.1 65.0 %all-gather.8.cloned.1.call-start = ((), (), s32[]{:S(2)}) async-start(), calls=%async_computation.6 | async-start | bytes 1310720 | tf_op jit(solution)/shard_map/all_gather | solution.py:299
  9.9 124.6 %all-gather.14.cloned.1.call-start = ((), (), s32[]{:S(2)}) async-start(), calls=%async_computation.9 | async-start | bytes 3604480 | tf_op jit(solution)/shard_map/all_gather | solution.py:299
  10.6 183.2 %all-gather.12.cloned.1.call-start = ((), (), s32[]{:S(2)}) async-start(), calls=%async_computation.8 | async-start | bytes 3604480 | tf_op jit(solution)/shard_map/all_gather | solution.py:299
  11.2 241.9 %all-gather.10.cloned.1.call-start = ((), (), s32[]{:S(2)}) async-start(), calls=%async_computation.7 | async-start | bytes 3604480 | tf_op jit(solution)/shard_map/all_gather | solution.py:299
  28.4 55.5 %collective-permute-start = (bf16[384,2048]{1,0:T(8,128)(2,1)}, bf16[384,2048]{1,0:T(8,128)(2,1)}, u32[]{:S(2)}, u32[]{:S(2)}) collective-permute-start(bf16[384,2048]{1,0:T(8,128)(2,1)} %multiply_convert_fusion.1), channel_id=1, source_target_pairs={{0,1},{1,0},{2,3},{3,2},{4,5},{5,4},{6,7},{7,6},{8,9},{9,8},{10,11... | collective-permute-start | bytes 4718600 | tf_op jit(solution)/shard_map/ppermute | solution.py:330
  31.4 891.5 %reduce-scatter.8.cloned.1.call-start = ((), (), s32[]{:S(2)}) async-start(), calls=%async_computation.11 | async-start | bytes 1310720 | tf_op jit(solution)/shard_map/reduce_scatter | solution.py:318
  45.6 44.8 %collective-permute-start.1 = (bf16[512,1280]{1,0:T(8,128)(2,1)}, bf16[512,1280]{1,0:T(8,128)(2,1)}, u32[]{:S(2)}, u32[]{:S(2)}) collective-permute-start(bf16[512,1280]{1,0:T(8,128)(2,1)} %all-gather.6.cloned.1.call-done), channel_id=1, source_target_pairs={{0,4},{4,0},{1,5},{5,1},{2,6},{6,2},{3,7},{7,3},{8,12},{12,8},{9,1... | collective-permute-start | bytes 3932168 | tf_op jit(solution)/shard_map/ppermute | solution.py:300
  83.9 148.1 %collective-permute-start.19 = (bf16[384,2048]{1,0:T(8,128)(2,1)}, bf16[384,2048]{1,0:T(8,128)(2,1)}, u32[]{:S(2)}, u32[]{:S(2)}) collective-permute-start(bf16[384,2048]{1,0:T(8,128)(2,1)} %reshape.112), channel_id=1, source_target_pairs={{0,1},{1,0},{2,3},{3,2},{4,5},{5,4},{6,7},{7,6},{8,9},{9,8},{10,11... | collective-permute-start | bytes 4718600 | tf_op jit(solution)/shard_map/ppermute | solution.py:330
  90.4 104.9 %collective-permute-start.3 = (bf16[512,1280]{1,0:T(8,128)(2,1)}, bf16[512,1280]{1,0:T(8,128)(2,1)S(1)}, u32[]{:S(2)}, u32[]{:S(2)}) collective-permute-start(bf16[512,1280]{1,0:T(8,128)(2,1)} %collective-permute-done.1), channel_id=1, source_target_pairs={{0,2},{2,0},{1,3},{3,1},{4,6},{6,4},{5,7},{7,5},{8,10},{10,8},{9,1... | collective-permute-start | bytes 3932168 | tf_op jit(solution)/shard_map/ppermute | solution.py:302
  134.5 130.9 %collective-permute-start.15 = (bf16[512,2816]{1,0:T(8,128)(2,1)}, bf16[512,2816]{1,0:T(8,128)(2,1)}, u32[]{:S(2)}, u32[]{:S(2)}) collective-permute-start(bf16[512,2816]{1,0:T(8,128)(2,1)} %all-gather.14.cloned.1.call-done), channel_id=1, source_target_pairs={{0,4},{4,0},{1,5},{5,1},{2,6},{6,2},{3,7},{7,3},{8,12},{12,8},{9,1... | collective-permute-start | bytes 8650760 | tf_op jit(solution)/shard_map/ppermute | solution.py:300
  193.8 77.0 %collective-permute-start.12 = (bf16[512,2816]{1,0:T(8,128)(2,1)}, bf16[512,2816]{1,0:T(8,128)(2,1)}, u32[]{:S(2)}, u32[]{:S(2)}) collective-permute-start(bf16[512,2816]{1,0:T(8,128)(2,1)} %all-gather.12.cloned.1.call-done), channel_id=1, source_target_pairs={{0,4},{4,0},{1,5},{5,1},{2,6},{6,2},{3,7},{7,3},{8,12},{12,8},{9,1... | collective-permute-start | bytes 8650760 | tf_op jit(solution)/shard_map/ppermute | solution.py:300
  237.2 41.9 %collective-permute-start.16 = (bf16[512,2816]{1,0:T(8,128)(2,1)}, bf16[512,2816]{1,0:T(8,128)(2,1)}, u32[]{:S(2)}, u32[]{:S(2)}) collective-permute-start(bf16[512,2816]{1,0:T(8,128)(2,1)} %all-gather.14.cloned.1.call-done), channel_id=1, source_target_pairs={{0,2},{2,0},{1,3},{3,1},{4,6},{6,4},{5,7},{7,5},{8,10},{10,8},{9,1... | collective-permute-start | bytes 8650760 | tf_op jit(solution)/shard_map/ppermute | solution.py:302
  253.1 69.3 %collective-permute-start.9 = (bf16[512,2816]{1,0:T(8,128)(2,1)}, bf16[512,2816]{1,0:T(8,128)(2,1)S(1)}, u32[]{:S(2)}, u32[]{:S(2)}) collective-permute-start(bf16[512,2816]{1,0:T(8,128)(2,1)} %all-gather.10.cloned.1.call-done), channel_id=1, source_target_pairs={{0,4},{4,0},{1,5},{5,1},{2,6},{6,2},{3,7},{7,3},{8,12},{12,8},{9,1... | collective-permute-start | bytes 8650760 | tf_op jit(solution)/shard_map/ppermute | solution.py:300
  265.3 61.5 %collective-permute-start.13 = (bf16[512,2816]{1,0:T(8,128)(2,1)}, bf16[512,2816]{1,0:T(8,128)(2,1)S(1)}, u32[]{:S(2)}, u32[]{:S(2)}) collective-permute-start(bf16[512,2816]{1,0:T(8,128)(2,1)} %all-gather.12.cloned.1.call-done), channel_id=1, source_target_pairs={{0,2},{2,0},{1,3},{3,1},{4,6},{6,4},{5,7},{7,5},{8,10},{10,8},{9,1... | collective-permute-start | bytes 8650760 | tf_op jit(solution)/shard_map/ppermute | solution.py:302
  265.3 63.8 %collective-permute-start.10 = (bf16[512,2816]{1,0:T(8,128)(2,1)}, bf16[512,2816]{1,0:T(8,128)(2,1)S(1)}, u32[]{:S(2)}, u32[]{:S(2)}) collective-permute-start(bf16[512,2816]{1,0:T(8,128)(2,1)} %all-gather.10.cloned.1.call-done), channel_id=1, source_target_pairs={{0,2},{2,0},{1,3},{3,1},{4,6},{6,4},{5,7},{7,5},{8,10},{10,8},{9,1... | collective-permute-start | bytes 8650760 | tf_op jit(solution)/shard_map/ppermute | solution.py:302
  270.8 61.7 %collective-permute-start.14 = (bf16[512,2816]{1,0:T(8,128)(2,1)}, bf16[512,2816]{1,0:T(8,128)(2,1)S(1)}, u32[]{:S(2)}, u32[]{:S(2)}) collective-permute-start(bf16[512,2816]{1,0:T(8,128)(2,1)} %collective-permute-done.12), channel_id=1, source_target_pairs={{0,2},{2,0},{1,3},{3,1},{4,6},{6,4},{5,7},{7,5},{8,10},{10,8},{9,1... | collective-permute-start | bytes 8650760 | tf_op jit(solution)/shard_map/ppermute | solution.py:302
  279.1 51.7 %collective-permute-start.8 = (bf16[384,2048]{1,0:T(8,128)(2,1)S(1)}, bf16[384,2048]{1,0:T(8,128)(2,1)S(1)}, u32[]{:S(2)}, u32[]{:S(2)}) collective-permute-start(bf16[384,2048]{1,0:T(8,128)(2,1)S(1)} %multiply_convert_fusion), channel_id=1, source_target_pairs={{0,1},{1,0},{2,3},{3,2},{4,5},{5,4},{6,7},{7,6},{8,9},{9,8},{10,11... | collective-permute-start | bytes 4718600 | tf_op jit(solution)/shard_map/ppermute | solution.py:330
  322.4 42.1 %collective-permute-start.17 = (bf16[512,2816]{1,0:T(8,128)(2,1)}, bf16[512,2816]{1,0:T(8,128)(2,1)S(1)}, u32[]{:S(2)}, u32[]{:S(2)}) collective-permute-start(bf16[512,2816]{1,0:T(8,128)(2,1)} %collective-permute-done.15), channel_id=1, source_target_pairs={{0,2},{2,0},{1,3},{3,1},{4,6},{6,4},{5,7},{7,5},{8,10},{10,8},{9,1... | collective-permute-start | bytes 8650760 | tf_op jit(solution)/shard_map/ppermute | solution.py:302
  409.5 36.6 %collective-permute-start.20 = (bf16[384,2048]{1,0:T(8,128)(2,1)}, bf16[384,2048]{1,0:T(8,128)(2,1)}, u32[]{:S(2)}, u32[]{:S(2)}) collective-permute-start(bf16[384,2048]{1,0:T(8,128)(2,1)} %add_convert_fusion.7), channel_id=1, source_target_pairs={{0,1},{1,0},{2,3},{3,2},{4,5},{5,4},{6,7},{7,6},{8,9},{9,8},{10,11... | collective-permute-start | bytes 4718600 | tf_op jit(solution)/shard_map/ppermute | solution.py:344
  465.6 109.1 %collective-permute-start.32 = (bf16[1024,2816]{1,0:T(8,128)(2,1)}, bf16[1024,2816]{1,0:T(8,128)(2,1)}, u32[]{:S(2)}, u32[]{:S(2)}) collective-permute-start(bf16[1024,2816]{1,0:T(8,128)(2,1)} %convolution_convert_fusion.2), channel_id=1, source_target_pairs={{0,2},{2,0},{1,3},{3,1},{4,6},{6,4},{5,7},{7,5},{8,10},{10,8},{9,1... | collective-permute-start | bytes 17301512 | tf_op jit(solution)/shard_map/ppermute | solution.py:310
  499.9 41.9 %collective-permute-start.25 = (bf16[1024,1024]{1,0:T(8,128)(2,1)S(1)}, bf16[1024,1024]{1,0:T(8,128)(2,1)S(1)}, u32[]{:S(2)}, u32[]{:S(2)}) collective-permute-start(bf16[1024,1024]{1,0:T(8,128)(2,1)S(1)} %convolution_convert_fusion.9), channel_id=1, source_target_pairs={{0,2},{2,0},{1,3},{3,1},{4,6},{6,4},{5,7},{7,5},{8,10},{10,8},{9,1... | collective-permute-start | bytes 6291464 | tf_op jit(solution)/shard_map/ppermute | solution.py:310
  551.0 129.6 %collective-permute-start.34 = (bf16[1024,2816]{1,0:T(8,128)(2,1)}, bf16[1024,2816]{1,0:T(8,128)(2,1)}, u32[]{:S(2)}, u32[]{:S(2)}) collective-permute-start(bf16[1024,2816]{1,0:T(8,128)(2,1)} %convolution_convert_fusion.1), channel_id=1, source_target_pairs={{0,2},{2,0},{1,3},{3,1},{4,6},{6,4},{5,7},{7,5},{8,10},{10,8},{9,1... | collective-permute-start | bytes 17301512 | tf_op jit(solution)/shard_map/ppermute | solution.py:310
  569.6 355.2 %reduce-scatter.6.cloned.1.call-start = ((), (), s32[]{:S(2)}) async-start(), calls=%async_computation.10 | async-start | bytes 1638400 | tf_op jit(solution)/shard_map/reduce_scatter | solution.py:318
  581.8 83.2 %collective-permute-start.33 = (bf16[512,2816]{1,0:T(8,128)(2,1)}, bf16[512,2816]{1,0:T(8,128)(2,1)}, u32[]{:S(2)}, u32[]{:S(2)}) collective-permute-start(bf16[512,2816]{1,0:T(8,128)(2,1)} %add_convert_fusion.5), channel_id=1, source_target_pairs={{0,4},{4,0},{1,5},{5,1},{2,6},{6,2},{3,7},{7,3},{8,12},{12,8},{9,1... | collective-permute-start | bytes 8650760 | tf_op jit(solution)/shard_map/ppermute | solution.py:312
  608.9 319.1 %reduce-scatter.10.cloned.1.call-start = ((), (), s32[]{:S(2)}) async-start(), calls=%async_computation.12 | async-start | bytes 3604480 | tf_op jit(solution)/shard_map/reduce_scatter | solution.py:318
  670.4 259.9 %reduce-scatter.12.cloned.1.call-start = ((), (), s32[]{:S(2)}) async-start(), calls=%async_computation.13 | async-start | bytes 3604480 | tf_op jit(solution)/shard_map/reduce_scatter | solution.py:318
  680.6 74.2 %collective-permute-start.36 = (bf16[1024,2816]{1,0:T(8,128)(2,1)}, bf16[1024,2816]{1,0:T(8,128)(2,1)}, u32[]{:S(2)}, u32[]{:S(2)}) collective-permute-start(bf16[1024,2816]{1,0:T(8,128)(2,1)} %convolution_convert_fusion), channel_id=1, source_target_pairs={{0,2},{2,0},{1,3},{3,1},{4,6},{6,4},{5,7},{7,5},{8,10},{10,8},{9,1... | collective-permute-start | bytes 17301512 | tf_op jit(solution)/shard_map/ppermute | solution.py:310
  684.9 65.0 %collective-permute-start.35 = (bf16[512,2816]{1,0:T(8,128)(2,1)S(1)}, bf16[512,2816]{1,0:T(8,128)(2,1)S(1)}, u32[]{:S(2)}, u32[]{:S(2)}) collective-permute-start(bf16[512,2816]{1,0:T(8,128)(2,1)S(1)} %add_convert_fusion.3), channel_id=1, source_target_pairs={{0,4},{4,0},{1,5},{5,1},{2,6},{6,2},{3,7},{7,3},{8,12},{12,8},{9,1... | collective-permute-start | bytes 8650760 | tf_op jit(solution)/shard_map/ppermute | solution.py:312
  754.5 178.1 %reduce-scatter.14.cloned.1.call-start = ((), (), s32[]{:S(2)}) async-start(), calls=%async_computation.14 | async-start | bytes 3604480 | tf_op jit(solution)/shard_map/reduce_scatter | solution.py:318
  762.1 64.4 %collective-permute-start.37 = (bf16[512,2816]{1,0:T(8,128)(2,1)}, bf16[512,2816]{1,0:T(8,128)(2,1)}, u32[]{:S(2)}, u32[]{:S(2)}) collective-permute-start(bf16[512,2816]{1,0:T(8,128)(2,1)} %add_convert_fusion.1), channel_id=1, source_target_pairs={{0,4},{4,0},{1,5},{5,1},{2,6},{6,2},{3,7},{7,3},{8,12},{12,8},{9,1... | collective-permute-start | bytes 8650760 | tf_op jit(solution)/shard_map/ppermute | solution.py:312
  774.3 73.1 %collective-permute-start.18 = (bf16[384,2048]{1,0:T(8,128)(2,1)}, bf16[384,2048]{1,0:T(8,128)(2,1)}, u32[]{:S(2)}, u32[]{:S(2)}) collective-permute-start(bf16[384,2048]{1,0:T(8,128)(2,1)} %convolution_convert_fusion.7), channel_id=1, source_target_pairs={{0,1},{1,0},{2,3},{3,2},{4,5},{5,4},{6,7},{7,6},{8,9},{9,8},{10,11... | collective-permute-start | bytes 4718600 | tf_op jit(solution)/shard_map/ppermute | solution.py:344
  (60 other events, 1087.8 us)
Sparse Core Ops, SparseCore 0:
  10.2 35.3 all-gather.5
  47.2 26.9 all-gather.7
  75.7 58.7 all-gather.13
  135.9 57.8 all-gather.11
  195.2 57.8 all-gather.9
  569.7 25.9 reduce-scatter.7
  609.0 29.9 reduce-scatter.5
  670.5 55.4 reduce-scatter.9
  754.6 55.3 reduce-scatter.11
  833.5 55.7 reduce-scatter.13

commit v2 on v1

--- a/solution.py
+++ b/solution.py
@@ -10,6 +10,7 @@
 HEAD_DIM = 64
 SWAP = ((0, 1), (1, 0))
 QUERIES = 256
+CHUNKS = 2
 VMEM = 40 * 2**20
 epsilon = 1e-05
 rope_base = 10000.0
@@ -280,6 +281,22 @@
     )
 
 
+def tie(array, *earlier):
+    return lax.optimization_barrier((array,) + earlier)[0]
+
+
+class Order:
+    def __init__(self):
+        self.last = None
+
+    def __call__(self, compute, *operands):
+        if self.last is not None:
+            operands = lax.optimization_barrier((*operands, self.last))[:-1]
+        result = compute(*operands)
+        self.last = result[0] if isinstance(result, tuple) else result
+        return result
+
+
 def make_shards(outer):
     def relative(array):
         rows, width = array.shape
@@ -295,27 +312,12 @@
         blocks = jnp.where(lax.axis_index("core") == 0, blocks, blocks[:, :, :, ::-1])
         return blocks.reshape(rows, width)
 
-    def gather(weight):
-        along = lax.all_gather(weight, "z", axis=0, tiled=True)
+    def gather(along):
         across = lax.ppermute(along, "x", SWAP)
         return jnp.concatenate(
             [along, across, lax.ppermute(along, "core", SWAP), lax.ppermute(across, "core", SWAP)],
             axis=0,
         )
-
-    def scatter(left, right):
-        half = left.shape[1] // 2
-        quarter = half // 2
-        for_core = dot_inner(left[:, half:], right).astype(bf16)
-        from_core = lax.ppermute(for_core, "core", SWAP)
-        for_x = (dot_inner(left[:, quarter:half], right) + from_core[quarter:].astype(f32)).astype(bf16)
-        from_x = lax.ppermute(for_x, "x", SWAP)
-        kept = (
-            dot_inner(left[:, :quarter], right)
-            + from_core[:quarter].astype(f32)
-            + from_x.astype(f32)
-        ).astype(bf16)
-        return lax.psum_scatter(kept, "z", scatter_dimension=0, tiled=True).astype(f32)
 
     def total(vector):
         for axis in ("core", "x", "tensor"):
@@ -326,23 +328,12 @@
             step *= 2
         return vector
 
-    def both_halves(own):
-        other = lax.ppermute(own, "tensor", SWAP)
-        return jnp.where(
-            lax.axis_index("tensor") == 0,
-            jnp.concatenate([own, other], axis=0),
-            jnp.concatenate([other, own], axis=0),
-        )
-
-    def reduce_halves(product, *operands):
-        rows = operands[0].shape[0] // 2
-        place = lax.axis_index("tensor")
-
-        def cut(at):
-            return [lax.dynamic_slice_in_dim(o, at * rows, rows, axis=0) for o in operands]
-
-        sent = lax.ppermute(product(*cut(1 - place)).astype(bf16), "tensor", SWAP)
-        return product(*cut(place)) + sent.astype(f32)
+    def join(own, other):
+        first = lax.axis_index("tensor") == 0
+        return jnp.concatenate([jnp.where(first, own, other), jnp.where(first, other, own)], axis=0)
+
+    def swap(own):
+        return lax.ppermute(own, "tensor", SWAP)
 
     def shards(
         tokens,
@@ -360,17 +351,66 @@
     ):
         query_width = q_weight.shape[1]
         key_width = k_weight.shape[1]
+        hidden_width = gate_weight.shape[1]
         score_scale = HEAD_DIM ** (-0.5)
-        qkv_full = gather(jnp.concatenate([q_weight, k_weight, v_weight], axis=1))
-        output_full = gather(o_weight)
-        gate_full = gather(gate_weight)
-        up_full = gather(up_weight)
-        down_full = gather(down_weight)
+        place = lax.axis_index("tensor")
+        order = Order()
+
+        def cut(weight):
+            width = hidden_width // CHUNKS
+            return [weight[:, i * width : i * width + width] for i in range(CHUNKS)]
+
+        names = ["qkv", "o"]
+        shard = {"qkv": jnp.concatenate([q_weight, k_weight, v_weight], axis=1), "o": o_weight}
+        for i, (gate, up) in enumerate(zip(cut(gate_weight), cut(up_weight))):
+            names += [("gate", i), ("up", i)]
+            shard["gate", i], shard["up", i] = gate, up
+        for i, down in enumerate(cut(down_weight)):
+            names.append(("down", i))
+            shard["down", i] = down
+        along = {}
+        for at, name in enumerate(names):
+            operand = shard[name]
+            if at > 1:
+                operand = tie(operand, along[names[at - 2]])
+            along[name] = lax.all_gather(operand, "z", axis=0, tiled=True)
+        full = {name: gather(along[name]) for name in names}
 
         attention_gain = relative(attention_gain[None])
         feed_gain = relative(feed_gain[None])
         tokens = relative(tokens)
         out_grad = relative(out_grad)
+        half = tokens.shape[1] // 2
+        quarter = half // 2
+        rows = tokens.shape[0]
+
+        def mine(array):
+            return lax.dynamic_slice_in_dim(array, place * rows, rows, axis=0)
+
+        def theirs(array):
+            return lax.dynamic_slice_in_dim(array, (1 - place) * rows, rows, axis=0)
+
+        from_core, from_x, summed = {}, {}, {}
+
+        def for_core(name, left, right):
+            part = order(lambda l, r: dot_inner(l[:, half:], r).astype(bf16), left, right)
+            from_core[name] = lax.ppermute(part, "core", SWAP)
+
+        def for_x(name, left, right):
+            part = order(
+                lambda l, r, c: (dot_inner(l[:, quarter:half], r) + c[quarter:].astype(f32)).astype(bf16),
+                left, right, from_core[name],
+            )
+            from_x[name] = lax.ppermute(part, "x", SWAP)
+
+        def keep(name, left, right):
+            part = order(
+                lambda l, r, c, x: (
+                    dot_inner(l[:, :quarter], r) + c[:quarter].astype(f32) + x.astype(f32)
+                ).astype(bf16),
+                left, right, from_core[name], from_x[name],
+            )
+            summed[name] = lax.psum_scatter(part, "z", scatter_dimension=0, tiled=True)
 
         segment_row = segments[0]
         cosine, sine = rotary_tables(segment_row)
@@ -378,73 +418,148 @@
         inputs = tokens.astype(f32)
         inverse_first = inverse_rms(inputs)
         normed_first = (inputs * inverse_first * attention_gain).astype(bf16)
-        normed_seq = both_halves(normed_first)
-        grad_seq = both_halves(out_grad)
-        qkv = dot_plain(normed_seq, qkv_full)
-        rotated = rope(qkv, cosine, sine, (query_width + key_width) // 128)
-        mixed, log_totals = attend(rotated, query_width, first_seen, segment_row, score_scale)
-        middle = inputs + reduce_halves(lambda m: dot_trans(m, output_full), mixed)
+        normed_seq = join(normed_first, swap(normed_first))
+        grad_seq = join(out_grad, swap(out_grad))
+
+        qkv = order(dot_plain, normed_seq, full["qkv"])
+        rotated = order(lambda a: rope(a, cosine, sine, (query_width + key_width) // 128), qkv)
+        mixed, log_totals = order(
+            lambda a: attend(a, query_width, first_seen, segment_row, score_scale), rotated
+        )
+        sent = swap(order(lambda m, w: dot_trans(theirs(m), w).astype(bf16), mixed, full["o"]))
+        own = order(lambda m, w: dot_trans(mine(m), w), mixed, full["o"])
+        middle = inputs + own + sent.astype(f32)
         inverse_second = inverse_rms(middle)
         normed_second = (middle * inverse_second * feed_gain).astype(bf16)
-        normed_feed = both_halves(normed_second)
-        gate_value = dot_plain(normed_feed, gate_full).astype(bf16)
-        up_value = dot_plain(normed_feed, up_full).astype(bf16)
-        hidden = (jax.nn.silu(gate_value.astype(f32)) * up_value.astype(f32)).astype(bf16)
-        down_weight_grad = scatter(grad_seq, hidden)
-        hidden_grad = dot_plain(grad_seq, down_full)
-        gate_value, up_value = gate_value.astype(f32), up_value.astype(f32)
-        sigmoid_gate = jax.nn.sigmoid(gate_value)
-        gate_grad = (
-            hidden_grad * up_value * sigmoid_gate * (1.0 + gate_value * (1.0 - sigmoid_gate))
-        ).astype(bf16)
-        up_grad = (hidden_grad * gate_value * sigmoid_gate).astype(bf16)
-        block_out = (middle + reduce_halves(lambda h: dot_trans(h, down_full), hidden)).astype(bf16)
-        feed_normed_grad = reduce_halves(
-            lambda g, u: dot_trans(g, gate_full) + dot_trans(u, up_full), gate_grad, up_grad
-        )
-        gate_weight_grad = scatter(normed_feed, gate_grad)
-        up_weight_grad = scatter(normed_feed, up_grad)
+        normed_feed = join(normed_second, swap(normed_second))
+
+        gates, ups, hiddens = [], [], []
+        for i in range(CHUNKS):
+            gate = order(lambda n, w: dot_plain(n, w).astype(bf16), normed_feed, full["gate", i])
+
+            def up_step(n, w, g):
+                u = dot_plain(n, w)
+                return u.astype(bf16), (jax.nn.silu(g.astype(f32)) * u).astype(bf16)
+
+            up, hidden = order(up_step, normed_feed, full["up", i], gate)
+            gates.append(gate)
+            ups.append(up)
+            hiddens.append(hidden)
+            for_core(("down", i), grad_seq, hidden)
+            if i > 0:
+                for_x(("down", i - 1), grad_seq, hiddens[i - 1])
+        for_x(("down", CHUNKS - 1), grad_seq, hiddens[-1])
+
+        gate_grads, up_grads = [], []
+        for i in range(CHUNKS):
+
+            def back_step(g, w, gate, up):
+                grad = dot_plain(g, w)
+                gate, up = gate.astype(f32), up.astype(f32)
+                sigmoid = jax.nn.sigmoid(gate)
+                return (
+                    (grad * up * sigmoid * (1.0 + gate * (1.0 - sigmoid))).astype(bf16),
+                    (grad * gate * sigmoid).astype(bf16),
+                )
+
+            gate_grad, up_grad = order(back_step, grad_seq, full["down", i], gates[i], ups[i])
+            gate_grads.append(gate_grad)
+            up_grads.append(up_grad)
+            if i < CHUNKS - 1:
+                for_core(("gate", i), normed_feed, gate_grad)
+                for_core(("up", i), normed_feed, up_grad)
+
+        def feed_back(pick):
+            total_grad = None
+            for i in range(CHUNKS):
+                for grad, name in ((gate_grads[i], "gate"), (up_grads[i], "up")):
+                    one = lambda g, w, t=None: dot_trans(pick(g), w) + (0.0 if t is None else t)
+                    more = () if total_grad is None else (total_grad,)
+                    total_grad = order(one, grad, full[name, i], *more)
+            return total_grad
+
+        sent = swap(feed_back(theirs).astype(bf16))
+        keep(("down", 0), grad_seq, hiddens[0])
+        for i in range(CHUNKS - 1):
+            for_x(("gate", i), normed_feed, gate_grads[i])
+            for_x(("up", i), normed_feed, up_grads[i])
+        for_core(("gate", CHUNKS - 1), normed_feed, gate_grads[-1])
+        for_core(("up", CHUNKS - 1), normed_feed, up_grads[-1])
+        own = feed_back(mine)
+        for_x(("gate", CHUNKS - 1), normed_feed, gate_grads[-1])
+        for_x(("up", CHUNKS - 1), normed_feed, up_grads[-1])
+        for i in range(1, CHUNKS):
+            keep(("down", i), grad_seq, hiddens[i])
+        own, sent = order(lambda a, b: (a, b), own, sent)
+        feed_normed_grad = own + sent.astype(f32)
         middle_grad = out_grad.astype(f32) + norm_back(
             middle, inverse_second, feed_gain, feed_normed_grad
         )
         feed_gain_part = jnp.sum(feed_normed_grad * middle * inverse_second, axis=0)
         attn_out_grad = middle_grad.astype(bf16)
-        attn_grad_seq = both_halves(attn_out_grad)
-        output_weight_grad = scatter(attn_grad_seq, mixed)
-        mixed_grad = dot_plain(attn_grad_seq, output_full).astype(bf16)
-        qkv_grad = jnp.concatenate(
-            attend_back(
-                rotated,
-                mixed_grad,
-                log_totals,
-                query_width,
-                first_seen,
-                segment_row,
-                cosine,
-                sine,
-                score_scale,
+        attn_out_grad, middle_grad, feed_gain_part = order(
+            lambda *a: a, attn_out_grad, middle_grad, feed_gain_part
+        )
+        attn_grad_other = swap(attn_out_grad)
+
+        def block(pick):
+            return lambda *a: sum(
+                dot_trans(pick(h), w) for h, w in zip(a[:CHUNKS], a[CHUNKS:])
+            )
+
+        downs = [full["down", i] for i in range(CHUNKS)]
+        sent = swap(order(lambda *a: block(theirs)(*a).astype(bf16), *hiddens, *downs))
+        keep(("gate", 0), normed_feed, gate_grads[0])
+        own = order(block(mine), *hiddens, *downs)
+        keep(("up", 0), normed_feed, up_grads[0])
+        attn_grad_seq = join(attn_out_grad, attn_grad_other)
+        mixed_grad = order(lambda g, w: dot_plain(g, w).astype(bf16), attn_grad_seq, full["o"])
+        for_core("o", attn_grad_seq, mixed)
+        block_out = order(lambda m, a, b: (m + a + b.astype(f32)).astype(bf16), middle, own, sent)
+        for_x("o", attn_grad_seq, mixed)
+        qkv_grad = order(
+            lambda r, g, l: jnp.concatenate(
+                attend_back(
+                    r, g, l, query_width, first_seen, segment_row, cosine, sine, score_scale
+                ),
+                axis=1,
             ),
-            axis=1,
+            rotated, mixed_grad, log_totals,
         )
-        qkv_weight_grad = scatter(normed_seq, qkv_grad)
-        normed_grad = reduce_halves(lambda g: dot_trans(g, qkv_full), qkv_grad)
+        for_core("qkv", normed_seq, qkv_grad)
+        for i in range(1, CHUNKS):
+            keep(("gate", i), normed_feed, gate_grads[i])
+        sent = swap(order(lambda g, w: dot_trans(theirs(g), w).astype(bf16), qkv_grad, full["qkv"]))
+        for_x("qkv", normed_seq, qkv_grad)
+        for i in range(1, CHUNKS):
+            keep(("up", i), normed_feed, up_grads[i])
+        own = order(lambda g, w: dot_trans(mine(g), w), qkv_grad, full["qkv"])
+        keep("o", attn_grad_seq, mixed)
+        feed_gain_grad = total(natural(feed_gain_part[None]))[0]
+        normed_grad = own + sent.astype(f32)
         input_grad = (
             middle_grad + norm_back(inputs, inverse_first, attention_gain, normed_grad)
         ).astype(bf16)
         attention_gain_part = jnp.sum(normed_grad * inputs * inverse_first, axis=0)
-        feed_gain_grad = total(natural(feed_gain_part[None]))[0]
+        input_grad, attention_gain_part = order(lambda *a: a, input_grad, attention_gain_part)
+        keep("qkv", normed_seq, qkv_grad)
         attention_gain_grad = total(natural(attention_gain_part[None]))[0]
+        qkv_weight_grad = summed["qkv"].astype(f32)
+
+        def whole(name):
+            return jnp.concatenate([summed[name, i] for i in range(CHUNKS)], axis=1).astype(f32)
+
         return (
             natural(block_out),
             natural(input_grad),
             qkv_weight_grad[:, :query_width],
             qkv_weight_grad[:, query_width : query_width + key_width],
             qkv_weight_grad[:, query_width + key_width :],
-            output_weight_grad,
+            summed["o"].astype(f32),
             attention_gain_grad,
-            gate_weight_grad,
-            up_weight_grad,
-            down_weight_grad,
+            whole("gate"),
+            whole("up"),
+            whole("down"),
             feed_gain_grad,
         )
 

time: 948 us -> 832 us (0.88)
  waiting for transfers between devices: 437 us -> 291 us
  matrix products: 225 us -> 250 us
  other arithmetic: 84.9 us -> 70.2 us
  local copies, waits for them, and re-layouts: 86.3 us -> 101 us
    ppermute x18 -> x24, waiting for transfers between devices: 256 us -> 62.2 us  [the longest x8 44.5 us: swap(): return lax.ppermute(own, 'tensor', SWAP)]
    all_gather x5 -> x8, waiting for transfers between devices: 126 us -> 51.5 us  [shards(): along[name] = lax.all_gather(operand, 'z', axis=0, tiled=True)]
    ppermute x5 -> x8, waiting for transfers between devices: 44.8 us -> 93.9 us  [gather(): across = lax.ppermute(along, 'x', SWAP)]
    reduce_scatter x5 -> x8, waiting for transfers between devices: 0.01 us -> 37 us  [keep(): summed[name] = lax.psum_scatter(part, 'z', scatter_dimension=0, tiled=True)]
    ppermute x6, waiting for transfers between devices: 5.66 us -> 32 us  [total(): vector = vector + lax.ppermute(vector, axis, SWAP)]
    dot_general x15 -> x24, matrix products: 71.3 us -> 95.8 us  [dot_inner(): lax.dot_general(left, right, (((0,), (0,)), ((), ())), preferred_element_...]
    unnamed x95 -> x202, local copies, waits for them, and re-layouts: 44.5 us -> 52.5 us
    convert_element_type x8 -> x7, other arithmetic: 26.9 us -> 19.1 us  [the longest x3 6.86 us: whole(): jnp.concatenate([summed[name, i] for i in range(CHUNKS)], axis=1)]
  transfers between devices with their start and end apart: 53 -> 74, of which waited for: 20 -> 27; matrix products, arithmetic and copies ran while one was open for 35% -> 49% of each run, Pallas kernels for 6% -> 7%
where the time goes in v2:
time: 832 us; the launch traced here: 823 us
  waiting for transfers between devices  291 us (35%)
  matrix products  250 us (30%)
  local copies, waits for them, and re-layouts  101 us (12%)
  other arithmetic  70.2 us (8%)
  Pallas kernels  56.8 us (7%)
  starting transfers between devices  38.5 us (5%)
  between operations  15.6 us (2%)
    dot_general x16, matrix products, dot_trans(): lax.dot_general(left, right, (((1,), (1,)), ((), ())), preferred_element_...  99.3 us
    dot_general x24, matrix products, dot_inner(): lax.dot_general(left, right, (((0,), (0,)), ((), ())), preferred_element_...  95.8 us
    ppermute x8, waiting for transfers between devices, gather(): across = lax.ppermute(along, 'x', SWAP)  93.9 us
    dot_general x8, matrix products, dot_plain(): return jnp.dot(left, right, preferred_element_type=f32)  55.1 us
    unnamed x202, local copies, waits for them, and re-layouts  52.5 us
    all_gather x8, waiting for transfers between devices, shards(): along[name] = lax.all_gather(operand, 'z', axis=0, tiled=True)  51.5 us
    ppermute x8, waiting for transfers between devices, swap(): return lax.ppermute(own, 'tensor', SWAP)  44.5 us
    reduce_scatter x8, waiting for transfers between devices, keep(): summed[name] = lax.psum_scatter(part, 'z', scatter_dimension=0, tiled=True)  37 us
  transfers between devices with their start and end apart: 74, of which 27 were waited for; matrix products, arithmetic and copies ran while one was open for 49% of the time, Pallas kernels for 7%

profile of v2, /device:TPU:0, one launch (start us, length us, event | category | flops | bytes accessed | tf_op | source)
XLA Modules:
  0.0 823.0 jit_solution(17402451867472241812)
XLA Ops:
  28.5 11.8 %all-gather.11.cloned.1.call-done = bf16[512,1024]{1,0:T(8,128)(2,1)} async-done(((bf16[128,1024]{1,0:T(8,128)(2,1)}), bf16[512,1024]{1,0:T(8,128)(2,1)}) %all-gather.11.cloned.1.call-update) | async-done | bytes 1048592 | tf_op jit(solution)/shard_map/all_gather | solution.py:376
  53.2 21.4 %all-gather.9.cloned.1.call-done = bf16[512,1280]{1,0:T(8,128)(2,1)} async-done(((bf16[128,1280]{1,0:T(8,128)(2,1)}), bf16[512,1280]{1,0:T(8,128)(2,1)}) %all-gather.9.cloned.1.call-update) | async-done | bytes 1310736 | tf_op jit(solution)/shard_map/all_gather | solution.py:376
  80.4 8.5 %collective-permute-done = bf16[384,2048]{1,0:T(8,128)(2,1)} collective-permute-done((bf16[384,2048]{1,0:T(8,128)(2,1)S(1)}, bf16[384,2048]{1,0:T(8,128)(2,1)}, u32[]{:S(2)}, u32[]{:S(2)}) %collective-permute-start) | collective-permute-done | bytes 1572896 | tf_op jit(solution)/shard_map/ppermute | solution.py:336
  93.4 17.4 %all-gather.13.cloned.1.call-done = bf16[512,1408]{1,0:T(8,128)(2,1)} async-done(((bf16[128,1408]{1,0:T(8,128)(2,1)}), bf16[512,1408]{1,0:T(8,128)(2,1)}) %all-gather.13.cloned.1.call-update) | async-done | bytes 1441808 | tf_op jit(solution)/shard_map/all_gather | solution.py:376
  114.9 17.4 %collective-permute-done.1 = bf16[512,1280]{1,0:T(8,128)(2,1)} collective-permute-done((bf16[512,1280]{1,0:T(8,128)(2,1)}, bf16[512,1280]{1,0:T(8,128)(2,1)}, u32[]{:S(2)}, u32[]{:S(2)}) %collective-permute-start.1) | collective-permute-done | bytes 1310752 | tf_op jit(solution)/shard_map/ppermute | solution.py:316
  150.8 7.2 fusion.113.qkv_ref
  161.9 17.4 %shard_map.204 = (bf16[768,1024]{1,0:T(8,128)(2,1)S(1)}, f32[768,256]{1,0:T(8,128)S(1)}) custom-call(s32[3]{0:T(128)S(1)} %convert_reduce_fusion.1.low_ref, bf16[768,1280]{1,0:T(8,128)(2,1)S(1)} %shard_map.203.q_ref.k_ref.v_ref, bf16[768,1280]{1,0:T(8,128)(2,1)S(1)} %shard_map.203.q_ref.k_ref.v_ref, bf16[768,1280]{1,0:T(8,128)(2,1)S(1)} %shard_map.203.q_ref.k_ref.v_ref, ...), custom_call_target="tpu_custom_call" | custom-call | flops 6039797760 | bytes 3145728 | tf_op jit(solution)/shard_map/pallas_call | solution.py:223
  192.8 16.1 %collective-permute-done.12 = bf16[512,1408]{1,0:T(8,128)(2,1)} collective-permute-done((bf16[512,1408]{1,0:T(8,128)(2,1)}, bf16[512,1408]{1,0:T(8,128)(2,1)}, u32[]{:S(2)}, u32[]{:S(2)}) %collective-permute-start.12) | collective-permute-done | bytes 1441824 | tf_op jit(solution)/shard_map/ppermute | solution.py:316
  238.0 11.6 %collective-permute-done.15 = bf16[512,1408]{1,0:T(8,128)(2,1)} collective-permute-done((bf16[512,1408]{1,0:T(8,128)(2,1)}, bf16[512,1408]{1,0:T(8,128)(2,1)}, u32[]{:S(2)}, u32[]{:S(2)}) %collective-permute-start.15) | collective-permute-done | bytes 1441824 | tf_op jit(solution)/shard_map/ppermute | solution.py:316
  255.0 6.7 collective-permute-done.8
  270.4 9.2 %collective-permute-done.18 = bf16[512,1408]{1,0:T(8,128)(2,1)} collective-permute-done((bf16[512,1408]{1,0:T(8,128)(2,1)S(1)}, bf16[512,1408]{1,0:T(8,128)(2,1)}, u32[]{:S(2)}, u32[]{:S(2)}) %collective-permute-start.18) | collective-permute-done | bytes 1441824 | tf_op jit(solution)/shard_map/ppermute | solution.py:316
  279.6 9.1 %fusion.116 = (bf16[768,1408]{1,0:T(8,128)(2,1)}, bf16[768,1408]{1,0:T(8,128)(2,1)S(1)}) fusion(bf16[768,1408]{1,0:T(8,128)(2,1)S(1)} %convolution_convert_fusion.8, bf16[768,2048]{1,0:T(8,128)(2,1)S(1)} %pad_maximum_fusion.1, bf16[2048,1408]{1,0:T(8,128)(2,1)} %constant_dynamic-update-slice_fusion.8), kind=kOutput, calls=%fused_computation.261 | convolution fusion | flops 4437835776 | bytes 15400960 | tf_op jit(solution)/shard_map/dot_general | solution.py:22
  304.8 8.0 convolution_convert_fusion.7
  322.4 9.3 %collective-permute-done.25 = bf16[512,1408]{1,0:T(8,128)(2,1)S(1)} collective-permute-done((bf16[512,1408]{1,0:T(8,128)(2,1)}, bf16[512,1408]{1,0:T(8,128)(2,1)S(1)}, u32[]{:S(2)}, u32[]{:S(2)}) %collective-permute-start.25) | collective-permute-done | bytes 1441824 | tf_op jit(solution)/shard_map/ppermute | solution.py:316
  331.9 30.3 %collective-permute-done.22 = bf16[512,1408]{1,0:T(8,128)(2,1)S(1)} collective-permute-done((bf16[512,1408]{1,0:T(8,128)(2,1)}, bf16[512,1408]{1,0:T(8,128)(2,1)S(1)}, u32[]{:S(2)}, u32[]{:S(2)}) %collective-permute-start.22) | collective-permute-done | bytes 1441824 | tf_op jit(solution)/shard_map/ppermute | solution.py:316
  381.4 7.5 fusion.15
  397.6 7.5 fusion.121
  407.6 6.3 fusion.71
  413.9 8.4 %convolution_add_fusion.20 = f32[384,2048]{1,0:T(8,128)} fusion(f32[384,2048]{1,0:T(8,128)} %fusion.71, bf16[2048,1408]{1,0:T(8,128)(2,1)} %constant_dynamic-update-slice_fusion.8, bf16[768,1408]{1,0:T(8,128)(2,1)S(1)} %get-tuple-element.272, s32[]{:T(128)S(6)} %select_n.143), kind=kOutput, calls=%fused_computation.107 | convolution fusion | flops 2215378944 | bytes 13139972 | tf_op jit(solution)/shard_map/dot_general | solution.py:26
  460.2 8.6 %convolution_add_fusion.17 = f32[384,2048]{1,0:T(8,128)} fusion(f32[384,2048]{1,0:T(8,128)} %fusion.66, bf16[2048,1408]{1,0:T(8,128)(2,1)} %constant_dynamic-update-slice_fusion.8, bf16[768,1408]{1,0:T(8,128)(2,1)S(1)} %copy-done.71, s32[]{:T(128)S(6)} %select_n.144), kind=kOutput, calls=%fused_computation.104 | convolution fusion | flops 2215378944 | bytes 13139972 | tf_op jit(solution)/shard_map/dot_general | solution.py:26
  468.8 8.6 %convolution_add_fusion.16 = f32[384,2048]{1,0:T(8,128)} fusion(f32[384,2048]{1,0:T(8,128)} %convolution_add_fusion.17, bf16[2048,1408]{1,0:T(8,128)(2,1)} %constant_dynamic-update-slice_fusion.20, bf16[768,1408]{1,0:T(8,128)(2,1)S(1)} %copy-done.27, s32[]{:T(128)S(6)} %select_n.144), kind=kOutput, calls=%fused_computation.103 | convolution fusion | flops 2215378944 | bytes 13139972 | tf_op jit(solution)/shard_map/dot_general | solution.py:26
  510.0 7.8 add_convert_fusion.2
  529.2 7.3 convolution_add_fusion.14
  556.6 17.5 %collective-permute-done.38 = bf16[384,2048]{1,0:T(8,128)(2,1)} collective-permute-done((bf16[384,2048]{1,0:T(8,128)(2,1)}, bf16[384,2048]{1,0:T(8,128)(2,1)}, u32[]{:S(2)}, u32[]{:S(2)}) %collective-permute-start.38) | collective-permute-done | bytes 1572896 | tf_op jit(solution)/shard_map/ppermute | solution.py:336
  583.0 35.5 %shard_map.205 = (bf16[768,1024]{1,0:T(8,128)(2,1)S(1)}, bf16[768,128]{1,0:T(8,128)(2,1)S(1)}, bf16[768,128]{1,0:T(8,128)(2,1)S(1)}) custom-call(s32[3]{0:T(128)S(1)} %convert_reduce_fusion.1.low_ref, bf16[768,1280]{1,0:T(8,128)(2,1)S(1)} %copy-done.1, bf16[768,1280]{1,0:T(8,128)(2,1)S(1)} %copy-done.1, bf16[768,1280]{1,0:T(8,128)(2,1)S(1)} %copy-done.1, ...), custom_call_target="tpu_custom_call" | custom-call | flops 18119393280 | bytes 6291456 | tf_op jit(solution)/shard_map/pallas_call | solution.py:252
  642.0 16.9 %collective-permute-done.42 = bf16[512,1408]{1,0:T(8,128)(2,1)} collective-permute-done((bf16[512,1408]{1,0:T(8,128)(2,1)}, bf16[512,1408]{1,0:T(8,128)(2,1)}, u32[]{:S(2)}, u32[]{:S(2)}) %collective-permute-start.42) | collective-permute-done | bytes 1441824 | tf_op jit(solution)/shard_map/ppermute | solution.py:404
  663.3 8.7 %collective-permute-done.45 = bf16[384,2048]{1,0:T(8,128)(2,1)} collective-permute-done((bf16[384,2048]{1,0:T(8,128)(2,1)}, bf16[384,2048]{1,0:T(8,128)(2,1)}, u32[]{:S(2)}, u32[]{:S(2)}) %collective-permute-start.45) | collective-permute-done | bytes 1572896 | tf_op jit(solution)/shard_map/ppermute | solution.py:336
  671.9 8.2 %multiply_reduce_fusion = (f32[2048]{0:T(1024)S(1)}, f32[384]{0:T(512)S(1)}, f32[384,2048]{1,0:T(8,128)}) fusion(f32[384,2048]{1,0:T(8,128)} %reshape.117, f32[384]{0:T(512)S(1)} %copy-done.55, bf16[384,2048]{1,0:T(8,128)(2,1)} %collective-permute-done.45, f32[2048]{0:T(1024)S(1)} %bitcast.101, bf16[2048,1280]{1,0:T(8,128)(2,1)} %constant_dynamic-update-slice_fusion, ...), kind=kOutput, calls=%fused_computation.73 | convolution fusion | flops 2019554944 | bytes 14109700 | tf_op jit(solution)/shard_map/dot_general | solution.py:26
  690.4 27.5 %collective-permute-done.54 = f32[1,2048]{1,0:T(1,128)S(1)} collective-permute-done((f32[1,2048]{1,0:T(1,128)S(1)}, f32[1,2048]{1,0:T(1,128)S(1)}, u32[]{:S(2)}, u32[]{:S(2)}) %collective-permute-start.54) | collective-permute-done | bytes 8224 | tf_op jit(solution)/shard_map/ppermute | solution.py:324
  734.5 6.3 add_convert_fusion
  773.8 6.8 reduce-scatter.19.cloned.1.call-done
  782.9 30.1 %reduce-scatter.9.cloned.1.call-done = bf16[128,1280]{1,0:T(8,128)(2,1)} async-done(((bf16[512,1280]{1,0:T(8,128)(2,1)}), bf16[128,1280]{1,0:T(8,128)(2,1)}) %reduce-scatter.9.cloned.1.call-update) | async-done | bytes 327696 | tf_op jit(solution)/shard_map/reduce_scatter | solution.py:413
  (486 shorter events, 386.4 us)
Async XLA Ops:
  7.9 66.7 %all-gather.9.cloned.1.call-start = ((), (), s32[]{:S(2)}) async-start(), calls=%async_computation.8 | async-start | bytes 1638400 | tf_op jit(solution)/shard_map/all_gather | solution.py:376
  9.7 101.0 %all-gather.13.cloned.1.call-start = ((), (), s32[]{:S(2)}) async-start(), calls=%async_computation.10 | async-start | bytes 1802240 | tf_op jit(solution)/shard_map/all_gather | solution.py:376
  17.5 93.3 %collective-permute-start.21 = (bf16[384,2048]{1,0:T(8,128)(2,1)}, bf16[384,2048]{1,0:T(8,128)(2,1)}, u32[]{:S(2)}, u32[]{:S(2)}) collective-permute-start(bf16[384,2048]{1,0:T(8,128)(2,1)} %reshape.110), channel_id=1, source_target_pairs={{0,1},{1,0},{2,3},{3,2},{4,5},{5,4},{6,7},{7,6},{8,9},{9,8},{10,11... | collective-permute-start | bytes 4718600 | tf_op jit(solution)/shard_map/ppermute | solution.py:336
  40.3 106.3 %all-gather.15.cloned.1.call-start = ((), (), s32[]{:S(2)}) async-start(), calls=%async_computation.11 | async-start | bytes 1802240 | tf_op jit(solution)/shard_map/all_gather | solution.py:376
  74.6 134.2 %all-gather.17.cloned.1.call-start = ((), (), s32[]{:S(2)}) async-start(), calls=%async_computation.12 | async-start | bytes 1802240 | tf_op jit(solution)/shard_map/all_gather | solution.py:376
  78.4 57.3 %collective-permute-start.5 = (bf16[512,1024]{1,0:T(8,128)(2,1)}, bf16[512,1024]{1,0:T(8,128)(2,1)}, u32[]{:S(2)}, u32[]{:S(2)}) collective-permute-start(bf16[512,1024]{1,0:T(8,128)(2,1)} %all-gather.11.cloned.1.call-done), channel_id=1, source_target_pairs={{0,2},{2,0},{1,3},{3,1},{4,6},{6,4},{5,7},{7,5},{8,10},{10,8},{9,1... | collective-permute-start | bytes 3145736 | tf_op jit(solution)/shard_map/ppermute | solution.py:318
  78.4 54.1 %collective-permute-start.4 = (bf16[512,1024]{1,0:T(8,128)(2,1)}, bf16[512,1024]{1,0:T(8,128)(2,1)}, u32[]{:S(2)}, u32[]{:S(2)}) collective-permute-start(bf16[512,1024]{1,0:T(8,128)(2,1)} %all-gather.11.cloned.1.call-done), channel_id=1, source_target_pairs={{0,4},{4,0},{1,5},{5,1},{2,6},{6,2},{3,7},{7,3},{8,12},{12,8},{9,1... | collective-permute-start | bytes 3145736 | tf_op jit(solution)/shard_map/ppermute | solution.py:316
  79.8 52.5 %collective-permute-start.1 = (bf16[512,1280]{1,0:T(8,128)(2,1)}, bf16[512,1280]{1,0:T(8,128)(2,1)}, u32[]{:S(2)}, u32[]{:S(2)}) collective-permute-start(bf16[512,1280]{1,0:T(8,128)(2,1)} %all-gather.9.cloned.1.call-done), channel_id=1, source_target_pairs={{0,4},{4,0},{1,5},{5,1},{2,6},{6,2},{3,7},{7,3},{8,12},{12,8},{9,1... | collective-permute-start | bytes 3932168 | tf_op jit(solution)/shard_map/ppermute | solution.py:316
  110.8 119.3 %all-gather.19.cloned.1.call-start = ((), (), s32[]{:S(2)}) async-start(), calls=%async_computation.13 | async-start | bytes 1802240 | tf_op jit(solution)/shard_map/all_gather | solution.py:376
  146.6 150.5 %all-gather.23.cloned.1.call-start = ((), (), s32[]{:S(2)}) async-start(), calls=%async_computation.15 | async-start | bytes 1802240 | tf_op jit(solution)/shard_map/all_gather | solution.py:376
  146.7 65.1 %collective-permute-start.13 = (bf16[512,1408]{1,0:T(8,128)(2,1)}, bf16[512,1408]{1,0:T(8,128)(2,1)}, u32[]{:S(2)}, u32[]{:S(2)}) collective-permute-start(bf16[512,1408]{1,0:T(8,128)(2,1)} %all-gather.15.cloned.1.call-done), channel_id=1, source_target_pairs={{0,2},{2,0},{1,3},{3,1},{4,6},{6,4},{5,7},{7,5},{8,10},{10,8},{9,1... | collective-permute-start | bytes 4325384 | tf_op jit(solution)/shard_map/ppermute | solution.py:318
  146.7 62.1 %collective-permute-start.12 = (bf16[512,1408]{1,0:T(8,128)(2,1)}, bf16[512,1408]{1,0:T(8,128)(2,1)}, u32[]{:S(2)}, u32[]{:S(2)}) collective-permute-start(bf16[512,1408]{1,0:T(8,128)(2,1)} %all-gather.15.cloned.1.call-done), channel_id=1, source_target_pairs={{0,4},{4,0},{1,5},{5,1},{2,6},{6,2},{3,7},{7,3},{8,12},{12,8},{9,1... | collective-permute-start | bytes 4325384 | tf_op jit(solution)/shard_map/ppermute | solution.py:316
  208.9 89.7 %all-gather.21.cloned.1.call-start = ((), (), s32[]{:S(2)}) async-start(), calls=%async_computation.14 | async-start | bytes 1802240 | tf_op jit(solution)/shard_map/all_gather | solution.py:376
  230.0 523.7 %reduce-scatter.21.cloned.1.call-start = ((), (), s32[]{:S(2)}) async-start(), calls=%async_computation.22 | async-start | bytes 1802240 | tf_op jit(solution)/shard_map/reduce_scatter | solution.py:413
  232.8 63.1 %collective-permute-start.19 = (bf16[512,1408]{1,0:T(8,128)(2,1)S(1)}, bf16[512,1408]{1,0:T(8,128)(2,1)S(1)}, u32[]{:S(2)}, u32[]{:S(2)}) collective-permute-start(bf16[512,1408]{1,0:T(8,128)(2,1)S(1)} %copy-done.30), channel_id=1, source_target_pairs={{0,2},{2,0},{1,3},{3,1},{4,6},{6,4},{5,7},{7,5},{8,10},{10,8},{9,1... | collective-permute-start | bytes 4325384 | tf_op jit(solution)/shard_map/ppermute | solution.py:318
  292.8 71.4 %collective-permute-start.29 = (bf16[1024,1408]{1,0:T(8,128)(2,1)}, bf16[1024,1408]{1,0:T(8,128)(2,1)}, u32[]{:S(2)}, u32[]{:S(2)}) collective-permute-start(bf16[1024,1408]{1,0:T(8,128)(2,1)} %convolution_convert_fusion.6), channel_id=1, source_target_pairs={{0,2},{2,0},{1,3},{3,1},{4,6},{6,4},{5,7},{7,5},{8,10},{10,8},{9,1... | collective-permute-start | bytes 8650760 | tf_op jit(solution)/shard_map/ppermute | solution.py:397
  298.6 63.6 %collective-permute-start.22 = (bf16[512,1408]{1,0:T(8,128)(2,1)}, bf16[512,1408]{1,0:T(8,128)(2,1)S(1)}, u32[]{:S(2)}, u32[]{:S(2)}) collective-permute-start(bf16[512,1408]{1,0:T(8,128)(2,1)} %all-gather.21.cloned.1.call-done), channel_id=1, source_target_pairs={{0,4},{4,0},{1,5},{5,1},{2,6},{6,2},{3,7},{7,3},{8,12},{12,8},{9,1... | collective-permute-start | bytes 4325384 | tf_op jit(solution)/shard_map/ppermute | solution.py:316
  321.6 51.5 %collective-permute-start.28 = (bf16[1024,1408]{1,0:T(8,128)(2,1)S(1)}, bf16[1024,1408]{1,0:T(8,128)(2,1)S(1)}, u32[]{:S(2)}, u32[]{:S(2)}) collective-permute-start(bf16[1024,1408]{1,0:T(8,128)(2,1)S(1)} %convolution_convert_fusion.5), channel_id=1, source_target_pairs={{0,2},{2,0},{1,3},{3,1},{4,6},{6,4},{5,7},{7,5},{8,10},{10,8},{9,1... | collective-permute-start | bytes 8650760 | tf_op jit(solution)/shard_map/ppermute | solution.py:397
  368.8 65.1 %collective-permute-start.31 = (bf16[512,1408]{1,0:T(8,128)(2,1)}, bf16[512,1408]{1,0:T(8,128)(2,1)}, u32[]{:S(2)}, u32[]{:S(2)}) collective-permute-start(bf16[512,1408]{1,0:T(8,128)(2,1)} %fusion.41), channel_id=1, source_target_pairs={{0,4},{4,0},{1,5},{5,1},{2,6},{6,2},{3,7},{7,3},{8,12},{12,8},{9,1... | collective-permute-start | bytes 4325384 | tf_op jit(solution)/shard_map/ppermute | solution.py:404
  380.9 107.7 %collective-permute-start.35 = (bf16[512,1408]{1,0:T(8,128)(2,1)}, bf16[512,1408]{1,0:T(8,128)(2,1)}, u32[]{:S(2)}, u32[]{:S(2)}) collective-permute-start(bf16[512,1408]{1,0:T(8,128)(2,1)} %fusion.42), channel_id=1, source_target_pairs={{0,4},{4,0},{1,5},{5,1},{2,6},{6,2},{3,7},{7,3},{8,12},{12,8},{9,1... | collective-permute-start | bytes 4325384 | tf_op jit(solution)/shard_map/ppermute | solution.py:404
  432.4 61.9 %collective-permute-start.34 = (bf16[384,2048]{1,0:T(8,128)(2,1)}, bf16[384,2048]{1,0:T(8,128)(2,1)S(1)}, u32[]{:S(2)}, u32[]{:S(2)}) collective-permute-start(bf16[384,2048]{1,0:T(8,128)(2,1)} %convolution_add_fusion.18), channel_id=1, source_target_pairs={{0,1},{1,0},{2,3},{3,2},{4,5},{5,4},{6,7},{7,6},{8,9},{9,8},{10,11... | collective-permute-start | bytes 4718600 | tf_op jit(solution)/shard_map/ppermute | solution.py:336
  438.4 315.3 %reduce-scatter.23.cloned.1.call-start = ((), (), s32[]{:S(2)}) async-start(), calls=%async_computation.23 | async-start | bytes 1802240 | tf_op jit(solution)/shard_map/reduce_scatter | solution.py:413
  447.5 88.9 %collective-permute-start.40 = (bf16[512,1408]{1,0:T(8,128)(2,1)}, bf16[512,1408]{1,0:T(8,128)(2,1)}, u32[]{:S(2)}, u32[]{:S(2)}) collective-permute-start(bf16[512,1408]{1,0:T(8,128)(2,1)} %fusion.44), channel_id=1, source_target_pairs={{0,4},{4,0},{1,5},{5,1},{2,6},{6,2},{3,7},{7,3},{8,12},{12,8},{9,1... | collective-permute-start | bytes 4325384 | tf_op jit(solution)/shard_map/ppermute | solution.py:404
  504.6 265.1 %reduce-scatter.13.cloned.1.call-start = ((), (), s32[]{:S(2)}) async-start(), calls=%async_computation.18 | async-start | bytes 1802240 | tf_op jit(solution)/shard_map/reduce_scatter | solution.py:413
  517.8 56.3 %collective-permute-start.38 = (bf16[384,2048]{1,0:T(8,128)(2,1)}, bf16[384,2048]{1,0:T(8,128)(2,1)}, u32[]{:S(2)}, u32[]{:S(2)}) collective-permute-start(bf16[384,2048]{1,0:T(8,128)(2,1)} %add_convert_fusion.2), channel_id=1, source_target_pairs={{0,1},{1,0},{2,3},{3,2},{4,5},{5,4},{6,7},{7,6},{8,9},{9,8},{10,11... | collective-permute-start | bytes 4718600 | tf_op jit(solution)/shard_map/ppermute | solution.py:336
  555.0 69.2 %collective-permute-start.44 = (bf16[512,1408]{1,0:T(8,128)(2,1)}, bf16[512,1408]{1,0:T(8,128)(2,1)}, u32[]{:S(2)}, u32[]{:S(2)}) collective-permute-start(bf16[512,1408]{1,0:T(8,128)(2,1)} %fusion.45), channel_id=1, source_target_pairs={{0,4},{4,0},{1,5},{5,1},{2,6},{6,2},{3,7},{7,3},{8,12},{12,8},{9,1... | collective-permute-start | bytes 4325384 | tf_op jit(solution)/shard_map/ppermute | solution.py:404
  556.5 213.2 %reduce-scatter.15.cloned.1.call-start = ((), (), s32[]{:S(2)}) async-start(), calls=%async_computation.19 | async-start | bytes 1802240 | tf_op jit(solution)/shard_map/reduce_scatter | solution.py:413
  635.5 136.5 %reduce-scatter.11.cloned.1.call-start = ((), (), s32[]{:S(2)}) async-start(), calls=%async_computation.17 | async-start | bytes 1310720 | tf_op jit(solution)/shard_map/reduce_scatter | solution.py:413
  685.8 88.0 %reduce-scatter.17.cloned.1.call-start = ((), (), s32[]{:S(2)}) async-start(), calls=%async_computation.20 | async-start | bytes 1802240 | tf_op jit(solution)/shard_map/reduce_scatter | solution.py:413
  686.4 94.2 %reduce-scatter.19.cloned.1.call-start = ((), (), s32[]{:S(2)}) async-start(), calls=%async_computation.21 | async-start | bytes 1802240 | tf_op jit(solution)/shard_map/reduce_scatter | solution.py:413
  686.9 126.0 %reduce-scatter.9.cloned.1.call-start = ((), (), s32[]{:S(2)}) async-start(), calls=%async_computation.16 | async-start | bytes 1638400 | tf_op jit(solution)/shard_map/reduce_scatter | solution.py:413
  687.1 53.8 %collective-permute-start.47 = (bf16[512,1280]{1,0:T(8,128)(2,1)}, bf16[512,1280]{1,0:T(8,128)(2,1)}, u32[]{:S(2)}, u32[]{:S(2)}) collective-permute-start(bf16[512,1280]{1,0:T(8,128)(2,1)} %fusion.47), channel_id=1, source_target_pairs={{0,4},{4,0},{1,5},{5,1},{2,6},{6,2},{3,7},{7,3},{8,12},{12,8},{9,1... | collective-permute-start | bytes 3932168 | tf_op jit(solution)/shard_map/ppermute | solution.py:404
  (130 other events, 2321.2 us)
Sparse Core Ops, SparseCore 0:
  9.6 30.6 all-gather.10
  42.4 32.1 all-gather.8
  76.8 33.9 all-gather.12
  112.7 33.8 all-gather.14
  148.6 33.8 all-gather.16
  184.4 33.8 all-gather.18
  220.4 33.8 all-gather.22
  256.4 33.8 all-gather.20
  438.5 31.3 reduce-scatter.20
  504.7 32.2 reduce-scatter.22
  556.6 30.5 reduce-scatter.12
  635.6 32.7 reduce-scatter.14
  685.9 25.2 reduce-scatter.10
  713.5 32.2 reduce-scatter.16
  748.1 32.4 reduce-scatter.18
  782.9 30.0 reduce-scatter.8

commit v3 on v1

--- a/solution.py
+++ b/solution.py
@@ -10,7 +10,9 @@
 HEAD_DIM = 64
 SWAP = ((0, 1), (1, 0))
 QUERIES = 256
-VMEM = 40 * 2**20
+CHUNKS = 2
+BLOCK = 256
+VMEM = 48 * 2**20
 epsilon = 1e-05
 rope_base = 10000.0
 bf16 = jnp.bfloat16
@@ -64,35 +66,6 @@
     low_half = lanes_of(block.shape) % HEAD_DIM < HEAD_DIM // 2
     other = jnp.where(low_half, pltpu.roll(block, 96, 1), pltpu.roll(block, 32, 1))
     return block * cosine + other * sine
-
-
-def rope_kernel(rotated, qkv_ref, cos_ref, sin_ref, out_ref):
-    block = qkv_ref[...]
-
-    @pl.when(pl.program_id(0) < rotated)
-    def _():
-        out_ref[...] = turn(block, cos_ref[...], sin_ref[...]).astype(bf16)
-
-    @pl.when(pl.program_id(0) >= rotated)
-    def _():
-        out_ref[...] = block.astype(bf16)
-
-
-def rope(qkv, cosine, sine, rotated):
-    length, width = qkv.shape
-    block = pl.BlockSpec((length, 128), lambda j: (0, j))
-    table = pl.BlockSpec((length, 128), lambda j: (0, 0))
-    return pl.pallas_call(
-        functools.partial(rope_kernel, rotated),
-        grid=(width // 128,),
-        in_specs=[block, table, table],
-        out_specs=block,
-        out_shape=jax.ShapeDtypeStruct((length, width), bf16),
-        compiler_params=pltpu.CompilerParams(vmem_limit_bytes=VMEM),
-        cost_estimate=pl.CostEstimate(
-            flops=4 * length * width, bytes_accessed=6 * length * width, transcendentals=0
-        ),
-    )(qkv, cosine, sine)
 
 
 def widen(pair_ref, wide_ref, group):
@@ -280,6 +253,225 @@
     )
 
 
+def feed_kernel(x_ref, g_ref, *refs):
+    pieces, (h_ref, gg_ref, ug_ref) = refs[:12], refs[12:]
+    depth = pieces[0].shape[0]
+
+    def product(act_ref, parts):
+        return sum(
+            dot_plain(act_ref[:, i * depth : i * depth + depth], part[...]) for i, part in enumerate(parts)
+        )
+
+    gate = product(x_ref, pieces[:4])
+    up = product(x_ref, pieces[4:8])
+    sigmoid = jax.nn.sigmoid(gate)
+    silu = gate * sigmoid
+    h_ref[...] = (silu * up).astype(bf16)
+    grad = product(g_ref, pieces[8:])
+    gg_ref[...] = (grad * up * (sigmoid * (1.0 + gate * (1.0 - sigmoid)))).astype(bf16)
+    ug_ref[...] = (grad * silu).astype(bf16)
+
+
+def feed(normed, grads, gate, up, down):
+    rows, width = normed.shape
+    units = gate[0].shape[1]
+    depth = width // 4
+    act = pl.BlockSpec((rows, width), lambda j: (0, 0))
+    part = pl.BlockSpec((depth, BLOCK), lambda j: (0, j))
+    out = pl.BlockSpec((rows, BLOCK), lambda j: (0, j))
+    return pl.pallas_call(
+        feed_kernel,
+        grid=(units // BLOCK,),
+        in_specs=[act, act] + [part] * 12,
+        out_specs=[out] * 3,
+        out_shape=[jax.ShapeDtypeStruct((rows, units), bf16)] * 3,
+        compiler_params=pltpu.CompilerParams(vmem_limit_bytes=VMEM),
+        cost_estimate=pl.CostEstimate(
+            flops=6 * rows * width * units, bytes_accessed=6 * width * units, transcendentals=0
+        ),
+    )(normed, grads, *gate, *up, *down)
+
+
+def project_kernel(rotated, place_ref, own_ref, other_ref, *refs):
+    parts, out_ref = refs[:4], refs[-1]
+    depth = parts[0].shape[0]
+    rows = own_ref.shape[0]
+    for act_ref, place in ((own_ref, place_ref[0]), (other_ref, 1 - place_ref[0])):
+        at = pl.ds(pl.multiple_of(place * rows, rows), rows)
+        total = sum(
+            dot_plain(act_ref[:, i * depth : i * depth + depth], part[...]) for i, part in enumerate(parts)
+        )
+        if rotated is None:
+            out_ref[at, :] = total.astype(bf16)
+        else:
+            cosine, sine = refs[4][at, :], refs[5][at, :]
+            for half in range(2):
+                piece = total[:, half * 128 : half * 128 + 128]
+                keep = 2 * pl.program_id(0) + half >= rotated
+                piece = jnp.where(keep, piece, turn(piece, cosine, sine))
+                out_ref[at, half * 128 : half * 128 + 128] = piece.astype(bf16)
+
+
+def project(place, own, other, weight, tables=(), rotated=None):
+    rows, width = own.shape
+    units = weight[0].shape[1]
+    act = pl.BlockSpec((rows, width), lambda j, s: (0, 0))
+    table = pl.BlockSpec((2 * rows, 128), lambda j, s: (0, 0))
+    part = pl.BlockSpec((width // 4, BLOCK), lambda j, s: (0, j))
+    return pl.pallas_call(
+        functools.partial(project_kernel, rotated),
+        grid_spec=pltpu.PrefetchScalarGridSpec(
+            num_scalar_prefetch=1,
+            grid=(units // BLOCK,),
+            in_specs=[act, act] + [part] * 4 + [table] * len(tables),
+            out_specs=pl.BlockSpec((2 * rows, BLOCK), lambda j, s: (0, j)),
+        ),
+        out_shape=jax.ShapeDtypeStruct((2 * rows, units), bf16),
+        compiler_params=pltpu.CompilerParams(vmem_limit_bytes=VMEM),
+        cost_estimate=pl.CostEstimate(
+            flops=4 * rows * width * units, bytes_accessed=2 * width * units, transcendentals=0
+        ),
+    )(place, own, other, *weight, *tables)
+
+
+def back_kernel(count, started, place_ref, *refs):
+    step = pl.program_id(0)
+    acts = refs[:count]
+    weights = refs[count : 5 * count]
+    starts = refs[5 * count : 5 * count + 2] if started else None
+    mine_ref, theirs_ref = refs[-2:]
+    rows = mine_ref.shape[0]
+
+    def run(part):
+        total = sum(dot_trans(a[...], weights[4 * i + part][...]) for i, a in enumerate(acts))
+        first = place_ref[0] == 0
+        mine = jnp.where(first, total[:rows], total[rows:])
+        theirs = jnp.where(first, total[rows:], total[:rows])
+        if started:
+            mine = mine + starts[0][...].astype(f32)
+            theirs = theirs + starts[1][...].astype(f32)
+        mine_ref[...] = mine.astype(mine_ref.dtype)
+        theirs_ref[...] = theirs.astype(theirs_ref.dtype)
+
+    for part in range(4):
+        pl.when(step // (pl.num_programs(0) // 4) == part)(functools.partial(run, part))
+
+
+def back(place, acts, weights, starts=None, kinds=(f32, bf16)):
+    rows = acts[0].shape[0]
+    depth = weights[0][0].shape[0]
+    width = 4 * depth
+    block = min(BLOCK, depth)
+    per = depth // block
+    half = pl.BlockSpec((rows // 2, block), lambda j, s: (0, j))
+    specs = [pl.BlockSpec(a.shape, lambda j, s: (0, 0)) for a in acts]
+    for weight in weights:
+        for p in range(4):
+            specs.append(
+                pl.BlockSpec(
+                    (block, weight[p].shape[1]),
+                    lambda j, s, p=p: (jnp.clip(j - p * per, 0, per - 1), 0),
+                )
+            )
+    operands = [*acts, *(piece for weight in weights for piece in weight)]
+    if starts is not None:
+        specs += [half, half]
+        operands += starts
+    units = sum(a.shape[1] for a in acts)
+    return pl.pallas_call(
+        functools.partial(back_kernel, len(acts), starts is not None),
+        grid_spec=pltpu.PrefetchScalarGridSpec(
+            num_scalar_prefetch=1, grid=(4 * per,), in_specs=specs, out_specs=[half, half]
+        ),
+        out_shape=[jax.ShapeDtypeStruct((rows // 2, width), kind) for kind in kinds],
+        compiler_params=pltpu.CompilerParams(vmem_limit_bytes=VMEM),
+        cost_estimate=pl.CostEstimate(
+            flops=2 * rows * width * units, bytes_accessed=2 * width * units, transcendentals=0
+        ),
+    )(place, *operands)
+
+
+def grad_kernel(which, added, *refs):
+    step, steps = pl.program_id(0), pl.num_programs(0)
+    acts = refs[: max(which) + 1]
+    count = len(which)
+    grads = refs[len(acts) : len(acts) + count]
+    others = refs[len(acts) + count : len(acts) + 2 * count]
+    for i in range(count):
+        total = dot_inner(acts[which[i]][...], grads[i][...])
+        if not added:
+            refs[i - count][...] = total.astype(bf16)
+            continue
+        total = (total + others[i][...].astype(f32)).astype(bf16)
+        sent_ref, kept_ref = refs[i - 2 * count], refs[i - count]
+
+        @pl.when(step < steps // 2)
+        def _():
+            sent_ref[...] = total
+
+        @pl.when(step >= steps // 2)
+        def _():
+            kept_ref[...] = total
+
+
+def grad(acts, which, grads, added=None):
+    tokens, width = acts[0].shape
+    block = min(BLOCK, width // 4)
+    steps = width // 2 // block
+    half = steps // 2
+    if added is None:
+        row = lambda j: j + steps
+    else:
+        row = lambda j: (j + half) % steps
+    specs = [pl.BlockSpec((tokens, block), lambda j: (0, row(j))) for _ in acts]
+    specs += [pl.BlockSpec(g.shape, lambda j: (0, 0)) for g in grads]
+    operands = [*acts, *grads]
+    if added is None:
+        outs = [pl.BlockSpec((block, g.shape[1]), lambda j: (j, 0)) for g in grads]
+        shapes = [jax.ShapeDtypeStruct((width // 2, g.shape[1]), bf16) for g in grads]
+    else:
+        specs += [pl.BlockSpec((block, g.shape[1]), lambda j: (row(j), 0)) for g in grads]
+        operands += added
+        outs = [pl.BlockSpec((block, g.shape[1]), lambda j: (jnp.minimum(j, half - 1), 0)) for g in grads]
+        outs += [pl.BlockSpec((block, g.shape[1]), lambda j: (jnp.maximum(j - half, 0), 0)) for g in grads]
+        shapes = [jax.ShapeDtypeStruct((width // 4, g.shape[1]), bf16) for g in grads] * 2
+    units = sum(g.shape[1] for g in grads)
+    return pl.pallas_call(
+        functools.partial(grad_kernel, which, added is not None),
+        grid=(steps,),
+        in_specs=specs,
+        out_specs=outs,
+        out_shape=shapes,
+        compiler_params=pltpu.CompilerParams(vmem_limit_bytes=VMEM),
+        cost_estimate=pl.CostEstimate(
+            flops=tokens * width * units, bytes_accessed=width * units, transcendentals=0
+        ),
+    )(*operands)
+
+
+def tie(array, *earlier):
+    return lax.optimization_barrier((array,) + earlier)[0]
+
+
+class Order:
+    def __init__(self, last):
+        self.last = last
+
+    def after(self, array):
+        return tie(array, self.last)
+
+    def __call__(self, compute, *operands):
+        operands = lax.optimization_barrier((*operands, self.last))[:-1]
+        result = compute(*operands)
+        self.last = result[0] if isinstance(result, (tuple, list)) else result
+        return result
+
+
+def chunk_edges(width):
+    blocks = width // BLOCK
+    return [width * 0] + [BLOCK * (blocks * (i + 1) // CHUNKS) for i in range(CHUNKS)]
+
+
 def make_shards(outer):
     def relative(array):
         rows, width = array.shape
@@ -295,27 +487,9 @@
         blocks = jnp.where(lax.axis_index("core") == 0, blocks, blocks[:, :, :, ::-1])
         return blocks.reshape(rows, width)
 
-    def gather(weight):
-        along = lax.all_gather(weight, "z", axis=0, tiled=True)
+    def spread(along):
         across = lax.ppermute(along, "x", SWAP)
-        return jnp.concatenate(
-            [along, across, lax.ppermute(along, "core", SWAP), lax.ppermute(across, "core", SWAP)],
-            axis=0,
-        )
-
-    def scatter(left, right):
-        half = left.shape[1] // 2
-        quarter = half // 2
-        for_core = dot_inner(left[:, half:], right).astype(bf16)
-        from_core = lax.ppermute(for_core, "core", SWAP)
-        for_x = (dot_inner(left[:, quarter:half], right) + from_core[quarter:].astype(f32)).astype(bf16)
-        from_x = lax.ppermute(for_x, "x", SWAP)
-        kept = (
-            dot_inner(left[:, :quarter], right)
-            + from_core[:quarter].astype(f32)
-            + from_x.astype(f32)
-        ).astype(bf16)
-        return lax.psum_scatter(kept, "z", scatter_dimension=0, tiled=True).astype(f32)
+        return [along, across, lax.ppermute(along, "core", SWAP), lax.ppermute(across, "core", SWAP)]
 
     def total(vector):
         for axis in ("core", "x", "tensor"):
@@ -326,23 +500,12 @@
             step *= 2
         return vector
 
-    def both_halves(own):
-        other = lax.ppermute(own, "tensor", SWAP)
-        return jnp.where(
-            lax.axis_index("tensor") == 0,
-            jnp.concatenate([own, other], axis=0),
-            jnp.concatenate([other, own], axis=0),
-        )
-
-    def reduce_halves(product, *operands):
-        rows = operands[0].shape[0] // 2
-        place = lax.axis_index("tensor")
-
-        def cut(at):
-            return [lax.dynamic_slice_in_dim(o, at * rows, rows, axis=0) for o in operands]
-
-        sent = lax.ppermute(product(*cut(1 - place)).astype(bf16), "tensor", SWAP)
-        return product(*cut(place)) + sent.astype(f32)
+    def join(own, other):
+        first = lax.axis_index("tensor") == 0
+        return jnp.concatenate([jnp.where(first, own, other), jnp.where(first, other, own)], axis=0)
+
+    def swap(own):
+        return lax.ppermute(own, "tensor", SWAP)
 
     def shards(
         tokens,
@@ -361,91 +524,204 @@
         query_width = q_weight.shape[1]
         key_width = k_weight.shape[1]
         score_scale = HEAD_DIM ** (-0.5)
-        qkv_full = gather(jnp.concatenate([q_weight, k_weight, v_weight], axis=1))
-        output_full = gather(o_weight)
-        gate_full = gather(gate_weight)
-        up_full = gather(up_weight)
-        down_full = gather(down_weight)
+        place = lax.axis_index("tensor").astype(jnp.int32).reshape(1)
+        here = jnp.zeros((1,), jnp.int32)
+        edges = chunk_edges(gate_weight.shape[1])
+
+        def gathered(operand):
+            return lax.all_gather(operand, "z", axis=0, tiled=True)
+
+        def chunk(weight, i):
+            return weight[:, edges[i] : edges[i + 1]]
+
+        along = {}
+        along["qkv"] = gathered(jnp.concatenate([q_weight, k_weight, v_weight], axis=1))
 
         attention_gain = relative(attention_gain[None])
         feed_gain = relative(feed_gain[None])
-        tokens = relative(tokens)
-        out_grad = relative(out_grad)
-
+        inputs = relative(tokens).astype(f32)
+        inverse_first = inverse_rms(inputs)
+        normed_first = (inputs * inverse_first * attention_gain).astype(bf16)
+        along["o"] = gathered(o_weight)
+        normed_other = swap(normed_first)
+        along["gate", 0] = gathered(tie(chunk(gate_weight, 0), normed_first))
+        out_grad = relative(tie(out_grad, normed_first))
+        grad_other = swap(out_grad)
+        along["up", 0] = gathered(tie(chunk(up_weight, 0), out_grad))
         segment_row = segments[0]
         cosine, sine = rotary_tables(segment_row)
         first_seen = first_blocks(segment_row)
-        inputs = tokens.astype(f32)
-        inverse_first = inverse_rms(inputs)
-        normed_first = (inputs * inverse_first * attention_gain).astype(bf16)
-        normed_seq = both_halves(normed_first)
-        grad_seq = both_halves(out_grad)
-        qkv = dot_plain(normed_seq, qkv_full)
-        rotated = rope(qkv, cosine, sine, (query_width + key_width) // 128)
-        mixed, log_totals = attend(rotated, query_width, first_seen, segment_row, score_scale)
-        middle = inputs + reduce_halves(lambda m: dot_trans(m, output_full), mixed)
-        inverse_second = inverse_rms(middle)
-        normed_second = (middle * inverse_second * feed_gain).astype(bf16)
-        normed_feed = both_halves(normed_second)
-        gate_value = dot_plain(normed_feed, gate_full).astype(bf16)
-        up_value = dot_plain(normed_feed, up_full).astype(bf16)
-        hidden = (jax.nn.silu(gate_value.astype(f32)) * up_value.astype(f32)).astype(bf16)
-        down_weight_grad = scatter(grad_seq, hidden)
-        hidden_grad = dot_plain(grad_seq, down_full)
-        gate_value, up_value = gate_value.astype(f32), up_value.astype(f32)
-        sigmoid_gate = jax.nn.sigmoid(gate_value)
-        gate_grad = (
-            hidden_grad * up_value * sigmoid_gate * (1.0 + gate_value * (1.0 - sigmoid_gate))
-        ).astype(bf16)
-        up_grad = (hidden_grad * gate_value * sigmoid_gate).astype(bf16)
-        block_out = (middle + reduce_halves(lambda h: dot_trans(h, down_full), hidden)).astype(bf16)
-        feed_normed_grad = reduce_halves(
-            lambda g, u: dot_trans(g, gate_full) + dot_trans(u, up_full), gate_grad, up_grad
-        )
-        gate_weight_grad = scatter(normed_feed, gate_grad)
-        up_weight_grad = scatter(normed_feed, up_grad)
-        middle_grad = out_grad.astype(f32) + norm_back(
-            middle, inverse_second, feed_gain, feed_normed_grad
-        )
-        feed_gain_part = jnp.sum(feed_normed_grad * middle * inverse_second, axis=0)
-        attn_out_grad = middle_grad.astype(bf16)
-        attn_grad_seq = both_halves(attn_out_grad)
-        output_weight_grad = scatter(attn_grad_seq, mixed)
-        mixed_grad = dot_plain(attn_grad_seq, output_full).astype(bf16)
-        qkv_grad = jnp.concatenate(
-            attend_back(
-                rotated,
-                mixed_grad,
-                log_totals,
-                query_width,
-                first_seen,
-                segment_row,
-                cosine,
-                sine,
-                score_scale,
+
+        full = {"qkv": spread(along["qkv"])}
+        order = Order(out_grad)
+        rotated = order(
+            lambda a, b, *w: project(
+                place, a, b, w[:4], (cosine, sine), (query_width + key_width) // 128
             ),
-            axis=1,
-        )
-        qkv_weight_grad = scatter(normed_seq, qkv_grad)
-        normed_grad = reduce_halves(lambda g: dot_trans(g, qkv_full), qkv_grad)
-        input_grad = (
-            middle_grad + norm_back(inputs, inverse_first, attention_gain, normed_grad)
-        ).astype(bf16)
-        attention_gain_part = jnp.sum(normed_grad * inputs * inverse_first, axis=0)
-        feed_gain_grad = total(natural(feed_gain_part[None]))[0]
-        attention_gain_grad = total(natural(attention_gain_part[None]))[0]
+            normed_first, normed_other, *full["qkv"],
+        )
+        along["down", 0] = gathered(order.after(chunk(down_weight, 0)))
+        full["o"] = spread(order.after(along["o"]))
+        mixed, log_totals = order(
+            lambda a: attend(a, query_width, first_seen, segment_row, score_scale), rotated
+        )
+        along["gate", 1] = gathered(order.after(chunk(gate_weight, 1)))
+        full["gate", 0] = spread(order.after(along["gate", 0]))
+        own, sent = order(lambda m, *w: back(place, (m,), (w,)), mixed, *full["o"])
+        other = swap(sent)
+        along["up", 1] = gathered(order.after(chunk(up_weight, 1)))
+        full["up", 0] = spread(order.after(along["up", 0]))
+
+        def feed_norm(inputs, own, other):
+            middle = inputs + own + other.astype(f32)
+            inverse = inverse_rms(middle)
+            return (middle * inverse * feed_gain).astype(bf16), middle, inverse
+
+        normed_second, middle, inverse_second = order(feed_norm, inputs, own, other)
+        along["down", 1] = gathered(order.after(chunk(down_weight, 1)))
+        normed_other_second = swap(normed_second)
+        full["down", 0] = spread(order.after(along["down", 0]))
+        grad_seq = order(lambda a, b: jnp.concatenate([a, b], axis=0), out_grad, grad_other)
+        normed_feed = order(
+            lambda a, b: jnp.concatenate([a, b], axis=0), normed_second, normed_other_second
+        )
+        names = ("gate", "up", "down")
+        hidden, gate_grad, up_grad = {}, {}, {}
+        from_core, from_x, kept, summed = {}, {}, {}, {}
+
+        def run_feed(i):
+            pieces = [piece for name in names for piece in full[name, i]]
+            hidden[i], gate_grad[i], up_grad[i] = order(
+                lambda n, g, *w: feed(n, g, w[:4], w[4:8], w[8:]), normed_feed, grad_seq, *pieces
+            )
+
+        def chunk_grads(i):
+            return gate_grad[i], up_grad[i], hidden[i]
+
+        def core_part(i):
+            parts = order(
+                lambda n, g, *d: grad((n, g), (0, 0, 1), d), normed_feed, grad_seq, *chunk_grads(i)
+            )
+            from_core[i] = [lax.ppermute(part, "core", SWAP) for part in parts]
+
+        def x_part(i):
+            parts = order(
+                lambda n, g, *d: grad((n, g), (0, 0, 1), d[:3], d[3:]),
+                normed_feed, grad_seq, *chunk_grads(i), *from_core[i],
+            )
+            from_x[i] = [lax.ppermute(part, "x", SWAP) for part in parts[:3]]
+            kept[i] = parts[3:]
+
+        def add(a, b):
+            return (a.astype(f32) + b.astype(f32)).astype(bf16)
+
+        def scattered(part):
+            return lax.psum_scatter(part, "z", scatter_dimension=0, tiled=True)
+
+        def finish(i, at):
+            summed[names[at], i] = scattered(order(add, kept[i][at], from_x[i][at]))
+
+        def feed_back(i, starts):
+            return order(
+                lambda a, b, *w: back(here, (a, b), (w[:4], w[4:8]), w[8:] or None, (f32, starts and bf16 or f32)),
+                gate_grad[i], up_grad[i], *full["gate", i], *full["up", i], *starts,
+            )
+
+        def block_back(i, starts):
+            return order(
+                lambda a, *w: back(here, (a,), (w[:4],), w[4:] or None, (f32, starts and bf16 or f32)),
+                hidden[i], *full["down", i], *starts,
+            )
+
+        run_feed(0)
+        full["gate", 1] = spread(order.after(along["gate", 1]))
+        core_part(0)
+        starts = feed_back(0, [])
+        full["up", 1] = spread(order.after(along["up", 1]))
+        x_part(0)
+        block_starts = block_back(0, [])
+        full["down", 1] = spread(order.after(along["down", 1]))
+        run_feed(1)
+        own, sent = feed_back(1, starts)
+        other = swap(sent)
+        core_part(1)
+        finish(0, 0)
+        finish(0, 1)
+        x_part(1)
+        finish(0, 2)
+
+        def middle_back(own, other, middle, out_grad):
+            feed_normed_grad = own + other.astype(f32)
+            middle_grad = out_grad.astype(f32) + norm_back(
+                middle, inverse_second, feed_gain, feed_normed_grad
+            )
+            gain_part = jnp.sum(feed_normed_grad * middle * inverse_second, axis=0)
+            return middle_grad.astype(bf16), middle_grad, gain_part
+
+        attn_out_grad, middle_grad, feed_gain_part = order(middle_back, own, other, middle, out_grad)
+        attn_other = swap(attn_out_grad)
+        block_own, block_sent = block_back(1, block_starts)
+        block_other = swap(block_sent)
+        finish(1, 0)
+        mixed_grad = order(lambda a, b, *w: project(place, a, b, w), attn_out_grad, attn_other, *full["o"])
+        attn_grad_seq = order(join, attn_out_grad, attn_other)
+        (part,) = order(lambda a, m: grad((a,), (0,), (m,)), attn_grad_seq, mixed)
+        from_core["o"] = lax.ppermute(part, "core", SWAP)
+        finish(1, 1)
+        part, kept["o"] = order(
+            lambda a, m, c: grad((a,), (0,), (m,), (c,)), attn_grad_seq, mixed, from_core["o"]
+        )
+        from_x["o"] = lax.ppermute(part, "x", SWAP)
+        qkv_grad = order(
+            lambda r, g, l: jnp.concatenate(
+                attend_back(
+                    r, g, l, query_width, first_seen, segment_row, cosine, sine, score_scale
+                ),
+                axis=1,
+            ),
+            rotated, mixed_grad, log_totals,
+        )
+        normed_seq = order(join, normed_first, normed_other)
+        (part,) = order(lambda a, m: grad((a,), (0,), (m,)), normed_seq, qkv_grad)
+        from_core["qkv"] = lax.ppermute(part, "core", SWAP)
+        own, sent = order(lambda g, *w: back(place, (g,), (w,)), qkv_grad, *full["qkv"])
+        other = swap(sent)
+        finish(1, 2)
+        part, kept["qkv"] = order(
+            lambda a, m, c: grad((a,), (0,), (m,), (c,)), normed_seq, qkv_grad, from_core["qkv"]
+        )
+        from_x["qkv"] = lax.ppermute(part, "x", SWAP)
+        summed["o"] = scattered(order(add, kept["o"], from_x["o"]))
+        block_out = order(
+            lambda m, a, b: natural((m + a + b.astype(f32)).astype(bf16)), middle, block_own, block_other
+        )
+
+        def input_back(own, other, inputs, middle_grad):
+            normed_grad = own + other.astype(f32)
+            input_grad = middle_grad + norm_back(inputs, inverse_first, attention_gain, normed_grad)
+            gain_part = jnp.sum(normed_grad * inputs * inverse_first, axis=0)
+            return input_grad.astype(bf16), gain_part
+
+        input_grad, attention_gain_part = order(input_back, own, other, inputs, middle_grad)
+        summed["qkv"] = scattered(order(add, kept["qkv"], from_x["qkv"]))
+        gains = total(natural(jnp.stack([attention_gain_part, feed_gain_part])))
+        qkv_weight_grad = summed["qkv"].astype(f32)
+
+        def whole(name):
+            return jnp.concatenate([summed[name, i] for i in range(CHUNKS)], axis=1).astype(f32)
+
         return (
-            natural(block_out),
+            block_out,
             natural(input_grad),
             qkv_weight_grad[:, :query_width],
             qkv_weight_grad[:, query_width : query_width + key_width],
             qkv_weight_grad[:, query_width + key_width :],
-            output_weight_grad,
-            attention_gain_grad,
-            gate_weight_grad,
-            up_weight_grad,
-            down_weight_grad,
-            feed_gain_grad,
+            summed["o"].astype(f32),
+            gains[0],
+            whole("gate"),
+            whole("up"),
+            whole("down"),
+            gains[1],
         )
 
     return shards

time: 948 us -> 905 us (0.955)
  matrix products: 225 us -> 0 us
  Pallas kernels: 54.9 us -> 258 us
  waiting for transfers between devices: 437 us -> 409 us
  local copies, waits for them, and re-layouts: 86.3 us -> 75.6 us
  starting transfers between devices: 38.6 us -> 48.8 us
    dot_general x30 -> x0, matrix products: 225 us -> none  [the longest x10 92.7 us: dot_trans(): lax.dot_general(left, right, (((1,), (1,)), ((), ())), preferred_element_...]
    pallas_call x1 -> x18, Pallas kernels: 3.72 us -> 207 us  [the longest x6 76.5 us: back(): pl.pallas_call(functools.partial(back_kernel, len(acts), starts is not No...]
    all_gather x5 -> x8, waiting for transfers between devices: 126 us -> 16.4 us  [gathered(): return lax.all_gather(operand, 'z', axis=0, tiled=True)]
    ppermute x33 -> x48, waiting for transfers between devices: 301 us -> 366 us  [the longest x8 160 us: spread(): across = lax.ppermute(along, 'x', SWAP)]
    reduce_scatter x5 -> x8, waiting for transfers between devices: 0.01 us -> 22.2 us  [scattered(): return lax.psum_scatter(part, 'z', scatter_dimension=0, tiled=True)]
    unnamed x95 -> x144, local copies, waits for them, and re-layouts: 44.5 us -> 30.9 us
    all_gather x5 -> x8, starting transfers between devices: 0.19 us -> 10.8 us  [gathered(): return lax.all_gather(operand, 'z', axis=0, tiled=True)]
    slice x0 -> x7, local copies, waits for them, and re-layouts: none -> 10.4 us  [the longest x6 9.74 us: chunk(): return weight[:, edges[i]:edges[i + 1]]]
  transfers between devices with their start and end apart: 53 -> 69, of which waited for: 20 -> 25; matrix products, arithmetic and copies ran while one was open for 35% -> 15% of each run, Pallas kernels for 6% -> 23%
where the time goes in v3:
time: 905 us; the launch traced here: 896 us
  waiting for transfers between devices  409 us (45%)
  Pallas kernels  258 us (29%)
  other arithmetic  89.1 us (10%)
  local copies, waits for them, and re-layouts  75.6 us (8%)
  starting transfers between devices  48.8 us (5%)
  between operations  15.4 us (2%)
    ppermute x8, waiting for transfers between devices, spread(): across = lax.ppermute(along, 'x', SWAP)  160 us
    ppermute x8, waiting for transfers between devices, swap(): return lax.ppermute(own, 'tensor', SWAP)  123 us
    pallas_call x6, Pallas kernels, back(): pl.pallas_call(functools.partial(back_kernel, len(acts), starts is not No...  76.5 us
    pallas_call x8, Pallas kernels, grad(): pl.pallas_call(functools.partial(grad_kernel, which, added is not None),...  74 us
    ppermute x6, waiting for transfers between devices, x_part(): from_x[i] = [lax.ppermute(part, 'x', SWAP) for part in parts[:3]]  61.9 us
    pallas_call x2, Pallas kernels, feed(): pl.pallas_call(feed_kernel, grid=(units // BLOCK,), in_specs=[act, act] +...  39.8 us
    pallas_call x1, Pallas kernels, attend_back(): pl.pallas_call(functools.partial(backward_kernel, scale), grid_spec=pltpu...  35.3 us
    unnamed x144, local copies, waits for them, and re-layouts  30.9 us
  transfers between devices with their start and end apart: 69, of which 25 were waited for; matrix products, arithmetic and copies ran while one was open for 15% of the time, Pallas kernels for 23%

profile of v3, /device:TPU:0, one launch (start us, length us, event | category | flops | bytes accessed | tf_op | source)
XLA Modules:
  0.0 895.8 jit_solution(9154158806197467357)
XLA Ops:
  29.2 16.3 %all-gather.9.cloned.1.call-done.refs_0_.refs_1_ = bf16[512,1280]{1,0:T(8,128)(2,1)} async-done(((bf16[128,1280]{1,0:T(8,128)(2,1)}), bf16[512,1280]{1,0:T(8,128)(2,1)}) %all-gather.9.cloned.1.call-update) | async-done | bytes 1310736 | tf_op jit(solution)/shard_map/all_gather | solution.py:532
  52.7 23.1 %collective-permute-done.1.refs_1_.refs_2_ = bf16[512,1280]{1,0:T(8,128)(2,1)} collective-permute-done((bf16[512,1280]{1,0:T(8,128)(2,1)}, bf16[512,1280]{1,0:T(8,128)(2,1)}, u32[]{:S(2)}, u32[]{:S(2)}) %collective-permute-start.1) | collective-permute-done | bytes 1310752 | tf_op jit(solution)/shard_map/ppermute | solution.py:491
  87.1 10.1 %shard_map.203.q_ref.k_ref.v_ref = bf16[768,1280]{1,0:T(8,128)(2,1)} custom-call(s32[1]{0:T(128)} %bitcast.1.place_ref, bf16[384,2048]{1,0:T(8,128)(2,1)} %multiply_convert_fusion.1.own_ref, bf16[384,2048]{1,0:T(8,128)(2,1)} %collective-permute-done.other_ref, bf16[512,1280]{1,0:T(8,128)(2,1)S(1)} %copy-done.14, ...), custom_call_target="tpu_custom_call" | custom-call | flops 4026531840 | bytes 5242880 | tf_op jit(solution)/shard_map/pallas_call | solution.py:321
  98.8 24.1 %collective-permute-done.4.refs_2_.refs_1_ = bf16[512,1024]{1,0:T(8,128)(2,1)S(1)} collective-permute-done((bf16[512,1024]{1,0:T(8,128)(2,1)}, bf16[512,1024]{1,0:T(8,128)(2,1)S(1)}, u32[]{:S(2)}, u32[]{:S(2)}) %collective-permute-start.4) | collective-permute-done | bytes 1048608 | tf_op jit(solution)/shard_map/ppermute | solution.py:491
  126.8 15.8 %shard_map.204 = (bf16[768,1024]{1,0:T(8,128)(2,1)S(1)}, f32[768,256]{1,0:T(8,128)S(1)}) custom-call(s32[3]{0:T(128)S(1)} %convert_reduce_fusion.1.low_ref, bf16[768,1280]{1,0:T(8,128)(2,1)S(1)} %copy-done.35, bf16[768,1280]{1,0:T(8,128)(2,1)S(1)} %copy-done.35, bf16[768,1280]{1,0:T(8,128)(2,1)S(1)} %copy-done.35, s32[768,1]{1,0:T(8,128)S(1)} %copy.65.col_ref, ...), custom_call_target="tpu_custom_call" | custom-call | flops 6039797760 | bytes 3145728 | tf_op jit(solution)/shard_map/pallas_call | solution.py:195
  145.0 8.9 shard_map.205
  159.7 31.6 %collective-permute-done.7 = bf16[384,2048]{1,0:T(8,128)(2,1)} collective-permute-done((bf16[384,2048]{1,0:T(8,128)(2,1)S(1)}, bf16[384,2048]{1,0:T(8,128)(2,1)}, u32[]{:S(2)}, u32[]{:S(2)}) %collective-permute-start.7) | collective-permute-done | bytes 1572896 | tf_op jit(solution)/shard_map/ppermute | solution.py:508
  201.0 24.1 %collective-permute-done.9 = bf16[384,2048]{1,0:T(8,128)(2,1)} collective-permute-done((bf16[384,2048]{1,0:T(8,128)(2,1)}, bf16[384,2048]{1,0:T(8,128)(2,1)}, u32[]{:S(2)}, u32[]{:S(2)}) %collective-permute-start.9) | collective-permute-done | bytes 1572896 | tf_op jit(solution)/shard_map/ppermute | solution.py:508
  231.5 27.6 %collective-permute-done.13.refs_5_.refs_7_ = bf16[512,1280]{1,0:T(8,128)(2,1)} collective-permute-done((bf16[512,1280]{1,0:T(8,128)(2,1)}, bf16[512,1280]{1,0:T(8,128)(2,1)}, u32[]{:S(2)}, u32[]{:S(2)}) %collective-permute-start.13) | collective-permute-done | bytes 1310752 | tf_op jit(solution)/shard_map/ppermute | solution.py:491
  259.1 24.5 %collective-permute-done.16.refs_9_.refs_2_ = bf16[512,1280]{1,0:T(8,128)(2,1)} collective-permute-done((bf16[512,1280]{1,0:T(8,128)(2,1)}, bf16[512,1280]{1,0:T(8,128)(2,1)}, u32[]{:S(2)}, u32[]{:S(2)}) %collective-permute-start.16) | collective-permute-done | bytes 1310752 | tf_op jit(solution)/shard_map/ppermute | solution.py:491
  285.8 10.3 %all-gather.23.cloned.1.call-start = ((), (), s32[]{:S(2)}) async-start(), calls=%async_computation.15 | async-start | bytes 1966080 | tf_op jit(solution)/shard_map/all_gather | solution.py:532
  305.6 18.5 %shard_map.206 = (bf16[768,1280]{1,0:T(8,128)(2,1)}, bf16[768,1280]{1,0:T(8,128)(2,1)}, bf16[768,1280]{1,0:T(8,128)(2,1)}) custom-call(bf16[768,2048]{1,0:T(8,128)(2,1)} %copy-done.51, bf16[768,2048]{1,0:T(8,128)(2,1)} %copy-done.52, bf16[512,1280]{1,0:T(8,128)(2,1)S(1)} %copy-done.16, bf16[512,1280]{1,0:T(8,128)(2,1)} %collective-permute-done.10.refs_1_.refs_3_, ...), custom_call_target="tpu_custom_call" | custom-call | flops 12079595520 | bytes 15728640 | tf_op jit(solution)/shard_map/pallas_call | solution.py:282
  328.7 9.1 %shard_map.207 = (bf16[1024,1280]{1,0:T(8,128)(2,1)}, bf16[1024,1280]{1,0:T(8,128)(2,1)}, bf16[1024,1280]{1,0:T(8,128)(2,1)}) custom-call(bf16[768,2048]{1,0:T(8,128)(2,1)} %copy-done.51, bf16[768,2048]{1,0:T(8,128)(2,1)} %copy-done.52, bf16[768,1280]{1,0:T(8,128)(2,1)S(1)} %copy-done.29, bf16[768,1280]{1,0:T(8,128)(2,1)S(1)} %copy-done.30, ...), custom_call_target="tpu_custom_call" | custom-call | flops 6039797760 | bytes 7864320 | tf_op jit(solution)/shard_map/pallas_call | solution.py:439
  342.6 15.2 %shard_map.208 = (f32[384,2048]{1,0:T(8,128)}, f32[384,2048]{1,0:T(8,128)}) custom-call(s32[1]{0:T(128)} %constant.30.clone.1.place_ref, bf16[768,1280]{1,0:T(8,128)(2,1)} %get-tuple-element.305.refs_2_.refs_0_, bf16[768,1280]{1,0:T(8,128)(2,1)} %get-tuple-element.306.refs_3_.refs_1_, bf16[512,1280]{1,0:T(8,128)(2,1)S(1)} %copy-done.16, ...), custom_call_target="tpu_custom_call" | custom-call | flops 8053063680 | bytes 10485760 | tf_op jit(solution)/shard_map/pallas_call | solution.py:381
  358.3 15.8 %shard_map.209 = (bf16[512,1280]{1,0:T(8,128)(2,1)S(1)}, bf16[512,1280]{1,0:T(8,128)(2,1)}, bf16[512,1280]{1,0:T(8,128)(2,1)}, bf16[512,1280]{1,0:T(8,128)(2,1)S...) custom-call(bf16[768,2048]{1,0:T(8,128)(2,1)} %copy-done.51, bf16[768,2048]{1,0:T(8,128)(2,1)} %copy-done.52, ...), custom_call_target="tpu_custom_call" | custom-call | flops 6039797760 | bytes 7864320 | tf_op jit(solution)/shard_map/pallas_call | solution.py:439
  375.2 11.0 %shard_map.210 = (f32[384,2048]{1,0:T(8,128)}, f32[384,2048]{1,0:T(8,128)}) custom-call(s32[1]{0:T(128)} %constant.30.clone.1.place_ref, bf16[768,1280]{1,0:T(8,128)(2,1)} %get-tuple-element.312.refs_4_.refs_0_, bf16[512,1280]{1,0:T(8,128)(2,1)S(1)} %copy-done.17, bf16[512,1280]{1,0:T(8,128)(2,1)} %collective-permute-done.16.refs_9_.refs_2_, ...), custom_call_target="tpu_custom_call" | custom-call | flops 4026531840 | bytes 5242880 | tf_op jit(solution)/shard_map/pallas_call | solution.py:381
  388.2 22.3 %collective-permute-done.22.refs_5_.refs_7_ = bf16[512,1536]{1,0:T(8,128)(2,1)} collective-permute-done((bf16[512,1536]{1,0:T(8,128)(2,1)}, bf16[512,1536]{1,0:T(8,128)(2,1)}, u32[]{:S(2)}, u32[]{:S(2)}) %collective-permute-start.22) | collective-permute-done | bytes 1572896 | tf_op jit(solution)/shard_map/ppermute | solution.py:491
  411.1 32.7 %collective-permute-done.28.refs_9_.refs_2_ = bf16[512,1536]{1,0:T(8,128)(2,1)S(1)} collective-permute-done((bf16[512,1536]{1,0:T(8,128)(2,1)}, bf16[512,1536]{1,0:T(8,128)(2,1)S(1)}, u32[]{:S(2)}, u32[]{:S(2)}) %collective-permute-start.28) | collective-permute-done | bytes 1572896 | tf_op jit(solution)/shard_map/ppermute | solution.py:491
  449.7 21.2 %shard_map.211 = (bf16[768,1536]{1,0:T(8,128)(2,1)}, bf16[768,1536]{1,0:T(8,128)(2,1)}, bf16[768,1536]{1,0:T(8,128)(2,1)}) custom-call(bf16[768,2048]{1,0:T(8,128)(2,1)} %copy-done.51, bf16[768,2048]{1,0:T(8,128)(2,1)} %copy-done.52, bf16[512,1536]{1,0:T(8,128)(2,1)S(1)} %copy-done.8, bf16[512,1536]{1,0:T(8,128)(2,1)} %collective-permute-done.19.refs_1_.refs_3_, ...), custom_call_target="tpu_custom_call" | custom-call | flops 14495514624 | bytes 18874368 | tf_op jit(solution)/shard_map/pallas_call | solution.py:282
  471.0 18.4 %shard_map.212 = (f32[384,2048]{1,0:T(8,128)}, bf16[384,2048]{1,0:T(8,128)(2,1)S(1)}) custom-call(s32[1]{0:T(128)} %constant.30.clone.1.place_ref, bf16[768,1536]{1,0:T(8,128)(2,1)} %get-tuple-element.371.refs_0_.refs_2_, bf16[768,1536]{1,0:T(8,128)(2,1)} %get-tuple-element.372.refs_1_.refs_3_, bf16[512,1536]{1,0:T(8,128)(2,1)S(1)} %copy-done.8, ...), custom_call_target="tpu_custom_call" | custom-call | flops 9663676416 | bytes 12582912 | tf_op jit(solution)/shard_map/pallas_call | solution.py:381
  490.6 11.1 %shard_map.213 = (bf16[1024,1536]{1,0:T(8,128)(2,1)}, bf16[1024,1536]{1,0:T(8,128)(2,1)}, bf16[1024,1536]{1,0:T(8,128)(2,1)}) custom-call(bf16[768,2048]{1,0:T(8,128)(2,1)} %copy-done.51, bf16[768,2048]{1,0:T(8,128)(2,1)} %copy-done.52, bf16[768,1536]{1,0:T(8,128)(2,1)S(1)} %copy-done.33, bf16[768,1536]{1,0:T(8,128)(2,1)S(1)} %copy-done.34, ...), custom_call_target="tpu_custom_call" | custom-call | flops 7247757312 | bytes 9437184 | tf_op jit(solution)/shard_map/pallas_call | solution.py:439
  504.4 29.6 %collective-permute-done.37 = bf16[512,1280]{1,0:T(8,128)(2,1)S(1)} collective-permute-done((bf16[512,1280]{1,0:T(8,128)(2,1)S(1)}, bf16[512,1280]{1,0:T(8,128)(2,1)S(1)}, u32[]{:S(2)}, u32[]{:S(2)}) %collective-permute-start.37) | collective-permute-done | bytes 1310752 | tf_op jit(solution)/shard_map/ppermute | solution.py:612
  537.2 25.0 %collective-permute-done.36 = bf16[512,1280]{1,0:T(8,128)(2,1)} collective-permute-done((bf16[512,1280]{1,0:T(8,128)(2,1)}, bf16[512,1280]{1,0:T(8,128)(2,1)}, u32[]{:S(2)}, u32[]{:S(2)}) %collective-permute-start.36) | collective-permute-done | bytes 1310752 | tf_op jit(solution)/shard_map/ppermute | solution.py:612
  565.5 17.3 %shard_map.214 = (bf16[512,1536]{1,0:T(8,128)(2,1)S(1)}, bf16[512,1536]{1,0:T(8,128)(2,1)}, bf16[512,1536]{1,0:T(8,128)(2,1)S(1)}, bf16[512,1536]{1,0:T(8,128)(2...) custom-call(bf16[768,2048]{1,0:T(8,128)(2,1)} %copy-done.51, bf16[768,2048]{1,0:T(8,128)(2,1)} %copy-done.52, ...), custom_call_target="tpu_custom_call" | custom-call | flops 7247757312 | bytes 9437184 | tf_op jit(solution)/shard_map/pallas_call | solution.py:439
  608.4 12.2 %shard_map.215 = (f32[384,2048]{1,0:T(8,128)}, bf16[384,2048]{1,0:T(8,128)(2,1)}) custom-call(s32[1]{0:T(128)} %constant.30.clone.1.place_ref, bf16[768,1536]{1,0:T(8,128)(2,1)} %get-tuple-element.384.refs_4_.refs_0_, bf16[512,1536]{1,0:T(8,128)(2,1)S(1)} %copy-done.9, bf16[512,1536]{1,0:T(8,128)(2,1)S(1)} %copy-done.12, bf16[512,1536]{1,0:T(8,128)(2,1)} %copy-done.65, ...), custom_call_target="tpu_custom_call" | custom-call | flops 4831838208 | bytes 6291456 | tf_op jit(solution)/shard_map/pallas_call | solution.py:381
  629.1 33.7 %collective-permute-done.39.other_ref = bf16[384,2048]{1,0:T(8,128)(2,1)} collective-permute-done((bf16[384,2048]{1,0:T(8,128)(2,1)}, bf16[384,2048]{1,0:T(8,128)(2,1)}, u32[]{:S(2)}, u32[]{:S(2)}) %collective-permute-start.39) | collective-permute-done | bytes 1572896 | tf_op jit(solution)/shard_map/ppermute | solution.py:508
  694.1 35.3 %shard_map.219 = (bf16[768,1024]{1,0:T(8,128)(2,1)S(1)}, bf16[768,128]{1,0:T(8,128)(2,1)S(1)}, bf16[768,128]{1,0:T(8,128)(2,1)S(1)}) custom-call(s32[3]{0:T(128)S(1)} %convert_reduce_fusion.1.low_ref, bf16[768,1280]{1,0:T(8,128)(2,1)} %shard_map.203.q_ref.k_ref.v_ref, bf16[768,1280]{1,0:T(8,128)(2,1)} %shard_map.203.q_ref.k_ref.v_ref, ...), custom_call_target="tpu_custom_call" | custom-call | flops 18119393280 | bytes 6291456 | tf_op jit(solution)/shard_map/pallas_call | solution.py:224
  740.6 10.8 %shard_map.221 = (f32[384,2048]{1,0:T(8,128)}, bf16[384,2048]{1,0:T(8,128)(2,1)}) custom-call(s32[1]{0:T(128)} %bitcast.1.place_ref, bf16[768,1280]{1,0:T(8,128)(2,1)} %copy-done, bf16[512,1280]{1,0:T(8,128)(2,1)S(1)} %copy-done.15, bf16[512,1280]{1,0:T(8,128)(2,1)} %collective-permute-done.1.refs_1_.refs_2_, ...), custom_call_target="tpu_custom_call" | custom-call | flops 4026531840 | bytes 5242880 | tf_op jit(solution)/shard_map/pallas_call | solution.py:381
  764.7 16.8 %collective-permute-done.43 = bf16[512,1024]{1,0:T(8,128)(2,1)S(1)} collective-permute-done((bf16[512,1024]{1,0:T(8,128)(2,1)}, bf16[512,1024]{1,0:T(8,128)(2,1)S(1)}, u32[]{:S(2)}, u32[]{:S(2)}) %collective-permute-start.43) | collective-permute-done | bytes 1048608 | tf_op jit(solution)/shard_map/ppermute | solution.py:674
  782.9 9.3 %collective-permute-done.38 = bf16[384,2048]{1,0:T(8,128)(2,1)} collective-permute-done((bf16[384,2048]{1,0:T(8,128)(2,1)}, bf16[384,2048]{1,0:T(8,128)(2,1)}, u32[]{:S(2)}, u32[]{:S(2)}) %collective-permute-start.38) | collective-permute-done | bytes 1572896 | tf_op jit(solution)/shard_map/ppermute | solution.py:508
  806.4 19.0 %collective-permute-done.46 = bf16[384,2048]{1,0:T(8,128)(2,1)} collective-permute-done((bf16[384,2048]{1,0:T(8,128)(2,1)}, bf16[384,2048]{1,0:T(8,128)(2,1)}, u32[]{:S(2)}, u32[]{:S(2)}) %collective-permute-start.46) | collective-permute-done | bytes 1572896 | tf_op jit(solution)/shard_map/ppermute | solution.py:508
  863.4 22.2 %reduce-scatter.9.cloned.1.call-done = bf16[128,1280]{1,0:T(8,128)(2,1)} async-done(((bf16[512,1280]{1,0:T(8,128)(2,1)}), bf16[128,1280]{1,0:T(8,128)(2,1)}) %reduce-scatter.9.cloned.1.call-update) | async-done | bytes 327696 | tf_op jit(solution)/shard_map/reduce_scatter | solution.py:619
  (375 shorter events, 257.6 us)
Async XLA Ops:
  9.0 88.2 %all-gather.11.cloned.1.call-start = ((), (), s32[]{:S(2)}) async-start(), calls=%async_computation.9 | async-start | bytes 1310720 | tf_op jit(solution)/shard_map/all_gather | solution.py:532
  9.7 189.2 %all-gather.15.cloned.1.call-start = ((), (), s32[]{:S(2)}) async-start(), calls=%async_computation.11 | async-start | bytes 1638400 | tf_op jit(solution)/shard_map/all_gather | solution.py:532
  29.2 169.9 %all-gather.17.cloned.1.call-start = ((), (), s32[]{:S(2)}) async-start(), calls=%async_computation.12 | async-start | bytes 1638400 | tf_op jit(solution)/shard_map/all_gather | solution.py:532
  84.1 116.8 %all-gather.19.cloned.1.call-start = ((), (), s32[]{:S(2)}) async-start(), calls=%async_computation.13 | async-start | bytes 1638400 | tf_op jit(solution)/shard_map/all_gather | solution.py:532
  125.2 214.0 %all-gather.13.cloned.1.call-start = ((), (), s32[]{:S(2)}) async-start(), calls=%async_computation.10 | async-start | bytes 1966080 | tf_op jit(solution)/shard_map/all_gather | solution.py:532
  155.4 69.6 %collective-permute-start.9 = (bf16[384,2048]{1,0:T(8,128)(2,1)}, bf16[384,2048]{1,0:T(8,128)(2,1)}, u32[]{:S(2)}, u32[]{:S(2)}) collective-permute-start(bf16[384,2048]{1,0:T(8,128)(2,1)} %reshape.116), channel_id=1, source_target_pairs={{0,1},{1,0},{2,3},{3,2},{4,5},{5,4},{6,7},{7,6},{8,9},{9,8},{10,11... | collective-permute-start | bytes 4718600 | tf_op jit(solution)/shard_map/ppermute | solution.py:508
  159.7 198.1 %all-gather.21.cloned.1.call-start = ((), (), s32[]{:S(2)}) async-start(), calls=%async_computation.14 | async-start | bytes 1966080 | tf_op jit(solution)/shard_map/all_gather | solution.py:532
  197.5 86.1 %collective-permute-start.8 = (bf16[384,2048]{1,0:T(8,128)(2,1)}, bf16[384,2048]{1,0:T(8,128)(2,1)}, u32[]{:S(2)}, u32[]{:S(2)}) collective-permute-start(bf16[384,2048]{1,0:T(8,128)(2,1)} %multiply_convert_fusion), channel_id=1, source_target_pairs={{0,1},{1,0},{2,3},{3,2},{4,5},{5,4},{6,7},{7,6},{8,9},{9,8},{10,11... | collective-permute-start | bytes 4718600 | tf_op jit(solution)/shard_map/ppermute | solution.py:508
  199.1 60.0 %collective-permute-start.13 = (bf16[512,1280]{1,0:T(8,128)(2,1)}, bf16[512,1280]{1,0:T(8,128)(2,1)}, u32[]{:S(2)}, u32[]{:S(2)}) collective-permute-start(bf16[512,1280]{1,0:T(8,128)(2,1)} %all-gather.17.cloned.1.call-done.refs_4_.refs_6_), channel_id=1, source_target_pairs={{0,4},{4,0},{1,5},{5,1},{2,6},{6,2},{3,7},{7,3},{8,12},{12,8},{9,1... | collective-permute-start | bytes 3932168 | tf_op jit(solution)/shard_map/ppermute | solution.py:491
  225.0 58.5 %collective-permute-start.16 = (bf16[512,1280]{1,0:T(8,128)(2,1)}, bf16[512,1280]{1,0:T(8,128)(2,1)}, u32[]{:S(2)}, u32[]{:S(2)}) collective-permute-start(bf16[512,1280]{1,0:T(8,128)(2,1)} %all-gather.19.cloned.1.call-done.refs_8_.refs_1_), channel_id=1, source_target_pairs={{0,4},{4,0},{1,5},{5,1},{2,6},{6,2},{3,7},{7,3},{8,12},{12,8},{9,1... | collective-permute-start | bytes 3932168 | tf_op jit(solution)/shard_map/ppermute | solution.py:491
  231.0 72.8 %collective-permute-start.12 = (bf16[512,1280]{1,0:T(8,128)(2,1)}, bf16[512,1280]{1,0:T(8,128)(2,1)}, u32[]{:S(2)}, u32[]{:S(2)}) collective-permute-start(bf16[512,1280]{1,0:T(8,128)(2,1)} %collective-permute-done.10.refs_1_.refs_3_), channel_id=1, source_target_pairs={{0,2},{2,0},{1,3},{3,1},{4,6},{6,4},{5,7},{7,5},{8,10},{10,8},{9,1... | collective-permute-start | bytes 3932168 | tf_op jit(solution)/shard_map/ppermute | solution.py:492
  231.0 72.8 %collective-permute-start.14 = (bf16[512,1280]{1,0:T(8,128)(2,1)}, bf16[512,1280]{1,0:T(8,128)(2,1)}, u32[]{:S(2)}, u32[]{:S(2)}) collective-permute-start(bf16[512,1280]{1,0:T(8,128)(2,1)} %all-gather.17.cloned.1.call-done.refs_4_.refs_6_), channel_id=1, source_target_pairs={{0,2},{2,0},{1,3},{3,1},{4,6},{6,4},{5,7},{7,5},{8,10},{10,8},{9,1... | collective-permute-start | bytes 3932168 | tf_op jit(solution)/shard_map/ppermute | solution.py:492
  285.8 100.3 %all-gather.23.cloned.1.call-start = ((), (), s32[]{:S(2)}) async-start(), calls=%async_computation.15 | async-start | bytes 1966080 | tf_op jit(solution)/shard_map/all_gather | solution.py:532
  339.2 500.5 %reduce-scatter.13.cloned.1.call-start = ((), (), s32[]{:S(2)}) async-start(), calls=%async_computation.18 | async-start | bytes 1638400 | tf_op jit(solution)/shard_map/reduce_scatter | solution.py:619
  341.1 69.5 %collective-permute-start.20 = (bf16[512,1536]{1,0:T(8,128)(2,1)}, bf16[512,1536]{1,0:T(8,128)(2,1)}, u32[]{:S(2)}, u32[]{:S(2)}) collective-permute-start(bf16[512,1536]{1,0:T(8,128)(2,1)} %all-gather.13.cloned.1.call-done.refs_0_.refs_2_), channel_id=1, source_target_pairs={{0,2},{2,0},{1,3},{3,1},{4,6},{6,4},{5,7},{7,5},{8,10},{10,8},{9,1... | collective-permute-start | bytes 4718600 | tf_op jit(solution)/shard_map/ppermute | solution.py:492
  386.1 57.6 %collective-permute-start.28 = (bf16[512,1536]{1,0:T(8,128)(2,1)}, bf16[512,1536]{1,0:T(8,128)(2,1)S(1)}, u32[]{:S(2)}, u32[]{:S(2)}) collective-permute-start(bf16[512,1536]{1,0:T(8,128)(2,1)} %all-gather.23.cloned.1.call-done.refs_8_.refs_1_), channel_id=1, source_target_pairs={{0,4},{4,0},{1,5},{5,1},{2,6},{6,2},{3,7},{7,3},{8,12},{12,8},{9,1... | collective-permute-start | bytes 4718600 | tf_op jit(solution)/shard_map/ppermute | solution.py:491
  387.7 56.0 %collective-permute-start.21 = (bf16[512,1536]{1,0:T(8,128)(2,1)}, bf16[512,1536]{1,0:T(8,128)(2,1)S(1)}, u32[]{:S(2)}, u32[]{:S(2)}) collective-permute-start(bf16[512,1536]{1,0:T(8,128)(2,1)} %collective-permute-done.19.refs_1_.refs_3_), channel_id=1, source_target_pairs={{0,2},{2,0},{1,3},{3,1},{4,6},{6,4},{5,7},{7,5},{8,10},{10,8},{9,1... | collective-permute-start | bytes 4718600 | tf_op jit(solution)/shard_map/ppermute | solution.py:492
  501.7 63.7 %collective-permute-start.33 = (bf16[1024,1536]{1,0:T(8,128)(2,1)}, bf16[1024,1536]{1,0:T(8,128)(2,1)}, u32[]{:S(2)}, u32[]{:S(2)}) collective-permute-start(bf16[1024,1536]{1,0:T(8,128)(2,1)} %get-tuple-element.359), channel_id=1, source_target_pairs={{0,2},{2,0},{1,3},{3,1},{4,6},{6,4},{5,7},{7,5},{8,10},{10,8},{9,1... | collective-permute-start | bytes 9437192 | tf_op jit(solution)/shard_map/ppermute | solution.py:605
  501.8 63.6 %collective-permute-start.34 = (bf16[1024,1536]{1,0:T(8,128)(2,1)}, bf16[1024,1536]{1,0:T(8,128)(2,1)}, u32[]{:S(2)}, u32[]{:S(2)}) collective-permute-start(bf16[1024,1536]{1,0:T(8,128)(2,1)} %get-tuple-element.360), channel_id=1, source_target_pairs={{0,2},{2,0},{1,3},{3,1},{4,6},{6,4},{5,7},{7,5},{8,10},{10,8},{9,1... | collective-permute-start | bytes 9437192 | tf_op jit(solution)/shard_map/ppermute | solution.py:605
  502.2 63.2 %collective-permute-start.35 = (bf16[1024,1536]{1,0:T(8,128)(2,1)}, bf16[1024,1536]{1,0:T(8,128)(2,1)}, u32[]{:S(2)}, u32[]{:S(2)}) collective-permute-start(bf16[1024,1536]{1,0:T(8,128)(2,1)} %get-tuple-element.361), channel_id=1, source_target_pairs={{0,2},{2,0},{1,3},{3,1},{4,6},{6,4},{5,7},{7,5},{8,10},{10,8},{9,1... | collective-permute-start | bytes 9437192 | tf_op jit(solution)/shard_map/ppermute | solution.py:605
  504.1 58.0 %collective-permute-start.36 = (bf16[512,1280]{1,0:T(8,128)(2,1)}, bf16[512,1280]{1,0:T(8,128)(2,1)}, u32[]{:S(2)}, u32[]{:S(2)}) collective-permute-start(bf16[512,1280]{1,0:T(8,128)(2,1)} %get-tuple-element.363), channel_id=1, source_target_pairs={{0,4},{4,0},{1,5},{5,1},{2,6},{6,2},{3,7},{7,3},{8,12},{12,8},{9,1... | collective-permute-start | bytes 3932168 | tf_op jit(solution)/shard_map/ppermute | solution.py:612
  534.0 56.3 %collective-permute-start.32 = (bf16[512,1280]{1,0:T(8,128)(2,1)}, bf16[512,1280]{1,0:T(8,128)(2,1)}, u32[]{:S(2)}, u32[]{:S(2)}) collective-permute-start(bf16[512,1280]{1,0:T(8,128)(2,1)} %get-tuple-element.353), channel_id=1, source_target_pairs={{0,4},{4,0},{1,5},{5,1},{2,6},{6,2},{3,7},{7,3},{8,12},{12,8},{9,1... | collective-permute-start | bytes 3932168 | tf_op jit(solution)/shard_map/ppermute | solution.py:612
  537.1 302.6 %reduce-scatter.15.cloned.1.call-start = ((), (), s32[]{:S(2)}) async-start(), calls=%async_computation.19 | async-start | bytes 1966080 | tf_op jit(solution)/shard_map/reduce_scatter | solution.py:619
  626.5 217.4 %reduce-scatter.17.cloned.1.call-start = ((), (), s32[]{:S(2)}) async-start(), calls=%async_computation.20 | async-start | bytes 1638400 | tf_op jit(solution)/shard_map/reduce_scatter | solution.py:619
  627.2 216.6 %reduce-scatter.19.cloned.1.call-start = ((), (), s32[]{:S(2)}) async-start(), calls=%async_computation.21 | async-start | bytes 1966080 | tf_op jit(solution)/shard_map/reduce_scatter | solution.py:619
  683.2 176.1 %reduce-scatter.21.cloned.1.call-start = ((), (), s32[]{:S(2)}) async-start(), calls=%async_computation.22 | async-start | bytes 1638400 | tf_op jit(solution)/shard_map/reduce_scatter | solution.py:619
  683.3 68.1 %collective-permute-start.45 = (bf16[512,1536]{1,0:T(8,128)(2,1)}, bf16[512,1536]{1,0:T(8,128)(2,1)}, u32[]{:S(2)}, u32[]{:S(2)}) collective-permute-start(bf16[512,1536]{1,0:T(8,128)(2,1)} %copy-done.10), channel_id=1, source_target_pairs={{0,4},{4,0},{1,5},{5,1},{2,6},{6,2},{3,7},{7,3},{8,12},{12,8},{9,1... | collective-permute-start | bytes 4718600 | tf_op jit(solution)/shard_map/ppermute | solution.py:612
  685.1 174.1 %reduce-scatter.23.cloned.1.call-start = ((), (), s32[]{:S(2)}) async-start(), calls=%async_computation.23 | async-start | bytes 1966080 | tf_op jit(solution)/shard_map/reduce_scatter | solution.py:619
  754.6 107.1 %reduce-scatter.11.cloned.1.call-start = ((), (), s32[]{:S(2)}) async-start(), calls=%async_computation.17 | async-start | bytes 1310720 | tf_op jit(solution)/shard_map/reduce_scatter | solution.py:619
  755.3 70.1 %collective-permute-start.46 = (bf16[384,2048]{1,0:T(8,128)(2,1)}, bf16[384,2048]{1,0:T(8,128)(2,1)}, u32[]{:S(2)}, u32[]{:S(2)}) collective-permute-start(bf16[384,2048]{1,0:T(8,128)(2,1)} %get-tuple-element.445), channel_id=1, source_target_pairs={{0,1},{1,0},{2,3},{3,2},{4,5},{5,4},{6,7},{7,6},{8,9},{9,8},{10,11... | collective-permute-start | bytes 4718600 | tf_op jit(solution)/shard_map/ppermute | solution.py:508
  762.6 73.0 %collective-permute-start.47 = (bf16[512,1280]{1,0:T(8,128)(2,1)}, bf16[512,1280]{1,0:T(8,128)(2,1)}, u32[]{:S(2)}, u32[]{:S(2)}) collective-permute-start(bf16[512,1280]{1,0:T(8,128)(2,1)} %get-tuple-element.439), channel_id=1, source_target_pairs={{0,4},{4,0},{1,5},{5,1},{2,6},{6,2},{3,7},{7,3},{8,12},{12,8},{9,1... | collective-permute-start | bytes 3932168 | tf_op jit(solution)/shard_map/ppermute | solution.py:693
  825.5 60.1 %reduce-scatter.9.cloned.1.call-start = ((), (), s32[]{:S(2)}) async-start(), calls=%async_computation.16 | async-start | bytes 1638400 | tf_op jit(solution)/shard_map/reduce_scatter | solution.py:619
  (107 other events, 1568.3 us)
Sparse Core Ops, SparseCore 0:
  10.2 35.3 all-gather.8
  47.1 26.9 all-gather.10
  76.3 32.1 all-gather.14
  110.5 31.6 all-gather.16
  144.2 31.6 all-gather.18
  177.9 36.0 all-gather.12
  286.0 37.4 all-gather.20
  339.3 37.5 all-gather.22
  537.3 30.7 reduce-scatter.12
  626.6 35.6 reduce-scatter.14
  664.6 30.1 reduce-scatter.16
  697.0 34.0 reduce-scatter.18
  733.4 30.1 reduce-scatter.20
  765.8 34.0 reduce-scatter.22
  825.6 27.8 reduce-scatter.10
  855.7 29.7 reduce-scatter.8

commit v4 on v1

v4 whole, which is shorter than its diff:
```python
import functools

import jax
import jax.numpy as jnp
from jax import lax
from jax.experimental import pallas as pl
from jax.experimental.pallas import tpu as pltpu
from jax.sharding import Mesh, PartitionSpec as P

HEAD_DIM = 64
SWAP = ((0, 1), (1, 0))
QUERIES = 256
CHUNKS = 4
BLOCK = 256
ROW_STEPS = 3
COST = 10**11
VMEM = 48 * 2**20
epsilon = 1e-05
rope_base = 10000.0
bf16 = jnp.bfloat16
f32 = jnp.float32


def dot_plain(left, right):
    return jnp.dot(left, right, preferred_element_type=f32)


def dot_trans(left, right):
    return lax.dot_general(left, right, (((1,), (1,)), ((), ())), preferred_element_type=f32)


def dot_inner(left, right):
    return lax.dot_general(left, right, (((0,), (0,)), ((), ())), preferred_element_type=f32)


def rotary_tables(segment_row):
    length = segment_row.shape[0]
    before = jnp.sum((segment_row[None, :] < segment_row[:, None]).astype(jnp.int32), axis=1)
    places = (jnp.arange(length, dtype=jnp.int32) - before).astype(f32)
    half_dim = HEAD_DIM // 2
    frequency = rope_base ** (-2.0 * jnp.arange(half_dim).astype(f32) / HEAD_DIM)
    angles = places[:, None] * frequency[None, :]
    cosine, sine = jnp.cos(angles), jnp.sin(angles)
    return (jnp.concatenate([cosine] * 4, axis=1), jnp.concatenate([-sine, sine] * 2, axis=1))


def first_blocks(segment_row):
    starts, ends = segment_row[::QUERIES], segment_row[QUERIES - 1 :: QUERIES]
    return jnp.sum((ends[None, :] < starts[:, None]).astype(jnp.int32), axis=1)


def lanes_of(shape):
    return lax.broadcasted_iota(jnp.int32, shape, len(shape) - 1)


def turn(block, cosine, sine):
    low_half = lanes_of(block.shape) % HEAD_DIM < HEAD_DIM // 2
    other = jnp.where(low_half, pltpu.roll(block, 96, 1), pltpu.roll(block, 32, 1))
    return block * cosine + other * sine


def widen(pair_ref, wide_ref, group):
    pair = pair_ref[...]
    keep = (lanes_of(pair.shape) < HEAD_DIM) == (group == 0)
    half = jnp.where(keep, pair, pltpu.roll(pair.astype(f32), HEAD_DIM, 1).astype(bf16))
    wide_ref[:, :128] = half
    wide_ref[:, 128:] = half


def seen_bias(col_ref, row_ref, start, keys, step):
    queries = col_ref.shape[0]
    same = col_ref[...] == row_ref[:, pl.ds(start, keys)]
    q_at = lax.broadcasted_iota(jnp.int32, (queries, keys), 0) + step * queries
    k_at = lax.broadcasted_iota(jnp.int32, (queries, keys), 1) + start
    return jnp.where(same & (q_at >= k_at), 0.0, -1e30).astype(f32)


def forward_kernel(scale, low_ref, q_ref, k_ref, v_ref, col_ref, row_ref, o_ref, lse_ref, kw_ref, vw_ref):
    group, step = pl.program_id(0), pl.program_id(1)
    queries = q_ref.shape[0]

    @pl.when(step == 0)
    def _():
        widen(k_ref, kw_ref, group)
        widen(v_ref, vw_ref, group)

    def run(blocks):
        keys = blocks * queries
        start = pl.multiple_of(low_ref[step] * queries, queries)
        bias = seen_bias(col_ref, row_ref, start, keys, step)
        key = kw_ref[pl.ds(start, keys), :]
        value = vw_ref[pl.ds(start, keys), :]
        head_of = lanes_of((queries, 256)) // HEAD_DIM
        lse = jnp.zeros((queries, 128), f32)
        for quad in range(q_ref.shape[1] // 256):
            wide = q_ref[:, quad * 256 : quad * 256 + 256]
            out = jnp.zeros((queries, 256), f32)
            for j in range(4):
                one = jnp.where(head_of == j, wide, jnp.zeros_like(wide))
                scores = dot_trans(one, key) * scale + bias
                top = jnp.max(scores, axis=1, keepdims=True)
                powers = jnp.exp(scores - top)
                sums = jnp.sum(powers, axis=1, keepdims=True)
                prob = (powers * (1.0 / sums)).astype(bf16)
                out = jnp.where(head_of == j, dot_plain(prob, value), out)
                lse = jnp.where(lanes_of(lse.shape) == quad * 4 + j, top + jnp.log(sums), lse)
            o_ref[:, quad * 256 : quad * 256 + 256] = out.astype(bf16)
        lse_ref[...] = lse

    for blocks in range(1, row_ref.shape[1] // queries + 1):
        pl.when(step + 1 - low_ref[step] == blocks)(functools.partial(run, blocks))


def backward_kernel(
    scale, low_ref, q_ref, k_ref, v_ref, g_ref, lse_ref, col_ref, row_ref, cos_ref, sin_ref, kcos_ref, ksin_ref,
    dq_ref, dk_ref, dv_ref, kw_ref, vw_ref, dkw_ref, dvw_ref,
):
    group, step = pl.program_id(0), pl.program_id(1)
    queries = q_ref.shape[0]

    @pl.when(step == 0)
    def _():
        widen(k_ref, kw_ref, group)
        widen(v_ref, vw_ref, group)
        dkw_ref[...] = jnp.zeros_like(dkw_ref)
        dvw_ref[...] = jnp.zeros_like(dvw_ref)

    def run(blocks):
        keys = blocks * queries
        start = pl.multiple_of(low_ref[step] * queries, queries)
        bias = seen_bias(col_ref, row_ref, start, keys, step)
        key = kw_ref[pl.ds(start, keys), :]
        value = vw_ref[pl.ds(start, keys), :]
        head_of = lanes_of((queries, 256)) // HEAD_DIM
        cosine, sine = cos_ref[...], sin_ref[...]
        for quad in range(q_ref.shape[1] // 256):
            wide = q_ref[:, quad * 256 : quad * 256 + 256]
            grads = g_ref[:, quad * 256 : quad * 256 + 256]
            out = jnp.zeros((queries, 256), f32)
            for j in range(4):
                at = quad * 4 + j
                one = jnp.where(head_of == j, wide, jnp.zeros_like(wide))
                grad = jnp.where(head_of == j, grads, jnp.zeros_like(grads))
                prob = jnp.exp(dot_trans(one, key) * scale + bias - lse_ref[:, at : at + 1])
                prob_grad = dot_trans(grad, value)
                centre = jnp.sum(prob * prob_grad, axis=1, keepdims=True)
                score_grad = (prob * (prob_grad - centre) * scale).astype(bf16)
                dvw_ref[pl.ds(start, keys), :] += dot_inner(prob.astype(bf16), grad)
                dkw_ref[pl.ds(start, keys), :] += dot_inner(score_grad, one)
                out = jnp.where(head_of == j, dot_plain(score_grad, key), out)
            for half in range(2):
                piece = turn(out[:, half * 128 : half * 128 + 128], cosine, -sine)
                dq_ref[:, quad * 256 + half * 128 : quad * 256 + half * 128 + 128] = piece.astype(bf16)

    for blocks in range(1, row_ref.shape[1] // queries + 1):
        pl.when(step + 1 - low_ref[step] == blocks)(functools.partial(run, blocks))

    @pl.when(step == pl.num_programs(1) - 1)
    def _():
        mine = (lanes_of(dk_ref.shape) < HEAD_DIM) == (group == 0)

        def fold(ref):
            pair = ref[:, :128] + ref[:, 128:]
            return pair + pltpu.roll(pair, HEAD_DIM, 1)

        dk = turn(fold(dkw_ref), kcos_ref[...], -ksin_ref[...]).astype(bf16)
        dk_ref[...] = jnp.where(mine, dk, dk_ref[...])
        dv_ref[...] = jnp.where(mine, fold(dvw_ref).astype(bf16), dv_ref[...])


def launch(kernel, scalars, operands, deps, grid, in_specs, out_specs, out_shape, scratch=(), aliases=()):
    count = len(scalars) + len(operands)

    def body(*refs):
        kernel(*refs[:count], *refs[count + len(deps) :])

    return pl.pallas_call(
        body,
        grid_spec=pltpu.PrefetchScalarGridSpec(
            num_scalar_prefetch=len(scalars),
            grid=grid,
            in_specs=[*in_specs, *([pl.BlockSpec(memory_space=pl.ANY)] * len(deps))],
            out_specs=out_specs,
            scratch_shapes=scratch,
        ),
        out_shape=out_shape,
        compiler_params=pltpu.CompilerParams(vmem_limit_bytes=VMEM),
        cost_estimate=pl.CostEstimate(flops=COST, bytes_accessed=1024, transcendentals=0),
        input_output_aliases=dict(aliases),
    )(*scalars, *operands, *deps)


def whole_block(array):
    return pl.BlockSpec(array.shape, lambda *at: (0,) * array.ndim)


def weight_columns(weight, column):
    both, across, across_core = weight
    depth = across.shape[0]
    specs = [
        pl.BlockSpec((depth, BLOCK), lambda j, s: (s[1], column(j))),
        pl.BlockSpec((depth, BLOCK), lambda j, s: (0, column(j))),
        pl.BlockSpec((depth, BLOCK), lambda j, s: (1 - s[1], column(j))),
        pl.BlockSpec((depth, BLOCK), lambda j, s: (0, column(j))),
    ]
    return specs, [both, across, both, across_core]


def weight_rows(weight, block, units, at):
    both, across, across_core = weight
    per = across.shape[0] // block

    def spec(quarter):
        def index(j, s):
            row = jnp.clip(j - quarter * per, 0, per - 1)
            if quarter % 2 == 0:
                row = row + per * (s[1] if quarter == 0 else 1 - s[1])
            return row, at

        return pl.BlockSpec((block, units), index)

    return [spec(quarter) for quarter in range(4)], [both, across, both, across_core]


def stack_kernel(*refs):
    first = 0
    for ref in refs[:-1]:
        refs[-1][:, first : first + ref.shape[1]] = ref[...]
        first += ref.shape[1]


def stack(parts, deps):
    shape = (parts[0].shape[0], sum(p.shape[1] for p in parts))
    return launch(
        stack_kernel,
        [],
        parts,
        deps,
        (1,),
        [whole_block(p) for p in parts],
        pl.BlockSpec(shape, lambda j: (0, 0)),
        jax.ShapeDtypeStruct(shape, bf16),
    )


def own_kernel(spot_ref, both_ref, out_ref):
    out_ref[...] = both_ref[...]


def own_rows(spot, both, deps):
    rows, width = both.shape
    steps = 4
    block = rows // 2 // steps
    return launch(
        own_kernel,
        [spot],
        [both],
        deps,
        (steps,),
        [pl.BlockSpec((block, width), lambda j, s: (s[1] * steps + j, 0))],
        pl.BlockSpec((block, width), lambda j, s: (j, 0)),
        jax.ShapeDtypeStruct((rows // 2, width), bf16),
    )


def gate_kernel(in_ref, out_ref):
    pass


def gate(array, deps):
    anywhere = pl.BlockSpec(memory_space=pl.ANY)
    return launch(
        gate_kernel,
        [],
        [array],
        deps,
        (1,),
        [anywhere],
        anywhere,
        jax.ShapeDtypeStruct(array.shape, array.dtype),
        aliases=((0, 0),),
    )


def product(act_ref, parts):
    depth = parts[0].shape[0]
    return sum(
        dot_plain(act_ref[:, i * depth : i * depth + depth], part[...]) for i, part in enumerate(parts)
    )


def feed_kernel(spot_ref, x_ref, g_ref, *refs):
    pieces, (h_ref, gg_ref, ug_ref) = refs[:12], refs[12:]
    gate = product(x_ref, pieces[:4])
    up = product(x_ref, pieces[4:8])
    sigmoid = jax.nn.sigmoid(gate)
    silu = gate * sigmoid
    h_ref[...] = (silu * up).astype(bf16)
    grad = product(g_ref, pieces[8:])
    gg_ref[...] = (grad * up * (sigmoid * (1.0 + gate * (1.0 - sigmoid)))).astype(bf16)
    ug_ref[...] = (grad * silu).astype(bf16)


def feed(spot, normed, grads, weight, deps):
    rows, width = normed.shape
    units = weight[0].shape[1] // 3
    blocks = units // BLOCK
    specs, operands = [whole_block(normed), whole_block(grads)], [normed, grads]
    for at in range(3):
        more = weight_columns(weight, lambda j, at=at: j + at * blocks)
        specs += more[0]
        operands += more[1]
    return launch(
        feed_kernel,
        [spot],
        operands,
        deps,
        (blocks,),
        specs,
        [pl.BlockSpec((rows, BLOCK), lambda j, s: (0, j))] * 3,
        [jax.ShapeDtypeStruct((rows, units), bf16)] * 3,
    )


def project_kernel(rotated, spot_ref, own_ref, other_ref, *refs):
    parts, out_ref = refs[:4], refs[-1]
    rows = own_ref.shape[0]
    for act_ref, place in ((own_ref, spot_ref[0]), (other_ref, 1 - spot_ref[0])):
        at = pl.ds(pl.multiple_of(place * rows, rows), rows)
        total = product(act_ref, parts)
        if rotated is None:
            out_ref[at, :] = total.astype(bf16)
        else:
            cosine, sine = refs[4][at, :], refs[5][at, :]
            for half in range(2):
                piece = total[:, half * 128 : half * 128 + 128]
                keep = 2 * pl.program_id(0) + half >= rotated
                piece = jnp.where(keep, piece, turn(piece, cosine, sine))
                out_ref[at, half * 128 : half * 128 + 128] = piece.astype(bf16)


def project(spot, own, other, weight, deps, tables=(), rotated=None):
    rows, width = own.shape
    units = weight[0].shape[1]
    specs, operands = weight_columns(weight, lambda j: j)
    return launch(
        functools.partial(project_kernel, rotated),
        [spot],
        [own, other, *operands, *tables],
        deps,
        (units // BLOCK,),
        [whole_block(own), whole_block(other), *specs, *(whole_block(t) for t in tables)],
        pl.BlockSpec((2 * rows, BLOCK), lambda j, s: (0, j)),
        jax.ShapeDtypeStruct((2 * rows, units), bf16),
    )


def back_kernel(count, started, placed, spot_ref, *refs):
    step = pl.program_id(0)
    acts = refs[:count]
    weights = refs[count : 5 * count]
    starts = refs[5 * count : 5 * count + 2] if started else None
    mine_ref, theirs_ref = refs[-2:]
    rows = mine_ref.shape[0]

    def run(part):
        total = sum(dot_trans(a[...], weights[4 * i + part][...]) for i, a in enumerate(acts))
        mine, theirs = total[:rows], total[rows:]
        if placed:
            first = spot_ref[0] == 0
            mine, theirs = jnp.where(first, mine, theirs), jnp.where(first, theirs, mine)
        if started:
            mine = mine + starts[0][...].astype(f32)
            theirs = theirs + starts[1][...].astype(f32)
        mine_ref[...] = mine.astype(mine_ref.dtype)
        theirs_ref[...] = theirs.astype(theirs_ref.dtype)

    for part in range(4):
        pl.when(step // (pl.num_programs(0) // 4) == part)(functools.partial(run, part))


def back(spot, acts, weights, deps, placed=False, starts=(), kinds=(f32, bf16)):
    rows = acts[0].shape[0]
    depth = weights[0][0][1].shape[0]
    width = 4 * depth
    block = min(BLOCK, depth)
    half = pl.BlockSpec((rows // 2, block), lambda j, s: (0, j))
    specs, operands = [whole_block(a) for a in acts], list(acts)
    for act, (weight, at) in zip(acts, weights):
        more = weight_rows(weight, block, act.shape[1], at)
        specs += more[0]
        operands += more[1]
    return launch(
        functools.partial(back_kernel, len(acts), len(starts) > 0, placed),
        [spot],
        [*operands, *starts],
        deps,
        (width // block,),
        [*specs, *([half] * len(starts))],
        [half, half],
        [jax.ShapeDtypeStruct((rows // 2, width), kind) for kind in kinds],
    )


def grad_kernel(which, added, *refs):
    step, steps = pl.program_id(0), pl.num_programs(0)
    acts = refs[: max(which) + 1]
    count = len(which)
    grads = refs[len(acts) : len(acts) + count]
    first = 0
    for i in range(count):
        at = slice(first, first + grads[i].shape[1])
        first = at.stop
        total = dot_inner(acts[which[i]][...], grads[i][...])
        if not added:
            refs[-1][:, at] = total.astype(bf16)
            continue
        total = (total + refs[-3][:, at].astype(f32)).astype(bf16)

        @pl.when(step < steps // 2)
        def _():
            refs[-2][:, at] = total

        @pl.when(step >= steps // 2)
        def _():
            refs[-1][:, at] = total


def grad(acts, which, grads, deps, added=None):
    tokens, width = acts[0].shape
    block = min(BLOCK, width // 4)
    steps = width // 2 // block
    half = steps // 2
    units = sum(g.shape[1] for g in grads)
    if added is None:
        row = lambda j: j + steps
        outs = pl.BlockSpec((block, units), lambda j: (j, 0))
        shapes = jax.ShapeDtypeStruct((width // 2, units), bf16)
    else:
        row = lambda j: (j + half) % steps
        outs = [
            pl.BlockSpec((block, units), lambda j: (jnp.minimum(j, half - 1), 0)),
            pl.BlockSpec((block, units), lambda j: (jnp.maximum(j - half, 0), 0)),
        ]
        shapes = [jax.ShapeDtypeStruct((width // 4, units), bf16)] * 2
    specs = [pl.BlockSpec((tokens, block), lambda j: (0, row(j))) for _ in acts]
    specs += [whole_block(g) for g in grads]
    operands = [*acts, *grads]
    if added is not None:
        specs.append(pl.BlockSpec((block, units), lambda j: (row(j), 0)))
        operands.append(added)
    return launch(
        functools.partial(grad_kernel, which, added is not None),
        [],
        operands,
        deps,
        (steps,),
        specs,
        outs,
        shapes,
    )


def attention_specs(length, queries, wide):
    pair = lambda first: pl.BlockSpec((length, 128), lambda g, i, low: (0, first))
    col = pl.BlockSpec((queries, 1), lambda g, i, low: (i, 0))
    row = pl.BlockSpec((1, length), lambda g, i, low: (0, 0))
    return pl.BlockSpec((queries, wide), lambda g, i, low: (i, g)), pair, col, row


def attend(rotated, query_width, first_seen, segment_row, scale, deps):
    length = rotated.shape[0]
    queries = length // first_seen.shape[0]
    groups = 2
    heads, pair, col, row = attention_specs(length, queries, query_width // groups)
    first = query_width // 128
    return launch(
        functools.partial(forward_kernel, scale),
        [first_seen],
        [rotated, rotated, rotated, segment_row.reshape(length, 1), segment_row.reshape(1, length)],
        deps,
        (groups, length // queries),
        [heads, pair(first), pair(first + 1), col, row],
        [heads, pl.BlockSpec((queries, 128), lambda g, i, low: (i, g))],
        [
            jax.ShapeDtypeStruct((length, query_width), bf16),
            jax.ShapeDtypeStruct((length, groups * 128), f32),
        ],
        [pltpu.VMEM((length, 256), bf16)] * 2,
    )


def attend_back(rotated, grads, lse, query_width, first_seen, segment_row, cosine, sine, scale, deps):
    length = rotated.shape[0]
    queries = length // first_seen.shape[0]
    groups = 2
    heads, pair, col, row = attention_specs(length, queries, query_width // groups)
    first = query_width // 128
    table = pl.BlockSpec((queries, 128), lambda g, i, low: (i, 0))
    return launch(
        functools.partial(backward_kernel, scale),
        [first_seen],
        [
            rotated, rotated, rotated, grads, lse, segment_row.reshape(length, 1),
            segment_row.reshape(1, length), cosine, sine, cosine, sine,
        ],
        deps,
        (groups, length // queries),
        [
            heads, pair(first), pair(first + 1), heads,
            pl.BlockSpec((queries, 128), lambda g, i, low: (i, g)), col, row, table, table, pair(0), pair(0),
        ],
        [heads, pair(0), pair(0)],
        [
            jax.ShapeDtypeStruct((length, query_width), bf16),
            jax.ShapeDtypeStruct((length, 128), bf16),
            jax.ShapeDtypeStruct((length, 128), bf16),
        ],
        [pltpu.VMEM((length, 256), bf16)] * 2 + [pltpu.VMEM((length, 256), f32)] * 2,
    )


def join_kernel(spot_ref, own_ref, other_ref, out_ref):
    rows = own_ref.shape[0]
    for ref, place in ((own_ref, spot_ref[0]), (other_ref, 1 - spot_ref[0])):
        out_ref[pl.ds(pl.multiple_of(place * rows, rows), rows), :] = ref[...]


def join(spot, own, other, deps):
    rows, width = own.shape
    block = width // 4
    half = pl.BlockSpec((rows, block), lambda j, s: (0, j))
    return launch(
        join_kernel,
        [spot],
        [own, other],
        deps,
        (4,),
        [half, half],
        pl.BlockSpec((2 * rows, block), lambda j, s: (0, j)),
        jax.ShapeDtypeStruct((2 * rows, width), bf16),
    )


def add_kernel(a_ref, b_ref, out_ref):
    out_ref[...] = (a_ref[...].astype(f32) + b_ref[...].astype(f32)).astype(bf16)


def add(a, b, deps):
    rows, width = a.shape
    block = pl.BlockSpec((rows // 4, width), lambda j: (j, 0))
    return launch(
        add_kernel, [], [a, b], deps, (4,), [block, block], block, jax.ShapeDtypeStruct(a.shape, bf16)
    )


def natural_block(spot_ref, outer, core, x, z):
    x = 1 - spot_ref[2] if x else spot_ref[2]
    core = 1 - spot_ref[1] if core else spot_ref[1]
    return (z * 2 + x) * 2 + core


def reorder(spot_ref, outer, width):
    size = width // (4 * outer)
    for core in range(2):
        for x in range(2):
            for z in range(outer):
                at = ((core * 2 + x) * outer + z) * size
                there = natural_block(spot_ref, outer, core, x, z) * size
                yield slice(at, at + size), pl.ds(pl.multiple_of(there, size), size)


def inverse_rms(activity):
    return lax.rsqrt(jnp.mean(activity * activity, axis=-1, keepdims=True) + epsilon)


def norm_back(activity, inverse, gain_vec, incoming):
    scaled = incoming * gain_vec
    return inverse * scaled - activity * (inverse * inverse * inverse) * jnp.mean(
        scaled * activity, axis=-1, keepdims=True
    )


def enter_kernel(outer, spot_ref, tokens_ref, gain_ref, out_ref, normed_ref):
    if outer:
        for here, there in reorder(spot_ref, outer, tokens_ref.shape[1]):
            out_ref[:, here] = tokens_ref[:, there]
    else:
        out_ref[...] = tokens_ref[...]
    inputs = out_ref[...].astype(f32)
    normed_ref[...] = (inputs * inverse_rms(inputs) * gain_ref[...]).astype(bf16)


def turn_kernel(outer, spot_ref, array_ref, out_ref):
    for here, there in reorder(spot_ref, outer, array_ref.shape[1]):
        out_ref[:, here] = array_ref[:, there]


def rows_spec(rows, width):
    return pl.BlockSpec((rows // ROW_STEPS, width), lambda j, *s: (j, 0))


def enter(spot, outer, tokens, gain, deps):
    spec = rows_spec(*tokens.shape)
    return launch(
        functools.partial(enter_kernel, outer),
        [spot],
        [tokens, gain],
        deps,
        (ROW_STEPS,),
        [spec, whole_block(gain)],
        [spec, spec],
        [jax.ShapeDtypeStruct(tokens.shape, bf16)] * 2,
    )


def to_order(spot, outer, array, deps):
    spec = rows_spec(*array.shape)
    return launch(
        functools.partial(turn_kernel, outer),
        [spot],
        [array],
        deps,
        (ROW_STEPS,),
        [spec],
        spec,
        jax.ShapeDtypeStruct(array.shape, bf16),
    )


def middle_kernel(tokens_ref, own_ref, other_ref, gain_ref, normed_ref, middle_ref):
    middle = tokens_ref[...].astype(f32) + own_ref[...] + other_ref[...].astype(f32)
    middle_ref[...] = middle
    normed_ref[...] = (middle * inverse_rms(middle) * gain_ref[...]).astype(bf16)


def middle_forward(tokens, own, other, gain, deps):
    spec = rows_spec(*tokens.shape)
    return launch(
        middle_kernel,
        [],
        [tokens, own, other, gain],
        deps,
        (ROW_STEPS,),
        [spec, spec, spec, whole_block(gain)],
        [spec, spec],
        [jax.ShapeDtypeStruct(tokens.shape, bf16), jax.ShapeDtypeStruct(tokens.shape, f32)],
    )


def gain_part(part_ref, product):
    @pl.when(pl.program_id(0) == 0)
    def _():
        part_ref[...] = jnp.zeros_like(part_ref)

    part_ref[...] += jnp.sum(product, axis=0, keepdims=True)


def middle_back_kernel(own_ref, other_ref, middle_ref, grad_ref, gain_ref, low_ref, out_ref, part_ref):
    incoming = own_ref[...] + other_ref[...].astype(f32)
    middle = middle_ref[...]
    inverse = inverse_rms(middle)
    out = grad_ref[...].astype(f32) + norm_back(middle, inverse, gain_ref[...], incoming)
    out_ref[...] = out
    low_ref[...] = out.astype(bf16)
    gain_part(part_ref, incoming * middle * inverse)


def middle_backward(own, other, middle, out_grad, gain, deps):
    spec = rows_spec(*own.shape)
    part = jax.ShapeDtypeStruct(gain.shape, f32)
    return launch(
        middle_back_kernel,
        [],
        [own, other, middle, out_grad, gain],
        deps,
        (ROW_STEPS,),
        [spec, spec, spec, spec, whole_block(gain)],
        [spec, spec, whole_block(gain)],
        [jax.ShapeDtypeStruct(own.shape, bf16), jax.ShapeDtypeStruct(own.shape, f32), part],
    )


def leave(outer, spot_ref, out_ref, value):
    value = value.astype(bf16)
    if outer:
        for here, there in reorder(spot_ref, outer, value.shape[1]):
            out_ref[:, there] = value[:, here]
    else:
        out_ref[...] = value


def block_out_kernel(outer, spot_ref, middle_ref, own_ref, other_ref, out_ref):
    leave(outer, spot_ref, out_ref, middle_ref[...] + own_ref[...] + other_ref[...].astype(f32))


def block_result(spot, outer, middle, own, other, deps):
    spec = rows_spec(*own.shape)
    return launch(
        functools.partial(block_out_kernel, outer),
        [spot],
        [middle, own, other],
        deps,
        (ROW_STEPS,),
        [spec, spec, spec],
        spec,
        jax.ShapeDtypeStruct(own.shape, bf16),
    )


def input_back_kernel(outer, spot_ref, own_ref, other_ref, tokens_ref, grad_ref, gain_ref, out_ref, part_ref):
    incoming = own_ref[...] + other_ref[...].astype(f32)
    inputs = tokens_ref[...].astype(f32)
    inverse = inverse_rms(inputs)
    leave(outer, spot_ref, out_ref, grad_ref[...] + norm_back(inputs, inverse, gain_ref[...], incoming))
    gain_part(part_ref, incoming * inputs * inverse)


def input_backward(spot, outer, own, other, tokens, middle_grad, gain, deps):
    spec = rows_spec(*own.shape)
    return launch(
        functools.partial(input_back_kernel, outer),
        [spot],
        [own, other, tokens, middle_grad, gain],
        deps,
        (ROW_STEPS,),
        [spec, spec, spec, spec, whole_block(gain)],
        [spec, whole_block(gain)],
        [jax.ShapeDtypeStruct(own.shape, bf16), jax.ShapeDtypeStruct(gain.shape, f32)],
    )


class Order:
    def __init__(self):
        self.before = []

    def wait(self, *arrays):
        self.before += arrays

    def __call__(self, compute, *operands, **options):
        result = compute(*operands, deps=self.before, **options)
        self.before = [result[0] if isinstance(result, (tuple, list)) else result]
        return result


def chunk_edges(width):
    blocks = width // BLOCK
    return [BLOCK * (-(-blocks * i // CHUNKS)) for i in range(CHUNKS + 1)]


def make_shards(outer):
    def relative(array):
        rows, width = array.shape
        blocks = array.reshape(rows, outer, 2, 2, width // (4 * outer))
        blocks = jnp.where(lax.axis_index("x") == 0, blocks, blocks[:, :, ::-1])
        blocks = jnp.where(lax.axis_index("core") == 0, blocks, blocks[:, :, :, ::-1])
        return blocks.transpose(0, 3, 2, 1, 4).reshape(rows, width)

    def natural(array):
        rows, width = array.shape
        blocks = array.reshape(rows, 2, 2, outer, width // (4 * outer)).transpose(0, 3, 2, 1, 4)
        blocks = jnp.where(lax.axis_index("x") == 0, blocks, blocks[:, :, ::-1])
        blocks = jnp.where(lax.axis_index("core") == 0, blocks, blocks[:, :, :, ::-1])
        return blocks.reshape(rows, width)

    def over_x(array):
        return lax.ppermute(array, "x", SWAP)

    def over_core(array):
        return lax.ppermute(array, "core", SWAP)

    def gather(operand):
        return lax.all_gather(operand, ("core", "z"), axis=0, tiled=True)

    def scatter(operand):
        return lax.psum_scatter(operand, "z", scatter_dimension=0, tiled=True)

    def total(vector):
        for axis in ("core", "x", "tensor"):
            vector = vector + lax.ppermute(vector, axis, SWAP)
        step = 1
        while step < outer:
            vector = vector + lax.ppermute(vector, "z", [(i, i ^ step) for i in range(outer)])
            step *= 2
        return vector

    def swap(own):
        return lax.ppermute(own, "tensor", SWAP)

    def shards(
        tokens,
        segments,
        q_weight,
        k_weight,
        v_weight,
        o_weight,
        attention_gain,
        gate_weight,
        up_weight,
        down_weight,
        feed_gain,
        out_grad,
    ):
        query_width = q_weight.shape[1]
        key_width = k_weight.shape[1]
        score_scale = HEAD_DIM ** (-0.5)
        place, core, cross = (lax.axis_index(axis) for axis in ("tensor", "core", "x"))
        spot = jnp.stack([place, core, cross]).astype(jnp.int32)
        here = jnp.zeros_like(spot)
        edges = chunk_edges(gate_weight.shape[1])
        order = Order()
        along, full = {}, {}

        def spread(name):
            full[name] = over_x(order(lambda deps: own_rows(spot, along[name], deps)))

        def land(name):
            across = order(lambda deps: gate(full[name], deps))
            full[name] = (along[name], across, over_core(across))

        def chunk(i):
            columns = slice(edges[i], edges[i + 1])
            parts = [w[:, columns] for w in (gate_weight, up_weight, down_weight)]
            along[i] = gather(order(lambda deps: stack(parts, deps)))

        tiles = outer if tokens.shape[1] // (4 * outer) % 128 == 0 else 0
        along["o"] = gather(o_weight)
        along["qkv"] = gather(order(lambda deps: stack([q_weight, k_weight, v_weight], deps)))
        for i in range(CHUNKS):
            chunk(i)
        attention_gain = relative(attention_gain[None])
        feed_gain = relative(feed_gain[None])
        if not tiles:
            tokens, out_grad = relative(tokens), relative(out_grad)
        tokens, normed_first = order(lambda deps: enter(spot, tiles, tokens, attention_gain, deps))
        normed_other = swap(normed_first)
        if tiles:
            out_grad = order(lambda deps: to_order(spot, tiles, out_grad, deps))
        grad_other = swap(out_grad)
        segment_row = segments[0]
        cosine, sine = rotary_tables(segment_row)
        first_seen = first_blocks(segment_row)
        spread("o")
        spread("qkv")
        land("o")
        grad_seq = order(lambda deps: join(here, out_grad, grad_other, deps))
        normed_seq = order(lambda deps: join(spot, normed_first, normed_other, deps))
        land("qkv")
        rotated = order(
            lambda deps: project(
                spot, normed_first, normed_other, full["qkv"], deps, (cosine, sine),
                (query_width + key_width) // 128,
            )
        )
        spread(0)
        mixed, log_totals = order(
            lambda deps: attend(rotated, query_width, first_seen, segment_row, score_scale, deps)
        )
        own, sent = order(lambda deps: back(spot, (mixed,), ((full["o"], 0),), deps, True))
        other = swap(sent)
        spread(1)
        land(0)
        normed_second, middle = order(lambda deps: middle_forward(tokens, own, other, feed_gain, deps))
        normed_third = swap(normed_second)
        spread(2)
        normed_feed = order(lambda deps: join(here, normed_second, normed_third, deps))
        land(1)
        hidden, gate_grad, up_grad = {}, {}, {}
        from_core, to_x, from_x, kept, summed = {}, {}, {}, {}, {}

        def run_feed(i):
            hidden[i], gate_grad[i], up_grad[i] = order(
                lambda deps: feed(spot, normed_feed, grad_seq, full[i], deps)
            )

        def core_part(i):
            grads = (gate_grad[i], up_grad[i], hidden[i])
            part = order(lambda deps: grad((normed_feed, grad_seq), (0, 0, 1), grads, deps))
            from_core[i] = over_core(part)

        def x_part(i):
            grads = (gate_grad[i], up_grad[i], hidden[i])
            to_x[i], kept[i] = order(
                lambda deps: grad((normed_feed, grad_seq), (0, 0, 1), grads, deps, from_core[i])
            )

        def send_x(i):
            from_x[i] = over_x(to_x[i])

        def finish(i):
            summed[i] = scatter(order(lambda deps: add(kept[i], from_x[i], deps))).astype(f32)

        def feed_back(chunks, starts, kinds):
            acts = [a[i] for i in chunks for a in (gate_grad, up_grad)]
            weights = [(full[i], at) for i in chunks for at in (0, 1)]
            return order(
                lambda deps: back(spot, acts, weights, deps, starts=starts, kinds=kinds)
            )

        run_feed(0)
        core_part(0)
        run_feed(1)
        spread(3)
        x_part(0)
        kept_along, sent_along = scatter(kept[0]), scatter(to_x[0])
        core_part(1)
        land(2)
        x_part(1)
        send_x(1)
        run_feed(2)
        core_part(2)
        starts = feed_back((0, 1, 2), (), (f32, f32))
        land(3)
        run_feed(3)
        own, sent = feed_back((3,), starts, (f32, bf16))
        other = swap(sent)
        x_part(2)
        send_x(2)
        core_part(3)
        from_along = over_x(sent_along)
        finish(1)
        x_part(3)
        send_x(3)
        attn_out_grad, middle_grad, feed_gain_part = order(
            lambda deps: middle_backward(own, other, middle, out_grad, feed_gain, deps)
        )
        attn_other = swap(attn_out_grad)
        order.wait(from_along)
        block_own, block_sent = order(
            lambda deps: back(
                spot, [hidden[i] for i in range(CHUNKS)], [(full[i], 2) for i in range(CHUNKS)], deps
            )
        )
        block_other = swap(block_sent)
        finish(2)
        attn_grad_seq = order(lambda deps: join(spot, attn_out_grad, attn_other, deps))
        from_core["o"] = over_core(order(lambda deps: grad((attn_grad_seq,), (0,), (mixed,), deps)))
        mixed_grad = order(lambda deps: project(spot, attn_out_grad, attn_other, full["o"], deps))
        to_x["o"], kept["o"] = order(
            lambda deps: grad((attn_grad_seq,), (0,), (mixed,), deps, from_core["o"])
        )
        send_x("o")
        qkv_grad = order(
            lambda deps: attend_back(
                rotated, mixed_grad, log_totals, query_width, first_seen, segment_row, cosine, sine,
                score_scale, deps,
            )
        )
        from_core["qkv"] = over_core(
            order(lambda deps: grad((normed_seq,), (0,) * 3, qkv_grad, deps))
        )
        order.wait(block_other)
        finish(3)
        finish("o")
        to_x["qkv"], kept["qkv"] = order(
            lambda deps: grad((normed_seq,), (0,) * 3, qkv_grad, deps, from_core["qkv"])
        )
        send_x("qkv")
        places = (0, query_width // key_width, query_width // key_width + 1)
        own, sent = order(
            lambda deps: back(spot, qkv_grad, [(full["qkv"], at) for at in places], deps, True)
        )
        other = swap(sent)
        block_out = order(lambda deps: block_result(spot, tiles, middle, block_own, block_other, deps))
        finish("qkv")
        input_grad, attention_gain_part = order(
            lambda deps: input_backward(spot, tiles, own, other, tokens, middle_grad, attention_gain, deps)
        )
        gains = total(natural(jnp.concatenate([attention_gain_part, feed_gain_part], axis=0)))
        if not tiles:
            block_out, input_grad = natural(block_out), natural(input_grad)
        summed[0] = kept_along.astype(f32) + from_along.astype(f32)
        qkv_weight_grad = summed["qkv"]

        def whole(at):
            parts = []
            for i in range(CHUNKS):
                units = edges[i + 1] - edges[i]
                parts.append(summed[i][:, at * units : at * units + units])
            return jnp.concatenate(parts, axis=1)

        return (
            block_out,
            input_grad,
            qkv_weight_grad[:, :query_width],
            qkv_weight_grad[:, query_width : query_width + key_width],
            qkv_weight_grad[:, query_width + key_width :],
            summed["o"],
            gains[0],
            whole(0),
            whole(1),
            whole(2),
            gains[1],
        )

    return shards


def solution(mesh):
    outer = mesh.shape["dp"] // 4
    fine = Mesh(
        mesh.devices.reshape(outer, 2, 2, mesh.shape["tensor"]), ("z", "x", "core", "tensor")
    )
    dp = ("z", "x", "core")
    every = P(dp + ("tensor",), None)
    weight = P(dp, "tensor")
    return jax.shard_map(
        make_shards(outer),
        mesh=fine,
        in_specs=(
            every,
            P(dp, None),
            weight,
            weight,
            weight,
            weight,
            P(),
            weight,
            weight,
            weight,
            P(),
            every,
        ),
        out_specs=(every, every, weight, weight, weight, weight, P(), weight, weight, weight, P()),
        check_vma=False,
    )
```

time: 948 us -> 689 us (0.73)
  Pallas kernels: 54.9 us -> 370 us
  waiting for transfers between devices: 437 us -> 196 us
  matrix products: 225 us -> 0 us
  other arithmetic: 84.9 us -> 9.65 us
  local copies, waits for them, and re-layouts: 86.3 us -> 54.4 us
    pallas_call x3 -> x57, Pallas kernels: 54.9 us -> 370 us  [launch(): pl.pallas_call(body, grid_spec=pltpu.PrefetchScalarGridSpec(num_scalar_pr...]
    dot_general x30 -> x0, matrix products: 225 us -> none  [the longest x10 92.7 us: dot_trans(): lax.dot_general(left, right, (((1,), (1,)), ((), ())), preferred_element_...]
    ppermute x33 -> x32, waiting for transfers between devices: 301 us -> 78.5 us  [the longest x8 41.6 us: swap(): return lax.ppermute(own, 'tensor', SWAP)]
    convert_element_type x13 -> x1, other arithmetic: 40.1 us -> 1.79 us  [finish(): scatter(order(lambda deps: add(kept[i], from_x[i], deps))).astype(f32)]
    all_gather x5 -> x6, waiting for transfers between devices: 126 us -> 91.2 us  [gather(): return lax.all_gather(operand, ('core', 'z'), axis=0, tiled=True)]
    reduce_scatter x5 -> x7, waiting for transfers between devices: 0.01 us -> 18.1 us  [scatter(): return lax.psum_scatter(operand, 'z', scatter_dimension=0, tiled=True)]
    select_n x4 -> x0, other arithmetic: 13.5 us -> none  [both_halves(): jnp.where(lax.axis_index('tensor') == 0, jnp.concatenate([own, other], ax...]
    reduce_sum x2 -> x0, other arithmetic: 9.72 us -> none  [the longest x1 5.09 us: shards(): feed_gain_part = jnp.sum(feed_normed_grad * middle * inverse_second, axis=0)]
  transfers between devices with their start and end apart: 53 -> 50, of which waited for: 20 -> 21; matrix products, arithmetic and copies ran while one was open for 35% -> 3% of each run, Pallas kernels for 6% -> 54%
where the time goes in v4:
time: 689 us; the launch traced here: 681 us
  Pallas kernels  370 us (54%)
  waiting for transfers between devices  196 us (28%)
  local copies, waits for them, and re-layouts  54.4 us (8%)
  starting transfers between devices  35.3 us (5%)
  between operations  15.1 us (2%)
  other arithmetic  9.65 us (1%)
    pallas_call x57, Pallas kernels, launch(): pl.pallas_call(body, grid_spec=pltpu.PrefetchScalarGridSpec(num_scalar_pr...  370 us
    all_gather x6, waiting for transfers between devices, gather(): return lax.all_gather(operand, ('core', 'z'), axis=0, tiled=True)  91.2 us
    ppermute x8, waiting for transfers between devices, swap(): return lax.ppermute(own, 'tensor', SWAP)  41.6 us
    unnamed x198, local copies, waits for them, and re-layouts  41.4 us
    ppermute x12, waiting for transfers between devices, over_x(): return lax.ppermute(array, 'x', SWAP)  27.4 us
    ppermute x12, starting transfers between devices, over_x(): return lax.ppermute(array, 'x', SWAP)  18.3 us
    reduce_scatter x7, waiting for transfers between devices, scatter(): return lax.psum_scatter(operand, 'z', scatter_dimension=0, tiled=True)  18.1 us
  transfers between devices with their start and end apart: 50, of which 21 were waited for; matrix products, arithmetic and copies ran while one was open for 3% of the time, Pallas kernels for 54%

profile of v4, /device:TPU:0, one launch (start us, length us, event | category | flops | bytes accessed | tf_op | source)
XLA Modules:
  0.0 681.0 jit_solution(16825284218578748392)
XLA Ops:
  28.2 13.2 %all-gather.9.cloned.1.call-done.refs_1_.refs_2_.refs_4_.refs_3_.refs_5_ = bf16[1024,1024]{1,0:T(8,128)(2,1)} async-done(((bf16[128,1024]{1,0:T(8,128)(2,1)}), bf16[1024,1024]{1,0:T(8,128)(2,1)}) %all-gather.9.cloned.1.call-update) | async-done | bytes 2097168 | tf_op jit(solution)/shard_map/all_gather | solution.py:773
  45.3 31.7 %all-gather.7.cloned.1.call-done.refs_1_.refs_3_.refs_5_.refs_4_.refs_6_.refs_8_.refs_10_.refs_12_.refs_14_ = bf16[1024,1280]{1,0:T(8,128)(2,1)} async-done(((bf16[128,1280]{1,0:T(8,128)(2,1)}), bf16[1024,1280]{1,0:T(8,128)(2,1)}) %all-gather.7.cloned.1.call-update) | async-done | bytes 2621456 | tf_op jit(solution)/shard_map/all_gather | solution.py:773
  87.3 9.2 %collective-permute-done.refs_2_ = bf16[384,2048]{1,0:T(8,128)(2,1)} collective-permute-done((bf16[384,2048]{1,0:T(8,128)(2,1)}, bf16[384,2048]{1,0:T(8,128)(2,1)}, u32[]{:S(2)}, u32[]{:S(2)}) %collective-permute-start) | collective-permute-done | bytes 1572896 | tf_op jit(solution)/shard_map/ppermute | solution.py:788
  101.3 10.9 %collective-permute-done.1.refs_0_ = bf16[512,1280]{1,0:T(8,128)(2,1)} collective-permute-done((bf16[512,1280]{1,0:T(8,128)(2,1)}, bf16[512,1280]{1,0:T(8,128)(2,1)}, u32[]{:S(2)}, u32[]{:S(2)}) %collective-permute-start.1) | collective-permute-done | bytes 1310752 | tf_op jit(solution)/shard_map/ppermute | solution.py:767
  118.1 10.7 %shard_map.216.refs_2_.refs_1_.refs_3_ = bf16[768,1280]{1,0:T(8,128)(2,1)} custom-call(s32[3]{0:T(128)S(1)} %copy-done.14, bf16[384,2048]{1,0:T(8,128)(2,1)} %get-tuple-element.60.refs_1_, bf16[384,2048]{1,0:T(8,128)(2,1)} %collective-permute-done.refs_2_, ...), custom_call_target="tpu_custom_call" | custom-call | flops 99999997952 | bytes 1024 | tf_op jit(solution)/shard_map/pallas_call | solution.py:177
  138.0 14.7 %shard_map.218 = (bf16[768,1024]{1,0:T(8,128)(2,1)S(1)}, f32[768,256]{1,0:T(8,128)S(1)}) custom-call(s32[3]{0:T(128)S(1)} %convert_reduce_fusion.1.refs_0_, bf16[768,1280]{1,0:T(8,128)(2,1)S(1)} %copy-done.58, bf16[768,1280]{1,0:T(8,128)(2,1)S(1)} %copy-done.58, bf16[768,1280]{1,0:T(8,128)(2,1)S(1)} %copy-done.58, s32[768,1]{1,0:T(8,128)S(1)} %copy.41.refs_4_.refs_6_, ...), custom_call_target="tpu_custom_call" | custom-call | flops 99999997952 | bytes 1024 | tf_op jit(solution)/shard_map/pallas_call | solution.py:177
  152.8 10.2 %shard_map.219 = (f32[384,2048]{1,0:T(8,128)}, bf16[384,2048]{1,0:T(8,128)(2,1)}) custom-call(s32[3]{0:T(128)S(1)} %copy-done.14, bf16[768,1024]{1,0:T(8,128)(2,1)S(1)} %get-tuple-element.61.refs_1_.refs_6_, bf16[1024,1024]{1,0:T(8,128)(2,1)} %all-gather.9.cloned.1.call-done.refs_1_.refs_2_.refs_4_.refs_3_.refs_5_, ...), custom_call_target="tpu_custom_call" | custom-call | flops 99999997952 | bytes 1024 | tf_op jit(solution)/shard_map/pallas_call | solution.py:177
  164.5 18.0 %all-gather.13.cloned.1.call-done.refs_1_.refs_3_.refs_5_.refs_7_.refs_9_.refs_11_.refs_13_.refs_15_.refs_17_.refs_19_.refs_21_ = bf16[1024,2304]{1,0:T(8,128)(2,1)} async-done(((bf16[128,2304]{1,0:T(8,128)(2,1)}), bf16[1024,2304]{1,0:T(8,128)(2,1)}) %all-gather.13.cloned.1.call-update) | async-done | bytes 4718608 | tf_op jit(solution)/shard_map/all_gather | solution.py:773
  190.4 9.3 %collective-permute-done.6.refs_2_ = bf16[384,2048]{1,0:T(8,128)(2,1)} collective-permute-done((bf16[384,2048]{1,0:T(8,128)(2,1)}, bf16[384,2048]{1,0:T(8,128)(2,1)}, u32[]{:S(2)}, u32[]{:S(2)}) %collective-permute-start.6) | collective-permute-done | bytes 1572896 | tf_op jit(solution)/shard_map/ppermute | solution.py:788
  206.3 28.2 %all-gather.15.cloned.1.call-done.refs_1_.refs_3_.refs_5_.refs_7_.refs_9_.refs_11_.refs_13_.refs_23_.refs_25_.refs_27_.refs_29_.refs_15_ = bf16[1024,2304]{1,0:T(8,128)(2,1)} async-done(((bf16[128,2304]{1,0:T(8,128)(2,1)}), bf16[1024,2304]{1,0:T(8,128)(2,1)}) %all-gather.15.cloned.1.call-update) | async-done | bytes 4718608 | tf_op jit(solution)/shard_map/all_gather | solution.py:773
  245.5 13.3 %shard_map.226 = (bf16[768,768]{1,0:T(8,128)(2,1)S(1)}, bf16[768,768]{1,0:T(8,128)(2,1)S(1)}, bf16[768,768]{1,0:T(8,128)(2,1)S(1)}) custom-call(s32[3]{0:T(128)S(1)} %copy-done.14, bf16[768,2048]{1,0:T(8,128)(2,1)} %shard_map.224.refs_1_.refs_0_, bf16[768,2048]{1,0:T(8,128)(2,1)} %shard_map.213.refs_3_.refs_2_.refs_1_, ...), custom_call_target="tpu_custom_call" | custom-call | flops 99999997952 | bytes 1024 | tf_op jit(solution)/shard_map/pallas_call | solution.py:177
  258.8 7.9 %shard_map.227.refs_15_ = bf16[1024,2304]{1,0:T(8,128)(2,1)} custom-call(bf16[768,2048]{1,0:T(8,128)(2,1)} %shard_map.224.refs_1_.refs_0_, bf16[768,2048]{1,0:T(8,128)(2,1)} %shard_map.213.refs_3_.refs_2_.refs_1_, bf16[768,768]{1,0:T(8,128)(2,1)S(1)} %get-tuple-element.67.refs_2_.refs_1_, bf16[768,768]{1,0:T(8,128)(2,1)S(1)} %get-tuple-element.68.refs_3_.refs_2_, ...), custom_call_target="tpu_custom_call" | custom-call | flops 99999997952 | bytes 1024 | tf_op jit(solution)/shard_map/pallas_call | solution.py:177
  267.2 13.1 %shard_map.228 = (bf16[768,768]{1,0:T(8,128)(2,1)S(1)}, bf16[768,768]{1,0:T(8,128)(2,1)S(1)}, bf16[768,768]{1,0:T(8,128)(2,1)S(1)}) custom-call(s32[3]{0:T(128)S(1)} %copy-done.14, bf16[768,2048]{1,0:T(8,128)(2,1)} %shard_map.224.refs_1_.refs_0_, bf16[768,2048]{1,0:T(8,128)(2,1)} %shard_map.213.refs_3_.refs_2_.refs_1_, ...), custom_call_target="tpu_custom_call" | custom-call | flops 99999997952 | bytes 1024 | tf_op jit(solution)/shard_map/pallas_call | solution.py:177
  289.3 10.5 %shard_map.230 = (bf16[512,2304]{1,0:T(8,128)(2,1)}, bf16[512,2304]{1,0:T(8,128)(2,1)}) custom-call(bf16[768,2048]{1,0:T(8,128)(2,1)} %shard_map.224.refs_1_.refs_0_, bf16[768,2048]{1,0:T(8,128)(2,1)} %shard_map.213.refs_3_.refs_2_.refs_1_, bf16[768,768]{1,0:T(8,128)(2,1)S(1)} %copy-done.42, bf16[768,768]{1,0:T(8,128)(2,1)S(1)} %copy-done.45, ...), custom_call_target="tpu_custom_call" | custom-call | flops 99999997952 | bytes 1024 | tf_op jit(solution)/shard_map/pallas_call | solution.py:177
  311.9 7.6 %collective-permute-done.15.refs_5_ = bf16[1024,2304]{1,0:T(8,128)(2,1)} collective-permute-done((bf16[1024,2304]{1,0:T(8,128)(2,1)}, bf16[1024,2304]{1,0:T(8,128)(2,1)}, u32[]{:S(2)}, u32[]{:S(2)}) %collective-permute-start.15) | collective-permute-done | bytes 4718624 | tf_op jit(solution)/shard_map/ppermute | solution.py:770
  320.8 10.9 %shard_map.233 = (bf16[512,2304]{1,0:T(8,128)(2,1)}, bf16[512,2304]{1,0:T(8,128)(2,1)}) custom-call(bf16[768,2048]{1,0:T(8,128)(2,1)} %shard_map.224.refs_1_.refs_0_, bf16[768,2048]{1,0:T(8,128)(2,1)} %shard_map.213.refs_3_.refs_2_.refs_1_, bf16[768,768]{1,0:T(8,128)(2,1)S(1)} %get-tuple-element.70.refs_2_.refs_3_, bf16[768,768]{1,0:T(8,128)(2,1)S(1)} %copy-done.51, ...), custom_call_target="tpu_custom_call" | custom-call | flops 99999997952 | bytes 1024 | tf_op jit(solution)/shard_map/pallas_call | solution.py:177
  331.7 13.0 %shard_map.234 = (bf16[768,768]{1,0:T(8,128)(2,1)S(1)}, bf16[768,768]{1,0:T(8,128)(2,1)S(1)}, bf16[768,768]{1,0:T(8,128)(2,1)S(1)}) custom-call(s32[3]{0:T(128)S(1)} %copy-done.15, bf16[768,2048]{1,0:T(8,128)(2,1)} %shard_map.224.refs_1_.refs_0_, bf16[768,2048]{1,0:T(8,128)(2,1)} %shard_map.213.refs_3_.refs_2_.refs_1_, ...), custom_call_target="tpu_custom_call" | custom-call | flops 99999997952 | bytes 1024 | tf_op jit(solution)/shard_map/pallas_call | solution.py:177
  344.8 7.4 %shard_map.235.refs_31_ = bf16[1024,2304]{1,0:T(8,128)(2,1)} custom-call(bf16[768,2048]{1,0:T(8,128)(2,1)} %shard_map.224.refs_1_.refs_0_, bf16[768,2048]{1,0:T(8,128)(2,1)} %shard_map.213.refs_3_.refs_2_.refs_1_, bf16[768,768]{1,0:T(8,128)(2,1)S(1)} %get-tuple-element.75.refs_2_.refs_5_, bf16[768,768]{1,0:T(8,128)(2,1)S(1)} %get-tuple-element.76.refs_3_.refs_6_, ...), custom_call_target="tpu_custom_call" | custom-call | flops 99999997952 | bytes 1024 | tf_op jit(solution)/shard_map/pallas_call | solution.py:177
  358.2 24.3 %shard_map.236 = (f32[384,2048]{1,0:T(8,128)}, f32[384,2048]{1,0:T(8,128)}) custom-call(s32[3]{0:T(128)S(1)} %copy-done.15, bf16[768,768]{1,0:T(8,128)(2,1)S(1)} %copy-done.43, bf16[768,768]{1,0:T(8,128)(2,1)S(1)} %copy-done.46, bf16[768,768]{1,0:T(8,128)(2,1)S(1)} %copy-done.48, bf16[768,768]{1,0:T(8,128)(2,1)S(1)} %copy-done.52, ...), custom_call_target="tpu_custom_call" | custom-call | flops 99999997952 | bytes 1024 | tf_op jit(solution)/shard_map/pallas_call | solution.py:177
  386.3 11.3 %reduce-scatter.14.cloned.1.call-done = bf16[128,2304]{1,0:T(8,128)(2,1)} async-done(((bf16[512,2304]{1,0:T(8,128)(2,1)}), bf16[128,2304]{1,0:T(8,128)(2,1)}) %reduce-scatter.14.cloned.1.call-update) | async-done | bytes 589840 | tf_op jit(solution)/shard_map/reduce_scatter | solution.py:776
  400.1 10.1 %shard_map.238 = (bf16[768,512]{1,0:T(8,128)(2,1)S(1)}, bf16[768,512]{1,0:T(8,128)(2,1)S(1)}, bf16[768,512]{1,0:T(8,128)(2,1)S(1)}) custom-call(s32[3]{0:T(128)S(1)} %copy-done.15, bf16[768,2048]{1,0:T(8,128)(2,1)} %shard_map.224.refs_1_.refs_0_, bf16[768,2048]{1,0:T(8,128)(2,1)} %shard_map.213.refs_3_.refs_2_.refs_1_, ...), custom_call_target="tpu_custom_call" | custom-call | flops 99999997952 | bytes 1024 | tf_op jit(solution)/shard_map/pallas_call | solution.py:177
  410.2 11.7 %shard_map.239 = (f32[384,2048]{1,0:T(8,128)}, bf16[384,2048]{1,0:T(8,128)(2,1)}) custom-call(s32[3]{0:T(128)S(1)} %copy-done.15, bf16[768,512]{1,0:T(8,128)(2,1)S(1)} %get-tuple-element.79.refs_1_.refs_2_, bf16[768,512]{1,0:T(8,128)(2,1)S(1)} %get-tuple-element.80.refs_2_.refs_3_, ...), custom_call_target="tpu_custom_call" | custom-call | flops 99999997952 | bytes 1024 | tf_op jit(solution)/shard_map/pallas_call | solution.py:177
  423.5 10.4 %shard_map.240 = (bf16[512,2304]{1,0:T(8,128)(2,1)}, bf16[512,2304]{1,0:T(8,128)(2,1)}) custom-call(bf16[768,2048]{1,0:T(8,128)(2,1)} %shard_map.224.refs_1_.refs_0_, bf16[768,2048]{1,0:T(8,128)(2,1)} %shard_map.213.refs_3_.refs_2_.refs_1_, bf16[768,768]{1,0:T(8,128)(2,1)S(1)} %copy-done.55, bf16[768,768]{1,0:T(8,128)(2,1)S(1)} %copy-done.57, ...), custom_call_target="tpu_custom_call" | custom-call | flops 99999997952 | bytes 1024 | tf_op jit(solution)/shard_map/pallas_call | solution.py:177
  448.5 8.0 %shard_map.243 = (bf16[512,1536]{1,0:T(8,128)(2,1)}, bf16[512,1536]{1,0:T(8,128)(2,1)S(1)}) custom-call(bf16[768,2048]{1,0:T(8,128)(2,1)} %shard_map.224.refs_1_.refs_0_, bf16[768,2048]{1,0:T(8,128)(2,1)} %shard_map.213.refs_3_.refs_2_.refs_1_, bf16[768,512]{1,0:T(8,128)(2,1)S(1)} %get-tuple-element.79.refs_1_.refs_2_, bf16[768,512]{1,0:T(8,128)(2,1)S(1)} %copy-done.81, ...), custom_call_target="tpu_custom_call" | custom-call | flops 99999997952 | bytes 1024 | tf_op jit(solution)/shard_map/pallas_call | solution.py:177
  458.3 8.0 %shard_map.244 = (bf16[384,2048]{1,0:T(8,128)(2,1)}, f32[384,2048]{1,0:T(8,128)}, f32[1,2048]{1,0:T(1,128)S(1)}) custom-call(f32[384,2048]{1,0:T(8,128)} %get-tuple-element.82.refs_6_.refs_0_, bf16[384,2048]{1,0:T(8,128)(2,1)} %collective-permute-done.18.refs_1_, f32[384,2048]{1,0:T(8,128)} %get-tuple-element.64.refs_2_.refs_1_, ...), custom_call_target="tpu_custom_call" | custom-call | flops 99999997952 | bytes 1024 | tf_op jit(solution)/shard_map/pallas_call | solution.py:177
  467.8 16.5 %shard_map.245 = (f32[384,2048]{1,0:T(8,128)}, bf16[384,2048]{1,0:T(8,128)(2,1)}) custom-call(s32[3]{0:T(128)S(1)} %copy-done.16, bf16[768,768]{1,0:T(8,128)(2,1)S(1)} %copy-done.67, bf16[768,768]{1,0:T(8,128)(2,1)S(1)} %copy-done.72, bf16[768,768]{1,0:T(8,128)(2,1)S(1)} %copy-done.75, bf16[768,512]{1,0:T(8,128)(2,1)S(1)} %get-tuple-element.78.refs_13_.refs_4_, ...), custom_call_target="tpu_custom_call" | custom-call | flops 99999997952 | bytes 1024 | tf_op jit(solution)/shard_map/pallas_call | solution.py:177
  495.7 8.2 %collective-permute-done.24.refs_2_ = bf16[384,2048]{1,0:T(8,128)(2,1)} collective-permute-done((bf16[384,2048]{1,0:T(8,128)(2,1)}, bf16[384,2048]{1,0:T(8,128)(2,1)}, u32[]{:S(2)}, u32[]{:S(2)}) %collective-permute-start.24) | collective-permute-done | bytes 1572896 | tf_op jit(solution)/shard_map/ppermute | solution.py:788
  529.9 32.1 %shard_map.251 = (bf16[768,1024]{1,0:T(8,128)(2,1)S(1)}, bf16[768,128]{1,0:T(8,128)(2,1)S(1)}, bf16[768,128]{1,0:T(8,128)(2,1)S(1)}) custom-call(s32[3]{0:T(128)S(1)} %copy-done.31, bf16[768,1280]{1,0:T(8,128)(2,1)} %shard_map.216.refs_2_.refs_1_.refs_3_, bf16[768,1280]{1,0:T(8,128)(2,1)} %shard_map.216.refs_2_.refs_1_.refs_3_, ...), custom_call_target="tpu_custom_call" | custom-call | flops 99999997952 | bytes 1024 | tf_op jit(solution)/shard_map/pallas_call | solution.py:177
  576.9 7.8 %shard_map.255 = (bf16[512,1280]{1,0:T(8,128)(2,1)}, bf16[512,1280]{1,0:T(8,128)(2,1)S(1)}) custom-call(bf16[768,2048]{1,0:T(8,128)(2,1)} %shard_map.214.refs_1_.refs_0_, bf16[768,1024]{1,0:T(8,128)(2,1)S(1)} %copy-done.60, bf16[768,128]{1,0:T(8,128)(2,1)S(1)} %copy-done.85, bf16[768,128]{1,0:T(8,128)(2,1)S(1)} %copy-done.87, ...), custom_call_target="tpu_custom_call" | custom-call | flops 99999997952 | bytes 1024 | tf_op jit(solution)/shard_map/pallas_call | solution.py:177
  588.5 11.6 %shard_map.256 = (f32[384,2048]{1,0:T(8,128)}, bf16[384,2048]{1,0:T(8,128)(2,1)}) custom-call(s32[3]{0:T(128)S(1)} %copy-done.16, bf16[768,1024]{1,0:T(8,128)(2,1)} %copy-done.59, bf16[768,128]{1,0:T(8,128)(2,1)S(1)} %copy-done.85, bf16[768,128]{1,0:T(8,128)(2,1)S(1)} %copy-done.87, ...), custom_call_target="tpu_custom_call" | custom-call | flops 99999997952 | bytes 1024 | tf_op jit(solution)/shard_map/pallas_call | solution.py:177
  606.5 11.8 %collective-permute-done.31.refs_1_ = bf16[512,1280]{1,0:T(8,128)(2,1)} collective-permute-done((bf16[512,1280]{1,0:T(8,128)(2,1)}, bf16[512,1280]{1,0:T(8,128)(2,1)}, u32[]{:S(2)}, u32[]{:S(2)}) %collective-permute-start.31) | collective-permute-done | bytes 1310752 | tf_op jit(solution)/shard_map/ppermute | solution.py:767
  623.5 13.6 %collective-permute-done.30.refs_2_ = bf16[384,2048]{1,0:T(8,128)(2,1)} collective-permute-done((bf16[384,2048]{1,0:T(8,128)(2,1)}, bf16[384,2048]{1,0:T(8,128)(2,1)}, u32[]{:S(2)}, u32[]{:S(2)}) %collective-permute-start.30) | collective-permute-done | bytes 1572896 | tf_op jit(solution)/shard_map/ppermute | solution.py:788
  (385 shorter events, 240.5 us)
Async XLA Ops:
  7.9 69.1 %all-gather.7.cloned.1.call-start = ((), (), s32[]{:S(2)}) async-start(), calls=%async_computation.7 | async-start | bytes 2949120 | tf_op jit(solution)/shard_map/all_gather | solution.py:773
  11.2 119.2 %all-gather.11.cloned.1.call-start = ((), (), s32[]{:S(2)}) async-start(), calls=%async_computation.9 | async-start | bytes 5308416 | tf_op jit(solution)/shard_map/all_gather | solution.py:773
  13.5 169.0 %all-gather.13.cloned.1.call-start = ((), (), s32[]{:S(2)}) async-start(), calls=%async_computation.10 | async-start | bytes 5308416 | tf_op jit(solution)/shard_map/all_gather | solution.py:773
  14.5 220.0 %all-gather.15.cloned.1.call-start = ((), (), s32[]{:S(2)}) async-start(), calls=%async_computation.11 | async-start | bytes 5308416 | tf_op jit(solution)/shard_map/all_gather | solution.py:773
  15.4 266.0 %all-gather.17.cloned.1.call-start = ((), (), s32[]{:S(2)}) async-start(), calls=%async_computation.12 | async-start | bytes 3538944 | tf_op jit(solution)/shard_map/all_gather | solution.py:773
  19.0 336.2 %reduce-scatter.8.cloned.1.call-start = ((), (), s32[]{:S(2)}) async-start(), calls=%async_computation.13 | async-start | bytes 2949120 | tf_op jit(solution)/shard_map/reduce_scatter | solution.py:776
  25.1 57.3 %collective-permute-start.2 = (bf16[384,2048]{1,0:T(8,128)(2,1)}, bf16[384,2048]{1,0:T(8,128)(2,1)}, u32[]{:S(2)}, u32[]{:S(2)}) collective-permute-start(bf16[384,2048]{1,0:T(8,128)(2,1)} %shard_map.209.refs_2_.refs_1_.refs_3_), channel_id=1, source_target_pairs={{0,1},{1,0},{2,3},{3,2},{4,5},{5,4},{6,7},{7,6},{8,9},{9,8},{10,11... | collective-permute-start | bytes 4718600 | tf_op jit(solution)/shard_map/ppermute | solution.py:788
  28.2 68.3 %collective-permute-start = (bf16[384,2048]{1,0:T(8,128)(2,1)}, bf16[384,2048]{1,0:T(8,128)(2,1)}, u32[]{:S(2)}, u32[]{:S(2)}) collective-permute-start(bf16[384,2048]{1,0:T(8,128)(2,1)} %get-tuple-element.60.refs_1_), channel_id=1, source_target_pairs={{0,1},{1,0},{2,3},{3,2},{4,5},{5,4},{6,7},{7,6},{8,9},{9,8},{10,11... | collective-permute-start | bytes 4718600 | tf_op jit(solution)/shard_map/ppermute | solution.py:788
  43.7 38.7 %collective-permute-start.3 = (bf16[512,1024]{1,0:T(8,128)(2,1)S(1)}, bf16[512,1024]{1,0:T(8,128)(2,1)}, u32[]{:S(2)}, u32[]{:S(2)}) collective-permute-start(bf16[512,1024]{1,0:T(8,128)(2,1)S(1)} %shard_map.210.refs_2_), channel_id=1, source_target_pairs={{0,4},{4,0},{1,5},{5,1},{2,6},{6,2},{3,7},{7,3},{8,12},{12,8},{9,1... | collective-permute-start | bytes 3145736 | tf_op jit(solution)/shard_map/ppermute | solution.py:767
  136.5 53.9 %collective-permute-start.7 = (bf16[512,2304]{1,0:T(8,128)(2,1)}, bf16[512,2304]{1,0:T(8,128)(2,1)}, u32[]{:S(2)}, u32[]{:S(2)}) collective-permute-start(bf16[512,2304]{1,0:T(8,128)(2,1)} %shard_map.217.refs_6_), channel_id=1, source_target_pairs={{0,4},{4,0},{1,5},{5,1},{2,6},{6,2},{3,7},{7,3},{8,12},{12,8},{9,1... | collective-permute-start | bytes 7077896 | tf_op jit(solution)/shard_map/ppermute | solution.py:767
  163.0 36.8 %collective-permute-start.6 = (bf16[384,2048]{1,0:T(8,128)(2,1)}, bf16[384,2048]{1,0:T(8,128)(2,1)}, u32[]{:S(2)}, u32[]{:S(2)}) collective-permute-start(bf16[384,2048]{1,0:T(8,128)(2,1)} %get-tuple-element.63), channel_id=1, source_target_pairs={{0,1},{1,0},{2,3},{3,2},{4,5},{5,4},{6,7},{7,6},{8,9},{9,8},{10,11... | collective-permute-start | bytes 4718600 | tf_op jit(solution)/shard_map/ppermute | solution.py:788
  188.8 54.6 %collective-permute-start.10 = (bf16[512,2304]{1,0:T(8,128)(2,1)}, bf16[512,2304]{1,0:T(8,128)(2,1)}, u32[]{:S(2)}, u32[]{:S(2)}) collective-permute-start(bf16[512,2304]{1,0:T(8,128)(2,1)} %shard_map.220.refs_1_), channel_id=1, source_target_pairs={{0,4},{4,0},{1,5},{5,1},{2,6},{6,2},{3,7},{7,3},{8,12},{12,8},{9,1... | collective-permute-start | bytes 7077896 | tf_op jit(solution)/shard_map/ppermute | solution.py:767
  190.4 55.1 %collective-permute-start.9 = (bf16[512,2304]{1,0:T(8,128)(2,1)}, bf16[512,2304]{1,0:T(8,128)(2,1)}, u32[]{:S(2)}, u32[]{:S(2)}) collective-permute-start(bf16[512,2304]{1,0:T(8,128)(2,1)} %shard_map.221.refs_4_.refs_8_.refs_12_.refs_6_), channel_id=1, source_target_pairs={{0,2},{2,0},{1,3},{3,1},{4,6},{6,4},{5,7},{7,5},{8,10},{10,8},{9,1... | collective-permute-start | bytes 7077896 | tf_op jit(solution)/shard_map/ppermute | solution.py:770
  204.9 35.6 %collective-permute-start.8 = (bf16[384,2048]{1,0:T(8,128)(2,1)S(1)}, bf16[384,2048]{1,0:T(8,128)(2,1)S(1)}, u32[]{:S(2)}, u32[]{:S(2)}) collective-permute-start(bf16[384,2048]{1,0:T(8,128)(2,1)S(1)} %get-tuple-element.65.refs_2_.refs_1_), channel_id=1, source_target_pairs={{0,1},{1,0},{2,3},{3,2},{4,5},{5,4},{6,7},{7,6},{8,9},{9,8},{10,11... | collective-permute-start | bytes 4718600 | tf_op jit(solution)/shard_map/ppermute | solution.py:788
  238.9 72.4 %collective-permute-start.12 = (bf16[512,2304]{1,0:T(8,128)(2,1)}, bf16[512,2304]{1,0:T(8,128)(2,1)}, u32[]{:S(2)}, u32[]{:S(2)}) collective-permute-start(bf16[512,2304]{1,0:T(8,128)(2,1)} %shard_map.223.refs_3_), channel_id=1, source_target_pairs={{0,4},{4,0},{1,5},{5,1},{2,6},{6,2},{3,7},{7,3},{8,12},{12,8},{9,1... | collective-permute-start | bytes 7077896 | tf_op jit(solution)/shard_map/ppermute | solution.py:767
  287.6 94.9 %collective-permute-start.16 = (bf16[512,1536]{1,0:T(8,128)(2,1)}, bf16[512,1536]{1,0:T(8,128)(2,1)}, u32[]{:S(2)}, u32[]{:S(2)}) collective-permute-start(bf16[512,1536]{1,0:T(8,128)(2,1)} %shard_map.229.refs_6_), channel_id=1, source_target_pairs={{0,4},{4,0},{1,5},{5,1},{2,6},{6,2},{3,7},{7,3},{8,12},{12,8},{9,1... | collective-permute-start | bytes 4718600 | tf_op jit(solution)/shard_map/ppermute | solution.py:767
  299.9 97.8 %reduce-scatter.14.cloned.1.call-start = ((), (), s32[]{:S(2)}) async-start(), calls=%async_computation.16 | async-start | bytes 2949120 | tf_op jit(solution)/shard_map/reduce_scatter | solution.py:776
  311.9 181.7 %reduce-scatter.16.cloned.1.call-start = ((), (), s32[]{:S(2)}) async-start(), calls=%async_computation.17 | async-start | bytes 2949120 | tf_op jit(solution)/shard_map/reduce_scatter | solution.py:776
  355.2 42.4 %collective-permute-start.22 = (bf16[128,2304]{1,0:T(8,128)(2,1)}, bf16[128,2304]{1,0:T(8,128)(2,1)}, u32[]{:S(2)}, u32[]{:S(2)}) collective-permute-start(bf16[128,2304]{1,0:T(8,128)(2,1)} %reduce-scatter.8.cloned.1.call-done), channel_id=1, source_target_pairs={{0,4},{4,0},{1,5},{5,1},{2,6},{6,2},{3,7},{7,3},{8,12},{12,8},{9,1... | collective-permute-start | bytes 1769480 | tf_op jit(solution)/shard_map/ppermute | solution.py:767
  384.5 56.9 %collective-permute-start.21 = (bf16[512,2304]{1,0:T(8,128)(2,1)}, bf16[512,2304]{1,0:T(8,128)(2,1)}, u32[]{:S(2)}, u32[]{:S(2)}) collective-permute-start(bf16[512,2304]{1,0:T(8,128)(2,1)} %get-tuple-element.73.refs_15_), channel_id=1, source_target_pairs={{0,4},{4,0},{1,5},{5,1},{2,6},{6,2},{3,7},{7,3},{8,12},{12,8},{9,1... | collective-permute-start | bytes 7077896 | tf_op jit(solution)/shard_map/ppermute | solution.py:767
  386.1 37.3 %collective-permute-start.19 = (bf16[1024,2304]{1,0:T(8,128)(2,1)}, bf16[1024,2304]{1,0:T(8,128)(2,1)}, u32[]{:S(2)}, u32[]{:S(2)}) collective-permute-start(bf16[1024,2304]{1,0:T(8,128)(2,1)} %shard_map.235.refs_31_), channel_id=1, source_target_pairs={{0,2},{2,0},{1,3},{3,1},{4,6},{6,4},{5,7},{7,5},{8,10},{10,8},{9,1... | collective-permute-start | bytes 14155784 | tf_op jit(solution)/shard_map/ppermute | solution.py:770
  421.9 36.3 %collective-permute-start.18 = (bf16[384,2048]{1,0:T(8,128)(2,1)}, bf16[384,2048]{1,0:T(8,128)(2,1)}, u32[]{:S(2)}, u32[]{:S(2)}) collective-permute-start(bf16[384,2048]{1,0:T(8,128)(2,1)} %get-tuple-element.83), channel_id=1, source_target_pairs={{0,1},{1,0},{2,3},{3,2},{4,5},{5,4},{6,7},{7,6},{8,9},{9,8},{10,11... | collective-permute-start | bytes 4718600 | tf_op jit(solution)/shard_map/ppermute | solution.py:788
  433.9 55.5 %collective-permute-start.25 = (bf16[512,2304]{1,0:T(8,128)(2,1)}, bf16[512,2304]{1,0:T(8,128)(2,1)}, u32[]{:S(2)}, u32[]{:S(2)}) collective-permute-start(bf16[512,2304]{1,0:T(8,128)(2,1)} %get-tuple-element.84.refs_5_), channel_id=1, source_target_pairs={{0,4},{4,0},{1,5},{5,1},{2,6},{6,2},{3,7},{7,3},{8,12},{12,8},{9,1... | collective-permute-start | bytes 7077896 | tf_op jit(solution)/shard_map/ppermute | solution.py:767
  445.5 198.7 %reduce-scatter.18.cloned.1.call-start = ((), (), s32[]{:S(2)}) async-start(), calls=%async_computation.18 | async-start | bytes 2949120 | tf_op jit(solution)/shard_map/reduce_scatter | solution.py:776
  456.5 111.7 %collective-permute-start.29 = (bf16[512,1536]{1,0:T(8,128)(2,1)}, bf16[512,1536]{1,0:T(8,128)(2,1)}, u32[]{:S(2)}, u32[]{:S(2)}) collective-permute-start(bf16[512,1536]{1,0:T(8,128)(2,1)} %get-tuple-element.86.refs_5_), channel_id=1, source_target_pairs={{0,4},{4,0},{1,5},{5,1},{2,6},{6,2},{3,7},{7,3},{8,12},{12,8},{9,1... | collective-permute-start | bytes 4718600 | tf_op jit(solution)/shard_map/ppermute | solution.py:767
  466.3 37.7 %collective-permute-start.24 = (bf16[384,2048]{1,0:T(8,128)(2,1)}, bf16[384,2048]{1,0:T(8,128)(2,1)}, u32[]{:S(2)}, u32[]{:S(2)}) collective-permute-start(bf16[384,2048]{1,0:T(8,128)(2,1)} %get-tuple-element.87.refs_21_.refs_1_), channel_id=1, source_target_pairs={{0,1},{1,0},{2,3},{3,2},{4,5},{5,4},{6,7},{7,6},{8,9},{9,8},{10,11... | collective-permute-start | bytes 4718600 | tf_op jit(solution)/shard_map/ppermute | solution.py:788
  484.3 83.9 %collective-permute-start.23 = (bf16[384,2048]{1,0:T(8,128)(2,1)}, bf16[384,2048]{1,0:T(8,128)(2,1)}, u32[]{:S(2)}, u32[]{:S(2)}) collective-permute-start(bf16[384,2048]{1,0:T(8,128)(2,1)} %get-tuple-element.89), channel_id=1, source_target_pairs={{0,1},{1,0},{2,3},{3,2},{4,5},{5,4},{6,7},{7,6},{8,9},{9,8},{10,11... | collective-permute-start | bytes 4718600 | tf_op jit(solution)/shard_map/ppermute | solution.py:788
  493.5 152.6 %reduce-scatter.20.cloned.1.call-start = ((), (), s32[]{:S(2)}) async-start(), calls=%async_computation.19 | async-start | bytes 1966080 | tf_op jit(solution)/shard_map/reduce_scatter | solution.py:776
  528.5 43.5 %collective-permute-start.28 = (bf16[512,1024]{1,0:T(8,128)(2,1)}, bf16[512,1024]{1,0:T(8,128)(2,1)}, u32[]{:S(2)}, u32[]{:S(2)}) collective-permute-start(bf16[512,1024]{1,0:T(8,128)(2,1)} %get-tuple-element.92.refs_12_), channel_id=1, source_target_pairs={{0,4},{4,0},{1,5},{5,1},{2,6},{6,2},{3,7},{7,3},{8,12},{12,8},{9,1... | collective-permute-start | bytes 3145736 | tf_op jit(solution)/shard_map/ppermute | solution.py:767
  572.0 88.9 %reduce-scatter.12.cloned.1.call-start = ((), (), s32[]{:S(2)}) async-start(), calls=%async_computation.15 | async-start | bytes 1310720 | tf_op jit(solution)/shard_map/reduce_scatter | solution.py:776
  576.8 94.2 %reduce-scatter.10.cloned.1.call-start = ((), (), s32[]{:S(2)}) async-start(), calls=%async_computation.14 | async-start | bytes 1638400 | tf_op jit(solution)/shard_map/reduce_scatter | solution.py:776
  600.0 37.0 %collective-permute-start.30 = (bf16[384,2048]{1,0:T(8,128)(2,1)}, bf16[384,2048]{1,0:T(8,128)(2,1)}, u32[]{:S(2)}, u32[]{:S(2)}) collective-permute-start(bf16[384,2048]{1,0:T(8,128)(2,1)} %get-tuple-element.100), channel_id=1, source_target_pairs={{0,1},{1,0},{2,3},{3,2},{4,5},{5,4},{6,7},{7,6},{8,9},{9,8},{10,11... | collective-permute-start | bytes 4718600 | tf_op jit(solution)/shard_map/ppermute | solution.py:788
  (117 other events, 1130.9 us)
Sparse Core Ops, SparseCore 0:
  9.6 31.7 all-gather.8
  43.6 33.3 all-gather.6
  79.2 50.6 all-gather.10
  132.0 50.5 all-gather.12
  184.0 50.5 all-gather.14
  236.5 38.8 all-gather.16
  300.0 47.6 reduce-scatter.7
  350.0 47.5 reduce-scatter.13
  445.6 45.9 reduce-scatter.15
  493.8 47.9 reduce-scatter.17
  572.1 37.6 reduce-scatter.19
  611.9 26.0 reduce-scatter.11
  640.4 30.5 reduce-scatter.9

commit v5 on v4

--- a/solution.py
+++ b/solution.py
@@ -13,7 +13,8 @@
 CHUNKS = 4
 BLOCK = 256
 ROW_STEPS = 3
-COST = 10**11
+COST = 10**10
+SHORT = 0.01
 VMEM = 48 * 2**20
 epsilon = 1e-05
 rope_base = 10000.0
@@ -168,7 +169,7 @@
         dv_ref[...] = jnp.where(mine, fold(dvw_ref).astype(bf16), dv_ref[...])
 
 
-def launch(kernel, scalars, operands, deps, grid, in_specs, out_specs, out_shape, scratch=(), aliases=()):
+def launch(kernel, scalars, operands, deps, grid, in_specs, out_specs, out_shape, scratch=(), aliases=(), us=3):
     count = len(scalars) + len(operands)
 
     def body(*refs):
@@ -185,7 +186,7 @@
         ),
         out_shape=out_shape,
         compiler_params=pltpu.CompilerParams(vmem_limit_bytes=VMEM),
-        cost_estimate=pl.CostEstimate(flops=COST, bytes_accessed=1024, transcendentals=0),
+        cost_estimate=pl.CostEstimate(flops=int(COST * us), bytes_accessed=1024, transcendentals=0),
         input_output_aliases=dict(aliases),
     )(*scalars, *operands, *deps)
 
@@ -240,6 +241,7 @@
         [whole_block(p) for p in parts],
         pl.BlockSpec(shape, lambda j: (0, 0)),
         jax.ShapeDtypeStruct(shape, bf16),
+        us=1.5,
     )
 
 
@@ -260,6 +262,7 @@
         [pl.BlockSpec((block, width), lambda j, s: (s[1] * steps + j, 0))],
         pl.BlockSpec((block, width), lambda j, s: (j, 0)),
         jax.ShapeDtypeStruct((rows // 2, width), bf16),
+        us=4,
     )
 
 
@@ -279,6 +282,7 @@
         anywhere,
         jax.ShapeDtypeStruct(array.shape, array.dtype),
         aliases=((0, 0),),
+        us=1,
     )
 
 
@@ -319,6 +323,7 @@
         specs,
         [pl.BlockSpec((rows, BLOCK), lambda j, s: (0, j))] * 3,
         [jax.ShapeDtypeStruct((rows, units), bf16)] * 3,
+        us=rows * width * units / 10**8,
     )
 
 
@@ -352,6 +357,7 @@
         [whole_block(own), whole_block(other), *specs, *(whole_block(t) for t in tables)],
         pl.BlockSpec((2 * rows, BLOCK), lambda j, s: (0, j)),
         jax.ShapeDtypeStruct((2 * rows, units), bf16),
+        us=rows * width * units / 10**8,
     )
 
 
@@ -399,6 +405,7 @@
         [*specs, *([half] * len(starts))],
         [half, half],
         [jax.ShapeDtypeStruct((rows // 2, width), kind) for kind in kinds],
+        us=rows * width * sum(a.shape[1] for a in acts) / 285000000,
     )
 
 
@@ -426,7 +433,7 @@
             refs[-1][:, at] = total
 
 
-def grad(acts, which, grads, deps, added=None):
+def grad(acts, which, grads, deps, added=None, us=None):
     tokens, width = acts[0].shape
     block = min(BLOCK, width // 4)
     steps = width // 2 // block
@@ -458,6 +465,7 @@
         specs,
         outs,
         shapes,
+        us=us or tokens * width * units / 480000000,
     )
 
 
@@ -487,6 +495,7 @@
             jax.ShapeDtypeStruct((length, groups * 128), f32),
         ],
         [pltpu.VMEM((length, 256), bf16)] * 2,
+        us=16,
     )
 
 
@@ -517,6 +526,7 @@
             jax.ShapeDtypeStruct((length, 128), bf16),
         ],
         [pltpu.VMEM((length, 256), bf16)] * 2 + [pltpu.VMEM((length, 256), f32)] * 2,
+        us=35,
     )
 
 
@@ -539,18 +549,19 @@
         [half, half],
         pl.BlockSpec((2 * rows, block), lambda j, s: (0, j)),
         jax.ShapeDtypeStruct((2 * rows, width), bf16),
+        us=4,
     )
 
 
 def add_kernel(a_ref, b_ref, out_ref):
-    out_ref[...] = (a_ref[...].astype(f32) + b_ref[...].astype(f32)).astype(bf16)
-
-
-def add(a, b, deps):
+    out_ref[...] = (a_ref[...].astype(f32) + b_ref[...].astype(f32)).astype(out_ref.dtype)
+
+
+def add(a, b, deps, us=4, kind=bf16):
     rows, width = a.shape
     block = pl.BlockSpec((rows // 4, width), lambda j: (j, 0))
     return launch(
-        add_kernel, [], [a, b], deps, (4,), [block, block], block, jax.ShapeDtypeStruct(a.shape, bf16)
+        add_kernel, [], [a, b], deps, (4,), [block, block], block, jax.ShapeDtypeStruct(a.shape, kind), us=us
     )
 
 
@@ -611,6 +622,7 @@
         [spec, whole_block(gain)],
         [spec, spec],
         [jax.ShapeDtypeStruct(tokens.shape, bf16)] * 2,
+        us=3,
     )
 
 
@@ -625,6 +637,7 @@
         [spec],
         spec,
         jax.ShapeDtypeStruct(array.shape, bf16),
+        us=3,
     )
 
 
@@ -645,6 +658,7 @@
         [spec, spec, spec, whole_block(gain)],
         [spec, spec],
         [jax.ShapeDtypeStruct(tokens.shape, bf16), jax.ShapeDtypeStruct(tokens.shape, f32)],
+        us=5,
     )
 
 
@@ -678,6 +692,7 @@
         [spec, spec, spec, spec, whole_block(gain)],
         [spec, spec, whole_block(gain)],
         [jax.ShapeDtypeStruct(own.shape, bf16), jax.ShapeDtypeStruct(own.shape, f32), part],
+        us=8,
     )
 
 
@@ -705,6 +720,7 @@
         [spec, spec, spec],
         spec,
         jax.ShapeDtypeStruct(own.shape, bf16),
+        us=5,
     )
 
 
@@ -727,6 +743,7 @@
         [spec, spec, spec, spec, whole_block(gain)],
         [spec, whole_block(gain)],
         [jax.ShapeDtypeStruct(own.shape, bf16), jax.ShapeDtypeStruct(gain.shape, f32)],
+        us=7,
     )
 
 
@@ -842,6 +859,7 @@
         first_seen = first_blocks(segment_row)
         spread("o")
         spread("qkv")
+        order.wait(cosine, sine, first_seen)
         land("o")
         grad_seq = order(lambda deps: join(here, out_grad, grad_other, deps))
         normed_seq = order(lambda deps: join(spot, normed_first, normed_other, deps))
@@ -887,45 +905,43 @@
         def send_x(i):
             from_x[i] = over_x(to_x[i])
 
-        def finish(i):
-            summed[i] = scatter(order(lambda deps: add(kept[i], from_x[i], deps))).astype(f32)
-
-        def feed_back(chunks, starts, kinds):
+        def finish(i, us=4):
+            summed[i] = scatter(order(lambda deps: add(kept[i], from_x[i], deps, us)))
+
+        def feed_back(chunks):
             acts = [a[i] for i in chunks for a in (gate_grad, up_grad)]
             weights = [(full[i], at) for i in chunks for at in (0, 1)]
-            return order(
-                lambda deps: back(spot, acts, weights, deps, starts=starts, kinds=kinds)
-            )
+            return order(lambda deps: back(spot, acts, weights, deps))
 
         run_feed(0)
         core_part(0)
         run_feed(1)
         spread(3)
         x_part(0)
-        kept_along, sent_along = scatter(kept[0]), scatter(to_x[0])
+        sent_along, kept_along = scatter(to_x[0]), scatter(kept[0])
         core_part(1)
         land(2)
+        run_feed(2)
         x_part(1)
         send_x(1)
-        run_feed(2)
+        from_along = over_x(order(lambda deps: gate(sent_along, deps)))
+        land(3)
         core_part(2)
-        starts = feed_back((0, 1, 2), (), (f32, f32))
-        land(3)
         run_feed(3)
-        own, sent = feed_back((3,), starts, (f32, bf16))
+        own, sent = feed_back(range(CHUNKS))
         other = swap(sent)
+        order.wait(kept_along)
         x_part(2)
         send_x(2)
         core_part(3)
-        from_along = over_x(sent_along)
+        order.wait(from_along)
         finish(1)
-        x_part(3)
-        send_x(3)
         attn_out_grad, middle_grad, feed_gain_part = order(
             lambda deps: middle_backward(own, other, middle, out_grad, feed_gain, deps)
         )
         attn_other = swap(attn_out_grad)
-        order.wait(from_along)
+        x_part(3)
+        send_x(3)
         block_own, block_sent = order(
             lambda deps: back(
                 spot, [hidden[i] for i in range(CHUNKS)], [(full[i], 2) for i in range(CHUNKS)], deps
@@ -940,6 +956,7 @@
             lambda deps: grad((attn_grad_seq,), (0,), (mixed,), deps, from_core["o"])
         )
         send_x("o")
+        finish(3)
         qkv_grad = order(
             lambda deps: attend_back(
                 rotated, mixed_grad, log_totals, query_width, first_seen, segment_row, cosine, sine,
@@ -947,10 +964,9 @@
             )
         )
         from_core["qkv"] = over_core(
-            order(lambda deps: grad((normed_seq,), (0,) * 3, qkv_grad, deps))
+            order(lambda deps: grad((normed_seq,), (0,) * 3, qkv_grad, deps, us=SHORT))
         )
-        order.wait(block_other)
-        finish(3)
+        order.wait(summed[3])
         finish("o")
         to_x["qkv"], kept["qkv"] = order(
             lambda deps: grad((normed_seq,), (0,) * 3, qkv_grad, deps, from_core["qkv"])
@@ -961,7 +977,9 @@
             lambda deps: back(spot, qkv_grad, [(full["qkv"], at) for at in places], deps, True)
         )
         other = swap(sent)
+        summed[0] = order(lambda deps: add(kept_along, from_along, deps, kind=f32))
         block_out = order(lambda deps: block_result(spot, tiles, middle, block_own, block_other, deps))
+        order.wait(summed["o"])
         finish("qkv")
         input_grad, attention_gain_part = order(
             lambda deps: input_backward(spot, tiles, own, other, tokens, middle_grad, attention_gain, deps)
@@ -969,14 +987,13 @@
         gains = total(natural(jnp.concatenate([attention_gain_part, feed_gain_part], axis=0)))
         if not tiles:
             block_out, input_grad = natural(block_out), natural(input_grad)
-        summed[0] = kept_along.astype(f32) + from_along.astype(f32)
-        qkv_weight_grad = summed["qkv"]
+        qkv_weight_grad = summed["qkv"].astype(f32)
 
         def whole(at):
             parts = []
             for i in range(CHUNKS):
                 units = edges[i + 1] - edges[i]
-                parts.append(summed[i][:, at * units : at * units + units])
+                parts.append(summed[i][:, at * units : at * units + units].astype(f32))
             return jnp.concatenate(parts, axis=1)
 
         return (
@@ -985,7 +1002,7 @@
             qkv_weight_grad[:, :query_width],
             qkv_weight_grad[:, query_width : query_width + key_width],
             qkv_weight_grad[:, query_width + key_width :],
-            summed["o"],
+            summed["o"].astype(f32),
             gains[0],
             whole(0),
             whole(1),

time: 689 us -> 669 us (0.971)
  waiting for transfers between devices: 196 us -> 174 us
    reduce_scatter x7, waiting for transfers between devices: 18.1 us -> 5.96 us  [scatter(): return lax.psum_scatter(operand, 'z', scatter_dimension=0, tiled=True)]
    unnamed x198 -> x228, local copies, waits for them, and re-layouts: 41.4 us -> 53.4 us
    pallas_call x57 -> x58, Pallas kernels: 370 us -> 365 us  [launch(): pl.pallas_call(body, grid_spec=pltpu.PrefetchScalarGridSpec(num_scalar_pr...]
  transfers between devices with their start and end apart: 50 -> 50, of which waited for: 21 -> 22; matrix products, arithmetic and copies ran while one was open for 3% -> 2% of each run, Pallas kernels for 54% -> 55%
where the time goes in v5:
time: 669 us; the launch traced here: 661 us
  Pallas kernels  365 us (55%)
  waiting for transfers between devices  174 us (26%)
  local copies, waits for them, and re-layouts  58 us (9%)
  starting transfers between devices  36.3 us (5%)
  between operations  15.3 us (2%)
  other arithmetic  12 us (2%)
    pallas_call x58, Pallas kernels, launch(): pl.pallas_call(body, grid_spec=pltpu.PrefetchScalarGridSpec(num_scalar_pr...  365 us
    all_gather x6, waiting for transfers between devices, gather(): return lax.all_gather(operand, ('core', 'z'), axis=0, tiled=True)  94.6 us
    unnamed x228, local copies, waits for them, and re-layouts  53.4 us
    ppermute x8, waiting for transfers between devices, swap(): return lax.ppermute(own, 'tensor', SWAP)  38.8 us
    ppermute x12, waiting for transfers between devices, over_x(): return lax.ppermute(array, 'x', SWAP)  21.2 us
    ppermute x12, starting transfers between devices, over_x(): return lax.ppermute(array, 'x', SWAP)  18.4 us
  transfers between devices with their start and end apart: 50, of which 22 were waited for; matrix products, arithmetic and copies ran while one was open for 2% of the time, Pallas kernels for 55%

profile of v5, /device:TPU:0, one launch (start us, length us, event | category | flops | bytes accessed | tf_op | source)
XLA Modules:
  0.0 661.1 jit_solution(17865159942198041624)
XLA Ops:
  27.2 14.2 %all-gather.9.cloned.1.call-done.refs_1_.refs_2_.refs_4_.refs_3_.refs_5_ = bf16[1024,1024]{1,0:T(8,128)(2,1)} async-done(((bf16[128,1024]{1,0:T(8,128)(2,1)}), bf16[1024,1024]{1,0:T(8,128)(2,1)}) %all-gather.9.cloned.1.call-update) | async-done | bytes 2097168 | tf_op jit(solution)/shard_map/all_gather | solution.py:790
  46.6 30.4 %all-gather.7.cloned.1.call-done.refs_1_.refs_3_.refs_5_.refs_4_.refs_6_.refs_8_.refs_10_.refs_12_.refs_14_ = bf16[1024,1280]{1,0:T(8,128)(2,1)} async-done(((bf16[128,1280]{1,0:T(8,128)(2,1)}), bf16[1024,1280]{1,0:T(8,128)(2,1)}) %all-gather.7.cloned.1.call-update) | async-done | bytes 2621456 | tf_op jit(solution)/shard_map/all_gather | solution.py:790
  85.7 6.8 %collective-permute-done.refs_2_ = bf16[384,2048]{1,0:T(8,128)(2,1)} collective-permute-done((bf16[384,2048]{1,0:T(8,128)(2,1)}, bf16[384,2048]{1,0:T(8,128)(2,1)}, u32[]{:S(2)}, u32[]{:S(2)}) %collective-permute-start) | collective-permute-done | bytes 1572896 | tf_op jit(solution)/shard_map/ppermute | solution.py:805
  97.2 13.4 %collective-permute-done.1.refs_0_ = bf16[512,1280]{1,0:T(8,128)(2,1)} collective-permute-done((bf16[512,1280]{1,0:T(8,128)(2,1)S(1)}, bf16[512,1280]{1,0:T(8,128)(2,1)}, u32[]{:S(2)}, u32[]{:S(2)}) %collective-permute-start.1) | collective-permute-done | bytes 1310752 | tf_op jit(solution)/shard_map/ppermute | solution.py:784
  115.8 10.8 %shard_map.216.refs_2_.refs_1_.refs_3_ = bf16[768,1280]{1,0:T(8,128)(2,1)} custom-call(s32[3]{0:T(128)S(1)} %pad_add_fusion.refs_0_, bf16[384,2048]{1,0:T(8,128)(2,1)} %get-tuple-element.58.refs_1_, bf16[384,2048]{1,0:T(8,128)(2,1)} %collective-permute-done.refs_2_, ...), custom_call_target="tpu_custom_call" | custom-call | flops 100663296000 | bytes 1024 | tf_op jit(solution)/shard_map/pallas_call | solution.py:178
  137.5 14.6 %shard_map.218 = (bf16[768,1024]{1,0:T(8,128)(2,1)S(1)}, f32[768,256]{1,0:T(8,128)S(1)}) custom-call(s32[3]{0:T(128)S(1)} %copy-done.44, bf16[768,1280]{1,0:T(8,128)(2,1)S(1)} %copy-done.63, bf16[768,1280]{1,0:T(8,128)(2,1)S(1)} %copy-done.63, bf16[768,1280]{1,0:T(8,128)(2,1)S(1)} %copy-done.63, s32[768,1]{1,0:T(8,128)S(1)} %copy.42.refs_4_.refs_6_, ...), custom_call_target="tpu_custom_call" | custom-call | flops 160000000000 | bytes 1024 | tf_op jit(solution)/shard_map/pallas_call | solution.py:178
  153.0 9.9 %shard_map.219 = (f32[384,2048]{1,0:T(8,128)}, bf16[384,2048]{1,0:T(8,128)(2,1)}) custom-call(s32[3]{0:T(128)S(1)} %pad_add_fusion.refs_0_, bf16[768,1024]{1,0:T(8,128)(2,1)S(1)} %get-tuple-element.59.refs_1_.refs_6_, bf16[1024,1024]{1,0:T(8,128)(2,1)} %all-gather.9.cloned.1.call-done.refs_1_.refs_2_.refs_4_.refs_3_.refs_5_, ...), custom_call_target="tpu_custom_call" | custom-call | flops 56512729088 | bytes 1024 | tf_op jit(solution)/shard_map/pallas_call | solution.py:178
  164.4 18.1 %all-gather.13.cloned.1.call-done.refs_1_.refs_3_.refs_5_.refs_7_.refs_9_.refs_11_.refs_13_.refs_17_.refs_19_.refs_21_.refs_23_ = bf16[1024,2304]{1,0:T(8,128)(2,1)} async-done(((bf16[128,2304]{1,0:T(8,128)(2,1)}), bf16[1024,2304]{1,0:T(8,128)(2,1)}) %all-gather.13.cloned.1.call-update) | async-done | bytes 4718608 | tf_op jit(solution)/shard_map/all_gather | solution.py:790
  189.7 9.8 %collective-permute-done.6.refs_2_ = bf16[384,2048]{1,0:T(8,128)(2,1)} collective-permute-done((bf16[384,2048]{1,0:T(8,128)(2,1)}, bf16[384,2048]{1,0:T(8,128)(2,1)}, u32[]{:S(2)}, u32[]{:S(2)}) %collective-permute-start.6) | collective-permute-done | bytes 1572896 | tf_op jit(solution)/shard_map/ppermute | solution.py:805
  206.6 28.5 %all-gather.15.cloned.1.call-done.refs_1_.refs_3_.refs_5_.refs_7_.refs_9_.refs_11_.refs_13_.refs_25_.refs_27_.refs_29_.refs_31_.refs_15_ = bf16[1024,2304]{1,0:T(8,128)(2,1)} async-done(((bf16[128,2304]{1,0:T(8,128)(2,1)}), bf16[1024,2304]{1,0:T(8,128)(2,1)}) %all-gather.15.cloned.1.call-update) | async-done | bytes 4718608 | tf_op jit(solution)/shard_map/all_gather | solution.py:790
  247.9 13.3 %shard_map.226 = (bf16[768,768]{1,0:T(8,128)(2,1)S(1)}, bf16[768,768]{1,0:T(8,128)(2,1)S(1)}, bf16[768,768]{1,0:T(8,128)(2,1)S(1)}) custom-call(s32[3]{0:T(128)S(1)} %pad_add_fusion.refs_0_, bf16[768,2048]{1,0:T(8,128)(2,1)} %shard_map.224.refs_1_.refs_0_, bf16[768,2048]{1,0:T(8,128)(2,1)} %shard_map.213.refs_3_.refs_2_.refs_1_, ...), custom_call_target="tpu_custom_call" | custom-call | flops 120795955200 | bytes 1024 | tf_op jit(solution)/shard_map/pallas_call | solution.py:178
  261.3 7.9 %shard_map.227.refs_15_ = bf16[1024,2304]{1,0:T(8,128)(2,1)} custom-call(bf16[768,2048]{1,0:T(8,128)(2,1)} %shard_map.224.refs_1_.refs_0_, bf16[768,2048]{1,0:T(8,128)(2,1)} %shard_map.213.refs_3_.refs_2_.refs_1_, bf16[768,768]{1,0:T(8,128)(2,1)S(1)} %get-tuple-element.65.refs_2_.refs_1_, bf16[768,768]{1,0:T(8,128)(2,1)S(1)} %get-tuple-element.66.refs_3_.refs_2_, ...), custom_call_target="tpu_custom_call" | custom-call | flops 75497472000 | bytes 1024 | tf_op jit(solution)/shard_map/pallas_call | solution.py:178
  269.9 13.1 %shard_map.228 = (bf16[768,768]{1,0:T(8,128)(2,1)S(1)}, bf16[768,768]{1,0:T(8,128)(2,1)S(1)}, bf16[768,768]{1,0:T(8,128)(2,1)S(1)}) custom-call(s32[3]{0:T(128)S(1)} %pad_add_fusion.refs_0_, bf16[768,2048]{1,0:T(8,128)(2,1)} %shard_map.224.refs_1_.refs_0_, bf16[768,2048]{1,0:T(8,128)(2,1)} %shard_map.213.refs_3_.refs_2_.refs_1_, ...), custom_call_target="tpu_custom_call" | custom-call | flops 120795955200 | bytes 1024 | tf_op jit(solution)/shard_map/pallas_call | solution.py:178
  289.6 10.5 %shard_map.230 = (bf16[512,2304]{1,0:T(8,128)(2,1)}, bf16[512,2304]{1,0:T(8,128)(2,1)}) custom-call(bf16[768,2048]{1,0:T(8,128)(2,1)} %shard_map.224.refs_1_.refs_0_, bf16[768,2048]{1,0:T(8,128)(2,1)} %shard_map.213.refs_3_.refs_2_.refs_1_, bf16[768,768]{1,0:T(8,128)(2,1)S(1)} %copy-done.96, bf16[768,768]{1,0:T(8,128)(2,1)S(1)} %copy-done.99, ...), custom_call_target="tpu_custom_call" | custom-call | flops 75497472000 | bytes 1024 | tf_op jit(solution)/shard_map/pallas_call | solution.py:178
  304.3 7.4 %shard_map.231.refs_1_ = bf16[1024,2304]{1,0:T(8,128)(2,1)} custom-call(bf16[768,2048]{1,0:T(8,128)(2,1)} %shard_map.224.refs_1_.refs_0_, bf16[768,2048]{1,0:T(8,128)(2,1)} %shard_map.213.refs_3_.refs_2_.refs_1_, bf16[768,768]{1,0:T(8,128)(2,1)S(1)} %copy-done.86, bf16[768,768]{1,0:T(8,128)(2,1)S(1)} %copy-done.90, ...), custom_call_target="tpu_custom_call" | custom-call | flops 75497472000 | bytes 1024 | tf_op jit(solution)/shard_map/pallas_call | solution.py:178
  316.6 13.3 %shard_map.233 = (bf16[768,768]{1,0:T(8,128)(2,1)S(1)}, bf16[768,768]{1,0:T(8,128)(2,1)S(1)}, bf16[768,768]{1,0:T(8,128)(2,1)S(1)}) custom-call(s32[3]{0:T(128)S(1)} %copy-done.21, bf16[768,2048]{1,0:T(8,128)(2,1)} %shard_map.224.refs_1_.refs_0_, bf16[768,2048]{1,0:T(8,128)(2,1)} %shard_map.213.refs_3_.refs_2_.refs_1_, ...), custom_call_target="tpu_custom_call" | custom-call | flops 120795955200 | bytes 1024 | tf_op jit(solution)/shard_map/pallas_call | solution.py:178
  331.1 11.3 %shard_map.234 = (bf16[512,2304]{1,0:T(8,128)(2,1)}, bf16[512,2304]{1,0:T(8,128)(2,1)}) custom-call(bf16[768,2048]{1,0:T(8,128)(2,1)} %shard_map.224.refs_1_.refs_0_, bf16[768,2048]{1,0:T(8,128)(2,1)} %shard_map.213.refs_3_.refs_2_.refs_1_, bf16[768,768]{1,0:T(8,128)(2,1)S(1)} %copy-done.87, bf16[768,768]{1,0:T(8,128)(2,1)S(1)} %copy-done.91, ...), custom_call_target="tpu_custom_call" | custom-call | flops 75497472000 | bytes 1024 | tf_op jit(solution)/shard_map/pallas_call | solution.py:178
  350.4 7.4 %shard_map.237.refs_15_ = bf16[1024,2304]{1,0:T(8,128)(2,1)} custom-call(bf16[768,2048]{1,0:T(8,128)(2,1)} %shard_map.224.refs_1_.refs_0_, bf16[768,2048]{1,0:T(8,128)(2,1)} %shard_map.213.refs_3_.refs_2_.refs_1_, bf16[768,768]{1,0:T(8,128)(2,1)S(1)} %copy-done.80, bf16[768,768]{1,0:T(8,128)(2,1)S(1)} %copy-done.83, ...), custom_call_target="tpu_custom_call" | custom-call | flops 75497472000 | bytes 1024 | tf_op jit(solution)/shard_map/pallas_call | solution.py:178
  358.3 10.5 %shard_map.238 = (bf16[768,512]{1,0:T(8,128)(2,1)S(1)}, bf16[768,512]{1,0:T(8,128)(2,1)S(1)}, bf16[768,512]{1,0:T(8,128)(2,1)S(1)}) custom-call(s32[3]{0:T(128)S(1)} %copy-done.21, bf16[768,2048]{1,0:T(8,128)(2,1)} %shard_map.224.refs_1_.refs_0_, bf16[768,2048]{1,0:T(8,128)(2,1)} %shard_map.213.refs_3_.refs_2_.refs_1_, ...), custom_call_target="tpu_custom_call" | custom-call | flops 80530636800 | bytes 1024 | tf_op jit(solution)/shard_map/pallas_call | solution.py:178
  368.8 30.0 %shard_map.239 = (f32[384,2048]{1,0:T(8,128)}, bf16[384,2048]{1,0:T(8,128)(2,1)}) custom-call(s32[3]{0:T(128)S(1)} %copy-done.21, bf16[768,768]{1,0:T(8,128)(2,1)S(1)} %copy-done.97, bf16[768,768]{1,0:T(8,128)(2,1)S(1)} %copy-done.100, bf16[768,768]{1,0:T(8,128)(2,1)S(1)} %copy-done.88, bf16[768,768]{1,0:T(8,128)(2,1)} %copy-done.89, ...), custom_call_target="tpu_custom_call" | custom-call | flops 310820012032 | bytes 1024 | tf_op jit(solution)/shard_map/pallas_call | solution.py:178
  405.2 10.4 %shard_map.240 = (bf16[512,2304]{1,0:T(8,128)(2,1)}, bf16[512,2304]{1,0:T(8,128)(2,1)}) custom-call(bf16[768,2048]{1,0:T(8,128)(2,1)} %shard_map.224.refs_1_.refs_0_, bf16[768,2048]{1,0:T(8,128)(2,1)} %shard_map.213.refs_3_.refs_2_.refs_1_, bf16[768,768]{1,0:T(8,128)(2,1)S(1)} %copy-done.81, bf16[768,768]{1,0:T(8,128)(2,1)S(1)} %copy-done.84, ...), custom_call_target="tpu_custom_call" | custom-call | flops 75497472000 | bytes 1024 | tf_op jit(solution)/shard_map/pallas_call | solution.py:178
  429.1 6.8 %collective-permute-done.20.refs_1_ = bf16[384,2048]{1,0:T(8,128)(2,1)} collective-permute-done((bf16[384,2048]{1,0:T(8,128)(2,1)}, bf16[384,2048]{1,0:T(8,128)(2,1)}, u32[]{:S(2)}, u32[]{:S(2)}) %collective-permute-start.20) | collective-permute-done | bytes 1572896 | tf_op jit(solution)/shard_map/ppermute | solution.py:805
  436.0 7.8 %shard_map.243 = (bf16[384,2048]{1,0:T(8,128)(2,1)}, f32[384,2048]{1,0:T(8,128)}, f32[1,2048]{1,0:T(1,128)S(1)}) custom-call(f32[384,2048]{1,0:T(8,128)} %get-tuple-element.78.refs_6_.refs_0_, bf16[384,2048]{1,0:T(8,128)(2,1)} %collective-permute-done.20.refs_1_, f32[384,2048]{1,0:T(8,128)} %get-tuple-element.62.refs_2_.refs_1_, ...), custom_call_target="tpu_custom_call" | custom-call | flops 80000000000 | bytes 1024 | tf_op jit(solution)/shard_map/pallas_call | solution.py:178
  445.3 7.9 %shard_map.244 = (bf16[512,1536]{1,0:T(8,128)(2,1)}, bf16[512,1536]{1,0:T(8,128)(2,1)S(1)}) custom-call(bf16[768,2048]{1,0:T(8,128)(2,1)} %shard_map.224.refs_1_.refs_0_, bf16[768,2048]{1,0:T(8,128)(2,1)} %shard_map.213.refs_3_.refs_2_.refs_1_, bf16[768,512]{1,0:T(8,128)(2,1)S(1)} %copy-done.73, bf16[768,512]{1,0:T(8,128)(2,1)S(1)} %copy-done.75, ...), custom_call_target="tpu_custom_call" | custom-call | flops 50331648000 | bytes 1024 | tf_op jit(solution)/shard_map/pallas_call | solution.py:178
  455.4 16.5 %shard_map.245 = (f32[384,2048]{1,0:T(8,128)}, bf16[384,2048]{1,0:T(8,128)(2,1)}) custom-call(s32[3]{0:T(128)S(1)} %copy-done.22, bf16[768,768]{1,0:T(8,128)(2,1)S(1)} %copy-done.94, bf16[768,768]{1,0:T(8,128)(2,1)S(1)} %copy-done.71, bf16[768,768]{1,0:T(8,128)(2,1)S(1)} %copy-done.78, bf16[768,512]{1,0:T(8,128)(2,1)S(1)} %get-tuple-element.75.refs_41_.refs_4_, ...), custom_call_target="tpu_custom_call" | custom-call | flops 155410006016 | bytes 1024 | tf_op jit(solution)/shard_map/pallas_call | solution.py:178
  491.7 7.3 %shard_map.249.refs_3_.refs_4_ = bf16[768,1024]{1,0:T(8,128)(2,1)S(1)} custom-call(s32[3]{0:T(128)S(1)} %copy-done.22, bf16[384,2048]{1,0:T(8,128)(2,1)} %get-tuple-element.83.refs_6_.refs_1_, bf16[384,2048]{1,0:T(8,128)(2,1)} %collective-permute-done.24.refs_2_, bf16[1024,1024]{1,0:T(8,128)(2,1)} %all-gather.9.cloned.1.call-done.refs_1_.refs_2_.refs_4_.refs_3_.refs_5_, ...), custom_call_target="tpu_custom_call" | custom-call | flops 80530636800 | bytes 1024 | tf_op jit(solution)/shard_map/pallas_call | solution.py:178
  518.9 32.0 %shard_map.252 = (bf16[768,1024]{1,0:T(8,128)(2,1)S(1)}, bf16[768,128]{1,0:T(8,128)(2,1)S(1)}, bf16[768,128]{1,0:T(8,128)(2,1)S(1)}) custom-call(s32[3]{0:T(128)S(1)} %copy-done.45, bf16[768,1280]{1,0:T(8,128)(2,1)} %shard_map.216.refs_2_.refs_1_.refs_3_, bf16[768,1280]{1,0:T(8,128)(2,1)} %shard_map.216.refs_2_.refs_1_.refs_3_, ...), custom_call_target="tpu_custom_call" | custom-call | flops 349999988736 | bytes 1024 | tf_op jit(solution)/shard_map/pallas_call | solution.py:178
  567.0 7.6 %shard_map.255 = (bf16[512,1280]{1,0:T(8,128)(2,1)}, bf16[512,1280]{1,0:T(8,128)(2,1)S(1)}) custom-call(bf16[768,2048]{1,0:T(8,128)(2,1)} %shard_map.214.refs_1_.refs_0_, bf16[768,1024]{1,0:T(8,128)(2,1)S(1)} %get-tuple-element.91.refs_1_.refs_4_, bf16[768,128]{1,0:T(8,128)(2,1)S(1)} %get-tuple-element.92.refs_2_, ...), custom_call_target="tpu_custom_call" | custom-call | flops 41943040000 | bytes 1024 | tf_op jit(solution)/shard_map/pallas_call | solution.py:178
  577.2 11.6 %shard_map.256 = (f32[384,2048]{1,0:T(8,128)}, bf16[384,2048]{1,0:T(8,128)(2,1)}) custom-call(s32[3]{0:T(128)S(1)} %copy-done.23, bf16[768,1024]{1,0:T(8,128)(2,1)} %copy-done, bf16[768,128]{1,0:T(8,128)(2,1)S(1)} %get-tuple-element.92.refs_2_, bf16[768,128]{1,0:T(8,128)(2,1)S(1)} %get-tuple-element.93.refs_3_, ...), custom_call_target="tpu_custom_call" | custom-call | flops 70640910336 | bytes 1024 | tf_op jit(solution)/shard_map/pallas_call | solution.py:178
  599.2 7.1 %collective-permute-done.31.refs_1_ = bf16[512,1280]{1,0:T(8,128)(2,1)} collective-permute-done((bf16[512,1280]{1,0:T(8,128)(2,1)}, bf16[512,1280]{1,0:T(8,128)(2,1)}, u32[]{:S(2)}, u32[]{:S(2)}) %collective-permute-start.31) | collective-permute-done | bytes 1310752 | tf_op jit(solution)/shard_map/ppermute | solution.py:784
  613.6 11.0 %collective-permute-done.30.refs_2_ = bf16[384,2048]{1,0:T(8,128)(2,1)S(1)} collective-permute-done((bf16[384,2048]{1,0:T(8,128)(2,1)}, bf16[384,2048]{1,0:T(8,128)(2,1)S(1)}, u32[]{:S(2)}, u32[]{:S(2)}) %collective-permute-start.30) | collective-permute-done | bytes 1572896 | tf_op jit(solution)/shard_map/ppermute | solution.py:805
  626.1 6.6 shard_map.260
  (415 shorter events, 232.1 us)
Async XLA Ops:
  7.9 69.1 %all-gather.7.cloned.1.call-start = ((), (), s32[]{:S(2)}) async-start(), calls=%async_computation.7 | async-start | bytes 2949120 | tf_op jit(solution)/shard_map/all_gather | solution.py:790
  11.2 118.7 %all-gather.11.cloned.1.call-start = ((), (), s32[]{:S(2)}) async-start(), calls=%async_computation.9 | async-start | bytes 5308416 | tf_op jit(solution)/shard_map/all_gather | solution.py:790
  13.5 169.0 %all-gather.13.cloned.1.call-start = ((), (), s32[]{:S(2)}) async-start(), calls=%async_computation.10 | async-start | bytes 5308416 | tf_op jit(solution)/shard_map/all_gather | solution.py:790
  14.5 220.6 %all-gather.15.cloned.1.call-start = ((), (), s32[]{:S(2)}) async-start(), calls=%async_computation.11 | async-start | bytes 5308416 | tf_op jit(solution)/shard_map/all_gather | solution.py:790
  15.4 269.6 %all-gather.17.cloned.1.call-start = ((), (), s32[]{:S(2)}) async-start(), calls=%async_computation.12 | async-start | bytes 3538944 | tf_op jit(solution)/shard_map/all_gather | solution.py:790
  21.3 59.8 %collective-permute-start.2 = (bf16[384,2048]{1,0:T(8,128)(2,1)S(1)}, bf16[384,2048]{1,0:T(8,128)(2,1)}, u32[]{:S(2)}, u32[]{:S(2)}) collective-permute-start(bf16[384,2048]{1,0:T(8,128)(2,1)S(1)} %shard_map.209.refs_2_.refs_1_.refs_3_), channel_id=1, source_target_pairs={{0,1},{1,0},{2,3},{3,2},{4,5},{5,4},{6,7},{7,6},{8,9},{9,8},{10,11... | collective-permute-start | bytes 4718600 | tf_op jit(solution)/shard_map/ppermute | solution.py:805
  24.2 68.2 %collective-permute-start = (bf16[384,2048]{1,0:T(8,128)(2,1)}, bf16[384,2048]{1,0:T(8,128)(2,1)}, u32[]{:S(2)}, u32[]{:S(2)}) collective-permute-start(bf16[384,2048]{1,0:T(8,128)(2,1)} %get-tuple-element.58.refs_1_), channel_id=1, source_target_pairs={{0,1},{1,0},{2,3},{3,2},{4,5},{5,4},{6,7},{7,6},{8,9},{9,8},{10,11... | collective-permute-start | bytes 4718600 | tf_op jit(solution)/shard_map/ppermute | solution.py:805
  112.5 234.6 %reduce-scatter.8.cloned.1.call-start = ((), (), s32[]{:S(2)}) async-start(), calls=%async_computation.13 | async-start | bytes 2949120 | tf_op jit(solution)/shard_map/reduce_scatter | solution.py:793
  113.5 39.5 %collective-permute-start.5 = (bf16[512,1024]{1,0:T(8,128)(2,1)}, bf16[512,1024]{1,0:T(8,128)(2,1)}, u32[]{:S(2)}, u32[]{:S(2)}) collective-permute-start(bf16[512,1024]{1,0:T(8,128)(2,1)} %shard_map.212.refs_3_.refs_4_), channel_id=1, source_target_pairs={{0,2},{2,0},{1,3},{3,1},{4,6},{6,4},{5,7},{7,5},{8,10},{10,8},{9,1... | collective-permute-start | bytes 3145736 | tf_op jit(solution)/shard_map/ppermute | solution.py:787
  136.0 53.7 %collective-permute-start.7 = (bf16[512,2304]{1,0:T(8,128)(2,1)}, bf16[512,2304]{1,0:T(8,128)(2,1)}, u32[]{:S(2)}, u32[]{:S(2)}) collective-permute-start(bf16[512,2304]{1,0:T(8,128)(2,1)} %shard_map.217.refs_6_), channel_id=1, source_target_pairs={{0,4},{4,0},{1,5},{5,1},{2,6},{6,2},{3,7},{7,3},{8,12},{12,8},{9,1... | collective-permute-start | bytes 7077896 | tf_op jit(solution)/shard_map/ppermute | solution.py:784
  162.9 36.6 %collective-permute-start.6 = (bf16[384,2048]{1,0:T(8,128)(2,1)}, bf16[384,2048]{1,0:T(8,128)(2,1)}, u32[]{:S(2)}, u32[]{:S(2)}) collective-permute-start(bf16[384,2048]{1,0:T(8,128)(2,1)} %get-tuple-element.61), channel_id=1, source_target_pairs={{0,1},{1,0},{2,3},{3,2},{4,5},{5,4},{6,7},{7,6},{8,9},{9,8},{10,11... | collective-permute-start | bytes 4718600 | tf_op jit(solution)/shard_map/ppermute | solution.py:805
  187.4 58.6 %collective-permute-start.10 = (bf16[512,2304]{1,0:T(8,128)(2,1)S(1)}, bf16[512,2304]{1,0:T(8,128)(2,1)}, u32[]{:S(2)}, u32[]{:S(2)}) collective-permute-start(bf16[512,2304]{1,0:T(8,128)(2,1)S(1)} %shard_map.220.refs_1_), channel_id=1, source_target_pairs={{0,4},{4,0},{1,5},{5,1},{2,6},{6,2},{3,7},{7,3},{8,12},{12,8},{9,1... | collective-permute-start | bytes 7077896 | tf_op jit(solution)/shard_map/ppermute | solution.py:784
  189.7 58.2 %collective-permute-start.9 = (bf16[512,2304]{1,0:T(8,128)(2,1)}, bf16[512,2304]{1,0:T(8,128)(2,1)}, u32[]{:S(2)}, u32[]{:S(2)}) collective-permute-start(bf16[512,2304]{1,0:T(8,128)(2,1)} %shard_map.221.refs_4_.refs_8_.refs_12_.refs_10_.refs_14_.refs_6_), channel_id=1, source_target_pairs={{0,2},{2,0},{1,3},{3,1},{4,6},{6,4},{5,7},{7,5},{8,10},{10,8},{9,1... | collective-permute-start | bytes 7077896 | tf_op jit(solution)/shard_map/ppermute | solution.py:787
  205.1 35.9 %collective-permute-start.8 = (bf16[384,2048]{1,0:T(8,128)(2,1)}, bf16[384,2048]{1,0:T(8,128)(2,1)}, u32[]{:S(2)}, u32[]{:S(2)}) collective-permute-start(bf16[384,2048]{1,0:T(8,128)(2,1)} %get-tuple-element.63.refs_2_.refs_1_), channel_id=1, source_target_pairs={{0,1},{1,0},{2,3},{3,2},{4,5},{5,4},{6,7},{7,6},{8,9},{9,8},{10,11... | collective-permute-start | bytes 4718600 | tf_op jit(solution)/shard_map/ppermute | solution.py:805
  239.5 72.1 %collective-permute-start.12 = (bf16[512,2304]{1,0:T(8,128)(2,1)}, bf16[512,2304]{1,0:T(8,128)(2,1)}, u32[]{:S(2)}, u32[]{:S(2)}) collective-permute-start(bf16[512,2304]{1,0:T(8,128)(2,1)} %shard_map.223.refs_3_), channel_id=1, source_target_pairs={{0,4},{4,0},{1,5},{5,1},{2,6},{6,2},{3,7},{7,3},{8,12},{12,8},{9,1... | collective-permute-start | bytes 7077896 | tf_op jit(solution)/shard_map/ppermute | solution.py:784
  300.1 100.2 %reduce-scatter.10.cloned.1.call-start = ((), (), s32[]{:S(2)}) async-start(), calls=%async_computation.14 | async-start | bytes 2949120 | tf_op jit(solution)/shard_map/reduce_scatter | solution.py:793
  311.8 38.5 %collective-permute-start.15 = (bf16[512,1536]{1,0:T(8,128)(2,1)}, bf16[512,1536]{1,0:T(8,128)(2,1)}, u32[]{:S(2)}, u32[]{:S(2)}) collective-permute-start(bf16[512,1536]{1,0:T(8,128)(2,1)} %shard_map.229.refs_6_), channel_id=1, source_target_pairs={{0,4},{4,0},{1,5},{5,1},{2,6},{6,2},{3,7},{7,3},{8,12},{12,8},{9,1... | collective-permute-start | bytes 4718600 | tf_op jit(solution)/shard_map/ppermute | solution.py:784
  314.2 186.1 %reduce-scatter.18.cloned.1.call-start = ((), (), s32[]{:S(2)}) async-start(), calls=%async_computation.18 | async-start | bytes 2949120 | tf_op jit(solution)/shard_map/reduce_scatter | solution.py:793
  342.3 82.6 %collective-permute-start.21 = (bf16[512,2304]{1,0:T(8,128)(2,1)}, bf16[512,2304]{1,0:T(8,128)(2,1)}, u32[]{:S(2)}, u32[]{:S(2)}) collective-permute-start(bf16[512,2304]{1,0:T(8,128)(2,1)} %get-tuple-element.72.refs_1_), channel_id=1, source_target_pairs={{0,4},{4,0},{1,5},{5,1},{2,6},{6,2},{3,7},{7,3},{8,12},{12,8},{9,1... | collective-permute-start | bytes 7077896 | tf_op jit(solution)/shard_map/ppermute | solution.py:784
  348.8 76.1 %collective-permute-start.22 = (bf16[128,2304]{1,0:T(8,128)(2,1)}, bf16[128,2304]{1,0:T(8,128)(2,1)}, u32[]{:S(2)}, u32[]{:S(2)}) collective-permute-start(bf16[128,2304]{1,0:T(8,128)(2,1)} %shard_map.235.refs_1_), channel_id=1, source_target_pairs={{0,4},{4,0},{1,5},{5,1},{2,6},{6,2},{3,7},{7,3},{8,12},{12,8},{9,1... | collective-permute-start | bytes 1769480 | tf_op jit(solution)/shard_map/ppermute | solution.py:784
  357.8 42.5 %collective-permute-start.18 = (bf16[1024,2304]{1,0:T(8,128)(2,1)}, bf16[1024,2304]{1,0:T(8,128)(2,1)}, u32[]{:S(2)}, u32[]{:S(2)}) collective-permute-start(bf16[1024,2304]{1,0:T(8,128)(2,1)} %shard_map.237.refs_15_), channel_id=1, source_target_pairs={{0,2},{2,0},{1,3},{3,1},{4,6},{6,4},{5,7},{7,5},{8,10},{10,8},{9,1... | collective-permute-start | bytes 14155784 | tf_op jit(solution)/shard_map/ppermute | solution.py:787
  398.9 37.1 %collective-permute-start.20 = (bf16[384,2048]{1,0:T(8,128)(2,1)}, bf16[384,2048]{1,0:T(8,128)(2,1)}, u32[]{:S(2)}, u32[]{:S(2)}) collective-permute-start(bf16[384,2048]{1,0:T(8,128)(2,1)} %get-tuple-element.81), channel_id=1, source_target_pairs={{0,1},{1,0},{2,3},{3,2},{4,5},{5,4},{6,7},{7,6},{8,9},{9,8},{10,11... | collective-permute-start | bytes 4718600 | tf_op jit(solution)/shard_map/ppermute | solution.py:805
  415.6 57.3 %collective-permute-start.25 = (bf16[512,2304]{1,0:T(8,128)(2,1)}, bf16[512,2304]{1,0:T(8,128)(2,1)}, u32[]{:S(2)}, u32[]{:S(2)}) collective-permute-start(bf16[512,2304]{1,0:T(8,128)(2,1)} %get-tuple-element.80.refs_5_), channel_id=1, source_target_pairs={{0,4},{4,0},{1,5},{5,1},{2,6},{6,2},{3,7},{7,3},{8,12},{12,8},{9,1... | collective-permute-start | bytes 7077896 | tf_op jit(solution)/shard_map/ppermute | solution.py:784
  429.1 127.8 %reduce-scatter.20.cloned.1.call-start = ((), (), s32[]{:S(2)}) async-start(), calls=%async_computation.19 | async-start | bytes 2949120 | tf_op jit(solution)/shard_map/reduce_scatter | solution.py:793
  443.8 37.7 %collective-permute-start.24 = (bf16[384,2048]{1,0:T(8,128)(2,1)}, bf16[384,2048]{1,0:T(8,128)(2,1)}, u32[]{:S(2)}, u32[]{:S(2)}) collective-permute-start(bf16[384,2048]{1,0:T(8,128)(2,1)} %get-tuple-element.83.refs_6_.refs_1_), channel_id=1, source_target_pairs={{0,1},{1,0},{2,3},{3,2},{4,5},{5,4},{6,7},{7,6},{8,9},{9,8},{10,11... | collective-permute-start | bytes 4718600 | tf_op jit(solution)/shard_map/ppermute | solution.py:805
  454.3 57.1 %collective-permute-start.26 = (bf16[512,1536]{1,0:T(8,128)(2,1)}, bf16[512,1536]{1,0:T(8,128)(2,1)}, u32[]{:S(2)}, u32[]{:S(2)}) collective-permute-start(bf16[512,1536]{1,0:T(8,128)(2,1)} %get-tuple-element.84.refs_21_), channel_id=1, source_target_pairs={{0,4},{4,0},{1,5},{5,1},{2,6},{6,2},{3,7},{7,3},{8,12},{12,8},{9,1... | collective-permute-start | bytes 4718600 | tf_op jit(solution)/shard_map/ppermute | solution.py:784
  471.9 122.4 %collective-permute-start.23 = (bf16[384,2048]{1,0:T(8,128)(2,1)}, bf16[384,2048]{1,0:T(8,128)(2,1)}, u32[]{:S(2)}, u32[]{:S(2)}) collective-permute-start(bf16[384,2048]{1,0:T(8,128)(2,1)} %get-tuple-element.86), channel_id=1, source_target_pairs={{0,1},{1,0},{2,3},{3,2},{4,5},{5,4},{6,7},{7,6},{8,9},{9,8},{10,11... | collective-permute-start | bytes 4718600 | tf_op jit(solution)/shard_map/ppermute | solution.py:805
  477.0 85.4 %reduce-scatter.12.cloned.1.call-start = ((), (), s32[]{:S(2)}) async-start(), calls=%async_computation.15 | async-start | bytes 1966080 | tf_op jit(solution)/shard_map/reduce_scatter | solution.py:793
  510.4 48.8 %collective-permute-start.29 = (bf16[512,1024]{1,0:T(8,128)(2,1)}, bf16[512,1024]{1,0:T(8,128)(2,1)}, u32[]{:S(2)}, u32[]{:S(2)}) collective-permute-start(bf16[512,1024]{1,0:T(8,128)(2,1)} %get-tuple-element.90.refs_2_), channel_id=1, source_target_pairs={{0,4},{4,0},{1,5},{5,1},{2,6},{6,2},{3,7},{7,3},{8,12},{12,8},{9,1... | collective-permute-start | bytes 3145736 | tf_op jit(solution)/shard_map/ppermute | solution.py:784
  515.2 91.2 %reduce-scatter.14.cloned.1.call-start = ((), (), s32[]{:S(2)}) async-start(), calls=%async_computation.16 | async-start | bytes 1310720 | tf_op jit(solution)/shard_map/reduce_scatter | solution.py:793
  566.9 83.9 %reduce-scatter.16.cloned.1.call-start = ((), (), s32[]{:S(2)}) async-start(), calls=%async_computation.17 | async-start | bytes 1638400 | tf_op jit(solution)/shard_map/reduce_scatter | solution.py:793
  588.7 35.9 %collective-permute-start.30 = (bf16[384,2048]{1,0:T(8,128)(2,1)}, bf16[384,2048]{1,0:T(8,128)(2,1)S(1)}, u32[]{:S(2)}, u32[]{:S(2)}) collective-permute-start(bf16[384,2048]{1,0:T(8,128)(2,1)} %get-tuple-element.97), channel_id=1, source_target_pairs={{0,1},{1,0},{2,3},{3,2},{4,5},{5,4},{6,7},{7,6},{8,9},{9,8},{10,11... | collective-permute-start | bytes 4718600 | tf_op jit(solution)/shard_map/ppermute | solution.py:805
  (132 other events, 1628.7 us)
Sparse Core Ops, SparseCore 0:
  9.6 31.7 all-gather.8
  43.6 33.3 all-gather.6
  79.2 50.6 all-gather.10
  132.0 50.5 all-gather.12
  184.5 50.5 all-gather.14
  237.1 40.7 all-gather.16
  300.2 46.8 reduce-scatter.7
  349.5 47.5 reduce-scatter.9
  429.2 45.7 reduce-scatter.17
  477.2 47.5 reduce-scatter.19
  527.6 34.7 reduce-scatter.11
  567.1 26.0 reduce-scatter.13
  613.8 30.4 reduce-scatter.15

commit v6 on v5

--- a/solution.py
+++ b/solution.py
@@ -841,8 +841,8 @@
             along[i] = gather(order(lambda deps: stack(parts, deps)))
 
         tiles = outer if tokens.shape[1] // (4 * outer) % 128 == 0 else 0
-        along["o"] = gather(o_weight)
         along["qkv"] = gather(order(lambda deps: stack([q_weight, k_weight, v_weight], deps)))
+        along["o"] = gather(order(lambda deps: stack([o_weight], deps)))
         for i in range(CHUNKS):
             chunk(i)
         attention_gain = relative(attention_gain[None])
@@ -851,38 +851,36 @@
             tokens, out_grad = relative(tokens), relative(out_grad)
         tokens, normed_first = order(lambda deps: enter(spot, tiles, tokens, attention_gain, deps))
         normed_other = swap(normed_first)
+        segment_row = segments[0]
+        cosine, sine = rotary_tables(segment_row)
+        first_seen = first_blocks(segment_row)
+        spread("qkv")
         if tiles:
             out_grad = order(lambda deps: to_order(spot, tiles, out_grad, deps))
         grad_other = swap(out_grad)
-        segment_row = segments[0]
-        cosine, sine = rotary_tables(segment_row)
-        first_seen = first_blocks(segment_row)
-        spread("o")
-        spread("qkv")
         order.wait(cosine, sine, first_seen)
-        land("o")
-        grad_seq = order(lambda deps: join(here, out_grad, grad_other, deps))
         normed_seq = order(lambda deps: join(spot, normed_first, normed_other, deps))
         land("qkv")
+        spread("o")
         rotated = order(
             lambda deps: project(
                 spot, normed_first, normed_other, full["qkv"], deps, (cosine, sine),
                 (query_width + key_width) // 128,
             )
         )
-        spread(0)
         mixed, log_totals = order(
             lambda deps: attend(rotated, query_width, first_seen, segment_row, score_scale, deps)
         )
+        land("o")
+        grad_seq = order(lambda deps: join(here, out_grad, grad_other, deps))
         own, sent = order(lambda deps: back(spot, (mixed,), ((full["o"], 0),), deps, True))
         other = swap(sent)
+        spread(0)
+        normed_second, middle = order(lambda deps: middle_forward(tokens, own, other, feed_gain, deps))
+        normed_third = swap(normed_second)
         spread(1)
         land(0)
-        normed_second, middle = order(lambda deps: middle_forward(tokens, own, other, feed_gain, deps))
-        normed_third = swap(normed_second)
-        spread(2)
         normed_feed = order(lambda deps: join(here, normed_second, normed_third, deps))
-        land(1)
         hidden, gate_grad, up_grad = {}, {}, {}
         from_core, to_x, from_x, kept, summed = {}, {}, {}, {}, {}
 
@@ -915,26 +913,27 @@
 
         run_feed(0)
         core_part(0)
+        spread(2)
+        land(1)
         run_feed(1)
+        core_part(1)
         spread(3)
         x_part(0)
         sent_along, kept_along = scatter(to_x[0]), scatter(kept[0])
-        core_part(1)
         land(2)
         run_feed(2)
         x_part(1)
         send_x(1)
+        core_part(2)
+        land(3)
+        run_feed(3)
         from_along = over_x(order(lambda deps: gate(sent_along, deps)))
-        land(3)
-        core_part(2)
-        run_feed(3)
         own, sent = feed_back(range(CHUNKS))
         other = swap(sent)
-        order.wait(kept_along)
         x_part(2)
         send_x(2)
         core_part(3)
-        order.wait(from_along)
+        order.wait(from_along, kept_along)
         finish(1)
         attn_out_grad, middle_grad, feed_gain_part = order(
             lambda deps: middle_backward(own, other, middle, out_grad, feed_gain, deps)

time: 669 us -> 656 us (0.981)
  waiting for transfers between devices: 174 us -> 163 us
  Pallas kernels: 365 us -> 373 us
    all_gather x6, waiting for transfers between devices: 94.6 us -> 33.4 us  [gather(): return lax.all_gather(operand, ('core', 'z'), axis=0, tiled=True)]
    ppermute x8, waiting for transfers between devices: 38.8 us -> 76.1 us  [swap(): return lax.ppermute(own, 'tensor', SWAP)]
    ppermute x12, waiting for transfers between devices: 21.2 us -> 35 us  [over_x(): return lax.ppermute(array, 'x', SWAP)]
    pallas_call x58 -> x59, Pallas kernels: 365 us -> 373 us  [launch(): pl.pallas_call(body, grid_spec=pltpu.PrefetchScalarGridSpec(num_scalar_pr...]
    unnamed x228 -> x220, local copies, waits for them, and re-layouts: 53.4 us -> 49.1 us
  transfers between devices with their start and end apart: 50 -> 50, of which waited for: 22 -> 22; matrix products, arithmetic and copies ran while one was open for 2% -> 2% of each run, Pallas kernels for 55% -> 57%
where the time goes in v6:
time: 656 us; the launch traced here: 648 us
  Pallas kernels  373 us (57%)
  waiting for transfers between devices  163 us (25%)
  local copies, waits for them, and re-layouts  53.7 us (8%)
  starting transfers between devices  31.3 us (5%)
  between operations  15.3 us (2%)
  other arithmetic  12 us (2%)
    pallas_call x59, Pallas kernels, launch(): pl.pallas_call(body, grid_spec=pltpu.PrefetchScalarGridSpec(num_scalar_pr...  373 us
    ppermute x8, waiting for transfers between devices, swap(): return lax.ppermute(own, 'tensor', SWAP)  76.1 us
    unnamed x220, local copies, waits for them, and re-layouts  49.1 us
    ppermute x12, waiting for transfers between devices, over_x(): return lax.ppermute(array, 'x', SWAP)  35 us
    all_gather x6, waiting for transfers between devices, gather(): return lax.all_gather(operand, ('core', 'z'), axis=0, tiled=True)  33.4 us
  transfers between devices with their start and end apart: 50, of which 22 were waited for; matrix products, arithmetic and copies ran while one was open for 2% of the time, Pallas kernels for 57%

profile of v6, /device:TPU:0, one launch (start us, length us, event | category | flops | bytes accessed | tf_op | source)
XLA Modules:
  0.0 648.1 jit_solution(16585461438454152587)
XLA Ops:
  27.7 19.5 %all-gather.7.cloned.1.call-done.refs_1_.refs_3_.refs_5_.refs_4_.refs_6_.refs_8_.refs_10_.refs_12_.refs_14_ = bf16[1024,1280]{1,0:T(8,128)(2,1)} async-done(((bf16[128,1280]{1,0:T(8,128)(2,1)}), bf16[1024,1280]{1,0:T(8,128)(2,1)}) %all-gather.7.cloned.1.call-update) | async-done | bytes 2621456 | tf_op jit(solution)/shard_map/all_gather | solution.py:790
  64.5 17.6 %collective-permute-done.1.refs_0_ = bf16[512,1280]{1,0:T(8,128)(2,1)} collective-permute-done((bf16[512,1280]{1,0:T(8,128)(2,1)S(1)}, bf16[512,1280]{1,0:T(8,128)(2,1)}, u32[]{:S(2)}, u32[]{:S(2)}) %collective-permute-start.1) | collective-permute-done | bytes 1310752 | tf_op jit(solution)/shard_map/ppermute | solution.py:784
  89.2 10.7 %shard_map.215.refs_1_.refs_2_.refs_3_.refs_6_ = bf16[768,1280]{1,0:T(8,128)(2,1)} custom-call(s32[3]{0:T(128)S(1)} %pad_add_fusion.refs_0_, bf16[384,2048]{1,0:T(8,128)(2,1)} %get-tuple-element.58.refs_1_, bf16[384,2048]{1,0:T(8,128)(2,1)} %copy-done.27, ...), custom_call_target="tpu_custom_call" | custom-call | flops 100663296000 | bytes 1024 | tf_op jit(solution)/shard_map/pallas_call | solution.py:178
  101.5 15.9 %shard_map.216 = (bf16[768,1024]{1,0:T(8,128)(2,1)S(1)}, f32[768,256]{1,0:T(8,128)S(1)}) custom-call(s32[3]{0:T(128)S(1)} %convert_reduce_fusion.1.refs_6_.refs_0_, bf16[768,1280]{1,0:T(8,128)(2,1)S(1)} %copy-done.94, bf16[768,1280]{1,0:T(8,128)(2,1)S(1)} %copy-done.94, bf16[768,1280]{1,0:T(8,128)(2,1)S(1)} %copy-done.94, ...), custom_call_target="tpu_custom_call" | custom-call | flops 160000000000 | bytes 1024 | tf_op jit(solution)/shard_map/pallas_call | solution.py:178
  123.5 9.2 %shard_map.219 = (f32[384,2048]{1,0:T(8,128)}, bf16[384,2048]{1,0:T(8,128)(2,1)}) custom-call(s32[3]{0:T(128)S(1)} %pad_add_fusion.refs_0_, bf16[768,1024]{1,0:T(8,128)(2,1)S(1)} %get-tuple-element.59.refs_1_, bf16[1024,1024]{1,0:T(8,128)(2,1)} %all-gather.9.cloned.1.call-done.refs_1_.refs_2_.refs_4_.refs_3_.refs_5_, ...), custom_call_target="tpu_custom_call" | custom-call | flops 56512729088 | bytes 1024 | tf_op jit(solution)/shard_map/pallas_call | solution.py:178
  141.0 28.6 %collective-permute-done.6.refs_2_ = bf16[384,2048]{1,0:T(8,128)(2,1)} collective-permute-done((bf16[384,2048]{1,0:T(8,128)(2,1)}, bf16[384,2048]{1,0:T(8,128)(2,1)}, u32[]{:S(2)}, u32[]{:S(2)}) %collective-permute-start.6) | collective-permute-done | bytes 1572896 | tf_op jit(solution)/shard_map/ppermute | solution.py:805
  176.7 6.2 all-gather.13.cloned.1.call-done.refs_1_.refs_3_.refs_5_.refs_7_.refs_9_.refs_11_.refs_13_.refs_17_.refs_19_.refs_21_.refs_23_
  188.8 6.2 collective-permute-done.8.refs_0_
  195.0 16.3 %collective-permute-done.7.refs_2_ = bf16[384,2048]{1,0:T(8,128)(2,1)} collective-permute-done((bf16[384,2048]{1,0:T(8,128)(2,1)}, bf16[384,2048]{1,0:T(8,128)(2,1)}, u32[]{:S(2)}, u32[]{:S(2)}) %collective-permute-start.7) | collective-permute-done | bytes 1572896 | tf_op jit(solution)/shard_map/ppermute | solution.py:805
  217.5 13.1 %shard_map.225 = (bf16[768,768]{1,0:T(8,128)(2,1)S(1)}, bf16[768,768]{1,0:T(8,128)(2,1)S(1)}, bf16[768,768]{1,0:T(8,128)(2,1)S(1)}) custom-call(s32[3]{0:T(128)S(1)} %pad_add_fusion.refs_0_, bf16[768,2048]{1,0:T(8,128)(2,1)} %shard_map.224.refs_1_.refs_15_.refs_0_, bf16[768,2048]{1,0:T(8,128)(2,1)} %shard_map.218.refs_6_.refs_2_.refs_1_, ...), custom_call_target="tpu_custom_call" | custom-call | flops 120795955200 | bytes 1024 | tf_op jit(solution)/shard_map/pallas_call | solution.py:178
  230.6 7.4 %shard_map.226.refs_2_ = bf16[1024,2304]{1,0:T(8,128)(2,1)} custom-call(bf16[768,2048]{1,0:T(8,128)(2,1)} %shard_map.224.refs_1_.refs_15_.refs_0_, bf16[768,2048]{1,0:T(8,128)(2,1)} %shard_map.218.refs_6_.refs_2_.refs_1_, bf16[768,768]{1,0:T(8,128)(2,1)S(1)} %get-tuple-element.65.refs_2_.refs_1_, bf16[768,768]{1,0:T(8,128)(2,1)S(1)} %get-tuple-element.66.refs_3_.refs_2_, ...), custom_call_target="tpu_custom_call" | custom-call | flops 75497472000 | bytes 1024 | tf_op jit(solution)/shard_map/pallas_call | solution.py:178
  251.8 13.1 %shard_map.229 = (bf16[768,768]{1,0:T(8,128)(2,1)S(1)}, bf16[768,768]{1,0:T(8,128)(2,1)S(1)}, bf16[768,768]{1,0:T(8,128)(2,1)S(1)}) custom-call(s32[3]{0:T(128)S(1)} %pad_add_fusion.refs_0_, bf16[768,2048]{1,0:T(8,128)(2,1)} %shard_map.224.refs_1_.refs_15_.refs_0_, bf16[768,2048]{1,0:T(8,128)(2,1)} %shard_map.218.refs_6_.refs_2_.refs_1_, ...), custom_call_target="tpu_custom_call" | custom-call | flops 120795955200 | bytes 1024 | tf_op jit(solution)/shard_map/pallas_call | solution.py:178
  264.9 7.2 %shard_map.230.refs_2_ = bf16[1024,2304]{1,0:T(8,128)(2,1)} custom-call(bf16[768,2048]{1,0:T(8,128)(2,1)} %shard_map.224.refs_1_.refs_15_.refs_0_, bf16[768,2048]{1,0:T(8,128)(2,1)} %shard_map.218.refs_6_.refs_2_.refs_1_, bf16[768,768]{1,0:T(8,128)(2,1)S(1)} %get-tuple-element.68.refs_2_.refs_3_, bf16[768,768]{1,0:T(8,128)(2,1)S(1)} %get-tuple-element.69.refs_3_.refs_4_, ...), custom_call_target="tpu_custom_call" | custom-call | flops 75497472000 | bytes 1024 | tf_op jit(solution)/shard_map/pallas_call | solution.py:178
  275.2 7.7 %all-gather.17.cloned.1.call-done.refs_1_.refs_3_.refs_5_.refs_7_.refs_9_.refs_11_.refs_13_.refs_33_.refs_35_.refs_37_.refs_39_.refs_17_.refs_19_ = bf16[1024,1536]{1,0:T(8,128)(2,1)} async-done(((bf16[128,1536]{1,0:T(8,128)(2,1)}), bf16[1024,1536]{1,0:T(8,128)(2,1)}) %all-gather.17.cloned.1.call-update) | async-done | bytes 3145744 | tf_op jit(solution)/shard_map/all_gather | solution.py:790
  287.1 10.5 %shard_map.232 = (bf16[512,2304]{1,0:T(8,128)(2,1)}, bf16[512,2304]{1,0:T(8,128)(2,1)}) custom-call(bf16[768,2048]{1,0:T(8,128)(2,1)} %shard_map.224.refs_1_.refs_15_.refs_0_, bf16[768,2048]{1,0:T(8,128)(2,1)} %shard_map.218.refs_6_.refs_2_.refs_1_, bf16[768,768]{1,0:T(8,128)(2,1)S(1)} %copy-done.81, bf16[768,768]{1,0:T(8,128)(2,1)S(1)} %copy-done.84, ...), custom_call_target="tpu_custom_call" | custom-call | flops 75497472000 | bytes 1024 | tf_op jit(solution)/shard_map/pallas_call | solution.py:178
  306.3 13.4 %shard_map.234 = (bf16[768,768]{1,0:T(8,128)(2,1)S(1)}, bf16[768,768]{1,0:T(8,128)(2,1)S(1)}, bf16[768,768]{1,0:T(8,128)(2,1)S(1)}) custom-call(s32[3]{0:T(128)S(1)} %pad_add_fusion.refs_0_, bf16[768,2048]{1,0:T(8,128)(2,1)} %shard_map.224.refs_1_.refs_15_.refs_0_, bf16[768,2048]{1,0:T(8,128)(2,1)} %shard_map.218.refs_6_.refs_2_.refs_1_, ...), custom_call_target="tpu_custom_call" | custom-call | flops 120795955200 | bytes 1024 | tf_op jit(solution)/shard_map/pallas_call | solution.py:178
  319.8 11.7 %shard_map.235 = (bf16[512,2304]{1,0:T(8,128)(2,1)}, bf16[512,2304]{1,0:T(8,128)(2,1)}) custom-call(bf16[768,2048]{1,0:T(8,128)(2,1)} %shard_map.224.refs_1_.refs_15_.refs_0_, bf16[768,2048]{1,0:T(8,128)(2,1)} %shard_map.218.refs_6_.refs_2_.refs_1_, bf16[768,768]{1,0:T(8,128)(2,1)S(1)} %copy-done.90, bf16[768,768]{1,0:T(8,128)(2,1)S(1)} %copy-done.93, ...), custom_call_target="tpu_custom_call" | custom-call | flops 75497472000 | bytes 1024 | tf_op jit(solution)/shard_map/pallas_call | solution.py:178
  331.5 7.2 %shard_map.236.refs_1_ = bf16[1024,2304]{1,0:T(8,128)(2,1)} custom-call(bf16[768,2048]{1,0:T(8,128)(2,1)} %shard_map.224.refs_1_.refs_15_.refs_0_, bf16[768,2048]{1,0:T(8,128)(2,1)} %shard_map.218.refs_6_.refs_2_.refs_1_, bf16[768,768]{1,0:T(8,128)(2,1)S(1)} %get-tuple-element.72.refs_2_.refs_5_, bf16[768,768]{1,0:T(8,128)(2,1)S(1)} %get-tuple-element.73.refs_3_.refs_6_, ...), custom_call_target="tpu_custom_call" | custom-call | flops 75497472000 | bytes 1024 | tf_op jit(solution)/shard_map/pallas_call | solution.py:178
  342.4 10.3 %shard_map.238 = (bf16[768,512]{1,0:T(8,128)(2,1)S(1)}, bf16[768,512]{1,0:T(8,128)(2,1)S(1)}, bf16[768,512]{1,0:T(8,128)(2,1)S(1)}) custom-call(s32[3]{0:T(128)S(1)} %pad_add_fusion.refs_0_, bf16[768,2048]{1,0:T(8,128)(2,1)} %shard_map.224.refs_1_.refs_15_.refs_0_, bf16[768,2048]{1,0:T(8,128)(2,1)} %shard_map.218.refs_6_.refs_2_.refs_1_, ...), custom_call_target="tpu_custom_call" | custom-call | flops 80530636800 | bytes 1024 | tf_op jit(solution)/shard_map/pallas_call | solution.py:178
  356.2 30.1 %shard_map.240 = (f32[384,2048]{1,0:T(8,128)}, bf16[384,2048]{1,0:T(8,128)(2,1)}) custom-call(s32[3]{0:T(128)S(1)} %pad_add_fusion.refs_0_, bf16[768,768]{1,0:T(8,128)(2,1)S(1)} %copy-done.82, bf16[768,768]{1,0:T(8,128)(2,1)S(1)} %copy-done.85, bf16[768,768]{1,0:T(8,128)(2,1)S(1)} %copy-done.91, bf16[768,768]{1,0:T(8,128)(2,1)} %copy-done.92, ...), custom_call_target="tpu_custom_call" | custom-call | flops 310820012032 | bytes 1024 | tf_op jit(solution)/shard_map/pallas_call | solution.py:178
  387.9 10.5 %shard_map.241 = (bf16[512,2304]{1,0:T(8,128)(2,1)}, bf16[512,2304]{1,0:T(8,128)(2,1)}) custom-call(bf16[768,2048]{1,0:T(8,128)(2,1)} %shard_map.224.refs_1_.refs_15_.refs_0_, bf16[768,2048]{1,0:T(8,128)(2,1)} %shard_map.218.refs_6_.refs_2_.refs_1_, bf16[768,768]{1,0:T(8,128)(2,1)S(1)} %copy-done.74, bf16[768,768]{1,0:T(8,128)(2,1)S(1)} %copy-done.76, ...), custom_call_target="tpu_custom_call" | custom-call | flops 75497472000 | bytes 1024 | tf_op jit(solution)/shard_map/pallas_call | solution.py:178
  411.4 11.8 %collective-permute-done.20.refs_1_ = bf16[384,2048]{1,0:T(8,128)(2,1)} collective-permute-done((bf16[384,2048]{1,0:T(8,128)(2,1)}, bf16[384,2048]{1,0:T(8,128)(2,1)}, u32[]{:S(2)}, u32[]{:S(2)}) %collective-permute-start.20) | collective-permute-done | bytes 1572896 | tf_op jit(solution)/shard_map/ppermute | solution.py:805
  423.1 8.0 %shard_map.244 = (bf16[384,2048]{1,0:T(8,128)(2,1)}, f32[384,2048]{1,0:T(8,128)}, f32[1,2048]{1,0:T(1,128)S(1)}) custom-call(f32[384,2048]{1,0:T(8,128)} %get-tuple-element.78.refs_6_.refs_0_, bf16[384,2048]{1,0:T(8,128)(2,1)} %collective-permute-done.20.refs_1_, f32[384,2048]{1,0:T(8,128)} %get-tuple-element.62.refs_2_.refs_1_, ...), custom_call_target="tpu_custom_call" | custom-call | flops 80000000000 | bytes 1024 | tf_op jit(solution)/shard_map/pallas_call | solution.py:178
  432.8 7.8 %shard_map.245 = (bf16[512,1536]{1,0:T(8,128)(2,1)}, bf16[512,1536]{1,0:T(8,128)(2,1)S(1)}) custom-call(bf16[768,2048]{1,0:T(8,128)(2,1)} %shard_map.224.refs_1_.refs_15_.refs_0_, bf16[768,2048]{1,0:T(8,128)(2,1)} %shard_map.218.refs_6_.refs_2_.refs_1_, bf16[768,512]{1,0:T(8,128)(2,1)S(1)} %copy-done.66, bf16[768,512]{1,0:T(8,128)(2,1)S(1)} %copy-done.69, ...), custom_call_target="tpu_custom_call" | custom-call | flops 50331648000 | bytes 1024 | tf_op jit(solution)/shard_map/pallas_call | solution.py:178
  441.6 16.5 %shard_map.246 = (f32[384,2048]{1,0:T(8,128)}, bf16[384,2048]{1,0:T(8,128)(2,1)}) custom-call(s32[3]{0:T(128)S(1)} %pad_add_fusion.refs_0_, bf16[768,768]{1,0:T(8,128)(2,1)S(1)} %copy-done.79, bf16[768,768]{1,0:T(8,128)(2,1)S(1)} %copy-done.88, bf16[768,768]{1,0:T(8,128)(2,1)S(1)} %copy-done.72, bf16[768,512]{1,0:T(8,128)(2,1)S(1)} %get-tuple-element.75.refs_1_.refs_4_, ...), custom_call_target="tpu_custom_call" | custom-call | flops 155410006016 | bytes 1024 | tf_op jit(solution)/shard_map/pallas_call | solution.py:178
  478.7 7.1 %shard_map.250.refs_3_.refs_4_ = bf16[768,1024]{1,0:T(8,128)(2,1)S(1)} custom-call(s32[3]{0:T(128)S(1)} %pad_add_fusion.refs_0_, bf16[384,2048]{1,0:T(8,128)(2,1)} %get-tuple-element.83.refs_6_.refs_1_, bf16[384,2048]{1,0:T(8,128)(2,1)} %collective-permute-done.24.refs_2_, ...), custom_call_target="tpu_custom_call" | custom-call | flops 80530636800 | bytes 1024 | tf_op jit(solution)/shard_map/pallas_call | solution.py:178
  505.6 35.4 %shard_map.253 = (bf16[768,1024]{1,0:T(8,128)(2,1)S(1)}, bf16[768,128]{1,0:T(8,128)(2,1)S(1)}, bf16[768,128]{1,0:T(8,128)(2,1)S(1)}) custom-call(s32[3]{0:T(128)S(1)} %copy-done.40, bf16[768,1280]{1,0:T(8,128)(2,1)} %shard_map.215.refs_1_.refs_2_.refs_3_.refs_6_, bf16[768,1280]{1,0:T(8,128)(2,1)} %shard_map.215.refs_1_.refs_2_.refs_3_.refs_6_, ...), custom_call_target="tpu_custom_call" | custom-call | flops 349999988736 | bytes 1024 | tf_op jit(solution)/shard_map/pallas_call | solution.py:178
  554.0 7.6 %shard_map.256 = (bf16[512,1280]{1,0:T(8,128)(2,1)}, bf16[512,1280]{1,0:T(8,128)(2,1)S(1)}) custom-call(bf16[768,2048]{1,0:T(8,128)(2,1)} %shard_map.212.refs_1_.refs_0_, bf16[768,1024]{1,0:T(8,128)(2,1)S(1)} %get-tuple-element.91.refs_1_.refs_4_, bf16[768,128]{1,0:T(8,128)(2,1)S(1)} %get-tuple-element.92.refs_2_, ...), custom_call_target="tpu_custom_call" | custom-call | flops 41943040000 | bytes 1024 | tf_op jit(solution)/shard_map/pallas_call | solution.py:178
  563.4 11.6 %shard_map.257 = (f32[384,2048]{1,0:T(8,128)}, bf16[384,2048]{1,0:T(8,128)(2,1)}) custom-call(s32[3]{0:T(128)S(1)} %copy-done.19, bf16[768,1024]{1,0:T(8,128)(2,1)} %copy-done, bf16[768,128]{1,0:T(8,128)(2,1)S(1)} %get-tuple-element.92.refs_2_, bf16[768,128]{1,0:T(8,128)(2,1)S(1)} %get-tuple-element.93.refs_3_, ...), custom_call_target="tpu_custom_call" | custom-call | flops 70640910336 | bytes 1024 | tf_op jit(solution)/shard_map/pallas_call | solution.py:178
  585.5 8.3 %collective-permute-done.31.refs_1_ = bf16[512,1280]{1,0:T(8,128)(2,1)} collective-permute-done((bf16[512,1280]{1,0:T(8,128)(2,1)}, bf16[512,1280]{1,0:T(8,128)(2,1)}, u32[]{:S(2)}, u32[]{:S(2)}) %collective-permute-start.31) | collective-permute-done | bytes 1310752 | tf_op jit(solution)/shard_map/ppermute | solution.py:784
  601.1 10.5 %collective-permute-done.30.refs_2_ = bf16[384,2048]{1,0:T(8,128)(2,1)S(1)} collective-permute-done((bf16[384,2048]{1,0:T(8,128)(2,1)}, bf16[384,2048]{1,0:T(8,128)(2,1)S(1)}, u32[]{:S(2)}, u32[]{:S(2)}) %collective-permute-start.30) | collective-permute-done | bytes 1572896 | tf_op jit(solution)/shard_map/ppermute | solution.py:805
  613.1 6.6 %shard_map.261 = (bf16[384,2048]{1,0:T(8,128)(2,1)}, f32[1,2048]{1,0:T(1,128)S(1)}) custom-call(s32[3]{0:T(128)S(1)} %copy-done.19, f32[384,2048]{1,0:T(8,128)} %get-tuple-element.96.refs_2_.refs_1_, bf16[384,2048]{1,0:T(8,128)(2,1)S(1)} %collective-permute-done.30.refs_2_, bf16[384,2048]{1,0:T(8,128)(2,1)S(1)} %copy-done.51, ...), custom_call_target="tpu_custom_call" | custom-call | flops 70000001024 | bytes 1024 | tf_op jit(solution)/shard_map/pallas_call | solution.py:178
  (408 shorter events, 229.1 us)
Async XLA Ops:
  7.2 40.0 %all-gather.7.cloned.1.call-start = ((), (), s32[]{:S(2)}) async-start(), calls=%async_computation.7 | async-start | bytes 2949120 | tf_op jit(solution)/shard_map/all_gather | solution.py:790
  10.5 73.6 %all-gather.9.cloned.1.call-start = ((), (), s32[]{:S(2)}) async-start(), calls=%async_computation.8 | async-start | bytes 2359296 | tf_op jit(solution)/shard_map/all_gather | solution.py:790
  11.5 122.8 %all-gather.11.cloned.1.call-start = ((), (), s32[]{:S(2)}) async-start(), calls=%async_computation.9 | async-start | bytes 5308416 | tf_op jit(solution)/shard_map/all_gather | solution.py:790
  13.8 169.2 %all-gather.13.cloned.1.call-start = ((), (), s32[]{:S(2)}) async-start(), calls=%async_computation.10 | async-start | bytes 5308416 | tf_op jit(solution)/shard_map/all_gather | solution.py:790
  14.7 226.4 %all-gather.15.cloned.1.call-start = ((), (), s32[]{:S(2)}) async-start(), calls=%async_computation.11 | async-start | bytes 5308416 | tf_op jit(solution)/shard_map/all_gather | solution.py:790
  15.7 267.2 %all-gather.17.cloned.1.call-start = ((), (), s32[]{:S(2)}) async-start(), calls=%async_computation.12 | async-start | bytes 3538944 | tf_op jit(solution)/shard_map/all_gather | solution.py:790
  21.5 38.4 %collective-permute-start = (bf16[384,2048]{1,0:T(8,128)(2,1)}, bf16[384,2048]{1,0:T(8,128)(2,1)S(1)}, u32[]{:S(2)}, u32[]{:S(2)}) collective-permute-start(bf16[384,2048]{1,0:T(8,128)(2,1)} %get-tuple-element.58.refs_1_), channel_id=1, source_target_pairs={{0,1},{1,0},{2,3},{3,2},{4,5},{5,4},{6,7},{7,6},{8,9},{9,8},{10,11... | collective-permute-start | bytes 4718600 | tf_op jit(solution)/shard_map/ppermute | solution.py:805
  55.1 63.5 %collective-permute-start.5 = (bf16[384,2048]{1,0:T(8,128)(2,1)}, bf16[384,2048]{1,0:T(8,128)(2,1)}, u32[]{:S(2)}, u32[]{:S(2)}) collective-permute-start(bf16[384,2048]{1,0:T(8,128)(2,1)} %shard_map.211.refs_3_.refs_1_), channel_id=1, source_target_pairs={{0,1},{1,0},{2,3},{3,2},{4,5},{5,4},{6,7},{7,6},{8,9},{9,8},{10,11... | collective-permute-start | bytes 4718600 | tf_op jit(solution)/shard_map/ppermute | solution.py:805
  132.8 36.9 %collective-permute-start.6 = (bf16[384,2048]{1,0:T(8,128)(2,1)}, bf16[384,2048]{1,0:T(8,128)(2,1)}, u32[]{:S(2)}, u32[]{:S(2)}) collective-permute-start(bf16[384,2048]{1,0:T(8,128)(2,1)} %get-tuple-element.61), channel_id=1, source_target_pairs={{0,1},{1,0},{2,3},{3,2},{4,5},{5,4},{6,7},{7,6},{8,9},{9,8},{10,11... | collective-permute-start | bytes 4718600 | tf_op jit(solution)/shard_map/ppermute | solution.py:805
  140.7 54.3 %collective-permute-start.8 = (bf16[512,2304]{1,0:T(8,128)(2,1)}, bf16[512,2304]{1,0:T(8,128)(2,1)S(1)}, u32[]{:S(2)}, u32[]{:S(2)}) collective-permute-start(bf16[512,2304]{1,0:T(8,128)(2,1)} %shard_map.220.refs_4_), channel_id=1, source_target_pairs={{0,4},{4,0},{1,5},{5,1},{2,6},{6,2},{3,7},{7,3},{8,12},{12,8},{9,1... | collective-permute-start | bytes 7077896 | tf_op jit(solution)/shard_map/ppermute | solution.py:784
  175.3 36.0 %collective-permute-start.7 = (bf16[384,2048]{1,0:T(8,128)(2,1)}, bf16[384,2048]{1,0:T(8,128)(2,1)}, u32[]{:S(2)}, u32[]{:S(2)}) collective-permute-start(bf16[384,2048]{1,0:T(8,128)(2,1)} %get-tuple-element.63.refs_2_.refs_1_), channel_id=1, source_target_pairs={{0,1},{1,0},{2,3},{3,2},{4,5},{5,4},{6,7},{7,6},{8,9},{9,8},{10,11... | collective-permute-start | bytes 4718600 | tf_op jit(solution)/shard_map/ppermute | solution.py:805
  187.3 58.3 %collective-permute-start.10 = (bf16[512,2304]{1,0:T(8,128)(2,1)}, bf16[512,2304]{1,0:T(8,128)(2,1)}, u32[]{:S(2)}, u32[]{:S(2)}) collective-permute-start(bf16[512,2304]{1,0:T(8,128)(2,1)} %shard_map.222.refs_1_), channel_id=1, source_target_pairs={{0,4},{4,0},{1,5},{5,1},{2,6},{6,2},{3,7},{7,3},{8,12},{12,8},{9,1... | collective-permute-start | bytes 7077896 | tf_op jit(solution)/shard_map/ppermute | solution.py:784
  245.7 108.0 %reduce-scatter.8.cloned.1.call-start = ((), (), s32[]{:S(2)}) async-start(), calls=%async_computation.13 | async-start | bytes 2949120 | tf_op jit(solution)/shard_map/reduce_scatter | solution.py:793
  245.7 54.0 %collective-permute-start.12 = (bf16[512,2304]{1,0:T(8,128)(2,1)}, bf16[512,2304]{1,0:T(8,128)(2,1)}, u32[]{:S(2)}, u32[]{:S(2)}) collective-permute-start(bf16[512,2304]{1,0:T(8,128)(2,1)} %shard_map.227.refs_1_), channel_id=1, source_target_pairs={{0,4},{4,0},{1,5},{5,1},{2,6},{6,2},{3,7},{7,3},{8,12},{12,8},{9,1... | collective-permute-start | bytes 7077896 | tf_op jit(solution)/shard_map/ppermute | solution.py:784
  246.8 40.3 %collective-permute-start.13 = (bf16[1024,2304]{1,0:T(8,128)(2,1)}, bf16[1024,2304]{1,0:T(8,128)(2,1)}, u32[]{:S(2)}, u32[]{:S(2)}) collective-permute-start(bf16[1024,2304]{1,0:T(8,128)(2,1)} %shard_map.226.refs_2_), channel_id=1, source_target_pairs={{0,2},{2,0},{1,3},{3,1},{4,6},{6,4},{5,7},{7,5},{8,10},{10,8},{9,1... | collective-permute-start | bytes 14155784 | tf_op jit(solution)/shard_map/ppermute | solution.py:787
  301.4 37.3 %collective-permute-start.15 = (bf16[512,1536]{1,0:T(8,128)(2,1)}, bf16[512,1536]{1,0:T(8,128)(2,1)}, u32[]{:S(2)}, u32[]{:S(2)}) collective-permute-start(bf16[512,1536]{1,0:T(8,128)(2,1)} %shard_map.231.refs_6_), channel_id=1, source_target_pairs={{0,4},{4,0},{1,5},{5,1},{2,6},{6,2},{3,7},{7,3},{8,12},{12,8},{9,1... | collective-permute-start | bytes 4718600 | tf_op jit(solution)/shard_map/ppermute | solution.py:784
  302.7 102.8 %reduce-scatter.10.cloned.1.call-start = ((), (), s32[]{:S(2)}) async-start(), calls=%async_computation.14 | async-start | bytes 2949120 | tf_op jit(solution)/shard_map/reduce_scatter | solution.py:793
  339.0 148.0 %reduce-scatter.18.cloned.1.call-start = ((), (), s32[]{:S(2)}) async-start(), calls=%async_computation.18 | async-start | bytes 2949120 | tf_op jit(solution)/shard_map/reduce_scatter | solution.py:793
  339.0 66.4 %collective-permute-start.21 = (bf16[512,2304]{1,0:T(8,128)(2,1)}, bf16[512,2304]{1,0:T(8,128)(2,1)}, u32[]{:S(2)}, u32[]{:S(2)}) collective-permute-start(bf16[512,2304]{1,0:T(8,128)(2,1)} %get-tuple-element.74.refs_5_), channel_id=1, source_target_pairs={{0,4},{4,0},{1,5},{5,1},{2,6},{6,2},{3,7},{7,3},{8,12},{12,8},{9,1... | collective-permute-start | bytes 7077896 | tf_op jit(solution)/shard_map/ppermute | solution.py:784
  340.1 47.8 %collective-permute-start.18 = (bf16[1024,2304]{1,0:T(8,128)(2,1)}, bf16[1024,2304]{1,0:T(8,128)(2,1)}, u32[]{:S(2)}, u32[]{:S(2)}) collective-permute-start(bf16[1024,2304]{1,0:T(8,128)(2,1)} %shard_map.236.refs_1_), channel_id=1, source_target_pairs={{0,2},{2,0},{1,3},{3,1},{4,6},{6,4},{5,7},{7,5},{8,10},{10,8},{9,1... | collective-permute-start | bytes 14155784 | tf_op jit(solution)/shard_map/ppermute | solution.py:787
  353.7 52.4 %collective-permute-start.22 = (bf16[128,2304]{1,0:T(8,128)(2,1)}, bf16[128,2304]{1,0:T(8,128)(2,1)}, u32[]{:S(2)}, u32[]{:S(2)}) collective-permute-start(bf16[128,2304]{1,0:T(8,128)(2,1)} %shard_map.239.refs_41_), channel_id=1, source_target_pairs={{0,4},{4,0},{1,5},{5,1},{2,6},{6,2},{3,7},{7,3},{8,12},{12,8},{9,1... | collective-permute-start | bytes 1769480 | tf_op jit(solution)/shard_map/ppermute | solution.py:784
  386.2 36.9 %collective-permute-start.20 = (bf16[384,2048]{1,0:T(8,128)(2,1)}, bf16[384,2048]{1,0:T(8,128)(2,1)}, u32[]{:S(2)}, u32[]{:S(2)}) collective-permute-start(bf16[384,2048]{1,0:T(8,128)(2,1)} %get-tuple-element.80), channel_id=1, source_target_pairs={{0,1},{1,0},{2,3},{3,2},{4,5},{5,4},{6,7},{7,6},{8,9},{9,8},{10,11... | collective-permute-start | bytes 4718600 | tf_op jit(solution)/shard_map/ppermute | solution.py:805
  398.5 60.6 %collective-permute-start.25 = (bf16[512,2304]{1,0:T(8,128)(2,1)}, bf16[512,2304]{1,0:T(8,128)(2,1)}, u32[]{:S(2)}, u32[]{:S(2)}) collective-permute-start(bf16[512,2304]{1,0:T(8,128)(2,1)} %get-tuple-element.79.refs_5_), channel_id=1, source_target_pairs={{0,4},{4,0},{1,5},{5,1},{2,6},{6,2},{3,7},{7,3},{8,12},{12,8},{9,1... | collective-permute-start | bytes 7077896 | tf_op jit(solution)/shard_map/ppermute | solution.py:784
  411.3 135.8 %reduce-scatter.20.cloned.1.call-start = ((), (), s32[]{:S(2)}) async-start(), calls=%async_computation.19 | async-start | bytes 2949120 | tf_op jit(solution)/shard_map/reduce_scatter | solution.py:793
  431.2 37.7 %collective-permute-start.24 = (bf16[384,2048]{1,0:T(8,128)(2,1)}, bf16[384,2048]{1,0:T(8,128)(2,1)}, u32[]{:S(2)}, u32[]{:S(2)}) collective-permute-start(bf16[384,2048]{1,0:T(8,128)(2,1)} %get-tuple-element.83.refs_6_.refs_1_), channel_id=1, source_target_pairs={{0,1},{1,0},{2,3},{3,2},{4,5},{5,4},{6,7},{7,6},{8,9},{9,8},{10,11... | collective-permute-start | bytes 4718600 | tf_op jit(solution)/shard_map/ppermute | solution.py:805
  440.6 57.5 %collective-permute-start.26 = (bf16[512,1536]{1,0:T(8,128)(2,1)}, bf16[512,1536]{1,0:T(8,128)(2,1)}, u32[]{:S(2)}, u32[]{:S(2)}) collective-permute-start(bf16[512,1536]{1,0:T(8,128)(2,1)} %get-tuple-element.84.refs_21_), channel_id=1, source_target_pairs={{0,4},{4,0},{1,5},{5,1},{2,6},{6,2},{3,7},{7,3},{8,12},{12,8},{9,1... | collective-permute-start | bytes 4718600 | tf_op jit(solution)/shard_map/ppermute | solution.py:784
  458.2 122.4 %collective-permute-start.23 = (bf16[384,2048]{1,0:T(8,128)(2,1)}, bf16[384,2048]{1,0:T(8,128)(2,1)}, u32[]{:S(2)}, u32[]{:S(2)}) collective-permute-start(bf16[384,2048]{1,0:T(8,128)(2,1)} %get-tuple-element.86), channel_id=1, source_target_pairs={{0,1},{1,0},{2,3},{3,2},{4,5},{5,4},{6,7},{7,6},{8,9},{9,8},{10,11... | collective-permute-start | bytes 4718600 | tf_op jit(solution)/shard_map/ppermute | solution.py:805
  463.2 86.2 %reduce-scatter.12.cloned.1.call-start = ((), (), s32[]{:S(2)}) async-start(), calls=%async_computation.15 | async-start | bytes 1966080 | tf_op jit(solution)/shard_map/reduce_scatter | solution.py:793
  497.1 52.4 %collective-permute-start.29 = (bf16[512,1024]{1,0:T(8,128)(2,1)}, bf16[512,1024]{1,0:T(8,128)(2,1)}, u32[]{:S(2)}, u32[]{:S(2)}) collective-permute-start(bf16[512,1024]{1,0:T(8,128)(2,1)} %get-tuple-element.90.refs_2_), channel_id=1, source_target_pairs={{0,4},{4,0},{1,5},{5,1},{2,6},{6,2},{3,7},{7,3},{8,12},{12,8},{9,1... | collective-permute-start | bytes 3145736 | tf_op jit(solution)/shard_map/ppermute | solution.py:784
  501.9 92.0 %reduce-scatter.14.cloned.1.call-start = ((), (), s32[]{:S(2)}) async-start(), calls=%async_computation.16 | async-start | bytes 1310720 | tf_op jit(solution)/shard_map/reduce_scatter | solution.py:793
  553.9 84.0 %reduce-scatter.16.cloned.1.call-start = ((), (), s32[]{:S(2)}) async-start(), calls=%async_computation.17 | async-start | bytes 1638400 | tf_op jit(solution)/shard_map/reduce_scatter | solution.py:793
  575.0 36.7 %collective-permute-start.30 = (bf16[384,2048]{1,0:T(8,128)(2,1)}, bf16[384,2048]{1,0:T(8,128)(2,1)S(1)}, u32[]{:S(2)}, u32[]{:S(2)}) collective-permute-start(bf16[384,2048]{1,0:T(8,128)(2,1)} %get-tuple-element.97), channel_id=1, source_target_pairs={{0,1},{1,0},{2,3},{3,2},{4,5},{5,4},{6,7},{7,6},{8,9},{9,8},{10,11... | collective-permute-start | bytes 4718600 | tf_op jit(solution)/shard_map/ppermute | solution.py:805
  (128 other events, 1599.2 us)
Sparse Core Ops, SparseCore 0:
  10.6 36.5 all-gather.6
  49.4 28.0 all-gather.8
  79.7 51.1 all-gather.10
  132.4 50.5 all-gather.12
  184.4 50.5 all-gather.14
  245.8 37.0 all-gather.16
  302.8 47.0 reduce-scatter.7
  352.2 47.5 reduce-scatter.9
  411.4 46.6 reduce-scatter.17
  463.3 46.6 reduce-scatter.19
  513.0 34.7 reduce-scatter.11
  554.0 26.2 reduce-scatter.13
  601.3 30.4 reduce-scatter.15

commit v7 on v6

--- a/solution.py
+++ b/solution.py
@@ -207,20 +207,21 @@
     return specs, [both, across, both, across_core]
 
 
-def weight_rows(weight, block, units, at):
+def weight_rows(weight, block, units, at, quarters):
     both, across, across_core = weight
     per = across.shape[0] // block
 
     def spec(quarter):
         def index(j, s):
-            row = jnp.clip(j - quarter * per, 0, per - 1)
+            row = jnp.clip(j - (quarter - quarters[0]) * per, 0, per - 1)
             if quarter % 2 == 0:
                 row = row + per * (s[1] if quarter == 0 else 1 - s[1])
             return row, at
 
         return pl.BlockSpec((block, units), index)
 
-    return [spec(quarter) for quarter in range(4)], [both, across, both, across_core]
+    pieces = [both, across, both, across_core]
+    return [spec(quarter) for quarter in quarters], [pieces[quarter] for quarter in quarters]
 
 
 def stack_kernel(*refs):
@@ -361,64 +362,69 @@
     )
 
 
-def back_kernel(count, started, placed, spot_ref, *refs):
+def back_kernel(count, parts, placed, spot_ref, *refs):
     step = pl.program_id(0)
     acts = refs[:count]
-    weights = refs[count : 5 * count]
-    starts = refs[5 * count : 5 * count + 2] if started else None
+    weights = refs[count : count + parts * count]
     mine_ref, theirs_ref = refs[-2:]
     rows = mine_ref.shape[0]
 
     def run(part):
-        total = sum(dot_trans(a[...], weights[4 * i + part][...]) for i, a in enumerate(acts))
+        total = sum(dot_trans(a[...], weights[parts * i + part][...]) for i, a in enumerate(acts))
         mine, theirs = total[:rows], total[rows:]
         if placed:
             first = spot_ref[0] == 0
             mine, theirs = jnp.where(first, mine, theirs), jnp.where(first, theirs, mine)
-        if started:
-            mine = mine + starts[0][...].astype(f32)
-            theirs = theirs + starts[1][...].astype(f32)
         mine_ref[...] = mine.astype(mine_ref.dtype)
         theirs_ref[...] = theirs.astype(theirs_ref.dtype)
 
-    for part in range(4):
-        pl.when(step // (pl.num_programs(0) // 4) == part)(functools.partial(run, part))
-
-
-def back(spot, acts, weights, deps, placed=False, starts=(), kinds=(f32, bf16)):
+    for part in range(parts):
+        pl.when(step // (pl.num_programs(0) // parts) == part)(functools.partial(run, part))
+
+
+def back(spot, acts, weights, deps, placed=False, quarters=(0, 1, 2, 3)):
     rows = acts[0].shape[0]
     depth = weights[0][0][1].shape[0]
-    width = 4 * depth
+    width = len(quarters) * depth
     block = min(BLOCK, depth)
     half = pl.BlockSpec((rows // 2, block), lambda j, s: (0, j))
     specs, operands = [whole_block(a) for a in acts], list(acts)
     for act, (weight, at) in zip(acts, weights):
-        more = weight_rows(weight, block, act.shape[1], at)
+        more = weight_rows(weight, block, act.shape[1], at, quarters)
         specs += more[0]
         operands += more[1]
     return launch(
-        functools.partial(back_kernel, len(acts), len(starts) > 0, placed),
+        functools.partial(back_kernel, len(acts), len(quarters), placed),
         [spot],
-        [*operands, *starts],
+        operands,
         deps,
         (width // block,),
-        [*specs, *([half] * len(starts))],
+        specs,
         [half, half],
-        [jax.ShapeDtypeStruct((rows // 2, width), kind) for kind in kinds],
+        [jax.ShapeDtypeStruct((rows // 2, width), kind) for kind in (f32, bf16)],
         us=rows * width * sum(a.shape[1] for a in acts) / 285000000,
     )
 
 
-def grad_kernel(which, added, *refs):
+def grad_kernel(which, added, placed, *refs):
+    if placed:
+        spot_ref, *refs = refs
     step, steps = pl.program_id(0), pl.num_programs(0)
-    acts = refs[: max(which) + 1]
+    acts = refs[: 2 if placed else max(which) + 1]
     count = len(which)
     grads = refs[len(acts) : len(acts) + count]
     first = 0
     for i in range(count):
         at = slice(first, first + grads[i].shape[1])
         first = at.stop
-        total = dot_inner(acts[which[i]][...], grads[i][...])
+        if placed:
+            rows = acts[0].shape[0]
+            total = 0.0
+            for act, place in ((acts[0], spot_ref[0]), (acts[1], 1 - spot_ref[0])):
+                here = pl.ds(pl.multiple_of(place * rows, rows), rows)
+                total = total + dot_inner(act[...], grads[i][here, :])
+        else:
+            total = dot_inner(acts[which[i]][...], grads[i][...])
         if not added:
             refs[-1][:, at] = total.astype(bf16)
             continue
@@ -433,7 +439,7 @@
             refs[-1][:, at] = total
 
 
-def grad(acts, which, grads, deps, added=None, us=None):
+def grad(acts, which, grads, deps, added=None, us=None, spot=None):
     tokens, width = acts[0].shape
     block = min(BLOCK, width // 4)
     steps = width // 2 // block
@@ -441,24 +447,24 @@
     units = sum(g.shape[1] for g in grads)
     if added is None:
         row = lambda j: j + steps
-        outs = pl.BlockSpec((block, units), lambda j: (j, 0))
+        outs = pl.BlockSpec((block, units), lambda j, *s: (j, 0))
         shapes = jax.ShapeDtypeStruct((width // 2, units), bf16)
     else:
         row = lambda j: (j + half) % steps
         outs = [
-            pl.BlockSpec((block, units), lambda j: (jnp.minimum(j, half - 1), 0)),
-            pl.BlockSpec((block, units), lambda j: (jnp.maximum(j - half, 0), 0)),
+            pl.BlockSpec((block, units), lambda j, *s: (jnp.minimum(j, half - 1), 0)),
+            pl.BlockSpec((block, units), lambda j, *s: (jnp.maximum(j - half, 0), 0)),
         ]
         shapes = [jax.ShapeDtypeStruct((width // 4, units), bf16)] * 2
-    specs = [pl.BlockSpec((tokens, block), lambda j: (0, row(j))) for _ in acts]
+    specs = [pl.BlockSpec((tokens, block), lambda j, *s: (0, row(j))) for _ in acts]
     specs += [whole_block(g) for g in grads]
     operands = [*acts, *grads]
     if added is not None:
-        specs.append(pl.BlockSpec((block, units), lambda j: (row(j), 0)))
+        specs.append(pl.BlockSpec((block, units), lambda j, *s: (row(j), 0)))
         operands.append(added)
     return launch(
-        functools.partial(grad_kernel, which, added is not None),
-        [],
+        functools.partial(grad_kernel, which, added is not None, spot is not None),
+        [] if spot is None else [spot],
         operands,
         deps,
         (steps,),
@@ -724,12 +730,33 @@
     )
 
 
-def input_back_kernel(outer, spot_ref, own_ref, other_ref, tokens_ref, grad_ref, gain_ref, out_ref, part_ref):
+def gain_kernel(own_ref, sent_ref, tokens_ref, other_ref, gain_ref, part_ref):
+    inputs = tokens_ref[...].astype(f32)
+    mine = own_ref[...] * inputs * inverse_rms(inputs)
+    theirs = sent_ref[...].astype(f32) * other_ref[...].astype(f32) / gain_ref[...]
+    gain_part(part_ref, mine + theirs)
+
+
+def gain_sum(own, sent, tokens, normed_other, gain, deps):
+    spec = rows_spec(*own.shape)
+    return launch(
+        gain_kernel,
+        [],
+        [own, sent, tokens, normed_other, gain],
+        deps,
+        (ROW_STEPS,),
+        [spec, spec, spec, spec, whole_block(gain)],
+        whole_block(gain),
+        jax.ShapeDtypeStruct(gain.shape, f32),
+        us=30,
+    )
+
+
+def input_back_kernel(outer, spot_ref, own_ref, other_ref, tokens_ref, grad_ref, gain_ref, out_ref):
     incoming = own_ref[...] + other_ref[...].astype(f32)
     inputs = tokens_ref[...].astype(f32)
     inverse = inverse_rms(inputs)
     leave(outer, spot_ref, out_ref, grad_ref[...] + norm_back(inputs, inverse, gain_ref[...], incoming))
-    gain_part(part_ref, incoming * inputs * inverse)
 
 
 def input_backward(spot, outer, own, other, tokens, middle_grad, gain, deps):
@@ -741,9 +768,9 @@
         deps,
         (ROW_STEPS,),
         [spec, spec, spec, spec, whole_block(gain)],
-        [spec, whole_block(gain)],
-        [jax.ShapeDtypeStruct(own.shape, bf16), jax.ShapeDtypeStruct(gain.shape, f32)],
-        us=7,
+        spec,
+        jax.ShapeDtypeStruct(own.shape, bf16),
+        us=SHORT,
     )
 
 
@@ -948,11 +975,11 @@
         )
         block_other = swap(block_sent)
         finish(2)
-        attn_grad_seq = order(lambda deps: join(spot, attn_out_grad, attn_other, deps))
-        from_core["o"] = over_core(order(lambda deps: grad((attn_grad_seq,), (0,), (mixed,), deps)))
+        both = (attn_out_grad, attn_other)
+        from_core["o"] = over_core(order(lambda deps: grad(both, (0,), (mixed,), deps, spot=spot)))
         mixed_grad = order(lambda deps: project(spot, attn_out_grad, attn_other, full["o"], deps))
         to_x["o"], kept["o"] = order(
-            lambda deps: grad((attn_grad_seq,), (0,), (mixed,), deps, from_core["o"])
+            lambda deps: grad(both, (0,), (mixed,), deps, from_core["o"], spot=spot)
         )
         send_x("o")
         finish(3)
@@ -962,15 +989,16 @@
                 score_scale, deps,
             )
         )
+        order.wait(from_x["o"], block_other)
         from_core["qkv"] = over_core(
             order(lambda deps: grad((normed_seq,), (0,) * 3, qkv_grad, deps, us=SHORT))
         )
+        to_x["qkv"], kept["qkv"] = order(
+            lambda deps: grad((normed_seq,), (0,) * 3, qkv_grad, deps, from_core["qkv"], us=SHORT)
+        )
+        send_x("qkv")
         order.wait(summed[3])
         finish("o")
-        to_x["qkv"], kept["qkv"] = order(
-            lambda deps: grad((normed_seq,), (0,) * 3, qkv_grad, deps, from_core["qkv"])
-        )
-        send_x("qkv")
         places = (0, query_width // key_width, query_width // key_width + 1)
         own, sent = order(
             lambda deps: back(spot, qkv_grad, [(full["qkv"], at) for at in places], deps, True)
@@ -980,7 +1008,10 @@
         block_out = order(lambda deps: block_result(spot, tiles, middle, block_own, block_other, deps))
         order.wait(summed["o"])
         finish("qkv")
-        input_grad, attention_gain_part = order(
+        attention_gain_part = order(
+            lambda deps: gain_sum(own, sent, tokens, normed_other, attention_gain, deps)
+        )
+        input_grad = order(
             lambda deps: input_backward(spot, tiles, own, other, tokens, middle_grad, attention_gain, deps)
         )
         gains = total(natural(jnp.concatenate([attention_gain_part, feed_gain_part], axis=0)))

time: 656 us -> 658 us (level)
  waiting for transfers between devices: 163 us -> 148 us
  Pallas kernels: 373 us -> 381 us
    ppermute x8, waiting for transfers between devices: 76.1 us -> 64 us  [swap(): return lax.ppermute(own, 'tensor', SWAP)]
    ppermute x12, waiting for transfers between devices: 35 us -> 25.9 us  [over_x(): return lax.ppermute(array, 'x', SWAP)]
    pallas_call x59, Pallas kernels: 373 us -> 381 us  [launch(): pl.pallas_call(body, grid_spec=pltpu.PrefetchScalarGridSpec(num_scalar_pr...]
    unnamed x220 -> x206, local copies, waits for them, and re-layouts: 49.1 us -> 48.7 us
  transfers between devices with their start and end apart: 50 -> 50, of which waited for: 22 -> 23; matrix products, arithmetic and copies ran while one was open for 2% -> 2% of each run, Pallas kernels for 57% -> 59%
where the time goes in v7:
time: 658 us; the launch traced here: 645 us
  Pallas kernels  381 us (58%)
  waiting for transfers between devices  148 us (22%)
  local copies, waits for them, and re-layouts  53.3 us (8%)
  starting transfers between devices  36.2 us (6%)
  between operations  15.2 us (2%)
  other arithmetic  11.7 us (2%)
    pallas_call x59, Pallas kernels, launch(): pl.pallas_call(body, grid_spec=pltpu.PrefetchScalarGridSpec(num_scalar_pr...  381 us
    ppermute x8, waiting for transfers between devices, swap(): return lax.ppermute(own, 'tensor', SWAP)  64 us
    unnamed x206, local copies, waits for them, and re-layouts  48.7 us
    all_gather x6, waiting for transfers between devices, gather(): return lax.all_gather(operand, ('core', 'z'), axis=0, tiled=True)  37 us
    ppermute x12, waiting for transfers between devices, over_x(): return lax.ppermute(array, 'x', SWAP)  25.9 us
    ppermute x8, starting transfers between devices, swap(): return lax.ppermute(own, 'tensor', SWAP)  13.2 us
  transfers between devices with their start and end apart: 50, of which 23 were waited for; matrix products, arithmetic and copies ran while one was open for 2% of the time, Pallas kernels for 59%

profile of v7, /device:TPU:0, one launch (start us, length us, event | category | flops | bytes accessed | tf_op | source)
XLA Modules:
  0.0 645.3 jit_solution(4467232032584110781)
XLA Ops:
  27.2 20.0 %all-gather.7.cloned.1.call-done.refs_1_.refs_3_.refs_5_.refs_4_.refs_6_.refs_8_.refs_10_.refs_12_.refs_14_ = bf16[1024,1280]{1,0:T(8,128)(2,1)} async-done(((bf16[128,1280]{1,0:T(8,128)(2,1)}), bf16[1024,1280]{1,0:T(8,128)(2,1)}) %all-gather.7.cloned.1.call-update) | async-done | bytes 2621456 | tf_op jit(solution)/shard_map/all_gather | solution.py:817
  64.4 16.3 %collective-permute-done.1.refs_0_ = bf16[512,1280]{1,0:T(8,128)(2,1)} collective-permute-done((bf16[512,1280]{1,0:T(8,128)(2,1)S(1)}, bf16[512,1280]{1,0:T(8,128)(2,1)}, u32[]{:S(2)}, u32[]{:S(2)}) %collective-permute-start.1) | collective-permute-done | bytes 1310752 | tf_op jit(solution)/shard_map/ppermute | solution.py:811
  87.8 10.8 %shard_map.215.refs_1_.refs_2_.refs_3_.refs_6_ = bf16[768,1280]{1,0:T(8,128)(2,1)} custom-call(s32[3]{0:T(128)S(1)} %pad_add_fusion.refs_0_, bf16[384,2048]{1,0:T(8,128)(2,1)} %get-tuple-element.56.refs_1_, bf16[384,2048]{1,0:T(8,128)(2,1)} %collective-permute-done.refs_2_.refs_3_, ...), custom_call_target="tpu_custom_call" | custom-call | flops 100663296000 | bytes 1024 | tf_op jit(solution)/shard_map/pallas_call | solution.py:178
  100.2 14.8 %shard_map.216 = (bf16[768,1024]{1,0:T(8,128)(2,1)S(1)}, f32[768,256]{1,0:T(8,128)S(1)}) custom-call(s32[3]{0:T(128)S(1)} %convert_reduce_fusion.1.refs_6_.refs_0_, bf16[768,1280]{1,0:T(8,128)(2,1)S(1)} %copy-done.87, bf16[768,1280]{1,0:T(8,128)(2,1)S(1)} %copy-done.87, bf16[768,1280]{1,0:T(8,128)(2,1)S(1)} %copy-done.87, ...), custom_call_target="tpu_custom_call" | custom-call | flops 160000000000 | bytes 1024 | tf_op jit(solution)/shard_map/pallas_call | solution.py:178
  122.3 9.2 %shard_map.219 = (f32[384,2048]{1,0:T(8,128)}, bf16[384,2048]{1,0:T(8,128)(2,1)}) custom-call(s32[3]{0:T(128)S(1)} %pad_add_fusion.refs_0_, bf16[768,1024]{1,0:T(8,128)(2,1)S(1)} %get-tuple-element.57.refs_1_.refs_3_, bf16[1024,1024]{1,0:T(8,128)(2,1)} %all-gather.9.cloned.1.call-done.refs_1_.refs_2_.refs_4_.refs_3_.refs_5_, ...), custom_call_target="tpu_custom_call" | custom-call | flops 56512729088 | bytes 1024 | tf_op jit(solution)/shard_map/pallas_call | solution.py:178
  140.0 28.2 %collective-permute-done.6.refs_2_ = bf16[384,2048]{1,0:T(8,128)(2,1)} collective-permute-done((bf16[384,2048]{1,0:T(8,128)(2,1)}, bf16[384,2048]{1,0:T(8,128)(2,1)}, u32[]{:S(2)}, u32[]{:S(2)}) %collective-permute-start.6) | collective-permute-done | bytes 1572896 | tf_op jit(solution)/shard_map/ppermute | solution.py:832
  175.2 7.7 %all-gather.13.cloned.1.call-done.refs_1_.refs_3_.refs_5_.refs_7_.refs_9_.refs_11_.refs_13_.refs_17_.refs_19_.refs_21_.refs_23_ = bf16[1024,2304]{1,0:T(8,128)(2,1)} async-done(((bf16[128,2304]{1,0:T(8,128)(2,1)}), bf16[1024,2304]{1,0:T(8,128)(2,1)}) %all-gather.13.cloned.1.call-update) | async-done | bytes 4718608 | tf_op jit(solution)/shard_map/all_gather | solution.py:817
  193.9 15.6 %collective-permute-done.7.refs_2_ = bf16[384,2048]{1,0:T(8,128)(2,1)S(1)} collective-permute-done((bf16[384,2048]{1,0:T(8,128)(2,1)}, bf16[384,2048]{1,0:T(8,128)(2,1)S(1)}, u32[]{:S(2)}, u32[]{:S(2)}) %collective-permute-start.7) | collective-permute-done | bytes 1572896 | tf_op jit(solution)/shard_map/ppermute | solution.py:832
  215.4 13.1 %shard_map.225 = (bf16[768,768]{1,0:T(8,128)(2,1)S(1)}, bf16[768,768]{1,0:T(8,128)(2,1)S(1)}, bf16[768,768]{1,0:T(8,128)(2,1)S(1)}) custom-call(s32[3]{0:T(128)S(1)} %pad_add_fusion.refs_0_, bf16[768,2048]{1,0:T(8,128)(2,1)} %shard_map.224.refs_1_.refs_15_.refs_0_, bf16[768,2048]{1,0:T(8,128)(2,1)} %shard_map.218.refs_6_.refs_2_.refs_1_, ...), custom_call_target="tpu_custom_call" | custom-call | flops 120795955200 | bytes 1024 | tf_op jit(solution)/shard_map/pallas_call | solution.py:178
  228.5 7.3 %shard_map.226.refs_2_ = bf16[1024,2304]{1,0:T(8,128)(2,1)} custom-call(bf16[768,2048]{1,0:T(8,128)(2,1)} %shard_map.224.refs_1_.refs_15_.refs_0_, bf16[768,2048]{1,0:T(8,128)(2,1)} %shard_map.218.refs_6_.refs_2_.refs_1_, bf16[768,768]{1,0:T(8,128)(2,1)S(1)} %get-tuple-element.63.refs_2_.refs_1_, bf16[768,768]{1,0:T(8,128)(2,1)S(1)} %get-tuple-element.64.refs_3_.refs_2_, ...), custom_call_target="tpu_custom_call" | custom-call | flops 75497472000 | bytes 1024 | tf_op jit(solution)/shard_map/pallas_call | solution.py:178
  248.2 13.5 %shard_map.229 = (bf16[768,768]{1,0:T(8,128)(2,1)S(1)}, bf16[768,768]{1,0:T(8,128)(2,1)S(1)}, bf16[768,768]{1,0:T(8,128)(2,1)S(1)}) custom-call(s32[3]{0:T(128)S(1)} %pad_add_fusion.refs_0_, bf16[768,2048]{1,0:T(8,128)(2,1)} %shard_map.224.refs_1_.refs_15_.refs_0_, bf16[768,2048]{1,0:T(8,128)(2,1)} %shard_map.218.refs_6_.refs_2_.refs_1_, ...), custom_call_target="tpu_custom_call" | custom-call | flops 120795955200 | bytes 1024 | tf_op jit(solution)/shard_map/pallas_call | solution.py:178
  261.7 7.3 %shard_map.230.refs_2_ = bf16[1024,2304]{1,0:T(8,128)(2,1)} custom-call(bf16[768,2048]{1,0:T(8,128)(2,1)} %shard_map.224.refs_1_.refs_15_.refs_0_, bf16[768,2048]{1,0:T(8,128)(2,1)} %shard_map.218.refs_6_.refs_2_.refs_1_, bf16[768,768]{1,0:T(8,128)(2,1)S(1)} %get-tuple-element.66.refs_2_.refs_3_, bf16[768,768]{1,0:T(8,128)(2,1)S(1)} %get-tuple-element.67.refs_3_.refs_4_, ...), custom_call_target="tpu_custom_call" | custom-call | flops 75497472000 | bytes 1024 | tf_op jit(solution)/shard_map/pallas_call | solution.py:178
  272.0 9.3 %all-gather.17.cloned.1.call-done.refs_1_.refs_3_.refs_5_.refs_7_.refs_9_.refs_11_.refs_13_.refs_33_.refs_35_.refs_37_.refs_39_.refs_17_.refs_19_ = bf16[1024,1536]{1,0:T(8,128)(2,1)} async-done(((bf16[128,1536]{1,0:T(8,128)(2,1)}), bf16[1024,1536]{1,0:T(8,128)(2,1)}) %all-gather.17.cloned.1.call-update) | async-done | bytes 3145744 | tf_op jit(solution)/shard_map/all_gather | solution.py:817
  285.5 10.5 %shard_map.232 = (bf16[512,2304]{1,0:T(8,128)(2,1)}, bf16[512,2304]{1,0:T(8,128)(2,1)}) custom-call(bf16[768,2048]{1,0:T(8,128)(2,1)} %shard_map.224.refs_1_.refs_15_.refs_0_, bf16[768,2048]{1,0:T(8,128)(2,1)} %shard_map.218.refs_6_.refs_2_.refs_1_, bf16[768,768]{1,0:T(8,128)(2,1)S(1)} %copy-done.74, bf16[768,768]{1,0:T(8,128)(2,1)S(1)} %copy-done.77, ...), custom_call_target="tpu_custom_call" | custom-call | flops 75497472000 | bytes 1024 | tf_op jit(solution)/shard_map/pallas_call | solution.py:178
  304.0 23.7 %shard_map.234 = (bf16[768,768]{1,0:T(8,128)(2,1)S(1)}, bf16[768,768]{1,0:T(8,128)(2,1)S(1)}, bf16[768,768]{1,0:T(8,128)(2,1)S(1)}) custom-call(s32[3]{0:T(128)S(1)} %pad_add_fusion.refs_0_, bf16[768,2048]{1,0:T(8,128)(2,1)} %shard_map.224.refs_1_.refs_15_.refs_0_, bf16[768,2048]{1,0:T(8,128)(2,1)} %shard_map.218.refs_6_.refs_2_.refs_1_, ...), custom_call_target="tpu_custom_call" | custom-call | flops 120795955200 | bytes 1024 | tf_op jit(solution)/shard_map/pallas_call | solution.py:178
  327.8 11.6 %shard_map.235 = (bf16[512,2304]{1,0:T(8,128)(2,1)}, bf16[512,2304]{1,0:T(8,128)(2,1)}) custom-call(bf16[768,2048]{1,0:T(8,128)(2,1)} %shard_map.224.refs_1_.refs_15_.refs_0_, bf16[768,2048]{1,0:T(8,128)(2,1)} %shard_map.218.refs_6_.refs_2_.refs_1_, bf16[768,768]{1,0:T(8,128)(2,1)S(1)} %copy-done.83, bf16[768,768]{1,0:T(8,128)(2,1)S(1)} %copy-done.86, ...), custom_call_target="tpu_custom_call" | custom-call | flops 75497472000 | bytes 1024 | tf_op jit(solution)/shard_map/pallas_call | solution.py:178
  339.5 7.2 %shard_map.236.refs_1_ = bf16[1024,2304]{1,0:T(8,128)(2,1)} custom-call(bf16[768,2048]{1,0:T(8,128)(2,1)} %shard_map.224.refs_1_.refs_15_.refs_0_, bf16[768,2048]{1,0:T(8,128)(2,1)} %shard_map.218.refs_6_.refs_2_.refs_1_, bf16[768,768]{1,0:T(8,128)(2,1)S(1)} %get-tuple-element.70.refs_2_.refs_5_, bf16[768,768]{1,0:T(8,128)(2,1)S(1)} %get-tuple-element.71.refs_3_.refs_6_, ...), custom_call_target="tpu_custom_call" | custom-call | flops 75497472000 | bytes 1024 | tf_op jit(solution)/shard_map/pallas_call | solution.py:178
  350.3 9.9 %shard_map.238 = (bf16[768,512]{1,0:T(8,128)(2,1)S(1)}, bf16[768,512]{1,0:T(8,128)(2,1)S(1)}, bf16[768,512]{1,0:T(8,128)(2,1)S(1)}) custom-call(s32[3]{0:T(128)S(1)} %pad_add_fusion.refs_0_, bf16[768,2048]{1,0:T(8,128)(2,1)} %shard_map.224.refs_1_.refs_15_.refs_0_, bf16[768,2048]{1,0:T(8,128)(2,1)} %shard_map.218.refs_6_.refs_2_.refs_1_, ...), custom_call_target="tpu_custom_call" | custom-call | flops 80530636800 | bytes 1024 | tf_op jit(solution)/shard_map/pallas_call | solution.py:178
  364.8 30.2 %shard_map.240 = (f32[384,2048]{1,0:T(8,128)}, bf16[384,2048]{1,0:T(8,128)(2,1)}) custom-call(s32[3]{0:T(128)S(1)} %pad_add_fusion.refs_0_, bf16[768,768]{1,0:T(8,128)(2,1)S(1)} %copy-done.75, bf16[768,768]{1,0:T(8,128)(2,1)S(1)} %copy-done.78, bf16[768,768]{1,0:T(8,128)(2,1)S(1)} %copy-done.84, bf16[768,768]{1,0:T(8,128)(2,1)} %copy-done.85, ...), custom_call_target="tpu_custom_call" | custom-call | flops 310820012032 | bytes 1024 | tf_op jit(solution)/shard_map/pallas_call | solution.py:178
  396.6 10.5 %shard_map.241 = (bf16[512,2304]{1,0:T(8,128)(2,1)}, bf16[512,2304]{1,0:T(8,128)(2,1)}) custom-call(bf16[768,2048]{1,0:T(8,128)(2,1)} %shard_map.224.refs_1_.refs_15_.refs_0_, bf16[768,2048]{1,0:T(8,128)(2,1)} %shard_map.218.refs_6_.refs_2_.refs_1_, bf16[768,768]{1,0:T(8,128)(2,1)S(1)} %copy-done.67, bf16[768,768]{1,0:T(8,128)(2,1)S(1)} %copy-done.69, ...), custom_call_target="tpu_custom_call" | custom-call | flops 75497472000 | bytes 1024 | tf_op jit(solution)/shard_map/pallas_call | solution.py:178
  407.6 6.0 shard_map.242.refs_2_
  420.9 10.9 %collective-permute-done.20.refs_1_ = bf16[384,2048]{1,0:T(8,128)(2,1)} collective-permute-done((bf16[384,2048]{1,0:T(8,128)(2,1)}, bf16[384,2048]{1,0:T(8,128)(2,1)}, u32[]{:S(2)}, u32[]{:S(2)}) %collective-permute-start.20) | collective-permute-done | bytes 1572896 | tf_op jit(solution)/shard_map/ppermute | solution.py:832
  431.8 8.2 %shard_map.244 = (bf16[384,2048]{1,0:T(8,128)(2,1)}, f32[384,2048]{1,0:T(8,128)}, f32[1,2048]{1,0:T(1,128)S(1)}) custom-call(f32[384,2048]{1,0:T(8,128)} %get-tuple-element.76.refs_6_.refs_0_, bf16[384,2048]{1,0:T(8,128)(2,1)} %collective-permute-done.20.refs_1_, f32[384,2048]{1,0:T(8,128)} %get-tuple-element.60.refs_2_.refs_1_, ...), custom_call_target="tpu_custom_call" | custom-call | flops 80000000000 | bytes 1024 | tf_op jit(solution)/shard_map/pallas_call | solution.py:178
  441.6 7.8 %shard_map.245 = (bf16[512,1536]{1,0:T(8,128)(2,1)}, bf16[512,1536]{1,0:T(8,128)(2,1)S(1)}) custom-call(bf16[768,2048]{1,0:T(8,128)(2,1)} %shard_map.224.refs_1_.refs_15_.refs_0_, bf16[768,2048]{1,0:T(8,128)(2,1)} %shard_map.218.refs_6_.refs_2_.refs_1_, bf16[768,512]{1,0:T(8,128)(2,1)S(1)} %copy-done.60, bf16[768,512]{1,0:T(8,128)(2,1)S(1)} %copy-done.62, ...), custom_call_target="tpu_custom_call" | custom-call | flops 50331648000 | bytes 1024 | tf_op jit(solution)/shard_map/pallas_call | solution.py:178
  451.1 16.5 %shard_map.246 = (f32[384,2048]{1,0:T(8,128)}, bf16[384,2048]{1,0:T(8,128)(2,1)}) custom-call(s32[3]{0:T(128)S(1)} %pad_add_fusion.refs_0_, bf16[768,768]{1,0:T(8,128)(2,1)S(1)} %copy-done.72, bf16[768,768]{1,0:T(8,128)(2,1)S(1)} %copy-done.81, bf16[768,768]{1,0:T(8,128)(2,1)S(1)} %copy-done.65, bf16[768,512]{1,0:T(8,128)(2,1)S(1)} %copy-done.48, ...), custom_call_target="tpu_custom_call" | custom-call | flops 155410006016 | bytes 1024 | tf_op jit(solution)/shard_map/pallas_call | solution.py:178
  477.7 5.9 shard_map.248.refs_7_
  483.7 7.2 %shard_map.249.refs_5_.refs_4_ = bf16[768,1024]{1,0:T(8,128)(2,1)S(1)} custom-call(s32[3]{0:T(128)S(1)} %pad_add_fusion.refs_0_, bf16[384,2048]{1,0:T(8,128)(2,1)} %get-tuple-element.81.refs_6_.refs_1_, bf16[384,2048]{1,0:T(8,128)(2,1)} %collective-permute-done.24.refs_2_, ...), custom_call_target="tpu_custom_call" | custom-call | flops 80530636800 | bytes 1024 | tf_op jit(solution)/shard_map/pallas_call | solution.py:178
  493.4 7.1 %shard_map.250 = (bf16[512,1024]{1,0:T(8,128)(2,1)}, bf16[512,1024]{1,0:T(8,128)(2,1)S(1)}) custom-call(s32[3]{0:T(128)S(1)} %pad_add_fusion.refs_0_, bf16[384,2048]{1,0:T(8,128)(2,1)} %get-tuple-element.81.refs_6_.refs_1_, bf16[384,2048]{1,0:T(8,128)(2,1)} %collective-permute-done.24.refs_2_, bf16[768,1024]{1,0:T(8,128)(2,1)} %copy-done.45, ...), custom_call_target="tpu_custom_call" | custom-call | flops 16777216000 | bytes 1024 | tf_op jit(solution)/shard_map/pallas_call | solution.py:178
  509.4 32.0 %shard_map.252 = (bf16[768,1024]{1,0:T(8,128)(2,1)S(1)}, bf16[768,128]{1,0:T(8,128)(2,1)S(1)}, bf16[768,128]{1,0:T(8,128)(2,1)S(1)}) custom-call(s32[3]{0:T(128)S(1)} %copy-done.42, bf16[768,1280]{1,0:T(8,128)(2,1)} %shard_map.215.refs_1_.refs_2_.refs_3_.refs_6_, bf16[768,1280]{1,0:T(8,128)(2,1)} %shard_map.215.refs_1_.refs_2_.refs_3_.refs_6_, ...), custom_call_target="tpu_custom_call" | custom-call | flops 349999988736 | bytes 1024 | tf_op jit(solution)/shard_map/pallas_call | solution.py:178
  555.8 7.5 %shard_map.254 = (bf16[512,1280]{1,0:T(8,128)(2,1)}, bf16[512,1280]{1,0:T(8,128)(2,1)S(1)}) custom-call(bf16[768,2048]{1,0:T(8,128)(2,1)} %shard_map.212.refs_1_.refs_0_, bf16[768,1024]{1,0:T(8,128)(2,1)S(1)} %get-tuple-element.89.refs_1_.refs_4_, bf16[768,128]{1,0:T(8,128)(2,1)S(1)} %get-tuple-element.90.refs_2_, ...), custom_call_target="tpu_custom_call" | custom-call | flops 100000000 | bytes 1024 | tf_op jit(solution)/shard_map/pallas_call | solution.py:178
  570.4 11.8 %shard_map.256 = (f32[384,2048]{1,0:T(8,128)}, bf16[384,2048]{1,0:T(8,128)(2,1)}) custom-call(s32[3]{0:T(128)S(1)} %copy-done.24, bf16[768,1024]{1,0:T(8,128)(2,1)} %copy-done, bf16[768,128]{1,0:T(8,128)(2,1)S(1)} %get-tuple-element.90.refs_2_, bf16[768,128]{1,0:T(8,128)(2,1)S(1)} %get-tuple-element.91.refs_3_, ...), custom_call_target="tpu_custom_call" | custom-call | flops 70640910336 | bytes 1024 | tf_op jit(solution)/shard_map/pallas_call | solution.py:178
  627.1 6.7 %shard_map.261 = bf16[384,2048]{1,0:T(8,128)(2,1)} custom-call(s32[3]{0:T(128)S(1)} %copy-done.25, f32[384,2048]{1,0:T(8,128)} %get-tuple-element.94.refs_2_.refs_0_.refs_1_, bf16[384,2048]{1,0:T(8,128)(2,1)} %collective-permute-done.30.refs_2_, bf16[384,2048]{1,0:T(8,128)(2,1)S(1)} %copy-done.5, f32[384,2048]{1,0:T(8,128)} %get-tuple-element.96.refs_4_, ...), custom_call_target="tpu_custom_call" | custom-call | flops 100000000 | bytes 1024 | tf_op jit(solution)/shard_map/pallas_call | solution.py:178
  (394 shorter events, 225.9 us)
Async XLA Ops:
  7.2 40.0 %all-gather.7.cloned.1.call-start = ((), (), s32[]{:S(2)}) async-start(), calls=%async_computation.7 | async-start | bytes 2949120 | tf_op jit(solution)/shard_map/all_gather | solution.py:817
  10.5 72.2 %all-gather.9.cloned.1.call-start = ((), (), s32[]{:S(2)}) async-start(), calls=%async_computation.8 | async-start | bytes 2359296 | tf_op jit(solution)/shard_map/all_gather | solution.py:817
  11.5 121.5 %all-gather.11.cloned.1.call-start = ((), (), s32[]{:S(2)}) async-start(), calls=%async_computation.9 | async-start | bytes 5308416 | tf_op jit(solution)/shard_map/all_gather | solution.py:817
  13.8 169.1 %all-gather.13.cloned.1.call-start = ((), (), s32[]{:S(2)}) async-start(), calls=%async_computation.10 | async-start | bytes 5308416 | tf_op jit(solution)/shard_map/all_gather | solution.py:817
  14.7 224.2 %all-gather.15.cloned.1.call-start = ((), (), s32[]{:S(2)}) async-start(), calls=%async_computation.11 | async-start | bytes 5308416 | tf_op jit(solution)/shard_map/all_gather | solution.py:817
  15.7 265.6 %all-gather.17.cloned.1.call-start = ((), (), s32[]{:S(2)}) async-start(), calls=%async_computation.12 | async-start | bytes 3538944 | tf_op jit(solution)/shard_map/all_gather | solution.py:817
  21.0 38.5 %collective-permute-start = (bf16[384,2048]{1,0:T(8,128)(2,1)}, bf16[384,2048]{1,0:T(8,128)(2,1)}, u32[]{:S(2)}, u32[]{:S(2)}) collective-permute-start(bf16[384,2048]{1,0:T(8,128)(2,1)} %get-tuple-element.56.refs_1_), channel_id=1, source_target_pairs={{0,1},{1,0},{2,3},{3,2},{4,5},{5,4},{6,7},{7,6},{8,9},{9,8},{10,11... | collective-permute-start | bytes 4718600 | tf_op jit(solution)/shard_map/ppermute | solution.py:832
  53.6 63.7 %collective-permute-start.5 = (bf16[384,2048]{1,0:T(8,128)(2,1)}, bf16[384,2048]{1,0:T(8,128)(2,1)}, u32[]{:S(2)}, u32[]{:S(2)}) collective-permute-start(bf16[384,2048]{1,0:T(8,128)(2,1)} %shard_map.211.refs_3_.refs_1_), channel_id=1, source_target_pairs={{0,1},{1,0},{2,3},{3,2},{4,5},{5,4},{6,7},{7,6},{8,9},{9,8},{10,11... | collective-permute-start | bytes 4718600 | tf_op jit(solution)/shard_map/ppermute | solution.py:832
  131.5 36.7 %collective-permute-start.6 = (bf16[384,2048]{1,0:T(8,128)(2,1)}, bf16[384,2048]{1,0:T(8,128)(2,1)}, u32[]{:S(2)}, u32[]{:S(2)}) collective-permute-start(bf16[384,2048]{1,0:T(8,128)(2,1)} %get-tuple-element.59), channel_id=1, source_target_pairs={{0,1},{1,0},{2,3},{3,2},{4,5},{5,4},{6,7},{7,6},{8,9},{9,8},{10,11... | collective-permute-start | bytes 4718600 | tf_op jit(solution)/shard_map/ppermute | solution.py:832
  139.4 54.5 %collective-permute-start.8 = (bf16[512,2304]{1,0:T(8,128)(2,1)}, bf16[512,2304]{1,0:T(8,128)(2,1)}, u32[]{:S(2)}, u32[]{:S(2)}) collective-permute-start(bf16[512,2304]{1,0:T(8,128)(2,1)} %shard_map.220.refs_4_), channel_id=1, source_target_pairs={{0,4},{4,0},{1,5},{5,1},{2,6},{6,2},{3,7},{7,3},{8,12},{12,8},{9,1... | collective-permute-start | bytes 7077896 | tf_op jit(solution)/shard_map/ppermute | solution.py:811
  173.8 35.7 %collective-permute-start.7 = (bf16[384,2048]{1,0:T(8,128)(2,1)}, bf16[384,2048]{1,0:T(8,128)(2,1)S(1)}, u32[]{:S(2)}, u32[]{:S(2)}) collective-permute-start(bf16[384,2048]{1,0:T(8,128)(2,1)} %get-tuple-element.61.refs_2_.refs_1_), channel_id=1, source_target_pairs={{0,1},{1,0},{2,3},{3,2},{4,5},{5,4},{6,7},{7,6},{8,9},{9,8},{10,11... | collective-permute-start | bytes 4718600 | tf_op jit(solution)/shard_map/ppermute | solution.py:832
  187.4 55.9 %collective-permute-start.10 = (bf16[512,2304]{1,0:T(8,128)(2,1)}, bf16[512,2304]{1,0:T(8,128)(2,1)}, u32[]{:S(2)}, u32[]{:S(2)}) collective-permute-start(bf16[512,2304]{1,0:T(8,128)(2,1)} %shard_map.222.refs_1_), channel_id=1, source_target_pairs={{0,4},{4,0},{1,5},{5,1},{2,6},{6,2},{3,7},{7,3},{8,12},{12,8},{9,1... | collective-permute-start | bytes 7077896 | tf_op jit(solution)/shard_map/ppermute | solution.py:811
  243.4 118.6 %reduce-scatter.8.cloned.1.call-start = ((), (), s32[]{:S(2)}) async-start(), calls=%async_computation.13 | async-start | bytes 2949120 | tf_op jit(solution)/shard_map/reduce_scatter | solution.py:820
  243.4 54.0 %collective-permute-start.12 = (bf16[512,2304]{1,0:T(8,128)(2,1)}, bf16[512,2304]{1,0:T(8,128)(2,1)}, u32[]{:S(2)}, u32[]{:S(2)}) collective-permute-start(bf16[512,2304]{1,0:T(8,128)(2,1)} %shard_map.227.refs_1_), channel_id=1, source_target_pairs={{0,4},{4,0},{1,5},{5,1},{2,6},{6,2},{3,7},{7,3},{8,12},{12,8},{9,1... | collective-permute-start | bytes 7077896 | tf_op jit(solution)/shard_map/ppermute | solution.py:811
  244.1 41.4 %collective-permute-start.13 = (bf16[1024,2304]{1,0:T(8,128)(2,1)}, bf16[1024,2304]{1,0:T(8,128)(2,1)}, u32[]{:S(2)}, u32[]{:S(2)}) collective-permute-start(bf16[1024,2304]{1,0:T(8,128)(2,1)} %shard_map.226.refs_2_), channel_id=1, source_target_pairs={{0,2},{2,0},{1,3},{3,1},{4,6},{6,4},{5,7},{7,5},{8,10},{10,8},{9,1... | collective-permute-start | bytes 14155784 | tf_op jit(solution)/shard_map/ppermute | solution.py:814
  299.1 47.6 %collective-permute-start.15 = (bf16[512,1536]{1,0:T(8,128)(2,1)}, bf16[512,1536]{1,0:T(8,128)(2,1)}, u32[]{:S(2)}, u32[]{:S(2)}) collective-permute-start(bf16[512,1536]{1,0:T(8,128)(2,1)} %shard_map.231.refs_6_), channel_id=1, source_target_pairs={{0,4},{4,0},{1,5},{5,1},{2,6},{6,2},{3,7},{7,3},{8,12},{12,8},{9,1... | collective-permute-start | bytes 4718600 | tf_op jit(solution)/shard_map/ppermute | solution.py:811
  300.0 113.7 %reduce-scatter.10.cloned.1.call-start = ((), (), s32[]{:S(2)}) async-start(), calls=%async_computation.14 | async-start | bytes 2949120 | tf_op jit(solution)/shard_map/reduce_scatter | solution.py:820
  346.8 204.1 %reduce-scatter.18.cloned.1.call-start = ((), (), s32[]{:S(2)}) async-start(), calls=%async_computation.18 | async-start | bytes 2949120 | tf_op jit(solution)/shard_map/reduce_scatter | solution.py:820
  346.9 66.7 %collective-permute-start.21 = (bf16[512,2304]{1,0:T(8,128)(2,1)}, bf16[512,2304]{1,0:T(8,128)(2,1)}, u32[]{:S(2)}, u32[]{:S(2)}) collective-permute-start(bf16[512,2304]{1,0:T(8,128)(2,1)} %get-tuple-element.72.refs_5_), channel_id=1, source_target_pairs={{0,4},{4,0},{1,5},{5,1},{2,6},{6,2},{3,7},{7,3},{8,12},{12,8},{9,1... | collective-permute-start | bytes 7077896 | tf_op jit(solution)/shard_map/ppermute | solution.py:811
  347.6 48.9 %collective-permute-start.18 = (bf16[1024,2304]{1,0:T(8,128)(2,1)}, bf16[1024,2304]{1,0:T(8,128)(2,1)}, u32[]{:S(2)}, u32[]{:S(2)}) collective-permute-start(bf16[1024,2304]{1,0:T(8,128)(2,1)} %shard_map.236.refs_1_), channel_id=1, source_target_pairs={{0,2},{2,0},{1,3},{3,1},{4,6},{6,4},{5,7},{7,5},{8,10},{10,8},{9,1... | collective-permute-start | bytes 14155784 | tf_op jit(solution)/shard_map/ppermute | solution.py:814
  362.1 51.9 %collective-permute-start.22 = (bf16[128,2304]{1,0:T(8,128)(2,1)}, bf16[128,2304]{1,0:T(8,128)(2,1)}, u32[]{:S(2)}, u32[]{:S(2)}) collective-permute-start(bf16[128,2304]{1,0:T(8,128)(2,1)} %shard_map.239.refs_41_), channel_id=1, source_target_pairs={{0,4},{4,0},{1,5},{5,1},{2,6},{6,2},{3,7},{7,3},{8,12},{12,8},{9,1... | collective-permute-start | bytes 1769480 | tf_op jit(solution)/shard_map/ppermute | solution.py:811
  395.0 36.8 %collective-permute-start.20 = (bf16[384,2048]{1,0:T(8,128)(2,1)}, bf16[384,2048]{1,0:T(8,128)(2,1)}, u32[]{:S(2)}, u32[]{:S(2)}) collective-permute-start(bf16[384,2048]{1,0:T(8,128)(2,1)} %get-tuple-element.78), channel_id=1, source_target_pairs={{0,1},{1,0},{2,3},{3,2},{4,5},{5,4},{6,7},{7,6},{8,9},{9,8},{10,11... | collective-permute-start | bytes 4718600 | tf_op jit(solution)/shard_map/ppermute | solution.py:832
  407.0 61.6 %collective-permute-start.25 = (bf16[512,2304]{1,0:T(8,128)(2,1)}, bf16[512,2304]{1,0:T(8,128)(2,1)}, u32[]{:S(2)}, u32[]{:S(2)}) collective-permute-start(bf16[512,2304]{1,0:T(8,128)(2,1)} %get-tuple-element.77.refs_5_), channel_id=1, source_target_pairs={{0,4},{4,0},{1,5},{5,1},{2,6},{6,2},{3,7},{7,3},{8,12},{12,8},{9,1... | collective-permute-start | bytes 7077896 | tf_op jit(solution)/shard_map/ppermute | solution.py:811
  420.8 132.2 %reduce-scatter.20.cloned.1.call-start = ((), (), s32[]{:S(2)}) async-start(), calls=%async_computation.19 | async-start | bytes 2949120 | tf_op jit(solution)/shard_map/reduce_scatter | solution.py:820
  440.0 37.7 %collective-permute-start.24 = (bf16[384,2048]{1,0:T(8,128)(2,1)}, bf16[384,2048]{1,0:T(8,128)(2,1)}, u32[]{:S(2)}, u32[]{:S(2)}) collective-permute-start(bf16[384,2048]{1,0:T(8,128)(2,1)} %get-tuple-element.81.refs_6_.refs_1_), channel_id=1, source_target_pairs={{0,1},{1,0},{2,3},{3,2},{4,5},{5,4},{6,7},{7,6},{8,9},{9,8},{10,11... | collective-permute-start | bytes 4718600 | tf_op jit(solution)/shard_map/ppermute | solution.py:832
  450.5 51.4 %collective-permute-start.26 = (bf16[512,1536]{1,0:T(8,128)(2,1)}, bf16[512,1536]{1,0:T(8,128)(2,1)}, u32[]{:S(2)}, u32[]{:S(2)}) collective-permute-start(bf16[512,1536]{1,0:T(8,128)(2,1)} %get-tuple-element.82.refs_21_), channel_id=1, source_target_pairs={{0,4},{4,0},{1,5},{5,1},{2,6},{6,2},{3,7},{7,3},{8,12},{12,8},{9,1... | collective-permute-start | bytes 4718600 | tf_op jit(solution)/shard_map/ppermute | solution.py:811
  467.6 73.8 %collective-permute-start.23 = (bf16[384,2048]{1,0:T(8,128)(2,1)}, bf16[384,2048]{1,0:T(8,128)(2,1)}, u32[]{:S(2)}, u32[]{:S(2)}) collective-permute-start(bf16[384,2048]{1,0:T(8,128)(2,1)} %get-tuple-element.84), channel_id=1, source_target_pairs={{0,1},{1,0},{2,3},{3,2},{4,5},{5,4},{6,7},{7,6},{8,9},{9,8},{10,11... | collective-permute-start | bytes 4718600 | tf_op jit(solution)/shard_map/ppermute | solution.py:832
  472.7 93.1 %reduce-scatter.12.cloned.1.call-start = ((), (), s32[]{:S(2)}) async-start(), calls=%async_computation.15 | async-start | bytes 1966080 | tf_op jit(solution)/shard_map/reduce_scatter | solution.py:820
  501.5 39.9 %collective-permute-start.28 = (bf16[512,1024]{1,0:T(8,128)(2,1)}, bf16[512,1024]{1,0:T(8,128)(2,1)}, u32[]{:S(2)}, u32[]{:S(2)}) collective-permute-start(bf16[512,1024]{1,0:T(8,128)(2,1)} %get-tuple-element.88.refs_2_), channel_id=1, source_target_pairs={{0,4},{4,0},{1,5},{5,1},{2,6},{6,2},{3,7},{7,3},{8,12},{12,8},{9,1... | collective-permute-start | bytes 3145736 | tf_op jit(solution)/shard_map/ppermute | solution.py:811
  505.7 91.3 %reduce-scatter.14.cloned.1.call-start = ((), (), s32[]{:S(2)}) async-start(), calls=%async_computation.16 | async-start | bytes 1310720 | tf_op jit(solution)/shard_map/reduce_scatter | solution.py:820
  570.4 64.8 %reduce-scatter.16.cloned.1.call-start = ((), (), s32[]{:S(2)}) async-start(), calls=%async_computation.17 | async-start | bytes 1638400 | tf_op jit(solution)/shard_map/reduce_scatter | solution.py:820
  582.2 44.9 %collective-permute-start.30 = (bf16[384,2048]{1,0:T(8,128)(2,1)}, bf16[384,2048]{1,0:T(8,128)(2,1)}, u32[]{:S(2)}, u32[]{:S(2)}) collective-permute-start(bf16[384,2048]{1,0:T(8,128)(2,1)} %get-tuple-element.95.refs_1_), channel_id=1, source_target_pairs={{0,1},{1,0},{2,3},{3,2},{4,5},{5,4},{6,7},{7,6},{8,9},{9,8},{10,11... | collective-permute-start | bytes 4718600 | tf_op jit(solution)/shard_map/ppermute | solution.py:832
  (121 other events, 1722.8 us)
Sparse Core Ops, SparseCore 0:
  10.6 36.5 all-gather.6
  48.8 28.0 all-gather.8
  79.1 51.1 all-gather.10
  132.4 50.5 all-gather.12
  184.4 50.5 all-gather.14
  243.5 37.7 all-gather.16
  300.1 48.1 reduce-scatter.7
  350.6 47.5 reduce-scatter.9
  421.0 47.4 reduce-scatter.17
  472.9 47.6 reduce-scatter.19
  523.5 34.7 reduce-scatter.11
  570.5 26.4 reduce-scatter.13
  604.5 30.6 reduce-scatter.15

commit v8 on v6

--- a/solution.py
+++ b/solution.py
@@ -94,11 +94,11 @@
         head_of = lanes_of((queries, 256)) // HEAD_DIM
         lse = jnp.zeros((queries, 128), f32)
         for quad in range(q_ref.shape[1] // 256):
-            wide = q_ref[:, quad * 256 : quad * 256 + 256]
+            wide = q_ref[:, quad * 256 : quad * 256 + 256] * scale
             out = jnp.zeros((queries, 256), f32)
             for j in range(4):
                 one = jnp.where(head_of == j, wide, jnp.zeros_like(wide))
-                scores = dot_trans(one, key) * scale + bias
+                scores = dot_trans(one, key) + bias
                 top = jnp.max(scores, axis=1, keepdims=True)
                 powers = jnp.exp(scores - top)
                 sums = jnp.sum(powers, axis=1, keepdims=True)
@@ -135,22 +135,22 @@
         head_of = lanes_of((queries, 256)) // HEAD_DIM
         cosine, sine = cos_ref[...], sin_ref[...]
         for quad in range(q_ref.shape[1] // 256):
-            wide = q_ref[:, quad * 256 : quad * 256 + 256]
+            wide = q_ref[:, quad * 256 : quad * 256 + 256] * scale
             grads = g_ref[:, quad * 256 : quad * 256 + 256]
             out = jnp.zeros((queries, 256), f32)
             for j in range(4):
                 at = quad * 4 + j
                 one = jnp.where(head_of == j, wide, jnp.zeros_like(wide))
                 grad = jnp.where(head_of == j, grads, jnp.zeros_like(grads))
-                prob = jnp.exp(dot_trans(one, key) * scale + bias - lse_ref[:, at : at + 1])
+                prob = jnp.exp(dot_trans(one, key) + bias - lse_ref[:, at : at + 1])
                 prob_grad = dot_trans(grad, value)
                 centre = jnp.sum(prob * prob_grad, axis=1, keepdims=True)
-                score_grad = (prob * (prob_grad - centre) * scale).astype(bf16)
+                score_grad = (prob * (prob_grad - centre)).astype(bf16)
                 dvw_ref[pl.ds(start, keys), :] += dot_inner(prob.astype(bf16), grad)
                 dkw_ref[pl.ds(start, keys), :] += dot_inner(score_grad, one)
                 out = jnp.where(head_of == j, dot_plain(score_grad, key), out)
             for half in range(2):
-                piece = turn(out[:, half * 128 : half * 128 + 128], cosine, -sine)
+                piece = turn(out[:, half * 128 : half * 128 + 128] * scale, cosine, -sine)
                 dq_ref[:, quad * 256 + half * 128 : quad * 256 + half * 128 + 128] = piece.astype(bf16)
 
     for blocks in range(1, row_ref.shape[1] // queries + 1):

time: 656 us -> 670 us (1.021)
  Pallas kernels: 373 us -> 383 us
    pallas_call x59, Pallas kernels: 373 us -> 383 us  [launch(): pl.pallas_call(body, grid_spec=pltpu.PrefetchScalarGridSpec(num_scalar_pr...]
  transfers between devices with their start and end apart: 50 -> 50, of which waited for: 22 -> 22; matrix products, arithmetic and copies ran while one was open for 2% -> 2% of each run, Pallas kernels for 57% -> 58%
where the time goes in v8:
time: 670 us; the launch traced here: 658 us
  Pallas kernels  383 us (57%)
  waiting for transfers between devices  166 us (25%)
  local copies, waits for them, and re-layouts  54.5 us (8%)
  starting transfers between devices  27.7 us (4%)
  between operations  15.2 us (2%)
  other arithmetic  11.9 us (2%)
    pallas_call x59, Pallas kernels, launch(): pl.pallas_call(body, grid_spec=pltpu.PrefetchScalarGridSpec(num_scalar_pr...  383 us
    ppermute x8, waiting for transfers between devices, swap(): return lax.ppermute(own, 'tensor', SWAP)  76.3 us
    unnamed x220, local copies, waits for them, and re-layouts  49.9 us
    ppermute x12, waiting for transfers between devices, over_x(): return lax.ppermute(array, 'x', SWAP)  35.5 us
    all_gather x6, waiting for transfers between devices, gather(): return lax.all_gather(operand, ('core', 'z'), axis=0, tiled=True)  32.7 us
  transfers between devices with their start and end apart: 50, of which 22 were waited for; matrix products, arithmetic and copies ran while one was open for 2% of the time, Pallas kernels for 58%

profile of v8, /device:TPU:0, one launch (start us, length us, event | category | flops | bytes accessed | tf_op | source)
XLA Modules:
  0.0 657.7 jit_solution(5008321704825579929)
XLA Ops:
  27.7 19.5 %all-gather.7.cloned.1.call-done.refs_1_.refs_3_.refs_5_.refs_4_.refs_6_.refs_8_.refs_10_.refs_12_.refs_14_ = bf16[1024,1280]{1,0:T(8,128)(2,1)} async-done(((bf16[128,1280]{1,0:T(8,128)(2,1)}), bf16[1024,1280]{1,0:T(8,128)(2,1)}) %all-gather.7.cloned.1.call-update) | async-done | bytes 2621456 | tf_op jit(solution)/shard_map/all_gather | solution.py:790
  64.5 17.6 %collective-permute-done.1.refs_0_ = bf16[512,1280]{1,0:T(8,128)(2,1)} collective-permute-done((bf16[512,1280]{1,0:T(8,128)(2,1)S(1)}, bf16[512,1280]{1,0:T(8,128)(2,1)}, u32[]{:S(2)}, u32[]{:S(2)}) %collective-permute-start.1) | collective-permute-done | bytes 1310752 | tf_op jit(solution)/shard_map/ppermute | solution.py:784
  89.2 10.7 %shard_map.215.refs_1_.refs_2_.refs_3_.refs_6_ = bf16[768,1280]{1,0:T(8,128)(2,1)} custom-call(s32[3]{0:T(128)S(1)} %pad_add_fusion.refs_0_, bf16[384,2048]{1,0:T(8,128)(2,1)} %get-tuple-element.58.refs_1_, bf16[384,2048]{1,0:T(8,128)(2,1)} %copy-done.27, ...), custom_call_target="tpu_custom_call" | custom-call | flops 100663296000 | bytes 1024 | tf_op jit(solution)/shard_map/pallas_call | solution.py:178
  101.5 15.9 %shard_map.216 = (bf16[768,1024]{1,0:T(8,128)(2,1)S(1)}, f32[768,256]{1,0:T(8,128)S(1)}) custom-call(s32[3]{0:T(128)S(1)} %convert_reduce_fusion.1.refs_6_.refs_0_, bf16[768,1280]{1,0:T(8,128)(2,1)S(1)} %copy-done.94, bf16[768,1280]{1,0:T(8,128)(2,1)S(1)} %copy-done.94, bf16[768,1280]{1,0:T(8,128)(2,1)S(1)} %copy-done.94, ...), custom_call_target="tpu_custom_call" | custom-call | flops 160000000000 | bytes 1024 | tf_op jit(solution)/shard_map/pallas_call | solution.py:178
  123.5 9.2 %shard_map.219 = (f32[384,2048]{1,0:T(8,128)}, bf16[384,2048]{1,0:T(8,128)(2,1)}) custom-call(s32[3]{0:T(128)S(1)} %pad_add_fusion.refs_0_, bf16[768,1024]{1,0:T(8,128)(2,1)S(1)} %get-tuple-element.59.refs_1_, bf16[1024,1024]{1,0:T(8,128)(2,1)} %all-gather.9.cloned.1.call-done.refs_1_.refs_2_.refs_4_.refs_3_.refs_5_, ...), custom_call_target="tpu_custom_call" | custom-call | flops 56512729088 | bytes 1024 | tf_op jit(solution)/shard_map/pallas_call | solution.py:178
  141.2 28.4 %collective-permute-done.6.refs_2_ = bf16[384,2048]{1,0:T(8,128)(2,1)} collective-permute-done((bf16[384,2048]{1,0:T(8,128)(2,1)}, bf16[384,2048]{1,0:T(8,128)(2,1)}, u32[]{:S(2)}, u32[]{:S(2)}) %collective-permute-start.6) | collective-permute-done | bytes 1572896 | tf_op jit(solution)/shard_map/ppermute | solution.py:805
  176.7 6.2 all-gather.13.cloned.1.call-done.refs_1_.refs_3_.refs_5_.refs_7_.refs_9_.refs_11_.refs_13_.refs_17_.refs_19_.refs_21_.refs_23_
  188.8 6.2 collective-permute-done.8.refs_0_
  195.0 16.3 %collective-permute-done.7.refs_2_ = bf16[384,2048]{1,0:T(8,128)(2,1)} collective-permute-done((bf16[384,2048]{1,0:T(8,128)(2,1)}, bf16[384,2048]{1,0:T(8,128)(2,1)}, u32[]{:S(2)}, u32[]{:S(2)}) %collective-permute-start.7) | collective-permute-done | bytes 1572896 | tf_op jit(solution)/shard_map/ppermute | solution.py:805
  217.5 12.9 %shard_map.225 = (bf16[768,768]{1,0:T(8,128)(2,1)S(1)}, bf16[768,768]{1,0:T(8,128)(2,1)S(1)}, bf16[768,768]{1,0:T(8,128)(2,1)S(1)}) custom-call(s32[3]{0:T(128)S(1)} %pad_add_fusion.refs_0_, bf16[768,2048]{1,0:T(8,128)(2,1)} %shard_map.224.refs_1_.refs_15_.refs_0_, bf16[768,2048]{1,0:T(8,128)(2,1)} %shard_map.218.refs_6_.refs_2_.refs_1_, ...), custom_call_target="tpu_custom_call" | custom-call | flops 120795955200 | bytes 1024 | tf_op jit(solution)/shard_map/pallas_call | solution.py:178
  230.5 7.3 %shard_map.226.refs_2_ = bf16[1024,2304]{1,0:T(8,128)(2,1)} custom-call(bf16[768,2048]{1,0:T(8,128)(2,1)} %shard_map.224.refs_1_.refs_15_.refs_0_, bf16[768,2048]{1,0:T(8,128)(2,1)} %shard_map.218.refs_6_.refs_2_.refs_1_, bf16[768,768]{1,0:T(8,128)(2,1)S(1)} %get-tuple-element.65.refs_2_.refs_1_, bf16[768,768]{1,0:T(8,128)(2,1)S(1)} %get-tuple-element.66.refs_3_.refs_2_, ...), custom_call_target="tpu_custom_call" | custom-call | flops 75497472000 | bytes 1024 | tf_op jit(solution)/shard_map/pallas_call | solution.py:178
  252.2 13.0 %shard_map.229 = (bf16[768,768]{1,0:T(8,128)(2,1)S(1)}, bf16[768,768]{1,0:T(8,128)(2,1)S(1)}, bf16[768,768]{1,0:T(8,128)(2,1)S(1)}) custom-call(s32[3]{0:T(128)S(1)} %pad_add_fusion.refs_0_, bf16[768,2048]{1,0:T(8,128)(2,1)} %shard_map.224.refs_1_.refs_15_.refs_0_, bf16[768,2048]{1,0:T(8,128)(2,1)} %shard_map.218.refs_6_.refs_2_.refs_1_, ...), custom_call_target="tpu_custom_call" | custom-call | flops 120795955200 | bytes 1024 | tf_op jit(solution)/shard_map/pallas_call | solution.py:178
  265.2 7.3 %shard_map.230.refs_2_ = bf16[1024,2304]{1,0:T(8,128)(2,1)} custom-call(bf16[768,2048]{1,0:T(8,128)(2,1)} %shard_map.224.refs_1_.refs_15_.refs_0_, bf16[768,2048]{1,0:T(8,128)(2,1)} %shard_map.218.refs_6_.refs_2_.refs_1_, bf16[768,768]{1,0:T(8,128)(2,1)S(1)} %get-tuple-element.68.refs_2_.refs_3_, bf16[768,768]{1,0:T(8,128)(2,1)S(1)} %get-tuple-element.69.refs_3_.refs_4_, ...), custom_call_target="tpu_custom_call" | custom-call | flops 75497472000 | bytes 1024 | tf_op jit(solution)/shard_map/pallas_call | solution.py:178
  275.6 7.0 %all-gather.17.cloned.1.call-done.refs_1_.refs_3_.refs_5_.refs_7_.refs_9_.refs_11_.refs_13_.refs_33_.refs_35_.refs_37_.refs_39_.refs_17_.refs_19_ = bf16[1024,1536]{1,0:T(8,128)(2,1)} async-done(((bf16[128,1536]{1,0:T(8,128)(2,1)}), bf16[1024,1536]{1,0:T(8,128)(2,1)}) %all-gather.17.cloned.1.call-update) | async-done | bytes 3145744 | tf_op jit(solution)/shard_map/all_gather | solution.py:790
  286.8 10.4 %shard_map.232 = (bf16[512,2304]{1,0:T(8,128)(2,1)}, bf16[512,2304]{1,0:T(8,128)(2,1)}) custom-call(bf16[768,2048]{1,0:T(8,128)(2,1)} %shard_map.224.refs_1_.refs_15_.refs_0_, bf16[768,2048]{1,0:T(8,128)(2,1)} %shard_map.218.refs_6_.refs_2_.refs_1_, bf16[768,768]{1,0:T(8,128)(2,1)S(1)} %copy-done.81, bf16[768,768]{1,0:T(8,128)(2,1)S(1)} %copy-done.84, ...), custom_call_target="tpu_custom_call" | custom-call | flops 75497472000 | bytes 1024 | tf_op jit(solution)/shard_map/pallas_call | solution.py:178
  306.1 23.7 %shard_map.234 = (bf16[768,768]{1,0:T(8,128)(2,1)S(1)}, bf16[768,768]{1,0:T(8,128)(2,1)S(1)}, bf16[768,768]{1,0:T(8,128)(2,1)S(1)}) custom-call(s32[3]{0:T(128)S(1)} %pad_add_fusion.refs_0_, bf16[768,2048]{1,0:T(8,128)(2,1)} %shard_map.224.refs_1_.refs_15_.refs_0_, bf16[768,2048]{1,0:T(8,128)(2,1)} %shard_map.218.refs_6_.refs_2_.refs_1_, ...), custom_call_target="tpu_custom_call" | custom-call | flops 120795955200 | bytes 1024 | tf_op jit(solution)/shard_map/pallas_call | solution.py:178
  329.9 11.7 %shard_map.235 = (bf16[512,2304]{1,0:T(8,128)(2,1)}, bf16[512,2304]{1,0:T(8,128)(2,1)}) custom-call(bf16[768,2048]{1,0:T(8,128)(2,1)} %shard_map.224.refs_1_.refs_15_.refs_0_, bf16[768,2048]{1,0:T(8,128)(2,1)} %shard_map.218.refs_6_.refs_2_.refs_1_, bf16[768,768]{1,0:T(8,128)(2,1)S(1)} %copy-done.90, bf16[768,768]{1,0:T(8,128)(2,1)S(1)} %copy-done.93, ...), custom_call_target="tpu_custom_call" | custom-call | flops 75497472000 | bytes 1024 | tf_op jit(solution)/shard_map/pallas_call | solution.py:178
  341.6 7.2 %shard_map.236.refs_1_ = bf16[1024,2304]{1,0:T(8,128)(2,1)} custom-call(bf16[768,2048]{1,0:T(8,128)(2,1)} %shard_map.224.refs_1_.refs_15_.refs_0_, bf16[768,2048]{1,0:T(8,128)(2,1)} %shard_map.218.refs_6_.refs_2_.refs_1_, bf16[768,768]{1,0:T(8,128)(2,1)S(1)} %get-tuple-element.72.refs_2_.refs_5_, bf16[768,768]{1,0:T(8,128)(2,1)S(1)} %get-tuple-element.73.refs_3_.refs_6_, ...), custom_call_target="tpu_custom_call" | custom-call | flops 75497472000 | bytes 1024 | tf_op jit(solution)/shard_map/pallas_call | solution.py:178
  352.5 9.9 %shard_map.238 = (bf16[768,512]{1,0:T(8,128)(2,1)S(1)}, bf16[768,512]{1,0:T(8,128)(2,1)S(1)}, bf16[768,512]{1,0:T(8,128)(2,1)S(1)}) custom-call(s32[3]{0:T(128)S(1)} %pad_add_fusion.refs_0_, bf16[768,2048]{1,0:T(8,128)(2,1)} %shard_map.224.refs_1_.refs_15_.refs_0_, bf16[768,2048]{1,0:T(8,128)(2,1)} %shard_map.218.refs_6_.refs_2_.refs_1_, ...), custom_call_target="tpu_custom_call" | custom-call | flops 80530636800 | bytes 1024 | tf_op jit(solution)/shard_map/pallas_call | solution.py:178
  365.9 30.0 %shard_map.240 = (f32[384,2048]{1,0:T(8,128)}, bf16[384,2048]{1,0:T(8,128)(2,1)}) custom-call(s32[3]{0:T(128)S(1)} %pad_add_fusion.refs_0_, bf16[768,768]{1,0:T(8,128)(2,1)S(1)} %copy-done.82, bf16[768,768]{1,0:T(8,128)(2,1)S(1)} %copy-done.85, bf16[768,768]{1,0:T(8,128)(2,1)S(1)} %copy-done.91, bf16[768,768]{1,0:T(8,128)(2,1)} %copy-done.92, ...), custom_call_target="tpu_custom_call" | custom-call | flops 310820012032 | bytes 1024 | tf_op jit(solution)/shard_map/pallas_call | solution.py:178
  397.4 10.5 %shard_map.241 = (bf16[512,2304]{1,0:T(8,128)(2,1)}, bf16[512,2304]{1,0:T(8,128)(2,1)}) custom-call(bf16[768,2048]{1,0:T(8,128)(2,1)} %shard_map.224.refs_1_.refs_15_.refs_0_, bf16[768,2048]{1,0:T(8,128)(2,1)} %shard_map.218.refs_6_.refs_2_.refs_1_, bf16[768,768]{1,0:T(8,128)(2,1)S(1)} %copy-done.74, bf16[768,768]{1,0:T(8,128)(2,1)S(1)} %copy-done.76, ...), custom_call_target="tpu_custom_call" | custom-call | flops 75497472000 | bytes 1024 | tf_op jit(solution)/shard_map/pallas_call | solution.py:178
  421.5 11.2 %collective-permute-done.20.refs_1_ = bf16[384,2048]{1,0:T(8,128)(2,1)} collective-permute-done((bf16[384,2048]{1,0:T(8,128)(2,1)}, bf16[384,2048]{1,0:T(8,128)(2,1)}, u32[]{:S(2)}, u32[]{:S(2)}) %collective-permute-start.20) | collective-permute-done | bytes 1572896 | tf_op jit(solution)/shard_map/ppermute | solution.py:805
  432.6 8.3 %shard_map.244 = (bf16[384,2048]{1,0:T(8,128)(2,1)}, f32[384,2048]{1,0:T(8,128)}, f32[1,2048]{1,0:T(1,128)S(1)}) custom-call(f32[384,2048]{1,0:T(8,128)} %get-tuple-element.78.refs_6_.refs_0_, bf16[384,2048]{1,0:T(8,128)(2,1)} %collective-permute-done.20.refs_1_, f32[384,2048]{1,0:T(8,128)} %get-tuple-element.62.refs_2_.refs_1_, ...), custom_call_target="tpu_custom_call" | custom-call | flops 80000000000 | bytes 1024 | tf_op jit(solution)/shard_map/pallas_call | solution.py:178
  442.4 7.9 %shard_map.245 = (bf16[512,1536]{1,0:T(8,128)(2,1)}, bf16[512,1536]{1,0:T(8,128)(2,1)S(1)}) custom-call(bf16[768,2048]{1,0:T(8,128)(2,1)} %shard_map.224.refs_1_.refs_15_.refs_0_, bf16[768,2048]{1,0:T(8,128)(2,1)} %shard_map.218.refs_6_.refs_2_.refs_1_, bf16[768,512]{1,0:T(8,128)(2,1)S(1)} %copy-done.66, bf16[768,512]{1,0:T(8,128)(2,1)S(1)} %copy-done.69, ...), custom_call_target="tpu_custom_call" | custom-call | flops 50331648000 | bytes 1024 | tf_op jit(solution)/shard_map/pallas_call | solution.py:178
  450.7 16.7 %shard_map.246 = (f32[384,2048]{1,0:T(8,128)}, bf16[384,2048]{1,0:T(8,128)(2,1)}) custom-call(s32[3]{0:T(128)S(1)} %pad_add_fusion.refs_0_, bf16[768,768]{1,0:T(8,128)(2,1)S(1)} %copy-done.79, bf16[768,768]{1,0:T(8,128)(2,1)S(1)} %copy-done.88, bf16[768,768]{1,0:T(8,128)(2,1)S(1)} %copy-done.72, bf16[768,512]{1,0:T(8,128)(2,1)S(1)} %get-tuple-element.75.refs_1_.refs_4_, ...), custom_call_target="tpu_custom_call" | custom-call | flops 155410006016 | bytes 1024 | tf_op jit(solution)/shard_map/pallas_call | solution.py:178
  488.4 7.1 %shard_map.250.refs_3_.refs_4_ = bf16[768,1024]{1,0:T(8,128)(2,1)S(1)} custom-call(s32[3]{0:T(128)S(1)} %pad_add_fusion.refs_0_, bf16[384,2048]{1,0:T(8,128)(2,1)} %get-tuple-element.83.refs_6_.refs_1_, bf16[384,2048]{1,0:T(8,128)(2,1)} %collective-permute-done.24.refs_2_, ...), custom_call_target="tpu_custom_call" | custom-call | flops 80530636800 | bytes 1024 | tf_op jit(solution)/shard_map/pallas_call | solution.py:178
  514.7 35.4 %shard_map.253 = (bf16[768,1024]{1,0:T(8,128)(2,1)S(1)}, bf16[768,128]{1,0:T(8,128)(2,1)S(1)}, bf16[768,128]{1,0:T(8,128)(2,1)S(1)}) custom-call(s32[3]{0:T(128)S(1)} %copy-done.40, bf16[768,1280]{1,0:T(8,128)(2,1)} %shard_map.215.refs_1_.refs_2_.refs_3_.refs_6_, bf16[768,1280]{1,0:T(8,128)(2,1)} %shard_map.215.refs_1_.refs_2_.refs_3_.refs_6_, ...), custom_call_target="tpu_custom_call" | custom-call | flops 349999988736 | bytes 1024 | tf_op jit(solution)/shard_map/pallas_call | solution.py:178
  563.1 7.6 %shard_map.256 = (bf16[512,1280]{1,0:T(8,128)(2,1)}, bf16[512,1280]{1,0:T(8,128)(2,1)S(1)}) custom-call(bf16[768,2048]{1,0:T(8,128)(2,1)} %shard_map.212.refs_1_.refs_0_, bf16[768,1024]{1,0:T(8,128)(2,1)S(1)} %get-tuple-element.91.refs_1_.refs_4_, bf16[768,128]{1,0:T(8,128)(2,1)S(1)} %get-tuple-element.92.refs_2_, ...), custom_call_target="tpu_custom_call" | custom-call | flops 41943040000 | bytes 1024 | tf_op jit(solution)/shard_map/pallas_call | solution.py:178
  573.4 11.6 %shard_map.257 = (f32[384,2048]{1,0:T(8,128)}, bf16[384,2048]{1,0:T(8,128)(2,1)}) custom-call(s32[3]{0:T(128)S(1)} %copy-done.19, bf16[768,1024]{1,0:T(8,128)(2,1)} %copy-done, bf16[768,128]{1,0:T(8,128)(2,1)S(1)} %get-tuple-element.92.refs_2_, bf16[768,128]{1,0:T(8,128)(2,1)S(1)} %get-tuple-element.93.refs_3_, ...), custom_call_target="tpu_custom_call" | custom-call | flops 70640910336 | bytes 1024 | tf_op jit(solution)/shard_map/pallas_call | solution.py:178
  595.4 7.6 %collective-permute-done.31.refs_1_ = bf16[512,1280]{1,0:T(8,128)(2,1)} collective-permute-done((bf16[512,1280]{1,0:T(8,128)(2,1)}, bf16[512,1280]{1,0:T(8,128)(2,1)}, u32[]{:S(2)}, u32[]{:S(2)}) %collective-permute-start.31) | collective-permute-done | bytes 1310752 | tf_op jit(solution)/shard_map/ppermute | solution.py:784
  610.3 11.0 %collective-permute-done.30.refs_2_ = bf16[384,2048]{1,0:T(8,128)(2,1)S(1)} collective-permute-done((bf16[384,2048]{1,0:T(8,128)(2,1)}, bf16[384,2048]{1,0:T(8,128)(2,1)S(1)}, u32[]{:S(2)}, u32[]{:S(2)}) %collective-permute-start.30) | collective-permute-done | bytes 1572896 | tf_op jit(solution)/shard_map/ppermute | solution.py:805
  622.7 6.6 shard_map.261
  (408 shorter events, 230.5 us)
Async XLA Ops:
  7.2 40.0 %all-gather.7.cloned.1.call-start = ((), (), s32[]{:S(2)}) async-start(), calls=%async_computation.7 | async-start | bytes 2949120 | tf_op jit(solution)/shard_map/all_gather | solution.py:790
  10.5 73.6 %all-gather.9.cloned.1.call-start = ((), (), s32[]{:S(2)}) async-start(), calls=%async_computation.8 | async-start | bytes 2359296 | tf_op jit(solution)/shard_map/all_gather | solution.py:790
  11.5 122.8 %all-gather.11.cloned.1.call-start = ((), (), s32[]{:S(2)}) async-start(), calls=%async_computation.9 | async-start | bytes 5308416 | tf_op jit(solution)/shard_map/all_gather | solution.py:790
  13.8 169.2 %all-gather.13.cloned.1.call-start = ((), (), s32[]{:S(2)}) async-start(), calls=%async_computation.10 | async-start | bytes 5308416 | tf_op jit(solution)/shard_map/all_gather | solution.py:790
  14.7 226.1 %all-gather.15.cloned.1.call-start = ((), (), s32[]{:S(2)}) async-start(), calls=%async_computation.11 | async-start | bytes 5308416 | tf_op jit(solution)/shard_map/all_gather | solution.py:790
  15.7 266.9 %all-gather.17.cloned.1.call-start = ((), (), s32[]{:S(2)}) async-start(), calls=%async_computation.12 | async-start | bytes 3538944 | tf_op jit(solution)/shard_map/all_gather | solution.py:790
  21.5 38.4 %collective-permute-start = (bf16[384,2048]{1,0:T(8,128)(2,1)}, bf16[384,2048]{1,0:T(8,128)(2,1)S(1)}, u32[]{:S(2)}, u32[]{:S(2)}) collective-permute-start(bf16[384,2048]{1,0:T(8,128)(2,1)} %get-tuple-element.58.refs_1_), channel_id=1, source_target_pairs={{0,1},{1,0},{2,3},{3,2},{4,5},{5,4},{6,7},{7,6},{8,9},{9,8},{10,11... | collective-permute-start | bytes 4718600 | tf_op jit(solution)/shard_map/ppermute | solution.py:805
  55.1 63.5 %collective-permute-start.5 = (bf16[384,2048]{1,0:T(8,128)(2,1)}, bf16[384,2048]{1,0:T(8,128)(2,1)}, u32[]{:S(2)}, u32[]{:S(2)}) collective-permute-start(bf16[384,2048]{1,0:T(8,128)(2,1)} %shard_map.211.refs_3_.refs_1_), channel_id=1, source_target_pairs={{0,1},{1,0},{2,3},{3,2},{4,5},{5,4},{6,7},{7,6},{8,9},{9,8},{10,11... | collective-permute-start | bytes 4718600 | tf_op jit(solution)/shard_map/ppermute | solution.py:805
  132.8 36.9 %collective-permute-start.6 = (bf16[384,2048]{1,0:T(8,128)(2,1)}, bf16[384,2048]{1,0:T(8,128)(2,1)}, u32[]{:S(2)}, u32[]{:S(2)}) collective-permute-start(bf16[384,2048]{1,0:T(8,128)(2,1)} %get-tuple-element.61), channel_id=1, source_target_pairs={{0,1},{1,0},{2,3},{3,2},{4,5},{5,4},{6,7},{7,6},{8,9},{9,8},{10,11... | collective-permute-start | bytes 4718600 | tf_op jit(solution)/shard_map/ppermute | solution.py:805
  140.7 54.3 %collective-permute-start.8 = (bf16[512,2304]{1,0:T(8,128)(2,1)}, bf16[512,2304]{1,0:T(8,128)(2,1)S(1)}, u32[]{:S(2)}, u32[]{:S(2)}) collective-permute-start(bf16[512,2304]{1,0:T(8,128)(2,1)} %shard_map.220.refs_4_), channel_id=1, source_target_pairs={{0,4},{4,0},{1,5},{5,1},{2,6},{6,2},{3,7},{7,3},{8,12},{12,8},{9,1... | collective-permute-start | bytes 7077896 | tf_op jit(solution)/shard_map/ppermute | solution.py:784
  175.3 36.0 %collective-permute-start.7 = (bf16[384,2048]{1,0:T(8,128)(2,1)}, bf16[384,2048]{1,0:T(8,128)(2,1)}, u32[]{:S(2)}, u32[]{:S(2)}) collective-permute-start(bf16[384,2048]{1,0:T(8,128)(2,1)} %get-tuple-element.63.refs_2_.refs_1_), channel_id=1, source_target_pairs={{0,1},{1,0},{2,3},{3,2},{4,5},{5,4},{6,7},{7,6},{8,9},{9,8},{10,11... | collective-permute-start | bytes 4718600 | tf_op jit(solution)/shard_map/ppermute | solution.py:805
  187.3 58.1 %collective-permute-start.10 = (bf16[512,2304]{1,0:T(8,128)(2,1)}, bf16[512,2304]{1,0:T(8,128)(2,1)}, u32[]{:S(2)}, u32[]{:S(2)}) collective-permute-start(bf16[512,2304]{1,0:T(8,128)(2,1)} %shard_map.222.refs_1_), channel_id=1, source_target_pairs={{0,4},{4,0},{1,5},{5,1},{2,6},{6,2},{3,7},{7,3},{8,12},{12,8},{9,1... | collective-permute-start | bytes 7077896 | tf_op jit(solution)/shard_map/ppermute | solution.py:784
  245.4 117.9 %reduce-scatter.8.cloned.1.call-start = ((), (), s32[]{:S(2)}) async-start(), calls=%async_computation.13 | async-start | bytes 2949120 | tf_op jit(solution)/shard_map/reduce_scatter | solution.py:793
  245.5 54.0 %collective-permute-start.12 = (bf16[512,2304]{1,0:T(8,128)(2,1)}, bf16[512,2304]{1,0:T(8,128)(2,1)}, u32[]{:S(2)}, u32[]{:S(2)}) collective-permute-start(bf16[512,2304]{1,0:T(8,128)(2,1)} %shard_map.227.refs_1_), channel_id=1, source_target_pairs={{0,4},{4,0},{1,5},{5,1},{2,6},{6,2},{3,7},{7,3},{8,12},{12,8},{9,1... | collective-permute-start | bytes 7077896 | tf_op jit(solution)/shard_map/ppermute | solution.py:784
  245.7 41.1 %collective-permute-start.13 = (bf16[1024,2304]{1,0:T(8,128)(2,1)}, bf16[1024,2304]{1,0:T(8,128)(2,1)}, u32[]{:S(2)}, u32[]{:S(2)}) collective-permute-start(bf16[1024,2304]{1,0:T(8,128)(2,1)} %shard_map.226.refs_2_), channel_id=1, source_target_pairs={{0,2},{2,0},{1,3},{3,1},{4,6},{6,4},{5,7},{7,5},{8,10},{10,8},{9,1... | collective-permute-start | bytes 14155784 | tf_op jit(solution)/shard_map/ppermute | solution.py:787
  301.2 47.7 %collective-permute-start.15 = (bf16[512,1536]{1,0:T(8,128)(2,1)}, bf16[512,1536]{1,0:T(8,128)(2,1)}, u32[]{:S(2)}, u32[]{:S(2)}) collective-permute-start(bf16[512,1536]{1,0:T(8,128)(2,1)} %shard_map.231.refs_6_), channel_id=1, source_target_pairs={{0,4},{4,0},{1,5},{5,1},{2,6},{6,2},{3,7},{7,3},{8,12},{12,8},{9,1... | collective-permute-start | bytes 4718600 | tf_op jit(solution)/shard_map/ppermute | solution.py:784
  301.8 112.7 %reduce-scatter.10.cloned.1.call-start = ((), (), s32[]{:S(2)}) async-start(), calls=%async_computation.14 | async-start | bytes 2949120 | tf_op jit(solution)/shard_map/reduce_scatter | solution.py:793
  349.0 147.6 %reduce-scatter.18.cloned.1.call-start = ((), (), s32[]{:S(2)}) async-start(), calls=%async_computation.18 | async-start | bytes 2949120 | tf_op jit(solution)/shard_map/reduce_scatter | solution.py:793
  349.1 65.3 %collective-permute-start.21 = (bf16[512,2304]{1,0:T(8,128)(2,1)}, bf16[512,2304]{1,0:T(8,128)(2,1)}, u32[]{:S(2)}, u32[]{:S(2)}) collective-permute-start(bf16[512,2304]{1,0:T(8,128)(2,1)} %get-tuple-element.74.refs_5_), channel_id=1, source_target_pairs={{0,4},{4,0},{1,5},{5,1},{2,6},{6,2},{3,7},{7,3},{8,12},{12,8},{9,1... | collective-permute-start | bytes 7077896 | tf_op jit(solution)/shard_map/ppermute | solution.py:784
  349.4 47.9 %collective-permute-start.18 = (bf16[1024,2304]{1,0:T(8,128)(2,1)}, bf16[1024,2304]{1,0:T(8,128)(2,1)}, u32[]{:S(2)}, u32[]{:S(2)}) collective-permute-start(bf16[1024,2304]{1,0:T(8,128)(2,1)} %shard_map.236.refs_1_), channel_id=1, source_target_pairs={{0,2},{2,0},{1,3},{3,1},{4,6},{6,4},{5,7},{7,5},{8,10},{10,8},{9,1... | collective-permute-start | bytes 14155784 | tf_op jit(solution)/shard_map/ppermute | solution.py:787
  363.4 52.8 %collective-permute-start.22 = (bf16[128,2304]{1,0:T(8,128)(2,1)}, bf16[128,2304]{1,0:T(8,128)(2,1)}, u32[]{:S(2)}, u32[]{:S(2)}) collective-permute-start(bf16[128,2304]{1,0:T(8,128)(2,1)} %shard_map.239.refs_41_), channel_id=1, source_target_pairs={{0,4},{4,0},{1,5},{5,1},{2,6},{6,2},{3,7},{7,3},{8,12},{12,8},{9,1... | collective-permute-start | bytes 1769480 | tf_op jit(solution)/shard_map/ppermute | solution.py:784
  395.8 36.8 %collective-permute-start.20 = (bf16[384,2048]{1,0:T(8,128)(2,1)}, bf16[384,2048]{1,0:T(8,128)(2,1)}, u32[]{:S(2)}, u32[]{:S(2)}) collective-permute-start(bf16[384,2048]{1,0:T(8,128)(2,1)} %get-tuple-element.80), channel_id=1, source_target_pairs={{0,1},{1,0},{2,3},{3,2},{4,5},{5,4},{6,7},{7,6},{8,9},{9,8},{10,11... | collective-permute-start | bytes 4718600 | tf_op jit(solution)/shard_map/ppermute | solution.py:805
  407.9 60.4 %collective-permute-start.25 = (bf16[512,2304]{1,0:T(8,128)(2,1)}, bf16[512,2304]{1,0:T(8,128)(2,1)}, u32[]{:S(2)}, u32[]{:S(2)}) collective-permute-start(bf16[512,2304]{1,0:T(8,128)(2,1)} %get-tuple-element.79.refs_5_), channel_id=1, source_target_pairs={{0,4},{4,0},{1,5},{5,1},{2,6},{6,2},{3,7},{7,3},{8,12},{12,8},{9,1... | collective-permute-start | bytes 7077896 | tf_op jit(solution)/shard_map/ppermute | solution.py:784
  421.4 134.9 %reduce-scatter.20.cloned.1.call-start = ((), (), s32[]{:S(2)}) async-start(), calls=%async_computation.19 | async-start | bytes 2949120 | tf_op jit(solution)/shard_map/reduce_scatter | solution.py:793
  440.9 37.7 %collective-permute-start.24 = (bf16[384,2048]{1,0:T(8,128)(2,1)}, bf16[384,2048]{1,0:T(8,128)(2,1)}, u32[]{:S(2)}, u32[]{:S(2)}) collective-permute-start(bf16[384,2048]{1,0:T(8,128)(2,1)} %get-tuple-element.83.refs_6_.refs_1_), channel_id=1, source_target_pairs={{0,1},{1,0},{2,3},{3,2},{4,5},{5,4},{6,7},{7,6},{8,9},{9,8},{10,11... | collective-permute-start | bytes 4718600 | tf_op jit(solution)/shard_map/ppermute | solution.py:805
  450.3 56.9 %collective-permute-start.26 = (bf16[512,1536]{1,0:T(8,128)(2,1)}, bf16[512,1536]{1,0:T(8,128)(2,1)}, u32[]{:S(2)}, u32[]{:S(2)}) collective-permute-start(bf16[512,1536]{1,0:T(8,128)(2,1)} %get-tuple-element.84.refs_21_), channel_id=1, source_target_pairs={{0,4},{4,0},{1,5},{5,1},{2,6},{6,2},{3,7},{7,3},{8,12},{12,8},{9,1... | collective-permute-start | bytes 4718600 | tf_op jit(solution)/shard_map/ppermute | solution.py:784
  467.4 123.1 %collective-permute-start.23 = (bf16[384,2048]{1,0:T(8,128)(2,1)}, bf16[384,2048]{1,0:T(8,128)(2,1)}, u32[]{:S(2)}, u32[]{:S(2)}) collective-permute-start(bf16[384,2048]{1,0:T(8,128)(2,1)} %get-tuple-element.86), channel_id=1, source_target_pairs={{0,1},{1,0},{2,3},{3,2},{4,5},{5,4},{6,7},{7,6},{8,9},{9,8},{10,11... | collective-permute-start | bytes 4718600 | tf_op jit(solution)/shard_map/ppermute | solution.py:805
  472.4 86.1 %reduce-scatter.12.cloned.1.call-start = ((), (), s32[]{:S(2)}) async-start(), calls=%async_computation.15 | async-start | bytes 1966080 | tf_op jit(solution)/shard_map/reduce_scatter | solution.py:793
  506.8 51.7 %collective-permute-start.29 = (bf16[512,1024]{1,0:T(8,128)(2,1)}, bf16[512,1024]{1,0:T(8,128)(2,1)}, u32[]{:S(2)}, u32[]{:S(2)}) collective-permute-start(bf16[512,1024]{1,0:T(8,128)(2,1)} %get-tuple-element.90.refs_2_), channel_id=1, source_target_pairs={{0,4},{4,0},{1,5},{5,1},{2,6},{6,2},{3,7},{7,3},{8,12},{12,8},{9,1... | collective-permute-start | bytes 3145736 | tf_op jit(solution)/shard_map/ppermute | solution.py:784
  510.9 92.1 %reduce-scatter.14.cloned.1.call-start = ((), (), s32[]{:S(2)}) async-start(), calls=%async_computation.16 | async-start | bytes 1310720 | tf_op jit(solution)/shard_map/reduce_scatter | solution.py:793
  563.0 84.6 %reduce-scatter.16.cloned.1.call-start = ((), (), s32[]{:S(2)}) async-start(), calls=%async_computation.17 | async-start | bytes 1638400 | tf_op jit(solution)/shard_map/reduce_scatter | solution.py:793
  584.9 36.4 %collective-permute-start.30 = (bf16[384,2048]{1,0:T(8,128)(2,1)}, bf16[384,2048]{1,0:T(8,128)(2,1)S(1)}, u32[]{:S(2)}, u32[]{:S(2)}) collective-permute-start(bf16[384,2048]{1,0:T(8,128)(2,1)} %get-tuple-element.97), channel_id=1, source_target_pairs={{0,1},{1,0},{2,3},{3,2},{4,5},{5,4},{6,7},{7,6},{8,9},{9,8},{10,11... | collective-permute-start | bytes 4718600 | tf_op jit(solution)/shard_map/ppermute | solution.py:805
  (128 other events, 1656.1 us)
Sparse Core Ops, SparseCore 0:
  10.6 36.5 all-gather.6
  49.4 28.0 all-gather.8
  79.7 51.1 all-gather.10
  132.4 50.5 all-gather.12
  184.4 50.5 all-gather.14
  245.6 36.9 all-gather.16
  301.9 47.7 reduce-scatter.7
  352.0 47.5 reduce-scatter.9
  421.5 46.6 reduce-scatter.17
  472.6 47.1 reduce-scatter.19
  522.7 34.7 reduce-scatter.11
  563.1 25.9 reduce-scatter.13
  610.5 29.8 reduce-scatter.15
